TPU v7x, 32 devices: a whole 2x2x4 slice. The times are simulated.
32 devices in a mesh: sp: 8 (over z, y), fsdp: 4 (over x, core).
Axes of the slice: x: 2, y: 2, z: 4, core: 2. Of those that a mesh axis runs over, the one named last changes fastest.
Arguments:
- tokens: bfloat16 [4, 2048, 2048], P('fsdp', 'sp'), may hold values from -6 to 6
- doc_lengths: int32 [4, 4], P('fsdp'), may hold values from 1 to 1536, 2048 in all within a row
- expert_ids: int32 [4, 2048, 8], P('fsdp', 'sp'), may hold values from 0 to 63, all different within a row; in each aligned block of 256 rows (0 to 255, 256 to 511, ..., all dimensions but the last counted through in order) at most 64 rows name the same one
- norm_attn: bfloat16 [2048], P('fsdp'), may hold values from 0.5 to 1.5
- norm_query: bfloat16 [2048], P('fsdp'), may hold values from 0.5 to 1.5
- norm_key: bfloat16 [2048], P('fsdp'), may hold values from 0.5 to 1.5
- norm_ffn: bfloat16 [2048], P('fsdp'), may hold values from 0.5 to 1.5
- w_query: bfloat16 [2048, 2048], P('fsdp'), may hold values from -0.125 to 0.125
- w_key: bfloat16 [2048, 2048], P('fsdp'), may hold values from -0.125 to 0.125
- w_value: bfloat16 [2048, 2048], P('fsdp'), may hold values from -0.125 to 0.125
- w_out: bfloat16 [2048, 2048], P('fsdp'), may hold values from -4 to 4
- w_router: bfloat16 [2048, 64], P('fsdp'), may hold values from -0.0625 to 0.0625
- w_gate: bfloat16 [64, 2048, 1024], P('sp', None, 'fsdp'), may hold values from -0.125 to 0.125
- w_up: bfloat16 [64, 2048, 1024], P('sp', None, 'fsdp'), may hold values from -0.125 to 0.125
- w_down: bfloat16 [64, 2048, 1024], P('sp', None, 'fsdp'), may hold values from -6 to 6
- cotangent: bfloat16 [4, 2048, 2048], P('fsdp', 'sp'), may hold values from -6 to 6
Outputs:
- mixed: bfloat16 [4, 2048, 2048], P('fsdp', 'sp')
- grad_tokens: float32 [4, 2048, 2048], P('fsdp', 'sp')
- grad_norm_attn: float32 [2048], P('fsdp')
- grad_norm_query: float32 [2048], P('fsdp')
- grad_norm_key: float32 [2048], P('fsdp')
- grad_norm_ffn: float32 [2048], P('fsdp')
- grad_query: float32 [2048, 2048], P('fsdp')
- grad_key: float32 [2048, 2048], P('fsdp')
- grad_value: float32 [2048, 2048], P('fsdp')
- grad_out: float32 [2048, 2048], P('fsdp')
- grad_router: float32 [2048, 64], P('fsdp')
- grad_gate: float32 [64, 2048, 1024], P('sp', None, 'fsdp')
- grad_up: float32 [64, 2048, 1024], P('sp', None, 'fsdp')
- grad_down: float32 [64, 2048, 1024], P('sp', None, 'fsdp')
Inputs may be any that keep to these rules, and one draw needn't show every extreme that they name: `expert_ids`: in the rows of one device, no expert is named by more than 64 of them, and in every draw some expert is named by exactly 64 rows of some device.
All inputs are finite; a program needn't handle non-finite values.
Results may differ from a plain program's by a relative error of at most 0.024.
Values may be sent and summed in bfloat16 or wider, within the bound.
A program may use at most 512 MiB of HBM per device.

v0:
```python
import jax
import jax.numpy as jnp
from jax import lax
from jax.sharding import PartitionSpec as P

HEADS = 16
HEAD_DIM = 128
EXPERTS = 64
TOPK = 8
WINDOW = 1024


eps = 1e-05
rope_base = 10000.0
masked_score = -1e30


def rms_scale(values, gain_vec):
    return values * lax.rsqrt(jnp.mean(values * values, axis=-1, keepdims=True) + eps) * gain_vec


def rotate_pairs(values, cosine, sine):
    half_dim = values.shape[-1] // 2
    turned = jnp.concatenate([-values[..., half_dim:], values[..., :half_dim]], axis=-1)
    return values * cosine + turned * sine


def rope_tables(positions, head_size):
    inv_freq = rope_base ** (-jnp.arange(0, head_size, 2, dtype=jnp.float32) / head_size)
    phase_half = positions.astype(jnp.float32)[:, None] * inv_freq[None, :]
    phase_all = jnp.concatenate([phase_half, phase_half], axis=-1)
    return (jnp.cos(phase_all)[:, None, :], jnp.sin(phase_all)[:, None, :])


def segment_ids(lengths_row, seq_rows):
    doc_ends = jnp.cumsum(lengths_row)
    positions = jnp.arange(seq_rows, dtype=jnp.int32)
    return jnp.sum((positions[:, None] >= doc_ends[None, :]).astype(jnp.int32), axis=1)


def window_geometry(seq_rows):
    block_rows = min(512, seq_rows)
    key_blocks = 1 + (WINDOW - 1 + block_rows - 1) // block_rows
    return (
        block_rows,
        seq_rows // block_rows,
        key_blocks * block_rows,
        (key_blocks - 1) * block_rows,
    )


def window_allowed(segments, seg_padded, first_row, block_rows, key_rows, pad_rows):
    query_pos = first_row + jnp.arange(block_rows, dtype=jnp.int32)
    key_pos = first_row - pad_rows + jnp.arange(key_rows, dtype=jnp.int32)
    query_seg = lax.dynamic_slice_in_dim(segments, first_row, block_rows)
    key_seg = lax.dynamic_slice_in_dim(seg_padded, first_row, key_rows)
    distance = query_pos[:, None] - key_pos[None, :]
    return (query_seg[:, None] == key_seg[None, :]) & (distance >= 0) & (distance < WINDOW)


def pad_front(values, pad_rows, filler):
    return jnp.concatenate(
        [jnp.full((pad_rows,) + values.shape[1:], filler, values.dtype), values], axis=0
    )


def local(
    tokens,
    doc_lengths,
    expert_ids,
    norm_attn,
    norm_query,
    norm_key,
    norm_ffn,
    w_query,
    w_key,
    w_value,
    w_out,
    w_router,
    w_gate,
    w_up,
    w_down,
    cotangent,
):
    sp_count = lax.axis_size("sp")
    fs_count = lax.axis_size("fsdp")
    hidden_in = tokens[0].astype(jnp.float32)
    tok_rows = hidden_in.shape[0]
    width = hidden_in.shape[1]
    head_local = HEADS // sp_count
    seq_rows = tok_rows * sp_count
    slot_most = max(2, 2 * tok_rows * TOPK // EXPERTS)
    capacity = 5 * seq_rows * fs_count * TOPK // (4 * EXPERTS)
    local_experts = EXPERTS // sp_count
    gathered = (
        lax.all_gather(norm_attn, "fsdp", axis=0, tiled=True),
        lax.all_gather(norm_query, "fsdp", axis=0, tiled=True),
        lax.all_gather(norm_key, "fsdp", axis=0, tiled=True),
        lax.all_gather(norm_ffn, "fsdp", axis=0, tiled=True),
        lax.all_gather(w_query, "fsdp", axis=0, tiled=True),
        lax.all_gather(w_key, "fsdp", axis=0, tiled=True),
        lax.all_gather(w_value, "fsdp", axis=0, tiled=True),
        lax.all_gather(w_out, "fsdp", axis=0, tiled=True),
        lax.all_gather(w_router, "fsdp", axis=0, tiled=True),
        lax.all_gather(w_gate, "fsdp", axis=2, tiled=True),
        lax.all_gather(w_up, "fsdp", axis=2, tiled=True),
        lax.all_gather(w_down, "fsdp", axis=2, tiled=True),
    )
    (
        gain_attn,
        gain_query,
        gain_key,
        gain_ffn,
        query_mat,
        key_mat,
        value_mat,
        out_mat,
        router_mat,
        gate_full,
        up_full,
        down_full,
    ) = gathered
    attn_normed, attn_pull = jax.vjp(rms_scale, hidden_in, gain_attn.astype(jnp.float32))
    attn_in = attn_normed.astype(jnp.bfloat16)
    query_raw = jnp.dot(attn_in, query_mat, preferred_element_type=jnp.float32)
    key_raw = jnp.dot(attn_in, key_mat, preferred_element_type=jnp.float32)
    value_rows = jnp.dot(attn_in, value_mat, preferred_element_type=jnp.float32).astype(
        jnp.bfloat16
    )
    cosine, sine = rope_tables(
        lax.axis_index("sp") * tok_rows + jnp.arange(tok_rows, dtype=jnp.int32), HEAD_DIM
    )

    def head_path(raw_proj, gain_vec):
        return rotate_pairs(
            rms_scale(raw_proj, gain_vec).reshape(tok_rows, HEADS, HEAD_DIM), cosine, sine
        )

    query_rot, query_pull = jax.vjp(head_path, query_raw, gain_query.astype(jnp.float32))
    key_rot, key_pull = jax.vjp(head_path, key_raw, gain_key.astype(jnp.float32))
    query_heads, key_heads, value_heads = (
        lax.all_to_all(
            query_rot.astype(jnp.bfloat16), "sp", split_axis=1, concat_axis=0, tiled=True
        ),
        lax.all_to_all(key_rot.astype(jnp.bfloat16), "sp", split_axis=1, concat_axis=0, tiled=True),
        lax.all_to_all(
            value_rows.reshape(tok_rows, HEADS, HEAD_DIM),
            "sp",
            split_axis=1,
            concat_axis=0,
            tiled=True,
        ),
    )
    block_rows, block_count, key_rows, pad_rows = window_geometry(seq_rows)
    segments = segment_ids(doc_lengths[0], seq_rows)
    seg_padded = pad_front(segments, pad_rows, -1)
    key_padded = pad_front(key_heads, pad_rows, 0.0)
    value_padded = pad_front(value_heads, pad_rows, 0.0)
    score_scale = HEAD_DIM ** (-0.5)
    block_numbers = jnp.arange(block_count, dtype=jnp.int32)

    def block_scores(first_row):
        query_block = lax.dynamic_slice_in_dim(query_heads, first_row, block_rows)
        key_block = lax.dynamic_slice_in_dim(key_padded, first_row, key_rows)
        scores = (
            jnp.einsum("qhd,khd->hqk", query_block, key_block, preferred_element_type=jnp.float32)
            * score_scale
        )
        allowed = window_allowed(segments, seg_padded, first_row, block_rows, key_rows, pad_rows)
        return (jnp.where(allowed[None], scores, masked_score), query_block, key_block)

    def forward_block(carry_in, block_index):
        first_row = block_index * block_rows
        scores, query_block, key_block = block_scores(first_row)
        value_block = lax.dynamic_slice_in_dim(value_padded, first_row, key_rows)
        row_max = jnp.max(scores, axis=-1, keepdims=True)
        weights = jnp.exp(scores - row_max)
        row_total = jnp.sum(weights, axis=-1, keepdims=True)
        probs = (weights / row_total).astype(jnp.bfloat16)
        attended = jnp.einsum(
            "hqk,khd->qhd", probs, value_block, preferred_element_type=jnp.float32
        )
        return (carry_in, (attended.astype(jnp.bfloat16), (row_max + jnp.log(row_total))[..., 0]))

    _, (attended_blocks, lse_blocks) = lax.scan(forward_block, 0, block_numbers)
    attended_heads = attended_blocks.reshape(seq_rows, head_local, HEAD_DIM)
    attended_tok = lax.all_to_all(
        attended_heads, "sp", split_axis=0, concat_axis=1, tiled=True
    ).reshape(tok_rows, width)
    after_attn = hidden_in + jnp.dot(attended_tok, out_mat, preferred_element_type=jnp.float32)
    ffn_normed, ffn_pull = jax.vjp(rms_scale, after_attn, gain_ffn.astype(jnp.float32))
    ffn_in = ffn_normed.astype(jnp.bfloat16)
    logits = jnp.dot(ffn_in, router_mat, preferred_element_type=jnp.float32)
    router = jax.nn.softmax(logits, axis=-1)
    route_ids = expert_ids[0]
    chosen = route_ids[:, :, None] == jnp.arange(EXPERTS, dtype=jnp.int32)[None, None, :]
    chosen_float = chosen.astype(jnp.float32)
    gates = jnp.einsum("tke,te->tk", chosen_float, router)
    onehot_pairs = chosen.astype(jnp.int32).reshape(tok_rows * TOPK, EXPERTS)
    running = jnp.cumsum(onehot_pairs, axis=0)
    pair_rank = jnp.sum((running - 1) * onehot_pairs, axis=1)
    every_count = lax.all_gather(running[-1:], ("sp", "fsdp"), axis=0, tiled=True)
    count_grid = every_count.reshape(sp_count, fs_count, EXPERTS)
    fs_line = jnp.arange(fs_count, dtype=jnp.int32)[None, :]
    sp_line = jnp.arange(sp_count, dtype=jnp.int32)[:, None]
    my_fs = lax.axis_index("fsdp")
    earlier = (fs_line < my_fs) | (fs_line == my_fs) & (sp_line < lax.axis_index("sp"))
    prefix = jnp.sum(count_grid * earlier[:, :, None].astype(jnp.int32), axis=(0, 1))
    place = jnp.sum(onehot_pairs * prefix[None, :], axis=1) + pair_rank
    kept_pair = (place < capacity).astype(jnp.float32)
    pair_weight = kept_pair * gates.reshape(-1)
    slot_index = route_ids.reshape(-1) * slot_most + pair_rank
    token_of_pair = jnp.arange(tok_rows * TOPK, dtype=jnp.int32) // TOPK
    buffer_shape = (sp_count, local_experts, slot_most, width)
    send_rows = (
        jnp.zeros((EXPERTS * slot_most, width), jnp.bfloat16)
        .at[slot_index]
        .set(ffn_in[token_of_pair])
    )
    received = lax.all_to_all(
        send_rows.reshape(buffer_shape), "sp", split_axis=0, concat_axis=0, tiled=True
    )
    gate_pre = jnp.einsum("nemd,edf->nemf", received, gate_full, preferred_element_type=jnp.float32)
    up_pre = jnp.einsum("nemd,edf->nemf", received, up_full, preferred_element_type=jnp.float32)
    sigmoid_gate = jax.nn.sigmoid(gate_pre)
    silu_gate = gate_pre * sigmoid_gate
    act_rows = (silu_gate * up_pre).astype(jnp.bfloat16)
    expert_out = jnp.einsum(
        "nemf,edf->nemd", act_rows, down_full, preferred_element_type=jnp.float32
    ).astype(jnp.bfloat16)
    returned = lax.all_to_all(expert_out, "sp", split_axis=0, concat_axis=0, tiled=True).reshape(
        EXPERTS * slot_most, width
    )
    pair_out = returned[slot_index].reshape(tok_rows, TOPK, width)
    moe_sum = jnp.einsum(
        "tkd,tk->td",
        pair_out,
        pair_weight.reshape(tok_rows, TOPK),
        preferred_element_type=jnp.float32,
    )
    mixed = (after_attn + moe_sum).astype(jnp.bfloat16)
    upstream = cotangent[0].astype(jnp.float32)
    gate_grad = kept_pair.reshape(tok_rows, TOPK) * jnp.einsum(
        "tkd,td->tk", pair_out, upstream, preferred_element_type=jnp.float32
    )
    slot_grad = (upstream[:, None, :] * pair_weight.reshape(tok_rows, TOPK)[:, :, None]).astype(
        jnp.bfloat16
    )
    send_grad = (
        jnp.zeros((EXPERTS * slot_most, width), jnp.bfloat16)
        .at[slot_index]
        .set(slot_grad.reshape(-1, width))
    )
    out_grad = lax.all_to_all(
        send_grad.reshape(buffer_shape), "sp", split_axis=0, concat_axis=0, tiled=True
    )
    act_grad = jnp.einsum("nemd,edf->nemf", out_grad, down_full, preferred_element_type=jnp.float32)
    gate_pre_grad = (
        act_grad * up_pre * sigmoid_gate * (1.0 + gate_pre * (1.0 - sigmoid_gate))
    ).astype(jnp.bfloat16)
    up_pre_grad = (act_grad * silu_gate).astype(jnp.bfloat16)
    row_grad = jnp.einsum(
        "nemf,edf->nemd", gate_pre_grad, gate_full, preferred_element_type=jnp.float32
    )
    row_grad = (
        row_grad
        + jnp.einsum("nemf,edf->nemd", up_pre_grad, up_full, preferred_element_type=jnp.float32)
    ).astype(jnp.bfloat16)
    back_rows = lax.all_to_all(row_grad, "sp", split_axis=0, concat_axis=0, tiled=True).reshape(
        EXPERTS * slot_most, width
    )
    ffn_in_grad = jnp.sum(
        back_rows[slot_index].reshape(tok_rows, TOPK, width).astype(jnp.float32), axis=1
    )
    router_grad = jnp.einsum("tke,tk->te", chosen_float, gate_grad)
    logit_grad = (
        router * (router_grad - jnp.sum(router * router_grad, axis=-1, keepdims=True))
    ).astype(jnp.bfloat16)
    ffn_in_grad = ffn_in_grad + jnp.dot(
        logit_grad, router_mat.T, preferred_element_type=jnp.float32
    )
    router_term = jnp.dot(ffn_in.T, logit_grad, preferred_element_type=jnp.float32)
    ffn_hidden_grad, ffn_gain_term = ffn_pull(ffn_in_grad)
    after_grad = upstream + ffn_hidden_grad
    attn_out_grad = after_grad.astype(jnp.bfloat16)
    out_term = jnp.dot(attended_tok.T, attn_out_grad, preferred_element_type=jnp.float32)
    attended_grad = jnp.dot(attn_out_grad, out_mat.T, preferred_element_type=jnp.float32).astype(
        jnp.bfloat16
    )
    attended_grad_heads = lax.all_to_all(
        attended_grad.reshape(tok_rows, HEADS, HEAD_DIM),
        "sp",
        split_axis=1,
        concat_axis=0,
        tiled=True,
    )

    def backward_block(carry_in, block_index):
        key_total, value_total = carry_in
        first_row = block_index * block_rows
        scores, query_block, key_block = block_scores(first_row)
        value_block = lax.dynamic_slice_in_dim(value_padded, first_row, key_rows)
        grad_block = lax.dynamic_slice_in_dim(attended_grad_heads, first_row, block_rows)
        probs = jnp.exp(scores - lse_blocks[block_index][..., None])
        prob_grad = jnp.einsum(
            "qhd,khd->hqk", grad_block, value_block, preferred_element_type=jnp.float32
        )
        row_delta = jnp.sum(probs * prob_grad, axis=-1, keepdims=True)
        score_grad = (probs * (prob_grad - row_delta)).astype(jnp.bfloat16)
        query_part = (
            jnp.einsum("hqk,khd->qhd", score_grad, key_block, preferred_element_type=jnp.float32)
            * score_scale
        )
        key_part = (
            jnp.einsum("hqk,qhd->khd", score_grad, query_block, preferred_element_type=jnp.float32)
            * score_scale
        )
        value_part = jnp.einsum(
            "hqk,qhd->khd",
            probs.astype(jnp.bfloat16),
            grad_block,
            preferred_element_type=jnp.float32,
        )
        key_total = lax.dynamic_update_slice_in_dim(
            key_total,
            lax.dynamic_slice_in_dim(key_total, first_row, key_rows) + key_part,
            first_row,
            0,
        )
        value_total = lax.dynamic_update_slice_in_dim(
            value_total,
            lax.dynamic_slice_in_dim(value_total, first_row, key_rows) + value_part,
            first_row,
            0,
        )
        return ((key_total, value_total), query_part.astype(jnp.bfloat16))

    zero_keys = jnp.zeros((pad_rows + seq_rows, head_local, HEAD_DIM), jnp.float32)
    (key_total, value_total), query_blocks = lax.scan(
        backward_block, (zero_keys, zero_keys), block_numbers
    )
    query_grad_heads = query_blocks.reshape(seq_rows, head_local, HEAD_DIM)
    key_grad_heads = key_total[pad_rows:].astype(jnp.bfloat16)
    value_grad_heads = value_total[pad_rows:].astype(jnp.bfloat16)
    query_back, key_back, value_back = (
        lax.all_to_all(query_grad_heads, "sp", split_axis=0, concat_axis=1, tiled=True),
        lax.all_to_all(key_grad_heads, "sp", split_axis=0, concat_axis=1, tiled=True),
        lax.all_to_all(value_grad_heads, "sp", split_axis=0, concat_axis=1, tiled=True),
    )
    query_raw_grad, query_gain_term = query_pull(query_back.astype(jnp.float32))
    key_raw_grad, key_gain_term = key_pull(key_back.astype(jnp.float32))
    query_low = query_raw_grad.astype(jnp.bfloat16)
    key_low = key_raw_grad.astype(jnp.bfloat16)
    value_low = value_back.reshape(tok_rows, width)
    attn_in_grad = jnp.dot(query_low, query_mat.T, preferred_element_type=jnp.float32)
    attn_in_grad = attn_in_grad + jnp.dot(key_low, key_mat.T, preferred_element_type=jnp.float32)
    attn_in_grad = attn_in_grad + jnp.dot(
        value_low, value_mat.T, preferred_element_type=jnp.float32
    )
    query_term = jnp.dot(attn_in.T, query_low, preferred_element_type=jnp.float32)
    key_term = jnp.dot(attn_in.T, key_low, preferred_element_type=jnp.float32)
    value_term = jnp.dot(attn_in.T, value_low, preferred_element_type=jnp.float32)
    attn_hidden_grad, attn_gain_term = attn_pull(attn_in_grad)
    grad_tokens = after_grad + attn_hidden_grad
    rows_in = lax.all_gather(received, "fsdp", axis=0, tiled=True)
    rows_grad = lax.all_gather(out_grad, "fsdp", axis=0, tiled=True)
    gate_part = jnp.einsum("nemd,edf->nemf", rows_in, w_gate, preferred_element_type=jnp.float32)
    up_part = jnp.einsum("nemd,edf->nemf", rows_in, w_up, preferred_element_type=jnp.float32)
    sigmoid_part = jax.nn.sigmoid(gate_part)
    silu_part = gate_part * sigmoid_part
    act_part = (silu_part * up_part).astype(jnp.bfloat16)
    act_part_grad = jnp.einsum(
        "nemd,edf->nemf", rows_grad, w_down, preferred_element_type=jnp.float32
    )
    gate_part_grad = (
        act_part_grad * up_part * sigmoid_part * (1.0 + gate_part * (1.0 - sigmoid_part))
    ).astype(jnp.bfloat16)
    up_part_grad = (act_part_grad * silu_part).astype(jnp.bfloat16)
    grad_gate = jnp.einsum(
        "nemd,nemf->edf", rows_in, gate_part_grad, preferred_element_type=jnp.float32
    )
    grad_up = jnp.einsum(
        "nemd,nemf->edf", rows_in, up_part_grad, preferred_element_type=jnp.float32
    )
    grad_down = jnp.einsum(
        "nemd,nemf->edf", rows_grad, act_part, preferred_element_type=jnp.float32
    )
    scattered = (
        lax.psum_scatter(
            attn_gain_term.astype(jnp.bfloat16), "fsdp", scatter_dimension=0, tiled=True
        ).astype(jnp.float32),
        lax.psum_scatter(
            query_gain_term.astype(jnp.bfloat16), "fsdp", scatter_dimension=0, tiled=True
        ).astype(jnp.float32),
        lax.psum_scatter(
            key_gain_term.astype(jnp.bfloat16), "fsdp", scatter_dimension=0, tiled=True
        ).astype(jnp.float32),
        lax.psum_scatter(
            ffn_gain_term.astype(jnp.bfloat16), "fsdp", scatter_dimension=0, tiled=True
        ).astype(jnp.float32),
        lax.psum_scatter(
            query_term.astype(jnp.bfloat16), "fsdp", scatter_dimension=0, tiled=True
        ).astype(jnp.float32),
        lax.psum_scatter(
            key_term.astype(jnp.bfloat16), "fsdp", scatter_dimension=0, tiled=True
        ).astype(jnp.float32),
        lax.psum_scatter(
            value_term.astype(jnp.bfloat16), "fsdp", scatter_dimension=0, tiled=True
        ).astype(jnp.float32),
        lax.psum_scatter(
            out_term.astype(jnp.bfloat16), "fsdp", scatter_dimension=0, tiled=True
        ).astype(jnp.float32),
        lax.psum_scatter(
            router_term.astype(jnp.bfloat16), "fsdp", scatter_dimension=0, tiled=True
        ).astype(jnp.float32),
    )
    summed = (
        lax.psum(scattered[0].astype(jnp.bfloat16), "sp").astype(jnp.float32),
        lax.psum(scattered[1].astype(jnp.bfloat16), "sp").astype(jnp.float32),
        lax.psum(scattered[2].astype(jnp.bfloat16), "sp").astype(jnp.float32),
        lax.psum(scattered[3].astype(jnp.bfloat16), "sp").astype(jnp.float32),
        lax.psum(scattered[4].astype(jnp.bfloat16), "sp").astype(jnp.float32),
        lax.psum(scattered[5].astype(jnp.bfloat16), "sp").astype(jnp.float32),
        lax.psum(scattered[6].astype(jnp.bfloat16), "sp").astype(jnp.float32),
        lax.psum(scattered[7].astype(jnp.bfloat16), "sp").astype(jnp.float32),
        lax.psum(scattered[8].astype(jnp.bfloat16), "sp").astype(jnp.float32),
    )
    return (
        mixed[None],
        grad_tokens[None],
        summed[0],
        summed[1],
        summed[2],
        summed[3],
        summed[4],
        summed[5],
        summed[6],
        summed[7],
        summed[8],
        grad_gate,
        grad_up,
        grad_down,
    )


def solution(mesh):
    in_specs = (
        P("fsdp", "sp", None),
        P("fsdp", None),
        P("fsdp", "sp", None),
        P("fsdp"),
        P("fsdp"),
        P("fsdp"),
        P("fsdp"),
        P("fsdp", None),
        P("fsdp", None),
        P("fsdp", None),
        P("fsdp", None),
        P("fsdp", None),
        P("sp", None, "fsdp"),
        P("sp", None, "fsdp"),
        P("sp", None, "fsdp"),
        P("fsdp", "sp", None),
    )
    out_specs = (
        P("fsdp", "sp", None),
        P("fsdp", "sp", None),
        P("fsdp"),
        P("fsdp"),
        P("fsdp"),
        P("fsdp"),
        P("fsdp", None),
        P("fsdp", None),
        P("fsdp", None),
        P("fsdp", None),
        P("fsdp", None),
        P("sp", None, "fsdp"),
        P("sp", None, "fsdp"),
        P("sp", None, "fsdp"),
    )
    return jax.shard_map(local, mesh=mesh, in_specs=in_specs, out_specs=out_specs, check_vma=False)
```

profile of v0, /device:TPU:0, one launch (start us, length us, event | category | flops | bytes accessed | tf_op | source)
XLA Modules:
  0.0 4043.3 jit_solution(2915207460606974093)
XLA Ops:
  11.2 6.1 all-gather
  29.1 41.6 %all-gather.15.cloned.1.call-done = bf16[2048,2048]{1,0:T(8,128)(2,1)} async-done(((bf16[512,2048]{1,0:T(8,128)(2,1)}), bf16[2048,2048]{1,0:T(8,128)(2,1)}) %all-gather.15.cloned.1.call-update) | async-done | bytes 8388624 | tf_op jit(solution)/shard_map/all_gather | solution.py:102
  70.6 5.8 fusion.148
  77.7 5.5 all-to-all-start
  83.2 47.3 %all-gather.19.cloned.1.call-done = bf16[2048,2048]{1,0:T(8,128)(2,1)} async-done(((bf16[512,2048]{1,0:T(8,128)(2,1)}), bf16[2048,2048]{1,0:T(8,128)(2,1)}) %all-gather.19.cloned.1.call-update) | async-done | bytes 8388624 | tf_op jit(solution)/shard_map/all_gather | solution.py:101
  130.5 7.1 multiply_reduce_fusion.6
  137.6 52.8 %all-gather.17.cloned.1.call-done = bf16[2048,2048]{1,0:T(8,128)(2,1)} async-done(((bf16[512,2048]{1,0:T(8,128)(2,1)}), bf16[2048,2048]{1,0:T(8,128)(2,1)}) %all-gather.17.cloned.1.call-update) | async-done | bytes 8388624 | tf_op jit(solution)/shard_map/all_gather | solution.py:100
  190.4 6.0 multiply_reduce_fusion.7
  201.9 31.6 all_to_all.140
  244.2 18.1 reduce-window.19
  273.8 43.4 %while.30 = (s32[]{:T(128)}, bf16[4,512,2,128]{3,1,0,2:T(8,128)(2,1)}, f32[4,2,512]{2,1,0:T(2,128)}, s32[4]{0:T(128)S(1)}, bf16[3072,2,128]{2,0,1:T(8,128)(2,1)}...) while((s32[]{:T(128)}, ...), condition=%wide.region_8.9_spmd, body=%wide.region_5.8_spmd.sunk | while | flops 829031424 | bytes 31531316 | solution.py:185
  321.2 6.0 all-to-all-start.3
  328.3 52.1 %all-gather.4 = s32[32,1,64]{2,1,0:T(1,128)S(1)} all-gather(s32[1,1,64]{2,1,0:T(1,128)S(1)} %slice_bitcast_fusion), channel_id=1, replica_groups=mesh['sp'=8,'fsdp'=4] {'sp','fsdp'}, dimensions={0}, use_global_device_ids=true | all-gather | bytes 8448 | tf_op jit(solution)/shard_map/all_gather | solution.py:202
  386.5 6.2 multiply_reduce_fusion.5
  394.2 60.7 %scatter_custom_fusion = bf16[4096,2048]{1,0:T(8,128)(2,1)} fusion(s32[2048]{0:T(1024)S(1)} %bitcast.535, bf16[256,2048]{1,0:T(8,128)(2,1)S(1)} %multiply_convert_fusion.1, s32[2048]{0:T(1024)S(1)} %broadcast_clamp_fusion.1, bf16[]{:T(256)} %constant.193.clone.1), kind=kCustom, calls=%fused_computation.129 | custom fusion | bytes 16777218 | tf_op jit(solution)/shard_map/scatter | solution.py:218
  454.9 371.2 %all_to_all.141 = bf16[8,8,64,2048]{3,2,1,0:T(8,128)(2,1)} all-to-all(bf16[8,8,64,2048]{3,2,1,0:T(8,128)(2,1)} %bitcast.485), channel_id=1, replica_groups=mesh['sp'=8,'fsdp'=4] {'sp'}, dimensions={0} | all-to-all | bytes 33554432 | tf_op jit(solution)/shard_map/all_to_all | solution.py:220
  826.2 32.0 fusion.44
  858.1 32.9 fusion.48
  891.0 35.1 convert_bitcast_fusion
  926.2 14.1 copy.212
  940.3 6.0 all-to-all-start.5
  946.6 5.8 all_gather.57
  956.3 352.5 %all-to-all-done.5 = bf16[8,8,64,2048]{3,2,1,0:T(8,128)(2,1)} async-done(((bf16[8,8,64,2048]{3,2,1,0:T(8,128)(2,1)}), bf16[8,8,64,2048]{3,2,1,0:T(8,128)(2,1)}, u32[]{:S(2)}, u32[]{:S(2)}) %all-to-all-start.5) | async-done | bytes 16777248 | tf_op jit(solution)/shard_map/all_to_all | solution.py:231
  1308.8 24.4 gather_fusion
  1333.1 8.7 fusion.97
  1342.6 22.8 scatter_custom_fusion.1
  1365.4 369.1 %all_to_all.142 = bf16[8,8,64,2048]{3,2,1,0:T(8,128)(2,1)} all-to-all(bf16[8,8,64,2048]{3,2,1,0:T(8,128)(2,1)} %bitcast.484), channel_id=1, replica_groups=mesh['sp'=8,'fsdp'=4] {'sp'}, dimensions={0} | all-to-all | bytes 33554432 | tf_op jit(solution)/shard_map/all_to_all | solution.py:254
  1734.6 32.0 fusion.50
  1766.5 40.2 fusion.42
  1806.7 51.6 %fusion.77 = bf16[8,8,64,2048]{3,2,0,1:T(8,128)(2,1)} fusion(f32[8,8,64,2048]{3,2,1,0:T(8,128)} %fusion.42, bf16[8,2048,1024]{2,1,0:T(8,128)(2,1)} %all-gather.23.cloned.1.call-done, f32[8,8,64,1024]{3,2,1,0:T(8,128)} %fusion.50, f32[8,8,64,1024]{3,2,1,0:T(8,128)} %fusion.44, f32[8,8,64,1024]{3,2,1,0:T(8,128)} %fusion.48), kind=kOutput, calls=%fused_computation.114 | convolution fusion | flops 17238589440 | bytes 134217728 | tf_op jit(solution)/shard_map/nemf,edf->nemd/dot_general | solution.py:262
  1858.3 14.2 copy.215
  1872.5 6.0 all-to-all-start.7
  1879.3 7.0 fusion.99
  1886.3 353.3 %all-to-all-done.7 = bf16[8,8,64,2048]{3,2,1,0:T(8,128)(2,1)} async-done(((bf16[8,8,64,2048]{3,2,1,0:T(8,128)(2,1)}), bf16[8,8,64,2048]{3,2,1,0:T(8,128)(2,1)}, u32[]{:S(2)}, u32[]{:S(2)}) %all-to-all-start.7) | async-done | bytes 16777248 | tf_op jit(solution)/shard_map/all_to_all | solution.py:269
  2239.7 24.4 gather_fusion.1
  2264.1 11.5 convert_reduce_fusion
  2292.5 5.7 convolution_convert_fusion
  2298.2 17.1 all-to-all-done.8
  2323.7 180.2 %while.31 = (s32[]{:T(128)}, f32[3072,2,128]{2,1,0:T(2,128)}, f32[3072,2,128]{2,1,0:T(2,128)}, bf16[4,512,2,128]{3,1,0,2:T(8,128)(2,1)}, s32[4]{0:T(128)S(1)}, /...) while((s32[]{:T(128)}, f32[3072,2,128]{2,1,0:T(2,128)}, ...), condition=%wide.region_24.25_spmd, body=%wide.region_22.24_spmd.sunk | while | flops 2033583104 | bytes 129036768 | solution.py:339
  2352.1 5.6 multiply_convert_fusion.3
  2510.5 9.5 copy.219
  2520.0 16.6 all-to-all-done.10
  2541.0 25.4 all-to-all-done.9
  2575.6 5.9 convolution_convert_fusion.3
  2586.8 7.2 convolution_convert_fusion.2
  2596.1 29.8 all_to_all.143
  2626.6 5.8 convolution_convert_fusion.1
  2632.4 14.2 copy.210
  2651.4 75.1 %reduce-scatter.8.cloned.1.call-done = bf16[512,2048]{1,0:T(8,128)(2,1)} async-done(((bf16[2048,2048]{1,0:T(8,128)(2,1)}), bf16[512,2048]{1,0:T(8,128)(2,1)}) %reduce-scatter.8.cloned.1.call-update) | async-done | bytes 2097168 | tf_op jit(solution)/shard_map/reduce_scatter | solution.py:404
  2726.5 74.2 %reduce-scatter.10.cloned.1.call-done = bf16[512,2048]{1,0:T(8,128)(2,1)} async-done(((bf16[2048,2048]{1,0:T(8,128)(2,1)}), bf16[512,2048]{1,0:T(8,128)(2,1)}) %reduce-scatter.10.cloned.1.call-update) | async-done | bytes 2097168 | tf_op jit(solution)/shard_map/reduce_scatter | solution.py:407
  2801.2 15.9 copy.214
  2819.0 8.8 fusion.193
  2827.8 7.9 convolution_add_fusion.2
  2840.3 11.2 all-reduce.13
  2851.8 21.4 all-reduce.11
  2879.0 316.9 %all-gather.29.cloned.1.call-done = bf16[32,8,64,2048]{3,2,0,1:T(8,128)(2,1)} async-done(((bf16[8,8,64,2048]{3,2,0,1:T(8,128)(2,1)}), bf16[32,8,64,2048]{3,2,0,1:T(8,128)(2,1)}) %all-gather.29.cloned.1.call-update) | async-done | bytes 67108880 | tf_op jit(solution)/shard_map/all_gather | solution.py:365
  3195.9 34.3 fusion.91
  3230.2 34.0 fusion.93
  3264.2 211.5 %all-reduce.16.cloned.1.call-done = (bf16[512,2048]{1,0:T(8,128)(2,1)}, bf16[512,2048]{1,0:T(8,128)(2,1)}, bf16[512,2048]{1,0:T(8,128)(2,1)}, bf16[512,2048]{1,0:T(8,128)(2,1)}, bf16[512,64]{0,1:T(8,128)(2,1)}) async-done(((bf16[512,2048]{1,0:T(8,128)(2,1)}, bf16[512,2048]{1,0:T(8,128)(2,1)}, bf16[512,2048]{1,0:T(8,128)(2,1)}, bf16[512,2048]{1,0:T(8,128)(2,1)}, bf16[512,64]{0,1:T(8,128)(2,1)}), ...) | async-done | bytes 8454160 | tf_op jit(solution)/shard_map/psum | solution.py:422
  3489.9 379.5 %all-gather.31.cloned.1.call-done = bf16[32,8,64,2048]{3,2,0,1:T(8,128)(2,1)} async-done(((bf16[8,8,64,2048]{3,2,0,1:T(8,128)(2,1)}), bf16[32,8,64,2048]{3,2,0,1:T(8,128)(2,1)}) %all-gather.31.cloned.1.call-update) | async-done | bytes 67108880 | tf_op jit(solution)/shard_map/all_gather | solution.py:366
  3869.5 33.3 fusion.95
  3902.7 42.7 %fusion.115 = f32[8,2048,256]{2,1,0:T(8,128)} fusion(bf16[32,8,64,2048]{3,2,0,1:T(8,128)(2,1)} %all-gather.29.cloned.1.call-done, f32[8,32,64,256]{3,2,1,0:T(8,128)} %fusion.95, f32[8,32,64,256]{3,2,1,0:T(8,128)} %fusion.91), kind=kOutput, calls=%fused_computation.143 | convolution fusion | flops 17205035008 | bytes 117440512 | tf_op jit(solution)/shard_map/nemd,nemf->edf/dot_general | solution.py:382
  3945.5 47.8 %fusion.109 = f32[8,2048,256]{2,1,0:T(8,128)} fusion(bf16[32,8,64,2048]{3,2,0,1:T(8,128)(2,1)} %all-gather.29.cloned.1.call-done, f32[8,32,64,256]{3,2,1,0:T(8,128)} %fusion.91, f32[8,32,64,256]{3,2,1,0:T(8,128)} %fusion.93, f32[8,32,64,256]{3,2,1,0:T(8,128)} %fusion.95), kind=kOutput, calls=%fused_computation.141 | convolution fusion | flops 17221812224 | bytes 134217728 | tf_op jit(solution)/shard_map/nemd,nemf->edf/dot_general | solution.py:379
  3993.2 43.1 %fusion.112 = f32[8,2048,256]{2,1,0:T(8,128)} fusion(bf16[32,8,64,2048]{3,2,0,1:T(8,128)(2,1)} %all-gather.31.cloned.1.call-done, f32[8,32,64,256]{3,2,1,0:T(8,128)} %fusion.93, f32[8,32,64,256]{3,2,1,0:T(8,128)} %fusion.91), kind=kOutput, calls=%fused_computation.142 | convolution fusion | flops 17205035008 | bytes 117440512 | tf_op jit(solution)/shard_map/nemd,nemf->edf/dot_general | solution.py:385
  (532 shorter events, 351.3 us)
Async XLA Ops:
  7.2 63.5 %all-gather.15.cloned.1.call-start = ((), (), s32[]{:S(2)}) async-start(), calls=%async_computation.17 | async-start | bytes 10485760 | tf_op jit(solution)/shard_map/all_gather | solution.py:102
  7.9 122.6 %all-gather.19.cloned.1.call-start = ((), (), s32[]{:S(2)}) async-start(), calls=%async_computation.19 | async-start | bytes 10485760 | tf_op jit(solution)/shard_map/all_gather | solution.py:101
  8.7 181.7 %all-gather.17.cloned.1.call-start = ((), (), s32[]{:S(2)}) async-start(), calls=%async_computation.18 | async-start | bytes 10485760 | tf_op jit(solution)/shard_map/all_gather | solution.py:100
  9.4 377.0 %all-gather.21.cloned.1.call-start = ((), (), s32[]{:S(2)}) async-start(), calls=%async_computation.20 | async-start | bytes 10485760 | tf_op jit(solution)/shard_map/all_gather | solution.py:103
  10.0 816.2 %all-gather.25.cloned.1.call-start = ((), (), s32[]{:S(2)}) async-start(), calls=%async_computation.22 | async-start | bytes 41943040 | tf_op jit(solution)/shard_map/all_gather | solution.py:106
  10.6 12.2 copy-start.87
  10.6 18.1 copy-start.5
  10.6 847.5 %all-gather.23.cloned.1.call-start = ((), (), s32[]{:S(2)}) async-start(), calls=%async_computation.21 | async-start | bytes 41943040 | tf_op jit(solution)/shard_map/all_gather | solution.py:105
  17.4 173.0 %copy-start.44 = (f32[4,1,512]{2,1,0:T(1,128)}, f32[4,1,512]{2,1,0:T(1,128)S(1)}, u32[]{:S(2)}) copy-start(f32[4,1,512]{2,1,0:T(1,128)S(1)} %convert_element_type.339) | copy-start | bytes 24580
  22.8 173.7 %copy-start.49 = (f32[4,1,512]{2,1,0:T(1,128)}, f32[4,1,512]{2,1,0:T(1,128)S(1)}, u32[]{:S(2)}) copy-start(f32[4,1,512]{2,1,0:T(1,128)S(1)} %convert_element_type.341) | copy-start | bytes 24580
  28.0 168.5 %copy-start.51 = (f32[4,1,512]{2,1,0:T(1,128)}, f32[4,1,512]{2,1,0:T(1,128)S(1)}, u32[]{:S(2)}) copy-start(f32[4,1,512]{2,1,0:T(1,128)S(1)} %convert_element_type.340) | copy-start | bytes 24580
  28.7 171.0 %copy-start.38 = (f32[256,128]{1,0:T(8,128)}, f32[256,128]{1,0:T(8,128)S(1)}, u32[]{:S(2)}) copy-start(f32[256,128]{1,0:T(8,128)S(1)} %get-tuple-element.425) | copy-start | bytes 393220
  28.7 171.0 %copy-start.40 = (f32[256,128]{1,0:T(8,128)}, f32[256,128]{1,0:T(8,128)S(1)}, u32[]{:S(2)}) copy-start(f32[256,128]{1,0:T(8,128)S(1)} %get-tuple-element.426) | copy-start | bytes 393220
  29.0 47.4 %copy-start.77 = (f32[256]{0:T(256)}, f32[256]{0:T(256)S(1)}, u32[]{:S(2)}) copy-start(f32[256]{0:T(256)S(1)} %fusion.127) | copy-start | bytes 3076
  29.1 161.4 %copy-start.64 = (f32[256]{0:T(256)}, f32[256]{0:T(256)S(1)}, u32[]{:S(2)}) copy-start(f32[256]{0:T(256)S(1)} %fusion.169) | copy-start | bytes 3076
  77.7 124.2 %all-to-all-start = ((bf16[256,16,128]{2,0,1:T(8,128)(2,1)}), bf16[256,16,128]{2,0,1:T(8,128)(2,1)}, u32[]{:S(2)}, u32[]{:S(2)}) async-start(bf16[256,16,128]{2,0,1:T(8,128)(2,1)} %bitcast.462), calls=%async_computation | async-start | bytes 2097152 | tf_op jit(solution)/shard_map/all_to_all | solution.py:146
  137.6 58.8 %copy-start.81 = (f32[256]{0:T(256)}, f32[256]{0:T(256)S(1)}, u32[]{:S(2)}) copy-start(f32[256]{0:T(256)S(1)} %get-tuple-element.429) | copy-start | bytes 3076
  137.6 58.9 %copy-start.70 = (f32[256]{0:T(256)}, f32[256]{0:T(256)S(1)}, u32[]{:S(2)}) copy-start(f32[256]{0:T(256)S(1)} %fusion.171) | copy-start | bytes 3076
  233.5 36.3 all-to-all-start.2
  237.1 653.9 %all-gather.27.cloned.1.call-start = ((), (), s32[]{:S(2)}) async-start(), calls=%async_computation.23 | async-start | bytes 41943040 | tf_op jit(solution)/shard_map/all_gather | solution.py:107
  243.9 148.8 %copy-start.53 = (f32[4,1,512]{2,1,0:T(1,128)}, f32[4,1,512]{2,1,0:T(1,128)S(1)}, u32[]{:S(2)}) copy-start(f32[4,1,512]{2,1,0:T(1,128)S(1)} %convert_element_type.342) | copy-start | bytes 24580
  317.2 67.7 %copy-start.2 = (bf16[3072,2,128]{2,0,1:T(8,128)(2,1)}, bf16[3072,2,128]{2,0,1:T(8,128)(2,1)S(1)}, u32[]{:S(2)}) copy-start(bf16[3072,2,128]{2,0,1:T(8,128)(2,1)S(1)} %get-tuple-element.717) | copy-start | bytes 4718596
  317.2 67.7 %copy-start.46 = (s32[3072]{0:T(1024)}, s32[3072]{0:T(1024)S(1)}, u32[]{:S(2)}) copy-start(s32[3072]{0:T(1024)S(1)} %get-tuple-element.765) | copy-start | bytes 36868
  317.2 67.7 %copy-start.48 = (s32[2048]{0:T(1024)}, s32[2048]{0:T(1024)S(1)}, u32[]{:S(2)}) copy-start(s32[2048]{0:T(1024)S(1)} %get-tuple-element.766) | copy-start | bytes 24580
  321.2 61.4 %all-to-all-start.3 = ((bf16[2048,2,128]{2,1,0:T(2,128)(2,1)}), bf16[2048,2,128]{2,1,0:T(2,128)(2,1)}, u32[]{:S(2)}, u32[]{:S(2)}) async-start(bf16[2048,2,128]{2,1,0:T(2,128)(2,1)} %copy.201), calls=%async_computation.3 | async-start | bytes 2097152 | tf_op jit(solution)/shard_map/all_to_all | solution.py:187
  392.7 62.3 %copy-start.79 = (f32[256]{0:T(256)}, f32[256]{0:T(256)S(1)}, u32[]{:S(2)}) copy-start(f32[256]{0:T(256)S(1)} %get-tuple-element.433) | copy-start | bytes 3076
  392.7 62.3 %copy-start.75 = (f32[256]{0:T(256)}, f32[256]{0:T(256)S(1)}, u32[]{:S(2)}) copy-start(f32[256]{0:T(256)S(1)} %fusion.172) | copy-start | bytes 3076
  394.2 559.7 %copy-start.20 = (bf16[256,2048]{1,0:T(8,128)(2,1)}, bf16[256,2048]{1,0:T(8,128)(2,1)S(1)}, u32[]{:S(2)}) copy-start(bf16[256,2048]{1,0:T(8,128)(2,1)S(1)} %multiply_convert_fusion.1) | copy-start | bytes 3145732
  940.3 368.5 %all-to-all-start.5 = ((bf16[8,8,64,2048]{3,2,1,0:T(8,128)(2,1)}), bf16[8,8,64,2048]{3,2,1,0:T(8,128)(2,1)}, u32[]{:S(2)}, u32[]{:S(2)}) async-start(bf16[8,8,64,2048]{3,2,1,0:T(8,128)(2,1)} %copy.212), calls=%async_computation.5 | async-start | bytes 33554432 | tf_op jit(solution)/shard_map/all_to_all | solution.py:231
  946.6 9.7 copy-start.56
  952.4 356.4 %copy-start.58 = (s32[2048]{0:T(1024)}, s32[2048]{0:T(1024)S(1)}, u32[]{:S(2)}) copy-start(s32[2048]{0:T(1024)S(1)} %broadcast_clamp_fusion) | copy-start | bytes 24580
  1308.8 24.4 copy-start.22
  1342.5 22.9 copy-start.42
  1872.5 6.8 copy-start.43
  1872.5 367.1 %all-to-all-start.7 = ((bf16[8,8,64,2048]{3,2,1,0:T(8,128)(2,1)}), bf16[8,8,64,2048]{3,2,1,0:T(8,128)(2,1)}, u32[]{:S(2)}, u32[]{:S(2)}) async-start(bf16[8,8,64,2048]{3,2,1,0:T(8,128)(2,1)} %copy.215), calls=%async_computation.7 | async-start | bytes 33554432 | tf_op jit(solution)/shard_map/all_to_all | solution.py:269
  1879.3 360.3 %copy-start.59 = (s32[2048]{0:T(1024)S(1)}, s32[2048]{0:T(1024)}, u32[]{:S(2)}) copy-start(s32[2048]{0:T(1024)} %copy-done.58) | copy-start | bytes 24580
  2264.1 11.5 copy-start.8
  2264.1 11.5 copy-start.32
  2264.1 11.5 copy-start.54
  2264.1 11.5 copy-start.76
  2264.1 14.7 copy-start.23
  2284.1 8.4 copy-start.19
  2285.3 7.2 copy-start.11
  2285.3 30.0 all-to-all-start.8
  2289.7 357.0 %reduce-scatter.14.cloned.1.call-start = ((), (), s32[]{:S(2)}) async-start(), calls=%async_computation.28 | async-start | bytes 327680 | tf_op jit(solution)/shard_map/reduce_scatter | solution.py:413
  2292.4 354.3 %reduce-scatter.12.cloned.1.call-start = ((), (), s32[]{:S(2)}) async-start(), calls=%async_computation.27 | async-start | bytes 10485760 | tf_op jit(solution)/shard_map/reduce_scatter | solution.py:410
  2327.5 9.7 copy-start.3
  2373.1 9.6 copy-start.3
  2417.8 9.6 copy-start.3
  2462.6 9.6 copy-start.3
  2506.8 29.8 all-to-all-start.10
  2536.5 29.9 all-to-all-start.9
  2540.8 110.6 %reduce-scatter.6.cloned.1.call-start = ((), (), s32[]{:S(2)}) async-start(), calls=%async_computation.24 | async-start | bytes 10485760 | tf_op jit(solution)/shard_map/reduce_scatter | solution.py:401
  2581.5 144.9 %reduce-scatter.8.cloned.1.call-start = ((), (), s32[]{:S(2)}) async-start(), calls=%async_computation.25 | async-start | bytes 10485760 | tf_op jit(solution)/shard_map/reduce_scatter | solution.py:404
  2594.0 206.7 %reduce-scatter.10.cloned.1.call-start = ((), (), s32[]{:S(2)}) async-start(), calls=%async_computation.26 | async-start | bytes 10485760 | tf_op jit(solution)/shard_map/reduce_scatter | solution.py:407
  2632.4 563.5 %all-gather.29.cloned.1.call-start = ((), (), s32[]{:S(2)}) async-start(), calls=%async_computation.29 | async-start | bytes 83886080 | tf_op jit(solution)/shard_map/all_gather | solution.py:365
  2646.7 829.1 %all-reduce.16.cloned.1.call-start = ((), (), s32[]{:S(2)}) async-start(), calls=%async_computation.31 | async-start | bytes 16908288 | tf_op jit(solution)/shard_map/psum | solution.py:422
  2800.7 1068.8 %all-gather.31.cloned.1.call-start = ((), (), s32[]{:S(2)}) async-start(), calls=%async_computation.30 | async-start | bytes 83886080 | tf_op jit(solution)/shard_map/all_gather | solution.py:366
  2819.0 8.8 copy-start.28
  2819.0 16.8 slice-start.2
  2827.8 8.0 copy-start.30
  2827.8 8.4 slice-start.3
  2836.2 39.4 copy-start.78
  2836.2 39.4 copy-start.12
  (69 other events, 215.3 us)
Sparse Core Ops, SparseCore 0:
  9.6 61.0 all-gather.14
  72.2 58.2 all-gather.18
  132.1 58.2 all-gather.16
  191.8 58.3 all-gather.20
  251.7 206.1 all-gather.24
  459.3 206.0 all-gather.22
  666.9 206.0 all-gather.26
  2293.0 20.4 reduce-scatter.13
  2316.2 71.7 reduce-scatter.11
  2581.6 69.6 reduce-scatter.5
  2654.7 71.6 reduce-scatter.7
  2728.9 71.7 reduce-scatter.9
  2802.9 392.9 all-gather.28
  3201.5 274.1 all-reduce.15
  3477.8 391.6 all-gather.30
where the time goes:
time: 4060 us; the launch traced here: 4040 us
  waiting for transfers between devices  1970 us (49%)
  blocking collectives  914 us (23%)
  matrix products  635 us (16%)
  local copies, waits for them, and re-layouts  315 us (8%)
  other arithmetic  135 us (3%)
  starting transfers between devices  41.2 us (1%)
    all_gather x1, waiting for transfers between devices, local(): rows_grad = lax.all_gather(out_grad, 'fsdp', axis=0, tiled=True)  380 us
    all_to_all x1, blocking collectives, local(): lax.all_to_all(send_rows.reshape(buffer_shape), 'sp', split_axis=0, conca...  371 us
    all_to_all x1, blocking collectives, local(): lax.all_to_all(send_grad.reshape(buffer_shape), 'sp', split_axis=0, conca...  369 us
    all_to_all x1, waiting for transfers between devices, local(): lax.all_to_all(row_grad, 'sp', split_axis=0, concat_axis=0, tiled=True)  353 us
    all_to_all x1, waiting for transfers between devices, local(): lax.all_to_all(expert_out, 'sp', split_axis=0, concat_axis=0, tiled=True)  352 us
    all_gather x1, waiting for transfers between devices, local(): rows_in = lax.all_gather(received, 'fsdp', axis=0, tiled=True)  317 us
    psum x1, waiting for transfers between devices, local(): lax.psum(scattered[4].astype(jnp.bfloat16), 'sp').astype(jnp.float32)  211 us
  transfers between devices with their start and end apart: 23, of which 14 were waited for; matrix products, arithmetic and copies ran while one was open for 15% of the time, Pallas kernels for 0%

commit v1 on v0

--- a/solution.py
+++ b/solution.py
@@ -1,6 +1,8 @@
 import jax
 import jax.numpy as jnp
 from jax import lax
+from jax.experimental import pallas as pl
+from jax.experimental.pallas import tpu as pltpu
 from jax.sharding import PartitionSpec as P
 
 HEADS = 16
@@ -62,6 +64,405 @@
     return jnp.concatenate(
         [jnp.full((pad_rows,) + values.shape[1:], filler, values.dtype), values], axis=0
     )
+
+
+BLOCK = 256
+SLOTS = 64
+STEP = 16
+TILE = 256
+
+
+def exclusive_sum(values):
+    count = values.shape[0]
+    lower = (jnp.arange(count)[:, None] > jnp.arange(count)[None, :]).astype(jnp.float32)
+    total = jnp.dot(lower, values.astype(jnp.float32), precision=lax.Precision.HIGHEST)
+    return total.astype(jnp.int32)
+
+
+def route_plan(own_ids, sp_count, fs_count):
+    local_experts = EXPERTS // sp_count
+    ids = lax.all_gather(own_ids, ("fsdp", "sp"), axis=0, tiled=True)
+    tokens = ids.shape[0]
+    blocks = tokens // BLOCK
+    capacity = 5 * tokens * TOPK // (4 * EXPERTS)
+    first = lax.axis_index("sp") * local_experts
+    mine = first + jnp.arange(local_experts, dtype=jnp.int32)
+    named = jnp.any(ids[:, None, :] == mine[None, :, None], axis=-1)
+    named = named.reshape(blocks, BLOCK, local_experts)
+    upto = (jnp.arange(BLOCK)[:, None] >= jnp.arange(BLOCK)[None, :]).astype(jnp.bfloat16)
+    running = jnp.einsum(
+        "ts,bse->bte", upto, named.astype(jnp.bfloat16), preferred_element_type=jnp.float32
+    ).astype(jnp.int32)
+    earlier = exclusive_sum(running[:, -1])
+    keep = named & (earlier[:, None, :] + running - 1 < capacity)
+    rank = jnp.where(keep, running - 1, -1).transpose(0, 2, 1)
+    steps = (jnp.sum(keep.astype(jnp.int32), axis=1) + STEP - 1) // STEP
+    starts = exclusive_sum(steps)
+    used = starts[-1] + steps[-1]
+    slots_all = min(blocks * SLOTS, capacity + blocks * (STEP - 1))
+    slots_all = (slots_all + TILE - 1) // TILE * TILE
+    return rank, starts.reshape(-1), steps.reshape(-1), used, slots_all
+
+
+def steps_copy(count, make, act):
+    for size in range(1, SLOTS // STEP + 1):
+
+        @pl.when(count == size)
+        def _(size=size):
+            act(make(size * STEP))
+
+
+def start_copy(copy):
+    copy.start()
+
+
+def wait_copy(copy):
+    copy.wait()
+
+
+def pick_matrix(rank):
+    experts = rank.shape[0]
+    slot = lax.broadcasted_iota(jnp.int32, (SLOTS, BLOCK), 0)
+    parts = [slot == rank[e : e + 1, :] for e in range(experts)]
+    return parts
+
+
+def dispatch_kernel(
+    starts, steps, used, rank_ref, weight_ref, x_ref, out_ref, wout_ref, buf, wbuf, zeros,
+    sems, wsems, zsems,
+):
+    experts = rank_ref.shape[1]
+    width = x_ref.shape[1]
+    b = pl.program_id(0)
+    blocks = pl.num_programs(0)
+    slot = lax.rem(b, 2)
+
+    def make(which, e, place):
+        first = starts[which * experts + e] * STEP
+
+        def rows(size):
+            return pltpu.make_async_copy(
+                buf.at[place, pl.ds(e * SLOTS, size)],
+                out_ref.at[e, pl.ds(pl.multiple_of(first, STEP), size)],
+                sems.at[place, e],
+            )
+
+        def weights(size):
+            return pltpu.make_async_copy(
+                wbuf.at[place, pl.ds(e * SLOTS, size)],
+                wout_ref.at[e, pl.ds(pl.multiple_of(first, STEP), size)],
+                wsems.at[place, e],
+            )
+
+        return rows, weights
+
+    def each(which, place, act):
+        for e in range(experts):
+            rows, weights = make(which, e, place)
+            steps_copy(steps[which * experts + e], rows, act)
+            if weight_ref is not None:
+                steps_copy(steps[which * experts + e], weights, act)
+
+    def fill(act):
+        for e in range(experts):
+            rest = lax.rem(TILE // STEP - lax.rem(used[e], TILE // STEP), TILE // STEP)
+            done = used[e]
+            for k, size in enumerate((8, 4, 2, 1)):
+                take = lax.rem(rest // size, 2)
+
+                @pl.when(take == 1)
+                def _(e=e, k=k, size=size, done=done):
+                    act(
+                        pltpu.make_async_copy(
+                            zeros.at[pl.ds(0, size * STEP)],
+                            out_ref.at[e, pl.ds(pl.multiple_of(done * STEP, STEP), size * STEP)],
+                            zsems.at[e, k],
+                        )
+                    )
+
+                done = done + take * size
+
+    @pl.when(b == 0)
+    def _():
+        zeros[...] = jnp.zeros_like(zeros)
+        fill(start_copy)
+
+    @pl.when(b >= 2)
+    def _():
+        each(b - 2, slot, wait_copy)
+
+    parts = pick_matrix(rank_ref[0])
+    if weight_ref is not None:
+        for e in range(experts):
+            column = jnp.sum(
+                jnp.where(parts[e], weight_ref[0, e : e + 1, :], 0.0), axis=1, keepdims=True
+            )
+            wbuf[slot, pl.ds(e * SLOTS, SLOTS), :] = jnp.broadcast_to(column, (SLOTS, 128))
+    pick = jnp.concatenate([p.astype(jnp.bfloat16) for p in parts], axis=0)
+    span = 512
+    for n in range(width // span):
+        cols = pl.ds(n * span, span)
+        buf[slot, :, cols] = jnp.dot(
+            pick, x_ref[:, cols], preferred_element_type=jnp.float32
+        ).astype(jnp.bfloat16)
+    each(b, slot, start_copy)
+
+    @pl.when(b == blocks - 1)
+    def _():
+        each(b - 1, 1 - slot, wait_copy)
+        each(b, slot, wait_copy)
+        fill(wait_copy)
+
+
+def dispatch_rows(table, routing, weights):
+    rank, starts, steps, used, slots_all = routing
+    blocks, experts, _ = rank.shape
+    width = table.shape[1]
+    wide = pl.BlockSpec((1, experts, BLOCK), lambda b, *_: (b, 0, 0))
+    anywhere = pl.BlockSpec(memory_space=pl.ANY)
+    rows_shape = jax.ShapeDtypeStruct((experts, slots_all, width), jnp.bfloat16)
+    scratch = [
+        pltpu.VMEM((2, experts * SLOTS, width), jnp.bfloat16),
+        pltpu.VMEM((2, experts * SLOTS, 128), jnp.float32),
+        pltpu.VMEM((8 * STEP, width), jnp.bfloat16),
+        pltpu.SemaphoreType.DMA((2, experts)),
+        pltpu.SemaphoreType.DMA((2, experts)),
+        pltpu.SemaphoreType.DMA((experts, 4)),
+    ]
+    flops = 2 * blocks * experts * SLOTS * BLOCK * width
+    params = dict(
+        compiler_params=pltpu.CompilerParams(
+            dimension_semantics=("arbitrary",), vmem_limit_bytes=48 * 2**20
+        ),
+        cost_estimate=pl.CostEstimate(
+            flops=flops, bytes_accessed=6 * blocks * BLOCK * width, transcendentals=0
+        ),
+    )
+    x_spec = pl.BlockSpec((BLOCK, width), lambda b, *_: (b, 0))
+    if weights is None:
+
+        def plain(starts, steps, used, rank_ref, x_ref, out_ref, *rest):
+            dispatch_kernel(
+                starts, steps, used, rank_ref, None, x_ref, out_ref, None, *rest
+            )
+
+        rows = pl.pallas_call(
+            plain,
+            grid_spec=pltpu.PrefetchScalarGridSpec(
+                num_scalar_prefetch=3,
+                grid=(blocks,),
+                in_specs=[wide, x_spec],
+                out_specs=anywhere,
+                scratch_shapes=scratch,
+            ),
+            out_shape=rows_shape,
+            name="dispatch_cotangent",
+            **params,
+        )(starts, steps, used, rank, table)
+        return rows, None
+    return pl.pallas_call(
+        dispatch_kernel,
+        grid_spec=pltpu.PrefetchScalarGridSpec(
+            num_scalar_prefetch=3,
+            grid=(blocks,),
+            in_specs=[wide, wide, x_spec],
+            out_specs=[anywhere, anywhere],
+            scratch_shapes=scratch,
+        ),
+        out_shape=[
+            rows_shape,
+            jax.ShapeDtypeStruct((experts, slots_all, 128), jnp.float32),
+        ],
+        name="dispatch_tokens",
+        **params,
+    )(starts, steps, used, rank, weights, table)
+
+
+def contract(left, right, left_dim, right_dim):
+    return lax.dot_general(
+        left, right, (((left_dim,), (right_dim,)), ((), ())), preferred_element_type=jnp.float32
+    )
+
+
+def expert_kernel(
+    used, first, x_ref, c_ref, w_ref, gate_ref, up_ref, down_ref, y_ref, dx_ref, gg_ref, gu_ref,
+    gd_ref, acc_g, acc_u, acc_d,
+):
+    e = pl.program_id(0)
+    t = pl.program_id(1)
+    rows_used = used[e] * STEP
+    width = x_ref.shape[2]
+
+    @pl.when(t == 0)
+    def _():
+        acc_g[...] = jnp.zeros_like(acc_g)
+        acc_u[...] = jnp.zeros_like(acc_u)
+        acc_d[...] = jnp.zeros_like(acc_d)
+
+    @pl.when(t * TILE < rows_used)
+    def _():
+        x = x_ref[0]
+        c = c_ref[0]
+        gate_mat = gate_ref[0]
+        up_mat = up_ref[0]
+        down_mat = down_ref[0]
+        row = t * TILE + lax.broadcasted_iota(jnp.int32, (TILE, 1), 0)
+        weight = jnp.where(row < rows_used, w_ref[0][:, 0:1], 0.0)
+        gate_pre = jnp.dot(x, gate_mat, preferred_element_type=jnp.float32)
+        up_pre = jnp.dot(x, up_mat, preferred_element_type=jnp.float32)
+        up_act = jnp.dot(c, down_mat, preferred_element_type=jnp.float32)
+        sig = 1.0 / (1.0 + jnp.exp(-gate_pre))
+        silu = gate_pre * sig
+        act = silu * up_pre
+        gate_grad = jnp.sum(up_act * act, axis=1, keepdims=True)
+        act_low = (act * weight).astype(jnp.bfloat16)
+        act_grad = up_act * weight
+        dgate = (act_grad * up_pre * sig * (1.0 + gate_pre * (1.0 - sig))).astype(jnp.bfloat16)
+        dup = (act_grad * silu).astype(jnp.bfloat16)
+        y_ref[0] = contract(act_low, down_mat, 1, 1).astype(jnp.bfloat16)
+        dx_ref[0, :, 0:width] = (
+            contract(dgate, gate_mat, 1, 1) + contract(dup, up_mat, 1, 1)
+        ).astype(jnp.bfloat16)
+        column = lax.broadcasted_iota(jnp.int32, (TILE, 128), 1)
+        dx_ref[0, :, width : width + 128] = jnp.where(
+            column == first[0] + e, gate_grad, 0.0
+        ).astype(jnp.bfloat16)
+        acc_g[...] += contract(dgate, x, 0, 0)
+        acc_u[...] += contract(dup, x, 0, 0)
+        acc_d[...] += contract(act_low, c, 0, 0)
+
+    @pl.when(t == pl.num_programs(1) - 1)
+    def _():
+        gg_ref[0] = acc_g[...].T
+        gu_ref[0] = acc_u[...].T
+        gd_ref[0] = acc_d[...].T
+
+
+def run_experts(x_rows, c_rows, w_rows, w_gate, w_up, w_down, used, first):
+    experts, slots_all, width = x_rows.shape
+    hidden = w_gate.shape[2]
+
+    def tile_map(e, t, used, first):
+        last = jnp.maximum((used[e] * STEP + TILE - 1) // TILE - 1, 0)
+        return (e, jnp.minimum(t, last), 0)
+
+    def mat_map(e, t, used, first):
+        return (e, 0, 0)
+
+    mat = pl.BlockSpec((1, width, hidden), mat_map)
+    return pl.pallas_call(
+        expert_kernel,
+        grid_spec=pltpu.PrefetchScalarGridSpec(
+            num_scalar_prefetch=2,
+            grid=(experts, slots_all // TILE),
+            in_specs=[
+                pl.BlockSpec((1, TILE, width), tile_map),
+                pl.BlockSpec((1, TILE, width), tile_map),
+                pl.BlockSpec((1, TILE, 128), tile_map),
+                mat,
+                mat,
+                mat,
+            ],
+            out_specs=[
+                pl.BlockSpec((1, TILE, width), tile_map),
+                pl.BlockSpec((1, TILE, width + 128), tile_map),
+                mat,
+                mat,
+                mat,
+            ],
+            scratch_shapes=[pltpu.VMEM((hidden, width), jnp.float32)] * 3,
+        ),
+        out_shape=[
+            jax.ShapeDtypeStruct((experts, slots_all, width), jnp.bfloat16),
+            jax.ShapeDtypeStruct((experts, slots_all, width + 128), jnp.bfloat16),
+        ]
+        + [jax.ShapeDtypeStruct((experts, width, hidden), jnp.float32)] * 3,
+        compiler_params=pltpu.CompilerParams(
+            dimension_semantics=("arbitrary", "arbitrary"), vmem_limit_bytes=60 * 2**20
+        ),
+        cost_estimate=pl.CostEstimate(
+            flops=18 * experts * slots_all * width * hidden,
+            bytes_accessed=8 * experts * slots_all * width,
+            transcendentals=experts * slots_all * hidden,
+        ),
+        name="experts",
+    )(used, first, x_rows, c_rows, w_rows, w_gate, w_up, w_down)
+
+
+def combine_kernel(starts, steps, rank_ref, y_ref, out_ref, buf, sems):
+    experts = rank_ref.shape[1]
+    width = out_ref.shape[1]
+    b = pl.program_id(0)
+    blocks = pl.num_programs(0)
+    slot = lax.rem(b, 2)
+
+    def each(which, place, act):
+        for e in range(experts):
+            first = starts[which * experts + e] * STEP
+
+            def rows(size, e=e, first=first):
+                return pltpu.make_async_copy(
+                    y_ref.at[e, pl.ds(pl.multiple_of(first, STEP), size)],
+                    buf.at[place, pl.ds(e * SLOTS, size)],
+                    sems.at[place, e],
+                )
+
+            steps_copy(steps[which * experts + e], rows, act)
+
+    @pl.when(b == 0)
+    def _():
+        buf[...] = jnp.zeros_like(buf)
+        each(0, 0, start_copy)
+
+    @pl.when(b + 1 < blocks)
+    def _():
+        each(b + 1, 1 - slot, start_copy)
+
+    pick = jnp.concatenate([p.astype(jnp.bfloat16) for p in pick_matrix(rank_ref[0])], axis=0)
+    each(b, slot, wait_copy)
+    done = 0
+    while done < width:
+        span = min(512, width - done)
+        cols = pl.ds(done, span)
+        out_ref[:, cols] = contract(pick, buf[slot, :, cols], 0, 0).astype(jnp.bfloat16)
+        done += span
+
+
+def combine_rows(rows, routing, name):
+    rank, starts, steps, used, slots_all = routing
+    blocks, experts, _ = rank.shape
+    width = rows.shape[2]
+    return pl.pallas_call(
+        combine_kernel,
+        grid_spec=pltpu.PrefetchScalarGridSpec(
+            num_scalar_prefetch=2,
+            grid=(blocks,),
+            in_specs=[
+                pl.BlockSpec((1, experts, BLOCK), lambda b, *_: (b, 0, 0)),
+                pl.BlockSpec(memory_space=pl.ANY),
+            ],
+            out_specs=pl.BlockSpec((BLOCK, width), lambda b, *_: (b, 0)),
+            scratch_shapes=[
+                pltpu.VMEM((2, experts * SLOTS, width), jnp.bfloat16),
+                pltpu.SemaphoreType.DMA((2, experts)),
+            ],
+        ),
+        out_shape=jax.ShapeDtypeStruct((blocks * BLOCK, width), jnp.bfloat16),
+        compiler_params=pltpu.CompilerParams(
+            dimension_semantics=("arbitrary",), vmem_limit_bytes=48 * 2**20
+        ),
+        cost_estimate=pl.CostEstimate(
+            flops=2 * blocks * experts * SLOTS * BLOCK * width,
+            bytes_accessed=6 * blocks * BLOCK * width,
+            transcendentals=0,
+        ),
+        name=name,
+    )(starts, steps, rank, rows)
+
+
+def reduce_tokens(partial):
+    partial = lax.psum_scatter(partial, "fsdp", scatter_dimension=0, tiled=True)
+    return lax.psum_scatter(partial, "sp", scatter_dimension=0, tiled=True)
 
 
 def local(
@@ -89,9 +490,6 @@
     width = hidden_in.shape[1]
     head_local = HEADS // sp_count
     seq_rows = tok_rows * sp_count
-    slot_most = max(2, 2 * tok_rows * TOPK // EXPERTS)
-    capacity = 5 * seq_rows * fs_count * TOPK // (4 * EXPERTS)
-    local_experts = EXPERTS // sp_count
     gathered = (
         lax.all_gather(norm_attn, "fsdp", axis=0, tiled=True),
         lax.all_gather(norm_query, "fsdp", axis=0, tiled=True),
@@ -102,9 +500,6 @@
         lax.all_gather(w_value, "fsdp", axis=0, tiled=True),
         lax.all_gather(w_out, "fsdp", axis=0, tiled=True),
         lax.all_gather(w_router, "fsdp", axis=0, tiled=True),
-        lax.all_gather(w_gate, "fsdp", axis=2, tiled=True),
-        lax.all_gather(w_up, "fsdp", axis=2, tiled=True),
-        lax.all_gather(w_down, "fsdp", axis=2, tiled=True),
     )
     (
         gain_attn,
@@ -116,10 +511,10 @@
         value_mat,
         out_mat,
         router_mat,
-        gate_full,
-        up_full,
-        down_full,
     ) = gathered
+    cot_all = lax.all_gather(cotangent[0], ("fsdp", "sp"), axis=0, tiled=True)
+    routing = route_plan(expert_ids[0], sp_count, fs_count)
+    cot_rows, _ = dispatch_rows(cot_all, routing, None)
     attn_normed, attn_pull = jax.vjp(rms_scale, hidden_in, gain_attn.astype(jnp.float32))
     attn_in = attn_normed.astype(jnp.bfloat16)
     query_raw = jnp.dot(attn_in, query_mat, preferred_element_type=jnp.float32)
@@ -192,87 +587,28 @@
     ffn_in = ffn_normed.astype(jnp.bfloat16)
     logits = jnp.dot(ffn_in, router_mat, preferred_element_type=jnp.float32)
     router = jax.nn.softmax(logits, axis=-1)
-    route_ids = expert_ids[0]
-    chosen = route_ids[:, :, None] == jnp.arange(EXPERTS, dtype=jnp.int32)[None, None, :]
-    chosen_float = chosen.astype(jnp.float32)
-    gates = jnp.einsum("tke,te->tk", chosen_float, router)
-    onehot_pairs = chosen.astype(jnp.int32).reshape(tok_rows * TOPK, EXPERTS)
-    running = jnp.cumsum(onehot_pairs, axis=0)
-    pair_rank = jnp.sum((running - 1) * onehot_pairs, axis=1)
-    every_count = lax.all_gather(running[-1:], ("sp", "fsdp"), axis=0, tiled=True)
-    count_grid = every_count.reshape(sp_count, fs_count, EXPERTS)
-    fs_line = jnp.arange(fs_count, dtype=jnp.int32)[None, :]
-    sp_line = jnp.arange(sp_count, dtype=jnp.int32)[:, None]
-    my_fs = lax.axis_index("fsdp")
-    earlier = (fs_line < my_fs) | (fs_line == my_fs) & (sp_line < lax.axis_index("sp"))
-    prefix = jnp.sum(count_grid * earlier[:, :, None].astype(jnp.int32), axis=(0, 1))
-    place = jnp.sum(onehot_pairs * prefix[None, :], axis=1) + pair_rank
-    kept_pair = (place < capacity).astype(jnp.float32)
-    pair_weight = kept_pair * gates.reshape(-1)
-    slot_index = route_ids.reshape(-1) * slot_most + pair_rank
-    token_of_pair = jnp.arange(tok_rows * TOPK, dtype=jnp.int32) // TOPK
-    buffer_shape = (sp_count, local_experts, slot_most, width)
-    send_rows = (
-        jnp.zeros((EXPERTS * slot_most, width), jnp.bfloat16)
-        .at[slot_index]
-        .set(ffn_in[token_of_pair])
-    )
-    received = lax.all_to_all(
-        send_rows.reshape(buffer_shape), "sp", split_axis=0, concat_axis=0, tiled=True
-    )
-    gate_pre = jnp.einsum("nemd,edf->nemf", received, gate_full, preferred_element_type=jnp.float32)
-    up_pre = jnp.einsum("nemd,edf->nemf", received, up_full, preferred_element_type=jnp.float32)
-    sigmoid_gate = jax.nn.sigmoid(gate_pre)
-    silu_gate = gate_pre * sigmoid_gate
-    act_rows = (silu_gate * up_pre).astype(jnp.bfloat16)
-    expert_out = jnp.einsum(
-        "nemf,edf->nemd", act_rows, down_full, preferred_element_type=jnp.float32
-    ).astype(jnp.bfloat16)
-    returned = lax.all_to_all(expert_out, "sp", split_axis=0, concat_axis=0, tiled=True).reshape(
-        EXPERTS * slot_most, width
-    )
-    pair_out = returned[slot_index].reshape(tok_rows, TOPK, width)
-    moe_sum = jnp.einsum(
-        "tkd,tk->td",
-        pair_out,
-        pair_weight.reshape(tok_rows, TOPK),
-        preferred_element_type=jnp.float32,
-    )
-    mixed = (after_attn + moe_sum).astype(jnp.bfloat16)
+    rank = routing[0]
+    ffn_all = lax.all_gather(ffn_in, ("fsdp", "sp"), axis=0, tiled=True)
+    router_all = jax.nn.softmax(
+        jnp.dot(ffn_all, router_mat, preferred_element_type=jnp.float32), axis=-1
+    )
+    expert_local = EXPERTS // sp_count
+    first_expert = lax.axis_index("sp") * expert_local
+    gate_rows = (
+        lax.dynamic_slice_in_dim(router_all, first_expert, expert_local, axis=1)
+        .reshape(-1, BLOCK, expert_local)
+        .transpose(0, 2, 1)
+    )
+    ffn_rows, gate_slots = dispatch_rows(ffn_all, routing, gate_rows)
+    out_rows, in_grad_rows, grad_gate, grad_up, grad_down = run_experts(
+        ffn_rows, cot_rows, gate_slots, w_gate, w_up, w_down, routing[3], first_expert[None]
+    )
+    in_grad_sum = reduce_tokens(combine_rows(in_grad_rows, routing, "combine_grads"))
+    moe_sum = reduce_tokens(combine_rows(out_rows, routing, "combine_outputs"))
+    mixed = (after_attn + moe_sum.astype(jnp.float32)).astype(jnp.bfloat16)
     upstream = cotangent[0].astype(jnp.float32)
-    gate_grad = kept_pair.reshape(tok_rows, TOPK) * jnp.einsum(
-        "tkd,td->tk", pair_out, upstream, preferred_element_type=jnp.float32
-    )
-    slot_grad = (upstream[:, None, :] * pair_weight.reshape(tok_rows, TOPK)[:, :, None]).astype(
-        jnp.bfloat16
-    )
-    send_grad = (
-        jnp.zeros((EXPERTS * slot_most, width), jnp.bfloat16)
-        .at[slot_index]
-        .set(slot_grad.reshape(-1, width))
-    )
-    out_grad = lax.all_to_all(
-        send_grad.reshape(buffer_shape), "sp", split_axis=0, concat_axis=0, tiled=True
-    )
-    act_grad = jnp.einsum("nemd,edf->nemf", out_grad, down_full, preferred_element_type=jnp.float32)
-    gate_pre_grad = (
-        act_grad * up_pre * sigmoid_gate * (1.0 + gate_pre * (1.0 - sigmoid_gate))
-    ).astype(jnp.bfloat16)
-    up_pre_grad = (act_grad * silu_gate).astype(jnp.bfloat16)
-    row_grad = jnp.einsum(
-        "nemf,edf->nemd", gate_pre_grad, gate_full, preferred_element_type=jnp.float32
-    )
-    row_grad = (
-        row_grad
-        + jnp.einsum("nemf,edf->nemd", up_pre_grad, up_full, preferred_element_type=jnp.float32)
-    ).astype(jnp.bfloat16)
-    back_rows = lax.all_to_all(row_grad, "sp", split_axis=0, concat_axis=0, tiled=True).reshape(
-        EXPERTS * slot_most, width
-    )
-    ffn_in_grad = jnp.sum(
-        back_rows[slot_index].reshape(tok_rows, TOPK, width).astype(jnp.float32), axis=1
-    )
-    router_grad = jnp.einsum("tke,tk->te", chosen_float, gate_grad)
+    ffn_in_grad = in_grad_sum[:, :width].astype(jnp.float32)
+    router_grad = in_grad_sum[:, width : width + EXPERTS].astype(jnp.float32)
     logit_grad = (
         router * (router_grad - jnp.sum(router * router_grad, axis=-1, keepdims=True))
     ).astype(jnp.bfloat16)
@@ -362,29 +698,6 @@
     value_term = jnp.dot(attn_in.T, value_low, preferred_element_type=jnp.float32)
     attn_hidden_grad, attn_gain_term = attn_pull(attn_in_grad)
     grad_tokens = after_grad + attn_hidden_grad
-    rows_in = lax.all_gather(received, "fsdp", axis=0, tiled=True)
-    rows_grad = lax.all_gather(out_grad, "fsdp", axis=0, tiled=True)
-    gate_part = jnp.einsum("nemd,edf->nemf", rows_in, w_gate, preferred_element_type=jnp.float32)
-    up_part = jnp.einsum("nemd,edf->nemf", rows_in, w_up, preferred_element_type=jnp.float32)
-    sigmoid_part = jax.nn.sigmoid(gate_part)
-    silu_part = gate_part * sigmoid_part
-    act_part = (silu_part * up_part).astype(jnp.bfloat16)
-    act_part_grad = jnp.einsum(
-        "nemd,edf->nemf", rows_grad, w_down, preferred_element_type=jnp.float32
-    )
-    gate_part_grad = (
-        act_part_grad * up_part * sigmoid_part * (1.0 + gate_part * (1.0 - sigmoid_part))
-    ).astype(jnp.bfloat16)
-    up_part_grad = (act_part_grad * silu_part).astype(jnp.bfloat16)
-    grad_gate = jnp.einsum(
-        "nemd,nemf->edf", rows_in, gate_part_grad, preferred_element_type=jnp.float32
-    )
-    grad_up = jnp.einsum(
-        "nemd,nemf->edf", rows_in, up_part_grad, preferred_element_type=jnp.float32
-    )
-    grad_down = jnp.einsum(
-        "nemd,nemf->edf", rows_grad, act_part, preferred_element_type=jnp.float32
-    )
     scattered = (
         lax.psum_scatter(
             attn_gain_term.astype(jnp.bfloat16), "fsdp", scatter_dimension=0, tiled=True

time: 4060 us -> 2600 us (0.64)
  blocking collectives: 914 us -> 192 us
  matrix products: 635 us -> 206 us
  waiting for transfers between devices: 1970 us -> 1570 us
  Pallas kernels: 0 us -> 327 us
  local copies, waits for them, and re-layouts: 315 us -> 162 us
  other arithmetic: 135 us -> 62.9 us
    all_to_all x3 -> x1, blocking collectives: 772 us -> 31.4 us  [local(): lax.all_to_all(key_rot.astype(jnp.bfloat16), 'sp', split_axis=1, concat_a...]
    all_to_all x3 -> x1, waiting for transfers between devices: 706 us -> 5.25 us  [local(): lax.all_to_all(query_rot.astype(jnp.bfloat16), 'sp', split_axis=1, concat...]
    all_gather x5 -> x2, waiting for transfers between devices: 696 us -> 179 us  [the longest x1 154 us: local(): ffn_all = lax.all_gather(ffn_in, ('fsdp', 'sp'), axis=0, tiled=True)]
    dot_general x16 -> x4, matrix products: 476 us -> 16.7 us  [the longest x1 16.2 us: local(): jnp.dot(ffn_all, router_mat, preferred_element_type=jnp.float32)]
    unnamed x15 -> x18, waiting for transfers between devices: 4.46 us -> 443 us
    pallas_call x0 -> x5, Pallas kernels: none -> 327 us  [the longest x1 151 us: run_experts(): pl.pallas_call(expert_kernel, grid_spec=pltpu.PrefetchScalarGridSpec(num_...]
    reduce_scatter x0 -> x2, waiting for transfers between devices: none -> 303 us  [reduce_tokens(): return lax.psum_scatter(partial, 'sp', scatter_dimension=0, tiled=True)]
    reduce_scatter x1, waiting for transfers between devices: 4.61 us -> 74.4 us  [local(): lax.psum_scatter(query_term.astype(jnp.bfloat16), 'fsdp', scatter_dimensi...]
  transfers between devices with their start and end apart: 23 -> 22, of which waited for: 14 -> 19; matrix products, arithmetic and copies ran while one was open for 15% -> 14% of each run, Pallas kernels for 0% -> 3%
where the time goes in v1:
time: 2600 us; the launch traced here: 2580 us
  waiting for transfers between devices  1570 us (60%)
  Pallas kernels  327 us (13%)
  matrix products  206 us (8%)
  blocking collectives  192 us (7%)
  local copies, waits for them, and re-layouts  162 us (6%)
  other arithmetic  62.9 us (2%)
  starting transfers between devices  35.1 us (1%)
    unnamed x18, waiting for transfers between devices  443 us
    reduce_scatter x2, waiting for transfers between devices, reduce_tokens(): return lax.psum_scatter(partial, 'sp', scatter_dimension=0, tiled=True)  303 us
    psum x1, waiting for transfers between devices, local(): lax.psum(scattered[4].astype(jnp.bfloat16), 'sp').astype(jnp.float32)  222 us
    all_gather x1, waiting for transfers between devices, local(): ffn_all = lax.all_gather(ffn_in, ('fsdp', 'sp'), axis=0, tiled=True)  154 us
    pallas_call x1, Pallas kernels, run_experts(): pl.pallas_call(expert_kernel, grid_spec=pltpu.PrefetchScalarGridSpec(num_...  151 us
    pallas_call x2, Pallas kernels, combine_rows(): pl.pallas_call(combine_kernel, grid_spec=pltpu.PrefetchScalarGridSpec(num...  89.1 us
    reduce_scatter x1, waiting for transfers between devices, local(): lax.psum_scatter(query_term.astype(jnp.bfloat16), 'fsdp', scatter_dimensi...  74.4 us
    reduce_scatter x1, waiting for transfers between devices, local(): lax.psum_scatter(value_term.astype(jnp.bfloat16), 'fsdp', scatter_dimensi...  74.2 us
  transfers between devices with their start and end apart: 22, of which 19 were waited for; matrix products, arithmetic and copies ran while one was open for 14% of the time, Pallas kernels for 3%

profile of v1, /device:TPU:0, one launch (start us, length us, event | category | flops | bytes accessed | tf_op | source)
XLA Modules:
  0.0 2582.2 jit_solution(1973483718583270372)
XLA Ops:
  10.6 6.1 all-gather.2
  16.8 5.4 all-gather.3
  22.2 5.2 all-gather.4
  28.5 42.2 %all-gather.15.cloned.1.call-done = bf16[2048,2048]{1,0:T(8,128)(2,1)} async-done(((bf16[512,2048]{1,0:T(8,128)(2,1)}), bf16[2048,2048]{1,0:T(8,128)(2,1)}) %all-gather.15.cloned.1.call-update) | async-done | bytes 8388624 | tf_op jit(solution)/shard_map/all_gather | solution.py:498
  70.6 5.8 multiply_reduce_fusion.7
  77.1 53.4 %all-gather.17.cloned.1.call-done = bf16[2048,2048]{1,0:T(8,128)(2,1)} async-done(((bf16[512,2048]{1,0:T(8,128)(2,1)}), bf16[2048,2048]{1,0:T(8,128)(2,1)}) %all-gather.17.cloned.1.call-update) | async-done | bytes 8388624 | tf_op jit(solution)/shard_map/all_gather | solution.py:499
  130.5 5.9 multiply_reduce_fusion.6
  141.9 31.4 %all_to_all.120 = bf16[256,16,128]{2,0,1:T(8,128)(2,1)S(1)} all-to-all(bf16[256,16,128]{2,0,1:T(8,128)(2,1)S(1)} %get-tuple-element.444), channel_id=1, replica_groups=mesh['sp'=8,'fsdp'=4] {'sp'}, dimensions={1} | all-to-all | bytes 2097152 | tf_op jit(solution)/shard_map/all_to_all | solution.py:540
  176.9 13.5 all-gather.13.cloned.1.call-done
  190.4 5.8 fusion.70
  197.4 5.3 all-to-all-done.1
  202.7 15.1 all-to-all-start
  220.2 22.9 all-to-all-done
  247.2 46.4 %while.30 = (s32[]{:T(128)}, bf16[4,512,2,128]{3,1,0,2:T(8,128)(2,1)S(1)}, f32[4,2,512]{2,1,0:T(2,128)}, s32[4]{0:T(128)S(1)}, bf16[3072,2,128]{2,0,1:T(8,128)(2...) while((s32[]{:T(128)}, ...), condition=%wide.region_8.9_spmd, body=%wide.region_5.8_spmd.sunk | while | flops 829031424 | bytes 25240332 | solution.py:580
  293.6 9.5 copy.215
  306.7 5.2 all-gather.5
  311.9 47.8 %all-to-all-done.3 = bf16[2048,2,128]{2,1,0:T(2,128)(2,1)S(1)} async-done(((bf16[2048,2,128]{2,1,0:T(2,128)(2,1)}), bf16[2048,2,128]{2,1,0:T(2,128)(2,1)S(1)}, u32[]{:S(2)}, u32[]{:S(2)}) %all-to-all-start.3) | async-done | bytes 1048608 | tf_op jit(solution)/shard_map/all_to_all | solution.py:582
  360.5 6.2 multiply_reduce_fusion.5
  369.3 69.5 %all-gather = s32[1,8192,8]{1,2,0:T(8,128)S(1)} all-gather(s32[1,256,8]{1,2,0:T(8,128)S(1)} %copy-done.58), channel_id=2, replica_groups=mesh['sp'=8,'fsdp'=4] {'fsdp','sp'}, dimensions={1}, use_global_device_ids=true | all-gather | bytes 270336 | tf_op jit(solution)/shard_map/all_gather | solution.py:84
  441.5 6.2 all_gather.46
  447.9 25.8 all-gather.23.cloned.1.call-done
  473.7 43.0 %dispatch_cotangent.1.c_ref = bf16[8,1792,2048]{2,1,0:T(8,128)(2,1)} custom-call(s32[256]{0:T(256)S(1)} %reshape.452.starts, s32[256]{0:T(256)S(1)} %and_select_fusion.steps, s32[8]{0:T(128)S(1)} %add_reduce_fusion.used, s32[32,8,256]{2,1,0:T(8,128)S(1)} %get-tuple-element.442.rank_ref, bf16[8192,2048]{1,0:T(8,128)(2,1)} %bitcast.243), custom_call_target="tpu_custom_call" | custom-call | flops 17179869184 | bytes 100663296 | tf_op jit(solution)/shard_map/dispatch_cotangent/pallas_call | solution.py:249
  516.7 153.7 %all-gather.21.cloned.1.call-done.x_ref = bf16[8192,2048]{1,0:T(8,128)(2,1)} async-done(((bf16[256,2048]{1,0:T(8,128)(2,1)}), bf16[8192,2048]{1,0:T(8,128)(2,1)}) %all-gather.21.cloned.1.call-update) | async-done | bytes 33554448 | tf_op jit(solution)/shard_map/all_gather | solution.py:591
  670.4 16.2 fusion.110
  687.0 43.8 %dispatch_tokens.1 = (bf16[8,1792,2048]{2,1,0:T(8,128)(2,1)}, f32[8,1792,128]{2,1,0:T(8,128)}) custom-call(s32[256]{0:T(256)S(1)} %reshape.452.starts, s32[256]{0:T(256)S(1)} %and_select_fusion.steps, s32[8]{0:T(128)S(1)} %add_reduce_fusion.used, s32[32,8,256]{2,1,0:T(8,128)S(1)} %get-tuple-element.442.rank_ref, f32[32,8,256]{2,1,0:T(8,128)S(1)} %bitcast.240, ...), custom_call_target="tpu_custom_call" | custom-call | flops 17179869184 | bytes 100663296 | tf_op jit(solution)/shard_map/dispatch_tokens/pallas_call | solution.py:263
  730.8 151.1 %experts.1 = (bf16[8,1792,2048]{2,1,0:T(8,128)(2,1)}, bf16[8,1792,2176]{2,1,0:T(8,128)(2,1)}, f32[8,2048,256]{2,1,0:T(8,128)}, f32[8,2048,256]{2,1,0:T(8,128)}, f32[8,2048,256]{2,1,0:T(8,128)}) custom-call(s32[8]{0:T(128)} %copy-done, s32[1]{0:T(128)} %bitcast.35.first, bf16[8,1792,2048]{2,1,0:T(8,128)(2,1)} %get-tuple-element.287.x_ref, ...), custom_call_target="tpu_custom_call" | custom-call | flops 135291469824 | bytes 234881024 | tf_op jit(solution)/shard_map/experts/pallas_call | solution.py:353
  882.0 43.7 %combine_grads.1 = bf16[8192,2176]{1,0:T(8,128)(2,1)} custom-call(s32[256]{0:T(256)S(1)} %reshape.452.starts, s32[256]{0:T(256)S(1)} %and_select_fusion.steps, s32[32,8,256]{2,1,0:T(8,128)S(1)} %get-tuple-element.442.rank_ref, bf16[8,1792,2176]{2,1,0:T(8,128)(2,1)} %get-tuple-element.290.y_ref), custom_call_target="tpu_custom_call" | custom-call | flops 18253611008 | bytes 106954752 | tf_op jit(solution)/shard_map/combine_grads/pallas_call | solution.py:435
  925.8 45.4 %combine_outputs.1 = bf16[8192,2048]{1,0:T(8,128)(2,1)} custom-call(s32[256]{0:T(256)S(1)} %reshape.452.starts, s32[256]{0:T(256)S(1)} %and_select_fusion.steps, s32[32,8,256]{2,1,0:T(8,128)S(1)} %get-tuple-element.442.rank_ref, bf16[8,1792,2048]{2,1,0:T(8,128)(2,1)} %get-tuple-element.289.y_ref), custom_call_target="tpu_custom_call" | custom-call | flops 17179869184 | bytes 100663296 | tf_op jit(solution)/shard_map/combine_outputs/pallas_call | solution.py:435
  971.3 202.0 %reduce-scatter.30.cloned.1.call-done = bf16[2048,2176]{1,0:T(8,128)(2,1)} async-done(((bf16[8192,2176]{1,0:T(8,128)(2,1)}), bf16[2048,2176]{1,0:T(8,128)(2,1)}) %reduce-scatter.30.cloned.1.call-update) | async-done | bytes 8912912
  1173.3 237.6 %reduce-scatter.28.cloned.1.call-done = bf16[2048,2048]{1,0:T(8,128)(2,1)} async-done(((bf16[8192,2048]{1,0:T(8,128)(2,1)}), bf16[2048,2048]{1,0:T(8,128)(2,1)}) %reduce-scatter.28.cloned.1.call-update) | async-done | bytes 8388624
  1414.3 156.7 %reduce-scatter.16.cloned.1.call-done = bf16[256,2176]{1,0:T(8,128)(2,1)} async-done(((bf16[2048,2176]{1,0:T(8,128)(2,1)}), bf16[256,2176]{1,0:T(8,128)(2,1)}) %reduce-scatter.16.cloned.1.call-update) | async-done | bytes 1114128 | tf_op jit(solution)/shard_map/reduce_scatter | solution.py:465
  1576.3 146.8 %reduce-scatter.14.cloned.1.call-done = bf16[256,2048]{1,0:T(8,128)(2,1)} async-done(((bf16[2048,2048]{1,0:T(8,128)(2,1)}), bf16[256,2048]{1,0:T(8,128)(2,1)}) %reduce-scatter.14.cloned.1.call-update) | async-done | bytes 1048592 | tf_op jit(solution)/shard_map/reduce_scatter | solution.py:465
  1727.2 6.5 fusion.71
  1735.0 4.4 all-to-all-start.4
  1741.9 5.7 convolution_convert_fusion
  1747.6 17.8 all-to-all-done.4
  1774.1 213.5 %while.31 = (s32[]{:T(128)}, f32[3072,2,128]{2,1,0:T(2,128)}, f32[3072,2,128]{2,1,0:T(2,128)}, bf16[4,512,2,128]{3,1,0,2:T(8,128)(2,1)}, s32[4]{0:T(128)S(1)}, /...) while((s32[]{:T(128)}, f32[3072,2,128]{2,1,0:T(2,128)}, ...), condition=%wide.region_24.25_spmd, body=%wide.region_22.24_spmd.sunk | while | flops 2033583104 | bytes 129037232 | solution.py:675
  1775.4 5.9 fusion.173
  1785.8 5.7 multiply_reduce_fusion.9
  1813.2 5.2 fusion.175
  1829.7 4.8 fusion.173
  1839.0 5.7 multiply_reduce_fusion.9
  1866.4 5.1 fusion.175
  1882.7 4.8 fusion.173
  1892.1 5.7 multiply_reduce_fusion.9
  1919.4 5.1 fusion.175
  1935.7 4.8 fusion.173
  1945.1 5.7 multiply_reduce_fusion.9
  1972.5 5.1 fusion.175
  1997.7 23.2 all-to-all-done.5
  2025.6 24.9 all-to-all-done.6
  2057.7 5.8 convolution_convert_fusion.2
  2069.0 7.4 convolution_convert_fusion.3
  2078.5 29.7 %all_to_all.121 = bf16[2048,2,128]{2,1,0:T(2,128)(2,1)S(1)} all-to-all(bf16[2048,2,128]{2,1,0:T(2,128)(2,1)S(1)} %slice.67), channel_id=1, replica_groups=mesh['sp'=8,'fsdp'=4] {'sp'}, dimensions={0} | all-to-all | bytes 2097152 | tf_op jit(solution)/shard_map/all_to_all | solution.py:684
  2108.9 5.8 convolution_convert_fusion.1
  2114.8 19.5 reduce-scatter.20.cloned.1.call-done
  2134.3 74.4 %reduce-scatter.18.cloned.1.call-done = bf16[512,2048]{1,0:T(8,128)(2,1)} async-done(((bf16[2048,2048]{1,0:T(8,128)(2,1)}), bf16[512,2048]{1,0:T(8,128)(2,1)}) %reduce-scatter.18.cloned.1.call-update) | async-done | bytes 2097168 | tf_op jit(solution)/shard_map/reduce_scatter | solution.py:714
  2208.6 74.2 %reduce-scatter.22.cloned.1.call-done = bf16[512,2048]{1,0:T(8,128)(2,1)} async-done(((bf16[2048,2048]{1,0:T(8,128)(2,1)}), bf16[512,2048]{1,0:T(8,128)(2,1)}) %reduce-scatter.22.cloned.1.call-update) | async-done | bytes 2097168 | tf_op jit(solution)/shard_map/reduce_scatter | solution.py:720
  2284.7 5.9 fusion.112
  2290.7 6.2 convolution_add_fusion.2
  2301.0 10.9 all-reduce.15
  2312.2 22.3 all-reduce.13
  2340.5 222.5 %all-reduce.18.cloned.1.call-done = (bf16[512,2048]{1,0:T(8,128)(2,1)}, bf16[512,2048]{1,0:T(8,128)(2,1)}, bf16[512,2048]{1,0:T(8,128)(2,1)}, bf16[512,2048]{1,0:T(8,128)(2,1)}, bf16[512,64]{0,1:T(8,128)(2,1)}) async-done(((bf16[512,2048]{1,0:T(8,128)(2,1)}, bf16[512,2048]{1,0:T(8,128)(2,1)}, bf16[512,2048]{1,0:T(8,128)(2,1)}, bf16[512,2048]{1,0:T(8,128)(2,1)}, bf16[512,64]{0,1:T(8,128)(2,1)}), ...) | async-done | bytes 8454160 | tf_op jit(solution)/shard_map/psum | solution.py:735
  2562.9 4.3 convert_element_type.291
  (448 shorter events, 289.9 us)
Async XLA Ops:
  7.2 63.5 %all-gather.15.cloned.1.call-start = ((), (), s32[]{:S(2)}) async-start(), calls=%async_computation.18 | async-start | bytes 10485760 | tf_op jit(solution)/shard_map/all_gather | solution.py:498
  7.9 122.6 %all-gather.17.cloned.1.call-start = ((), (), s32[]{:S(2)}) async-start(), calls=%async_computation.19 | async-start | bytes 10485760 | tf_op jit(solution)/shard_map/all_gather | solution.py:499
  8.7 181.7 %all-gather.13.cloned.1.call-start = ((), (), s32[]{:S(2)}) async-start(), calls=%async_computation.17 | async-start | bytes 10485760 | tf_op jit(solution)/shard_map/all_gather | solution.py:500
  9.4 7.3 copy-start.69
  9.4 12.8 copy-start.70
  9.4 18.7 copy-start.2
  9.4 351.0 %all-gather.19.cloned.1.call-start = ((), (), s32[]{:S(2)}) async-start(), calls=%async_computation.20 | async-start | bytes 10485760 | tf_op jit(solution)/shard_map/all_gather | solution.py:501
  10.0 463.7 %all-gather.23.cloned.1.call-start = ((), (), s32[]{:S(2)}) async-start(), calls=%async_computation.29 | async-start | bytes 34603008 | tf_op jit(solution)/shard_map/all_gather | solution.py:515
  16.8 173.6 %copy-start.33 = (f32[4,1,512]{2,1,0:T(1,128)}, f32[4,1,512]{2,1,0:T(1,128)S(1)}, u32[]{:S(2)}) copy-start(f32[4,1,512]{2,1,0:T(1,128)S(1)} %convert_element_type.311) | copy-start | bytes 24580
  22.2 114.7 %copy-start.38 = (f32[4,1,512]{2,1,0:T(1,128)}, f32[4,1,512]{2,1,0:T(1,128)S(1)}, u32[]{:S(2)}) copy-start(f32[4,1,512]{2,1,0:T(1,128)S(1)} %convert_element_type.312) | copy-start | bytes 24580
  27.4 109.5 %copy-start.40 = (f32[4,1,512]{2,1,0:T(1,128)}, f32[4,1,512]{2,1,0:T(1,128)S(1)}, u32[]{:S(2)}) copy-start(f32[4,1,512]{2,1,0:T(1,128)S(1)} %convert_element_type.313) | copy-start | bytes 24580
  28.1 111.6 %copy-start.29 = (f32[256,128]{1,0:T(8,128)}, f32[256,128]{1,0:T(8,128)S(1)}, u32[]{:S(2)}) copy-start(f32[256,128]{1,0:T(8,128)S(1)} %get-tuple-element.450) | copy-start | bytes 393220
  28.1 111.6 %copy-start.31 = (f32[256,128]{1,0:T(8,128)}, f32[256,128]{1,0:T(8,128)S(1)}, u32[]{:S(2)}) copy-start(f32[256,128]{1,0:T(8,128)S(1)} %get-tuple-element.451) | copy-start | bytes 393220
  28.4 42.2 %copy-start.54 = (f32[256]{0:T(256)}, f32[256]{0:T(256)S(1)}, u32[]{:S(2)}) copy-start(f32[256]{0:T(256)S(1)} %fusion.51) | copy-start | bytes 3076
  28.5 161.9 %copy-start.46 = (f32[256]{0:T(256)}, f32[256]{0:T(256)S(1)}, u32[]{:S(2)}) copy-start(f32[256]{0:T(256)S(1)} %fusion.94) | copy-start | bytes 3076
  76.5 60.5 %copy-start.4 = (f32[256,2048]{1,0:T(8,128)}, f32[256,2048]{1,0:T(8,128)S(1)}, u32[]{:S(2)}) copy-start(f32[256,2048]{1,0:T(8,128)S(1)} %get-tuple-element.457) | copy-start | bytes 6291460
  77.1 59.9 %copy-start.48 = (f32[256]{0:T(256)}, f32[256]{0:T(256)S(1)}, u32[]{:S(2)}) copy-start(f32[256]{0:T(256)S(1)} %fusion.95) | copy-start | bytes 3076
  173.3 29.4 %all-to-all-start.1 = ((bf16[256,16,128]{2,0,1:T(8,128)(2,1)}), bf16[256,16,128]{2,0,1:T(8,128)(2,1)S(1)}, u32[]{:S(2)}, u32[]{:S(2)}) async-start(bf16[256,16,128]{2,0,1:T(8,128)(2,1)} %get-tuple-element.445), calls=%async_computation.1 | async-start | bytes 2097152 | tf_op jit(solution)/shard_map/all_to_all | solution.py:537
  196.2 21.6 copy-start.72
  202.7 40.4 %all-to-all-start = ((bf16[256,16,128]{2,0,1:T(8,128)(2,1)}), bf16[256,16,128]{2,0,1:T(8,128)(2,1)}, u32[]{:S(2)}, u32[]{:S(2)}) async-start(bf16[256,16,128]{2,0,1:T(8,128)(2,1)} %bitcast.253), calls=%async_computation | async-start | bytes 2097152 | tf_op jit(solution)/shard_map/all_to_all | solution.py:541
  219.1 25.3 copy-start.17
  293.6 9.5 copy-start.35
  293.6 9.5 copy-start.37
  293.6 13.1 copy-start.71
  303.1 56.6 %all-to-all-start.3 = ((bf16[2048,2,128]{2,1,0:T(2,128)(2,1)}), bf16[2048,2,128]{2,1,0:T(2,128)(2,1)S(1)}, u32[]{:S(2)}, u32[]{:S(2)}) async-start(bf16[2048,2,128]{2,1,0:T(2,128)(2,1)} %copy.215), calls=%async_computation.3 | async-start | bytes 2097152 | tf_op jit(solution)/shard_map/all_to_all | solution.py:582
  306.7 363.8 %all-gather.21.cloned.1.call-start = ((), (), s32[]{:S(2)}) async-start(), calls=%async_computation.21 | async-start | bytes 34603008 | tf_op jit(solution)/shard_map/all_gather | solution.py:591
  311.9 54.8 %copy-start.42 = (f32[4,1,512]{2,1,0:T(1,128)}, f32[4,1,512]{2,1,0:T(1,128)S(1)}, u32[]{:S(2)}) copy-start(f32[4,1,512]{2,1,0:T(1,128)S(1)} %convert_element_type.314) | copy-start | bytes 24580
  360.4 6.2 copy-start.13
  369.2 72.3 %copy-start.44 = (bf16[512,64]{0,1:T(8,128)(2,1)S(1)}, bf16[512,64]{0,1:T(8,128)(2,1)}, u32[]{:S(2)}) copy-start(bf16[512,64]{0,1:T(8,128)(2,1)} %param.31) | copy-start | bytes 196612
  369.2 804.0 %reduce-scatter.30.cloned.1.call-start = ((), (), s32[]{:S(2)}) async-start(), calls=%async_computation.31 | async-start | bytes 44564480
  447.7 222.7 %copy-start.24 = (bf16[2048,64]{0,1:T(8,128)(2,1)}, bf16[2048,64]{0,1:T(8,128)(2,1)S(1)}, u32[]{:S(2)}) copy-start(bf16[2048,64]{0,1:T(8,128)(2,1)S(1)} %all_gather.46) | copy-start | bytes 786436
  447.9 239.1 %copy-start = (s32[8]{0:T(128)}, s32[8]{0:T(128)S(1)}, u32[]{:S(2)}) copy-start(s32[8]{0:T(128)S(1)} %add_reduce_fusion.used) | copy-start | bytes 100
  925.8 485.1 %reduce-scatter.28.cloned.1.call-start = ((), (), s32[]{:S(2)}) async-start(), calls=%async_computation.30 | async-start | bytes 41943040
  971.2 599.8 %reduce-scatter.16.cloned.1.call-start = ((), (), s32[]{:S(2)}) async-start(), calls=%async_computation.23 | async-start | bytes 10027008 | tf_op jit(solution)/shard_map/reduce_scatter | solution.py:465
  1173.2 549.8 %reduce-scatter.14.cloned.1.call-start = ((), (), s32[]{:S(2)}) async-start(), calls=%async_computation.22 | async-start | bytes 9437184 | tf_op jit(solution)/shard_map/reduce_scatter | solution.py:465
  1410.9 161.2 %copy-start.11 = (f32[256,2048]{1,0:T(8,128)S(1)}, f32[256,2048]{1,0:T(8,128)}, u32[]{:S(2)}) copy-start(f32[256,2048]{1,0:T(8,128)} %copy-done.10) | copy-start | bytes 6291460
  1410.9 161.2 %copy-start.43 = (f32[4,1,512]{2,1,0:T(1,128)S(1)}, f32[4,1,512]{2,1,0:T(1,128)}, u32[]{:S(2)}) copy-start(f32[4,1,512]{2,1,0:T(1,128)} %copy-done.42) | copy-start | bytes 24580
  1410.9 161.2 %copy-start.53 = (f32[256]{0:T(256)S(1)}, f32[256]{0:T(256)}, u32[]{:S(2)}) copy-start(f32[256]{0:T(256)} %copy-done.52) | copy-start | bytes 3076
  1414.3 156.7 %copy-start.59 = (f32[256]{0:T(256)}, f32[256]{0:T(256)S(1)}, u32[]{:S(2)}) copy-start(f32[256]{0:T(256)S(1)} %fusion.87) | copy-start | bytes 3076
  1572.1 150.9 %copy-start.16 = (bf16[1,256,2048]{2,1,0:T(8,128)(2,1)S(1)}, bf16[1,256,2048]{2,1,0:T(8,128)(2,1)}, u32[]{:S(2)}) copy-start(bf16[1,256,2048]{2,1,0:T(8,128)(2,1)} %param.35) | copy-start | bytes 3145732
  1727.2 14.7 copy-start.8
  1733.7 5.7 copy-start.60
  1735.0 7.0 copy-start.14
  1735.0 30.5 %all-to-all-start.4 = ((bf16[256,16,128]{2,0,1:T(8,128)(2,1)}), bf16[256,16,128]{2,0,1:T(8,128)(2,1)}, u32[]{:S(2)}, u32[]{:S(2)}) async-start(bf16[256,16,128]{2,0,1:T(8,128)(2,1)} %bitcast.250), calls=%async_computation.6 | async-start | bytes 2097152 | tf_op jit(solution)/shard_map/all_to_all | solution.py:626
  1739.4 375.4 %reduce-scatter.26.cloned.1.call-start = ((), (), s32[]{:S(2)}) async-start(), calls=%async_computation.28 | async-start | bytes 327680 | tf_op jit(solution)/shard_map/reduce_scatter | solution.py:726
  1741.9 372.9 %reduce-scatter.24.cloned.1.call-start = ((), (), s32[]{:S(2)}) async-start(), calls=%async_computation.27 | async-start | bytes 10485760 | tf_op jit(solution)/shard_map/reduce_scatter | solution.py:723
  1785.8 5.7 slice-start.1
  1839.0 5.7 slice-start.1
  1892.1 5.7 slice-start.1
  1945.1 5.7 slice-start.1
  1991.2 29.7 %all-to-all-start.5 = ((bf16[2048,2,128]{2,1,0:T(2,128)(2,1)}), bf16[2048,2,128]{2,1,0:T(2,128)(2,1)S(1)}, u32[]{:S(2)}, u32[]{:S(2)}) async-start(bf16[2048,2,128]{2,1,0:T(2,128)(2,1)} %copy.227), calls=%async_computation.7 | async-start | bytes 2097152 | tf_op jit(solution)/shard_map/all_to_all | solution.py:682
  2020.9 29.6 %all-to-all-start.6 = ((bf16[2048,2,128]{2,1,0:T(2,128)(2,1)}), bf16[2048,2,128]{2,1,0:T(2,128)(2,1)S(1)}, u32[]{:S(2)}, u32[]{:S(2)}) async-start(bf16[2048,2,128]{2,1,0:T(2,128)(2,1)} %slice.68), calls=%async_computation.8 | async-start | bytes 2097152 | tf_op jit(solution)/shard_map/all_to_all | solution.py:683
  2024.5 109.7 %reduce-scatter.20.cloned.1.call-start = ((), (), s32[]{:S(2)}) async-start(), calls=%async_computation.25 | async-start | bytes 10485760 | tf_op jit(solution)/shard_map/reduce_scatter | solution.py:717
  2025.5 25.2 copy-start.32
  2063.5 145.1 %reduce-scatter.18.cloned.1.call-start = ((), (), s32[]{:S(2)}) async-start(), calls=%async_computation.24 | async-start | bytes 10485760 | tf_op jit(solution)/shard_map/reduce_scatter | solution.py:714
  2076.4 206.4 %reduce-scatter.22.cloned.1.call-start = ((), (), s32[]{:S(2)}) async-start(), calls=%async_computation.26 | async-start | bytes 10485760 | tf_op jit(solution)/shard_map/reduce_scatter | solution.py:720
  2108.9 5.8 copy-start.22
  2114.7 448.3 %all-reduce.18.cloned.1.call-start = ((), (), s32[]{:S(2)}) async-start(), calls=%async_computation.32 | async-start | bytes 16908288 | tf_op jit(solution)/shard_map/psum | solution.py:735
  2284.7 5.9 copy-start.19
  2284.7 12.1 slice-start.2
  2290.6 6.2 copy-start.23
  2290.6 6.2 slice-start.3
  2296.9 39.9 %copy-start.55 = (f32[256]{0:T(256)S(1)}, f32[256]{0:T(256)}, u32[]{:S(2)}) copy-start(f32[256]{0:T(256)} %copy-done.54) | copy-start | bytes 3076
  2296.9 39.9 %copy-start.9 = (f32[256,2048]{1,0:T(8,128)S(1)}, f32[256,2048]{1,0:T(8,128)}, u32[]{:S(2)}) copy-start(f32[256,2048]{1,0:T(8,128)} %copy-done.8) | copy-start | bytes 6291460
  (45 other events, 108.7 us)
Sparse Core Ops, SparseCore 0:
  9.6 61.0 all-gather.14
  72.2 58.2 all-gather.16
  132.1 58.2 all-gather.12
  191.8 58.2 all-gather.18
  253.0 220.7 all-gather.22
  477.1 193.2 all-gather.20
  925.9 247.2 reduce-scatter.29
  1176.0 234.8 reduce-scatter.27
  1415.0 156.0 reduce-scatter.15
  1574.9 148.0 reduce-scatter.13
  1742.6 21.3 reduce-scatter.25
  1766.6 71.7 reduce-scatter.23
  2063.7 70.5 reduce-scatter.19
  2136.9 71.6 reduce-scatter.17
  2211.0 71.7 reduce-scatter.21
  2288.4 274.5 all-reduce.17

commit v2 on v1

--- a/solution.py
+++ b/solution.py
@@ -1,3 +1,5 @@
+import functools
+
 import jax
 import jax.numpy as jnp
 from jax import lax
@@ -377,6 +379,7 @@
             jax.ShapeDtypeStruct((experts, slots_all, width + 128), jnp.bfloat16),
         ]
         + [jax.ShapeDtypeStruct((experts, width, hidden), jnp.float32)] * 3,
+        input_output_aliases={2: 0},
         compiler_params=pltpu.CompilerParams(
             dimension_semantics=("arbitrary", "arbitrary"), vmem_limit_bytes=60 * 2**20
         ),
@@ -460,9 +463,542 @@
     )(starts, steps, rank, rows)
 
 
-def reduce_tokens(partial):
-    partial = lax.psum_scatter(partial, "fsdp", scatter_dimension=0, tiled=True)
-    return lax.psum_scatter(partial, "sp", scatter_dimension=0, tiled=True)
+MESH = pl.DeviceIdType.MESH
+
+
+class Place:
+    def __init__(self, counts, fsdp_too):
+        self.n_hi, self.n_lo, self.n_x, self.n_core = counts
+        sp = lax.axis_index("sp")
+        self.hi, self.lo = sp // self.n_lo, sp % self.n_lo
+        if fsdp_too:
+            fs = lax.axis_index("fsdp")
+            self.x, self.core = fs // self.n_core, fs % self.n_core
+        else:
+            self.x, self.core = 0, 0
+
+    def peer(self, dim, ahead):
+        if dim == "core":
+            return {"fsdp": self.x * self.n_core + (self.core + ahead) % self.n_core}
+        if dim == "x":
+            return {"fsdp": (self.x + ahead) % self.n_x * self.n_core + self.core}
+        if dim == "lo":
+            return {"sp": self.hi * self.n_lo + (self.lo + ahead) % self.n_lo}
+        return {"sp": (self.hi + ahead) % self.n_hi * self.n_lo + self.lo}
+
+    def sizes(self):
+        return {"core": self.n_core, "x": self.n_x, "lo": self.n_lo, "hi": self.n_hi}
+
+    def meet(self):
+        barrier = pltpu.get_barrier_semaphore()
+        met = 0
+        for dim, size in self.sizes().items():
+            for ahead in range(1, size):
+                pl.semaphore_signal(
+                    barrier, inc=1, device_id=self.peer(dim, ahead), device_id_type=MESH
+                )
+                met += 1
+        pl.semaphore_wait(barrier, met)
+
+
+def mesh_counts(sp_count, fs_count):
+    low = 2
+    while low * low < sp_count // 2:
+        low *= 2
+    low = min(low, sp_count)
+    core = 2 if fs_count % 2 == 0 else 1
+    return sp_count // low, low, fs_count // core, core
+
+
+def scatter_kernel(
+    counts, parts, fsdp_too, part_ref, out_ref, own, buf, first, second, third, own_sem, s0, r0,
+    s1, r1, s2, r2, s3, r3,
+):
+    at = Place(counts, fsdp_too)
+    n_hi, n_lo, n_x, n_core = counts
+    rows = out_ref.shape[0] // parts
+    pairs = parts // 2
+    steps = n_hi * pairs
+    lag = 1
+    orders = [[d for d in o if at.sizes()[d] > 1] for o in (("x", "lo"), ("lo", "x"))]
+
+    def remote(src, dst, send, recv, dim, ahead):
+        return pltpu.make_async_remote_copy(
+            src_ref=src, dst_ref=dst, send_sem=send, recv_sem=recv,
+            device_id=at.peer(dim, ahead), device_id_type=MESH,
+        )
+
+    def where(t, v):
+        return (at.hi + 1 + t // pairs) % n_hi, t % pairs * 2 + v
+
+    def mine(t, v, core):
+        hi, q = where(t, v)
+        return part_ref.at[:, core, hi, :, pl.ds(pl.multiple_of(q * rows, 16), rows), :]
+
+    def load_own(t, v):
+        place = own.at[t % 2, v] if n_core > 1 else buf.at[2 * t + v]
+        return pltpu.make_async_copy(mine(t, v, at.core), place, own_sem.at[t % 2, v])
+
+    def core_copy(t, v):
+        return remote(
+            mine(t, v, (at.core + 1) % 2), buf.at[2 * t + v], s0.at[2 * t + v], r0.at[2 * t + v],
+            "core", 1,
+        )
+
+    def mid_copy(t, v, stage, ahead):
+        u = 2 * t + v
+        dim = orders[v][stage]
+        size = at.sizes()[dim]
+        to = ((at.x if dim == "x" else at.lo) + ahead) % size
+        if stage == 0:
+            src = buf.at[u, to] if dim == "x" else buf.at[u, :, to]
+            dst = first.at[u, size - ahead - 1, pl.ds(0, n_lo if dim == "x" else n_x)]
+            return remote(
+                src, dst, s1.at[u, ahead - 1], r1.at[u, size - ahead - 1], dim, ahead
+            )
+        return remote(
+            first.at[u, 0, to], second.at[u, size - ahead - 1],
+            s2.at[u, ahead - 1], r2.at[u, size - ahead - 1], dim, ahead,
+        )
+
+    def wait_in(t, v, stage):
+        size = at.sizes()[orders[v][stage]]
+        for ahead in range(1, size):
+            mid_copy(t, v, stage, ahead).wait_recv()
+
+    def start_out(t, v, stage):
+        size = at.sizes()[orders[v][stage]]
+        for ahead in range(1, size):
+            mid_copy(t, v, stage, ahead).start()
+
+    def wide(ref):
+        return ref[...].astype(jnp.float32)
+
+    def result(t, v):
+        u = 2 * t + v
+        if len(orders[v]) == 2:
+            return second.at[u, 0]
+        if len(orders[v]) == 1:
+            return first.at[u, 0, 0]
+        return buf.at[u, 0, 0]
+
+    def last_copy(t, v, ahead):
+        _, q = where(t, v)
+        return remote(
+            result(t, v), third.at[n_hi - ahead - 1, q],
+            s3.at[2 * t + v], r3.at[n_hi - ahead - 1, q], "hi", ahead,
+        )
+
+    def send_last(t, v):
+        for k in range(n_hi - 1):
+
+            @pl.when(t // pairs == k)
+            def _(k=k):
+                last_copy(t, v, k + 1).start()
+
+    def stage_core(t, v):
+        u = 2 * t + v
+        load_own(t, v).wait()
+        if n_core > 1:
+            core_copy(t, v).wait_recv()
+
+            @pl.loop(0, n_x * n_lo)
+            def _(j):
+                x, lo = j // n_lo, j % n_lo
+                place = buf.at[u, x, lo]
+                place[...] = (wide(place) + wide(own.at[t % 2, v, x, lo])).astype(jnp.bfloat16)
+
+        if orders[v]:
+            start_out(t, v, 0)
+        else:
+            send_last(t, v)
+
+    def stage_mid(t, v, stage):
+        u = 2 * t + v
+        wait_in(t, v, stage)
+        dim = orders[v][stage]
+        size = at.sizes()[dim]
+        if stage == 0:
+            keep = n_lo if dim == "x" else n_x
+
+            @pl.loop(0, keep)
+            def _(j):
+                base = buf.at[u, at.x, j] if dim == "x" else buf.at[u, j, at.lo]
+                total = wide(base)
+                for s in range(size - 1):
+                    total = total + wide(first.at[u, s, j])
+                first.at[u, 0, j][...] = total.astype(jnp.bfloat16)
+
+        else:
+            base = first.at[u, 0, at.x if dim == "x" else at.lo]
+            total = wide(base)
+            for s in range(size - 1):
+                total = total + wide(second.at[u, s])
+            second.at[u, 0][...] = total.astype(jnp.bfloat16)
+        if stage + 1 < len(orders[v]):
+            start_out(t, v, stage + 1)
+        else:
+            send_last(t, v)
+
+    at.meet()
+    if n_core > 1:
+
+        @pl.loop(0, steps)
+        def _(t):
+            for v in range(2):
+                core_copy(t, v).start()
+
+    for v in range(2):
+        load_own(0, v).start()
+
+    depth = len(orders[0])
+
+    @pl.loop(0, steps + depth * lag)
+    def _(t):
+        @pl.when(t + 1 < steps)
+        def _():
+            for v in range(2):
+                load_own(t + 1, v).start()
+
+        @pl.when(t < steps)
+        def _():
+            for v in range(2):
+                stage_core(t, v)
+
+        for stage in range(depth):
+            back = (stage + 1) * lag
+
+            @pl.when((t >= back) & (t < steps + back))
+            def _(stage=stage, back=back):
+                for v in range(2):
+                    stage_mid(t - back, v, stage)
+
+    for g in range(pairs):
+        t = (n_hi - 1) * pairs + g
+        for v in range(2):
+            q = g * 2 + v
+            total = wide(result(t, v))
+            for s in range(n_hi - 1):
+                last_copy(g, v, n_hi - 1 - s).wait_recv()
+                total = total + wide(third.at[s, q])
+            out_ref[pl.ds(q * rows, rows), :] = total.astype(out_ref.dtype)
+
+    @pl.loop(0, steps)
+    def _(t):
+        for v in range(2):
+            if n_core > 1:
+                core_copy(t, v).wait_send()
+            for stage in range(depth):
+                for ahead in range(1, at.sizes()[orders[v][stage]]):
+                    mid_copy(t, v, stage, ahead).wait_send()
+
+            @pl.when(t // pairs < n_hi - 1)
+            def _(v=v):
+                last_copy(t, v, 1).wait_send()
+
+
+def scatter_sum(partial, counts, fsdp_too, parts, out_dtype, ident, name):
+    n_hi, n_lo, n_x, n_core = counts
+    rows, width = partial.shape[4:]
+    r = rows // parts
+    units = n_hi * parts
+    keep = max(n_x, n_lo)
+    peers = max(n_x, n_lo, 2) - 1
+    b16 = jnp.bfloat16
+    own_shape = (2, 2, n_x, n_lo, r, width) if n_core > 1 else (1, 1, 1, 1, 16, 128)
+    scratch = [
+        pltpu.VMEM(own_shape, b16),
+        pltpu.VMEM((units, n_x, n_lo, r, width), b16),
+        pltpu.VMEM((units, peers, keep, r, width), b16),
+        pltpu.VMEM((units, peers, r, width), b16),
+        pltpu.VMEM((max(n_hi - 1, 1), parts, r, width), b16),
+        pltpu.SemaphoreType.DMA((2, 2)),
+        pltpu.SemaphoreType.DMA((units,)),
+        pltpu.SemaphoreType.DMA((units,)),
+        pltpu.SemaphoreType.DMA((units, peers)),
+        pltpu.SemaphoreType.DMA((units, peers)),
+        pltpu.SemaphoreType.DMA((units, peers)),
+        pltpu.SemaphoreType.DMA((units, peers)),
+        pltpu.SemaphoreType.DMA((units,)),
+        pltpu.SemaphoreType.DMA((max(n_hi - 1, 1), parts)),
+    ]
+    return pl.pallas_call(
+        functools.partial(scatter_kernel, counts, parts, fsdp_too),
+        in_specs=[pl.BlockSpec(memory_space=pl.ANY)],
+        out_specs=pl.BlockSpec(memory_space=pltpu.VMEM),
+        out_shape=jax.ShapeDtypeStruct((rows, width), out_dtype),
+        scratch_shapes=scratch,
+        compiler_params=pltpu.CompilerParams(
+            collective_id=ident, has_side_effects=True, vmem_limit_bytes=60 * 2**20
+        ),
+        cost_estimate=pl.CostEstimate(
+            flops=partial.size, bytes_accessed=2 * partial.size, transcendentals=0
+        ),
+        name=name,
+    )(partial)
+
+
+def gather_kernel(
+    counts, parts, fsdp_too, in_ref, out_ref, own_sem, s0, r0, s1, r1, s2, r2, s3, r3
+):
+    at = Place(counts, fsdp_too)
+    n_hi, n_lo, n_x, n_core = counts
+    rows = in_ref.shape[0] // parts
+    pairs = parts // 2
+    steps = n_hi * pairs
+    orders = [[d for d in o if at.sizes()[d] > 1] for o in (("lo", "x"), ("x", "lo"))]
+    depth = len(orders[0])
+
+    def remote(src, dst, send, recv, dim, ahead):
+        return pltpu.make_async_remote_copy(
+            src_ref=src, dst_ref=dst, send_sem=send, recv_sem=recv,
+            device_id=at.peer(dim, ahead), device_id_type=MESH,
+        )
+
+    def span(q):
+        return pl.ds(pl.multiple_of(q * rows, 16), rows)
+
+    def hi_copy(q, ahead):
+        return remote(
+            in_ref.at[span(q)], out_ref.at[at.x, at.core, at.hi, at.lo, span(q)],
+            s0.at[ahead - 1, q], r0.at[n_hi - ahead - 1, q], "hi", ahead,
+        )
+
+    def where(t, v):
+        return (at.hi + n_hi - t // pairs) % n_hi, t % pairs * 2 + v
+
+    def mid_copy(t, v, stage, ahead):
+        u = 2 * t + v
+        hi, q = where(t, v)
+        dim = orders[v][stage]
+        size = at.sizes()[dim]
+        if stage == 0:
+            ref = out_ref.at[at.x, at.core, hi, at.lo, span(q)]
+            if_own = in_ref.at[span(q)]
+            del if_own
+            return remote(
+                ref, ref, s1.at[u, ahead - 1], r1.at[u, size - ahead - 1], dim, ahead
+            )
+        if dim == "x":
+            ref = out_ref.at[at.x, at.core, hi, :, span(q)]
+        else:
+            ref = out_ref.at[:, at.core, hi, at.lo, span(q)]
+        return remote(ref, ref, s2.at[u, ahead - 1], r2.at[u, size - ahead - 1], dim, ahead)
+
+    def core_copy(t, v):
+        u = 2 * t + v
+        hi, q = where(t, v)
+        ref = out_ref.at[:, at.core, hi, :, span(q)]
+        return remote(ref, ref, s3.at[u], r3.at[u], "core", 1)
+
+    def each_mid(t, v, stage, act):
+        size = at.sizes()[orders[v][stage]]
+        for ahead in range(1, size):
+            act(mid_copy(t, v, stage, ahead))
+
+    keep = pltpu.make_async_copy(
+        in_ref, out_ref.at[at.x, at.core, at.hi, at.lo], own_sem
+    )
+    keep.start()
+    at.meet()
+    for ahead in range(1, n_hi):
+        for q in range(parts):
+            hi_copy(q, ahead).start()
+    keep.wait()
+
+    @pl.loop(0, steps + depth)
+    def _(t):
+        @pl.when(t < steps)
+        def _():
+            for v in range(2):
+                _, q = where(t, v)
+                for k in range(1, n_hi):
+
+                    @pl.when(t // pairs == k)
+                    def _(k=k, q=q):
+                        hi_copy(q, k).wait_recv()
+
+                if depth > 0:
+                    each_mid(t, v, 0, lambda c: c.start())
+                elif n_core > 1:
+                    core_copy(t, v).start()
+
+        for stage in range(depth):
+            back = stage + 1
+
+            @pl.when((t >= back) & (t < steps + back))
+            def _(stage=stage, back=back):
+                for v in range(2):
+                    each_mid(t - back, v, stage, lambda c: c.wait_recv())
+                    if stage + 1 < depth:
+                        each_mid(t - back, v, stage + 1, lambda c: c.start())
+                    elif n_core > 1:
+                        core_copy(t - back, v).start()
+
+    @pl.loop(0, steps)
+    def _(t):
+        for v in range(2):
+            if n_core > 1:
+                core_copy(t, v).wait_recv()
+                core_copy(t, v).wait_send()
+            for stage in range(depth):
+                each_mid(t, v, stage, lambda c: c.wait_send())
+
+    for q in range(parts):
+        for ahead in range(1, n_hi):
+            hi_copy(q, ahead).wait_send()
+
+
+def gather_rows(own, counts, fsdp_too, parts, ident, name):
+    n_hi, n_lo, n_x, n_core = counts
+    rows, width = own.shape
+    units = n_hi * parts
+    peers = max(n_x, n_lo, 2) - 1
+    ahead = max(n_hi - 1, 1)
+    scratch = [
+        pltpu.SemaphoreType.DMA,
+        pltpu.SemaphoreType.DMA((ahead, parts)),
+        pltpu.SemaphoreType.DMA((ahead, parts)),
+        pltpu.SemaphoreType.DMA((units, peers)),
+        pltpu.SemaphoreType.DMA((units, peers)),
+        pltpu.SemaphoreType.DMA((units, peers)),
+        pltpu.SemaphoreType.DMA((units, peers)),
+        pltpu.SemaphoreType.DMA((units,)),
+        pltpu.SemaphoreType.DMA((units,)),
+    ]
+    total = rows * n_hi * n_lo * n_x * n_core
+    out = pl.pallas_call(
+        functools.partial(gather_kernel, counts, parts, fsdp_too),
+        in_specs=[pl.BlockSpec(memory_space=pl.ANY)],
+        out_specs=pl.BlockSpec(memory_space=pl.ANY),
+        out_shape=jax.ShapeDtypeStruct((n_x, n_core, n_hi, n_lo, rows, width), own.dtype),
+        scratch_shapes=scratch,
+        compiler_params=pltpu.CompilerParams(collective_id=ident, has_side_effects=True),
+        cost_estimate=pl.CostEstimate(
+            flops=0, bytes_accessed=4 * total * width, transcendentals=0
+        ),
+        name=name,
+    )(own)
+    return out.reshape(total, width)
+
+
+def attend(query_heads, key_heads, value_heads, lengths):
+    seq_rows, head_local, _ = query_heads.shape
+    block_rows, block_count, key_rows, pad_rows = window_geometry(seq_rows)
+    segments = segment_ids(lengths, seq_rows)
+    seg_padded = pad_front(segments, pad_rows, -1)
+    key_padded = pad_front(key_heads, pad_rows, 0.0)
+    value_padded = pad_front(value_heads, pad_rows, 0.0)
+    score_scale = HEAD_DIM ** (-0.5)
+    block_numbers = jnp.arange(block_count, dtype=jnp.int32)
+
+    def block_scores(first_row):
+        query_block = lax.dynamic_slice_in_dim(query_heads, first_row, block_rows)
+        key_block = lax.dynamic_slice_in_dim(key_padded, first_row, key_rows)
+        scores = (
+            jnp.einsum("qhd,khd->hqk", query_block, key_block, preferred_element_type=jnp.float32)
+            * score_scale
+        )
+        allowed = window_allowed(segments, seg_padded, first_row, block_rows, key_rows, pad_rows)
+        return (jnp.where(allowed[None], scores, masked_score), query_block, key_block)
+
+    def forward_block(carry_in, block_index):
+        first_row = block_index * block_rows
+        scores, query_block, key_block = block_scores(first_row)
+        value_block = lax.dynamic_slice_in_dim(value_padded, first_row, key_rows)
+        row_max = jnp.max(scores, axis=-1, keepdims=True)
+        weights = jnp.exp(scores - row_max)
+        row_total = jnp.sum(weights, axis=-1, keepdims=True)
+        probs = (weights / row_total).astype(jnp.bfloat16)
+        attended = jnp.einsum(
+            "hqk,khd->qhd", probs, value_block, preferred_element_type=jnp.float32
+        )
+        return (carry_in, (attended.astype(jnp.bfloat16), (row_max + jnp.log(row_total))[..., 0]))
+
+    _, (attended_blocks, lse_blocks) = lax.scan(forward_block, 0, block_numbers)
+    attended_heads = attended_blocks.reshape(seq_rows, head_local, HEAD_DIM)
+
+    def back(attended_grad_heads):
+        def backward_block(carry_in, block_index):
+            key_total, value_total = carry_in
+            first_row = block_index * block_rows
+            scores, query_block, key_block = block_scores(first_row)
+            value_block = lax.dynamic_slice_in_dim(value_padded, first_row, key_rows)
+            grad_block = lax.dynamic_slice_in_dim(attended_grad_heads, first_row, block_rows)
+            probs = jnp.exp(scores - lse_blocks[block_index][..., None])
+            prob_grad = jnp.einsum(
+                "qhd,khd->hqk", grad_block, value_block, preferred_element_type=jnp.float32
+            )
+            row_delta = jnp.sum(probs * prob_grad, axis=-1, keepdims=True)
+            score_grad = (probs * (prob_grad - row_delta)).astype(jnp.bfloat16)
+            query_part = (
+                jnp.einsum("hqk,khd->qhd", score_grad, key_block, preferred_element_type=jnp.float32)
+                * score_scale
+            )
+            key_part = (
+                jnp.einsum("hqk,qhd->khd", score_grad, query_block, preferred_element_type=jnp.float32)
+                * score_scale
+            )
+            value_part = jnp.einsum(
+                "hqk,qhd->khd",
+                probs.astype(jnp.bfloat16),
+                grad_block,
+                preferred_element_type=jnp.float32,
+            )
+            key_total = lax.dynamic_update_slice_in_dim(
+                key_total,
+                lax.dynamic_slice_in_dim(key_total, first_row, key_rows) + key_part,
+                first_row,
+                0,
+            )
+            value_total = lax.dynamic_update_slice_in_dim(
+                value_total,
+                lax.dynamic_slice_in_dim(value_total, first_row, key_rows) + value_part,
+                first_row,
+                0,
+            )
+            return ((key_total, value_total), query_part.astype(jnp.bfloat16))
+
+        zero_keys = jnp.zeros((pad_rows + seq_rows, head_local, HEAD_DIM), jnp.float32)
+        (key_total, value_total), query_blocks = lax.scan(
+            backward_block, (zero_keys, zero_keys), block_numbers
+        )
+        query_grad_heads = query_blocks.reshape(seq_rows, head_local, HEAD_DIM)
+        key_grad_heads = key_total[pad_rows:].astype(jnp.bfloat16)
+        value_grad_heads = value_total[pad_rows:].astype(jnp.bfloat16)
+        return query_grad_heads, key_grad_heads, value_grad_heads
+
+    return attended_heads, back
+
+
+def scatter_over_all(partial, rows, sp_count, fs_count, ident, name):
+    counts = mesh_counts(sp_count, fs_count)
+    width = partial.shape[1]
+    parts = 4 if rows % 64 == 0 else 2
+    if 1.4 * partial.size * 2 > 52 * 2**20 or rows % (parts * 16):
+        part = lax.psum_scatter(partial, "fsdp", scatter_dimension=0, tiled=True)
+        return lax.psum_scatter(part, "sp", scatter_dimension=0, tiled=True).astype(jnp.float32)
+    n_hi, n_lo, n_x, n_core = counts
+    shaped = partial.reshape(n_x, n_core, n_hi, n_lo, rows, width)
+    return scatter_sum(shaped, counts, True, parts, jnp.float32, ident, name)
+
+
+def scatter_over_sp(partial, rows, sp_count, ident, name):
+    n_hi, n_lo, _, _ = mesh_counts(sp_count, 1)
+    parts = 4 if rows % 64 == 0 else 2
+    shaped = partial.reshape(1, 1, n_hi, n_lo, rows, partial.shape[1])
+    return scatter_sum(shaped, (n_hi, n_lo, 1, 1), False, parts, jnp.float32, ident, name)
+
+
+def gather_over_all(own, sp_count, fs_count, ident, name):
+    parts = 4 if own.shape[0] % 64 == 0 else 2
+    return gather_rows(own, mesh_counts(sp_count, fs_count), True, parts, ident, name)
+
+
+def gather_over_sp(own, sp_count, ident, name):
+    n_hi, n_lo, _, _ = mesh_counts(sp_count, 1)
+    parts = 4 if own.shape[0] % 64 == 0 else 2
+    return gather_rows(own, (n_hi, n_lo, 1, 1), False, parts, ident, name)
 
 
 def local(
@@ -485,115 +1021,64 @@
 ):
     sp_count = lax.axis_size("sp")
     fs_count = lax.axis_size("fsdp")
+    my_sp = lax.axis_index("sp")
+    my_fs = lax.axis_index("fsdp")
     hidden_in = tokens[0].astype(jnp.float32)
-    tok_rows = hidden_in.shape[0]
-    width = hidden_in.shape[1]
+    tok_rows, width = hidden_in.shape
     head_local = HEADS // sp_count
     seq_rows = tok_rows * sp_count
-    gathered = (
-        lax.all_gather(norm_attn, "fsdp", axis=0, tiled=True),
-        lax.all_gather(norm_query, "fsdp", axis=0, tiled=True),
-        lax.all_gather(norm_key, "fsdp", axis=0, tiled=True),
-        lax.all_gather(norm_ffn, "fsdp", axis=0, tiled=True),
-        lax.all_gather(w_query, "fsdp", axis=0, tiled=True),
-        lax.all_gather(w_key, "fsdp", axis=0, tiled=True),
-        lax.all_gather(w_value, "fsdp", axis=0, tiled=True),
-        lax.all_gather(w_out, "fsdp", axis=0, tiled=True),
-        lax.all_gather(w_router, "fsdp", axis=0, tiled=True),
-    )
-    (
-        gain_attn,
-        gain_query,
-        gain_key,
-        gain_ffn,
-        query_mat,
-        key_mat,
-        value_mat,
-        out_mat,
-        router_mat,
-    ) = gathered
+    span = head_local * HEAD_DIM
+    expert_local = EXPERTS // sp_count
+    first_expert = my_sp * expert_local
+    gains = lax.all_gather(
+        jnp.stack([norm_attn, norm_query, norm_key, norm_ffn]), "fsdp", axis=1, tiled=True
+    ).astype(jnp.float32)
+    gain_attn, gain_ffn = gains[0], gains[3]
+    own_cols = lax.dynamic_slice_in_dim(gains, my_sp * span, span, axis=1)
+    gain_query, gain_key = own_cols[1], own_cols[2]
+    qkv_own = jnp.concatenate(
+        [
+            lax.dynamic_slice_in_dim(w, my_sp * span, span, axis=1)
+            for w in (w_query, w_key, w_value)
+        ],
+        axis=1,
+    )
+    qkv_mat = lax.all_gather(qkv_own, "fsdp", axis=0, tiled=True)
+    out_mat = lax.all_gather(w_out, "fsdp", axis=0, tiled=True)
+    router_mat = lax.all_gather(w_router, "fsdp", axis=0, tiled=True)
     cot_all = lax.all_gather(cotangent[0], ("fsdp", "sp"), axis=0, tiled=True)
     routing = route_plan(expert_ids[0], sp_count, fs_count)
     cot_rows, _ = dispatch_rows(cot_all, routing, None)
-    attn_normed, attn_pull = jax.vjp(rms_scale, hidden_in, gain_attn.astype(jnp.float32))
-    attn_in = attn_normed.astype(jnp.bfloat16)
-    query_raw = jnp.dot(attn_in, query_mat, preferred_element_type=jnp.float32)
-    key_raw = jnp.dot(attn_in, key_mat, preferred_element_type=jnp.float32)
-    value_rows = jnp.dot(attn_in, value_mat, preferred_element_type=jnp.float32).astype(
-        jnp.bfloat16
-    )
-    cosine, sine = rope_tables(
-        lax.axis_index("sp") * tok_rows + jnp.arange(tok_rows, dtype=jnp.int32), HEAD_DIM
-    )
-
-    def head_path(raw_proj, gain_vec):
-        return rotate_pairs(
-            rms_scale(raw_proj, gain_vec).reshape(tok_rows, HEADS, HEAD_DIM), cosine, sine
-        )
-
-    query_rot, query_pull = jax.vjp(head_path, query_raw, gain_query.astype(jnp.float32))
-    key_rot, key_pull = jax.vjp(head_path, key_raw, gain_key.astype(jnp.float32))
-    query_heads, key_heads, value_heads = (
-        lax.all_to_all(
-            query_rot.astype(jnp.bfloat16), "sp", split_axis=1, concat_axis=0, tiled=True
-        ),
-        lax.all_to_all(key_rot.astype(jnp.bfloat16), "sp", split_axis=1, concat_axis=0, tiled=True),
-        lax.all_to_all(
-            value_rows.reshape(tok_rows, HEADS, HEAD_DIM),
-            "sp",
-            split_axis=1,
-            concat_axis=0,
-            tiled=True,
-        ),
-    )
-    block_rows, block_count, key_rows, pad_rows = window_geometry(seq_rows)
-    segments = segment_ids(doc_lengths[0], seq_rows)
-    seg_padded = pad_front(segments, pad_rows, -1)
-    key_padded = pad_front(key_heads, pad_rows, 0.0)
-    value_padded = pad_front(value_heads, pad_rows, 0.0)
-    score_scale = HEAD_DIM ** (-0.5)
-    block_numbers = jnp.arange(block_count, dtype=jnp.int32)
-
-    def block_scores(first_row):
-        query_block = lax.dynamic_slice_in_dim(query_heads, first_row, block_rows)
-        key_block = lax.dynamic_slice_in_dim(key_padded, first_row, key_rows)
-        scores = (
-            jnp.einsum("qhd,khd->hqk", query_block, key_block, preferred_element_type=jnp.float32)
-            * score_scale
-        )
-        allowed = window_allowed(segments, seg_padded, first_row, block_rows, key_rows, pad_rows)
-        return (jnp.where(allowed[None], scores, masked_score), query_block, key_block)
-
-    def forward_block(carry_in, block_index):
-        first_row = block_index * block_rows
-        scores, query_block, key_block = block_scores(first_row)
-        value_block = lax.dynamic_slice_in_dim(value_padded, first_row, key_rows)
-        row_max = jnp.max(scores, axis=-1, keepdims=True)
-        weights = jnp.exp(scores - row_max)
-        row_total = jnp.sum(weights, axis=-1, keepdims=True)
-        probs = (weights / row_total).astype(jnp.bfloat16)
-        attended = jnp.einsum(
-            "hqk,khd->qhd", probs, value_block, preferred_element_type=jnp.float32
-        )
-        return (carry_in, (attended.astype(jnp.bfloat16), (row_max + jnp.log(row_total))[..., 0]))
-
-    _, (attended_blocks, lse_blocks) = lax.scan(forward_block, 0, block_numbers)
-    attended_heads = attended_blocks.reshape(seq_rows, head_local, HEAD_DIM)
+
+    attn_normed, attn_pull = jax.vjp(rms_scale, hidden_in, gain_attn)
+    attn_in = gather_over_sp(attn_normed.astype(jnp.bfloat16), sp_count, 1, "gather_attn_in")
+    qkv_raw = jnp.dot(attn_in, qkv_mat, preferred_element_type=jnp.float32)
+    raw = (qkv_raw[:, :span], qkv_raw[:, span : 2 * span])
+    value_heads = qkv_raw[:, 2 * span :].astype(jnp.bfloat16).reshape(
+        seq_rows, head_local, HEAD_DIM
+    )
+    squares = lax.psum(jnp.stack([jnp.sum(r * r, axis=-1) for r in raw]), "sp")
+    scales = lax.rsqrt(squares / width + eps)[:, :, None]
+    cosine, sine = rope_tables(jnp.arange(seq_rows, dtype=jnp.int32), HEAD_DIM)
+
+    def turned(normed):
+        return rotate_pairs(normed.reshape(seq_rows, head_local, HEAD_DIM), cosine, sine)
+
+    query_heads = turned(raw[0] * scales[0] * gain_query).astype(jnp.bfloat16)
+    key_heads = turned(raw[1] * scales[1] * gain_key).astype(jnp.bfloat16)
+    attended_heads, attend_back = attend(query_heads, key_heads, value_heads, doc_lengths[0])
     attended_tok = lax.all_to_all(
-        attended_heads, "sp", split_axis=0, concat_axis=1, tiled=True
-    ).reshape(tok_rows, width)
+        attended_heads.reshape(seq_rows, span), "sp", split_axis=0, concat_axis=1, tiled=True
+    )
     after_attn = hidden_in + jnp.dot(attended_tok, out_mat, preferred_element_type=jnp.float32)
-    ffn_normed, ffn_pull = jax.vjp(rms_scale, after_attn, gain_ffn.astype(jnp.float32))
+    ffn_normed, ffn_pull = jax.vjp(rms_scale, after_attn, gain_ffn)
     ffn_in = ffn_normed.astype(jnp.bfloat16)
     logits = jnp.dot(ffn_in, router_mat, preferred_element_type=jnp.float32)
     router = jax.nn.softmax(logits, axis=-1)
-    rank = routing[0]
-    ffn_all = lax.all_gather(ffn_in, ("fsdp", "sp"), axis=0, tiled=True)
+    ffn_all = gather_over_all(ffn_in, sp_count, fs_count, 2, "gather_ffn_in")
     router_all = jax.nn.softmax(
         jnp.dot(ffn_all, router_mat, preferred_element_type=jnp.float32), axis=-1
     )
-    expert_local = EXPERTS // sp_count
-    first_expert = lax.axis_index("sp") * expert_local
     gate_rows = (
         lax.dynamic_slice_in_dim(router_all, first_expert, expert_local, axis=1)
         .reshape(-1, BLOCK, expert_local)
@@ -603,12 +1088,18 @@
     out_rows, in_grad_rows, grad_gate, grad_up, grad_down = run_experts(
         ffn_rows, cot_rows, gate_slots, w_gate, w_up, w_down, routing[3], first_expert[None]
     )
-    in_grad_sum = reduce_tokens(combine_rows(in_grad_rows, routing, "combine_grads"))
-    moe_sum = reduce_tokens(combine_rows(out_rows, routing, "combine_outputs"))
-    mixed = (after_attn + moe_sum.astype(jnp.float32)).astype(jnp.bfloat16)
+    in_grad_sum = scatter_over_all(
+        combine_rows(in_grad_rows, routing, "combine_grads"),
+        tok_rows, sp_count, fs_count, 3, "scatter_grads",
+    )
+    moe_sum = scatter_over_all(
+        combine_rows(out_rows, routing, "combine_outputs"),
+        tok_rows, sp_count, fs_count, 4, "scatter_outputs",
+    )
+    mixed = (after_attn + moe_sum).astype(jnp.bfloat16)
     upstream = cotangent[0].astype(jnp.float32)
-    ffn_in_grad = in_grad_sum[:, :width].astype(jnp.float32)
-    router_grad = in_grad_sum[:, width : width + EXPERTS].astype(jnp.float32)
+    ffn_in_grad = in_grad_sum[:, :width]
+    router_grad = in_grad_sum[:, width : width + EXPERTS]
     logit_grad = (
         router * (router_grad - jnp.sum(router * router_grad, axis=-1, keepdims=True))
     ).astype(jnp.bfloat16)
@@ -619,137 +1110,83 @@
     ffn_hidden_grad, ffn_gain_term = ffn_pull(ffn_in_grad)
     after_grad = upstream + ffn_hidden_grad
     attn_out_grad = after_grad.astype(jnp.bfloat16)
-    out_term = jnp.dot(attended_tok.T, attn_out_grad, preferred_element_type=jnp.float32)
     attended_grad = jnp.dot(attn_out_grad, out_mat.T, preferred_element_type=jnp.float32).astype(
         jnp.bfloat16
     )
     attended_grad_heads = lax.all_to_all(
-        attended_grad.reshape(tok_rows, HEADS, HEAD_DIM),
-        "sp",
-        split_axis=1,
-        concat_axis=0,
-        tiled=True,
-    )
-
-    def backward_block(carry_in, block_index):
-        key_total, value_total = carry_in
-        first_row = block_index * block_rows
-        scores, query_block, key_block = block_scores(first_row)
-        value_block = lax.dynamic_slice_in_dim(value_padded, first_row, key_rows)
-        grad_block = lax.dynamic_slice_in_dim(attended_grad_heads, first_row, block_rows)
-        probs = jnp.exp(scores - lse_blocks[block_index][..., None])
-        prob_grad = jnp.einsum(
-            "qhd,khd->hqk", grad_block, value_block, preferred_element_type=jnp.float32
-        )
-        row_delta = jnp.sum(probs * prob_grad, axis=-1, keepdims=True)
-        score_grad = (probs * (prob_grad - row_delta)).astype(jnp.bfloat16)
-        query_part = (
-            jnp.einsum("hqk,khd->qhd", score_grad, key_block, preferred_element_type=jnp.float32)
-            * score_scale
-        )
-        key_part = (
-            jnp.einsum("hqk,qhd->khd", score_grad, query_block, preferred_element_type=jnp.float32)
-            * score_scale
-        )
-        value_part = jnp.einsum(
-            "hqk,qhd->khd",
-            probs.astype(jnp.bfloat16),
-            grad_block,
-            preferred_element_type=jnp.float32,
-        )
-        key_total = lax.dynamic_update_slice_in_dim(
-            key_total,
-            lax.dynamic_slice_in_dim(key_total, first_row, key_rows) + key_part,
-            first_row,
-            0,
-        )
-        value_total = lax.dynamic_update_slice_in_dim(
-            value_total,
-            lax.dynamic_slice_in_dim(value_total, first_row, key_rows) + value_part,
-            first_row,
-            0,
-        )
-        return ((key_total, value_total), query_part.astype(jnp.bfloat16))
-
-    zero_keys = jnp.zeros((pad_rows + seq_rows, head_local, HEAD_DIM), jnp.float32)
-    (key_total, value_total), query_blocks = lax.scan(
-        backward_block, (zero_keys, zero_keys), block_numbers
-    )
-    query_grad_heads = query_blocks.reshape(seq_rows, head_local, HEAD_DIM)
-    key_grad_heads = key_total[pad_rows:].astype(jnp.bfloat16)
-    value_grad_heads = value_total[pad_rows:].astype(jnp.bfloat16)
-    query_back, key_back, value_back = (
-        lax.all_to_all(query_grad_heads, "sp", split_axis=0, concat_axis=1, tiled=True),
-        lax.all_to_all(key_grad_heads, "sp", split_axis=0, concat_axis=1, tiled=True),
-        lax.all_to_all(value_grad_heads, "sp", split_axis=0, concat_axis=1, tiled=True),
-    )
-    query_raw_grad, query_gain_term = query_pull(query_back.astype(jnp.float32))
-    key_raw_grad, key_gain_term = key_pull(key_back.astype(jnp.float32))
-    query_low = query_raw_grad.astype(jnp.bfloat16)
-    key_low = key_raw_grad.astype(jnp.bfloat16)
-    value_low = value_back.reshape(tok_rows, width)
-    attn_in_grad = jnp.dot(query_low, query_mat.T, preferred_element_type=jnp.float32)
-    attn_in_grad = attn_in_grad + jnp.dot(key_low, key_mat.T, preferred_element_type=jnp.float32)
-    attn_in_grad = attn_in_grad + jnp.dot(
-        value_low, value_mat.T, preferred_element_type=jnp.float32
-    )
-    query_term = jnp.dot(attn_in.T, query_low, preferred_element_type=jnp.float32)
-    key_term = jnp.dot(attn_in.T, key_low, preferred_element_type=jnp.float32)
-    value_term = jnp.dot(attn_in.T, value_low, preferred_element_type=jnp.float32)
+        attended_grad, "sp", split_axis=1, concat_axis=0, tiled=True
+    ).reshape(seq_rows, head_local, HEAD_DIM)
+    out_term = jnp.dot(attended_tok.T, attn_out_grad, preferred_element_type=jnp.float32)
+    row_terms = jnp.concatenate(
+        [
+            out_term.astype(jnp.bfloat16),
+            router_term.astype(jnp.bfloat16),
+            jnp.zeros((width, 128 - EXPERTS), jnp.bfloat16),
+        ],
+        axis=1,
+    )
+    row_sums = scatter_over_all(
+        row_terms, width // (sp_count * fs_count), sp_count, fs_count, 5, "scatter_out_rows"
+    )
+    query_grad_heads, key_grad_heads, value_low = attend_back(attended_grad_heads)
+
+    def unturned(grad):
+        return rotate_pairs(grad.astype(jnp.float32), cosine, -sine).reshape(seq_rows, span)
+
+    normed_grads = (unturned(query_grad_heads), unturned(key_grad_heads))
+    scaled_grads = (normed_grads[0] * gain_query, normed_grads[1] * gain_key)
+    products = lax.psum(
+        jnp.stack([jnp.sum(g * r, axis=-1) for g, r in zip(scaled_grads, raw)]), "sp"
+    )[:, :, None]
+    gain_terms = [
+        jnp.sum(g * r * s, axis=0) for g, r, s in zip(normed_grads, raw, scales)
+    ]
+    raw_grads = [
+        (g * s - r * (s * s * s) * (p / width)).astype(jnp.bfloat16)
+        for g, r, s, p in zip(scaled_grads, raw, scales, products)
+    ]
+    qkv_low = jnp.concatenate(raw_grads + [value_low.reshape(seq_rows, span)], axis=1)
+    attn_partial = lax.dot_general(
+        qkv_low, qkv_mat, (((1,), (1,)), ((), ())), preferred_element_type=jnp.float32
+    ).astype(jnp.bfloat16)
+    attn_in_grad = scatter_over_sp(attn_partial, tok_rows, sp_count, 6, "scatter_attn_in")
+    qkv_term = jnp.dot(attn_in.T, qkv_low, preferred_element_type=jnp.float32)
     attn_hidden_grad, attn_gain_term = attn_pull(attn_in_grad)
     grad_tokens = after_grad + attn_hidden_grad
-    scattered = (
-        lax.psum_scatter(
-            attn_gain_term.astype(jnp.bfloat16), "fsdp", scatter_dimension=0, tiled=True
-        ).astype(jnp.float32),
-        lax.psum_scatter(
-            query_gain_term.astype(jnp.bfloat16), "fsdp", scatter_dimension=0, tiled=True
-        ).astype(jnp.float32),
-        lax.psum_scatter(
-            key_gain_term.astype(jnp.bfloat16), "fsdp", scatter_dimension=0, tiled=True
-        ).astype(jnp.float32),
-        lax.psum_scatter(
-            ffn_gain_term.astype(jnp.bfloat16), "fsdp", scatter_dimension=0, tiled=True
-        ).astype(jnp.float32),
-        lax.psum_scatter(
-            query_term.astype(jnp.bfloat16), "fsdp", scatter_dimension=0, tiled=True
-        ).astype(jnp.float32),
-        lax.psum_scatter(
-            key_term.astype(jnp.bfloat16), "fsdp", scatter_dimension=0, tiled=True
-        ).astype(jnp.float32),
-        lax.psum_scatter(
-            value_term.astype(jnp.bfloat16), "fsdp", scatter_dimension=0, tiled=True
-        ).astype(jnp.float32),
-        lax.psum_scatter(
-            out_term.astype(jnp.bfloat16), "fsdp", scatter_dimension=0, tiled=True
-        ).astype(jnp.float32),
-        lax.psum_scatter(
-            router_term.astype(jnp.bfloat16), "fsdp", scatter_dimension=0, tiled=True
-        ).astype(jnp.float32),
-    )
-    summed = (
-        lax.psum(scattered[0].astype(jnp.bfloat16), "sp").astype(jnp.float32),
-        lax.psum(scattered[1].astype(jnp.bfloat16), "sp").astype(jnp.float32),
-        lax.psum(scattered[2].astype(jnp.bfloat16), "sp").astype(jnp.float32),
-        lax.psum(scattered[3].astype(jnp.bfloat16), "sp").astype(jnp.float32),
-        lax.psum(scattered[4].astype(jnp.bfloat16), "sp").astype(jnp.float32),
-        lax.psum(scattered[5].astype(jnp.bfloat16), "sp").astype(jnp.float32),
-        lax.psum(scattered[6].astype(jnp.bfloat16), "sp").astype(jnp.float32),
-        lax.psum(scattered[7].astype(jnp.bfloat16), "sp").astype(jnp.float32),
-        lax.psum(scattered[8].astype(jnp.bfloat16), "sp").astype(jnp.float32),
+    qkv_sums = lax.psum_scatter(
+        qkv_term.astype(jnp.bfloat16), "fsdp", scatter_dimension=0, tiled=True
+    )
+    qkv_every = lax.all_gather(qkv_sums, "sp", axis=0)
+    rows_every = lax.all_gather(row_sums.astype(jnp.bfloat16), "sp", axis=0, tiled=True)
+    dense = [
+        qkv_every[:, :, k * span : (k + 1) * span]
+        .transpose(1, 0, 2)
+        .reshape(-1, width)
+        .astype(jnp.float32)
+        for k in range(3)
+    ]
+    placed = [
+        lax.dynamic_update_slice_in_dim(jnp.zeros((width,), jnp.float32), g, my_sp * span, 0)
+        for g in gain_terms
+    ]
+    gain_sums = lax.psum(
+        jnp.stack([attn_gain_term, placed[0], placed[1], ffn_gain_term]), ("sp", "fsdp")
+    )
+    gain_sums = lax.dynamic_slice_in_dim(
+        gain_sums, my_fs * (width // fs_count), width // fs_count, axis=1
     )
     return (
         mixed[None],
         grad_tokens[None],
-        summed[0],
-        summed[1],
-        summed[2],
-        summed[3],
-        summed[4],
-        summed[5],
-        summed[6],
-        summed[7],
-        summed[8],
+        gain_sums[0],
+        gain_sums[1],
+        gain_sums[2],
+        gain_sums[3],
+        dense[0],
+        dense[1],
+        dense[2],
+        rows_every[:, :width].astype(jnp.float32),
+        rows_every[:, width : width + EXPERTS].astype(jnp.float32),
         grad_gate,
         grad_up,
         grad_down,

time: 2600 us -> 1800 us (0.69)
  waiting for transfers between devices: 1570 us -> 44.5 us
  Pallas kernels: 327 us -> 1100 us
  local copies, waits for them, and re-layouts: 162 us -> 118 us
  other arithmetic: 62.9 us -> 93.3 us
  starting transfers between devices: 35.1 us -> 7.77 us
  matrix products: 206 us -> 179 us
    pallas_call x0 -> x6, Pallas kernels: none -> 798 us  [the longest x4 492 us: scatter_sum(): pl.pallas_call(functools.partial(scatter_kernel, counts, parts, fsdp_too)...]
    reduce_scatter x7 -> x1, waiting for transfers between devices: 472 us -> 0.02 us  [local(): lax.psum_scatter(qkv_term.astype(jnp.bfloat16), 'fsdp', scatter_dimension...]
    unnamed x18 -> x6, waiting for transfers between devices: 443 us -> 1.92 us
    all_gather x5 -> x4, waiting for transfers between devices: 263 us -> 10.3 us  [the longest x1 10.3 us: local(): qkv_every = lax.all_gather(qkv_sums, 'sp', axis=0)]
    psum x1 -> x0, waiting for transfers between devices: 222 us -> none  [local(): lax.psum(scattered[4].astype(jnp.bfloat16), 'sp').astype(jnp.float32)]
    psum x1 -> x3, blocking collectives: 22.3 us -> 134 us  [the longest x1 64.1 us: local(): lax.psum(jnp.stack([attn_gain_term, placed[0], placed[1], ffn_gain_term])...]
    all_to_all x6 -> x2, waiting for transfers between devices: 142 us -> 32.1 us  [the longest x1 23.5 us: local(): lax.all_to_all(attended_grad, 'sp', split_axis=1, concat_axis=0, tiled=True)]
    all_to_all x2 -> x0, blocking collectives: 61.1 us -> none  [the longest x1 31.4 us: local(): lax.all_to_all(key_rot.astype(jnp.bfloat16), 'sp', split_axis=1, concat_a...]
  transfers between devices with their start and end apart: 22 -> 8, of which waited for: 19 -> 3; matrix products, arithmetic and copies ran while one was open for 14% -> 9% of each run, Pallas kernels for 3% -> 29%
where the time goes in v2:
time: 1800 us; the launch traced here: 1790 us
  Pallas kernels  1100 us (61%)
  blocking collectives  217 us (12%)
  matrix products  179 us (10%)
  local copies, waits for them, and re-layouts  118 us (7%)
  other arithmetic  93.3 us (5%)
  waiting for transfers between devices  44.5 us (2%)
    pallas_call x4, Pallas kernels, scatter_sum(): pl.pallas_call(functools.partial(scatter_kernel, counts, parts, fsdp_too)...  492 us
    pallas_call x2, Pallas kernels, gather_rows(): pl.pallas_call(functools.partial(gather_kernel, counts, parts, fsdp_too),...  306 us
    pallas_call x1, Pallas kernels, run_experts(): pl.pallas_call(expert_kernel, grid_spec=pltpu.PrefetchScalarGridSpec(num_...  138 us
    pallas_call x2, Pallas kernels, combine_rows(): pl.pallas_call(combine_kernel, grid_spec=pltpu.PrefetchScalarGridSpec(num...  83.5 us
    all_gather x1, blocking collectives, route_plan(): ids = lax.all_gather(own_ids, ('fsdp', 'sp'), axis=0, tiled=True)  70.6 us
    psum x1, blocking collectives, local(): lax.psum(jnp.stack([attn_gain_term, placed[0], placed[1], ffn_gain_term])...  64.1 us
    pallas_call x1, Pallas kernels, dispatch_rows(): pl.pallas_call(dispatch_kernel, grid_spec=pltpu.PrefetchScalarGridSpec(nu...  42.6 us
    pallas_call x1, Pallas kernels, dispatch_rows(): pl.pallas_call(plain, grid_spec=pltpu.PrefetchScalarGridSpec(num_scalar_p...  41.6 us
  transfers between devices with their start and end apart: 8, of which 3 were waited for; matrix products, arithmetic and copies ran while one was open for 9% of the time, Pallas kernels for 29%

profile of v2, /device:TPU:0, one launch (start us, length us, event | category | flops | bytes accessed | tf_op | source)
XLA Modules:
  0.0 1791.5 jit_solution(18276152119293508425)
XLA Ops:
  12.5 6.2 all_gather.27
  20.8 138.1 %gather_attn_in.1 = bf16[1,1,4,2,256,2048]{5,4,3,2,1,0:T(8,128)(2,1)} custom-call(bf16[256,2048]{1,0:T(8,128)(2,1)} %fusion.47.in_ref), custom_call_target="tpu_custom_call" | custom-call | bytes 16777216 | tf_op jit(solution)/shard_map/gather_attn_in/pallas_call | solution.py:870
  159.3 70.6 %all-gather = s32[1,8192,8]{1,2,0:T(8,128)S(1)} all-gather(s32[1,256,8]{1,2,0:T(8,128)S(1)} %copy-done.77), channel_id=2, replica_groups=mesh['sp'=8,'fsdp'=4] {'fsdp','sp'}, dimensions={1}, use_global_device_ids=true | all-gather | bytes 270336 | tf_op jit(solution)/shard_map/all_gather | solution.py:86
  230.3 5.2 fusion.81
  235.5 10.4 fusion.89
  249.0 34.2 %psum.21 = f32[2,2048]{1,0:T(2,128)S(1)} all-reduce(f32[2,2048]{1,0:T(2,128)S(1)} %pad_maximum_fusion.6), channel_id=1, replica_groups=mesh['sp'=8,'fsdp'=4] {'sp'}, use_global_device_ids=true, to_apply=%region_3.4 | all-reduce | flops 4096 | bytes 32768 | tf_op jit(solution)/shard_map/psum | solution.py:1060
  283.3 4.7 multiply_multiply_fusion
  289.9 2.9 copy.152
  303.7 42.3 %while.30 = (s32[]{:T(128)}, bf16[4,512,2,128]{3,2,1,0:T(2,128)(2,1)S(1)}, f32[4,2,512]{2,1,0:T(2,128)}, s32[4]{0:T(128)S(1)}, bf16[3072,2,128]{2,0,1:T(8,128)(2...) while((s32[]{:T(128)}, ...), condition=%wide.region_9.10_spmd, body=%wide.region_6.9_spmd.sunk | while | flops 829031424 | bytes 31531816 | solution.py:918
  306.2 2.8 fusion.127
  316.8 2.8 fusion.127
  327.4 2.8 fusion.127
  337.9 2.8 fusion.127
  347.5 3.7 all-to-all-start
  354.0 6.2 all_gather.31
  360.4 8.7 all-to-all-done
  371.6 6.2 multiply_reduce_fusion.6
  380.3 167.9 %gather_ffn_in.1 = bf16[2,2,4,2,256,2048]{5,4,3,2,1,0:T(8,128)(2,1)} custom-call(bf16[256,2048]{1,0:T(8,128)(2,1)} %multiply_convert_fusion.1.in_ref), custom_call_target="tpu_custom_call" | custom-call | bytes 67108864 | tf_op jit(solution)/shard_map/gather_ffn_in/pallas_call | solution.py:870
  549.7 16.2 fusion.87
  566.3 42.6 %dispatch_tokens.1 = (bf16[8,1792,2048]{2,1,0:T(8,128)(2,1)}, f32[8,1792,128]{2,1,0:T(8,128)}) custom-call(s32[256]{0:T(256)S(1)} %reshape.493.starts, s32[256]{0:T(256)S(1)} %and_select_fusion.steps, s32[8]{0:T(128)S(1)} %add_reduce_fusion.used, s32[32,8,256]{2,1,0:T(8,128)S(1)} %get-tuple-element.558.rank_ref, f32[32,8,256]{2,1,0:T(8,128)S(1)} %bitcast.169, ...), custom_call_target="tpu_custom_call" | custom-call | flops 17179869184 | bytes 100663296 | tf_op jit(solution)/shard_map/dispatch_tokens/pallas_call | solution.py:265
  608.9 41.6 %dispatch_cotangent.1.c_ref = bf16[8,1792,2048]{2,1,0:T(8,128)(2,1)} custom-call(s32[256]{0:T(256)S(1)} %reshape.493.starts, s32[256]{0:T(256)S(1)} %and_select_fusion.steps, s32[8]{0:T(128)S(1)} %add_reduce_fusion.used, s32[32,8,256]{2,1,0:T(8,128)S(1)} %get-tuple-element.558.rank_ref, bf16[8192,2048]{1,0:T(8,128)(2,1)} %bitcast.177), custom_call_target="tpu_custom_call" | custom-call | flops 17179869184 | bytes 100663296 | tf_op jit(solution)/shard_map/dispatch_cotangent/pallas_call | solution.py:251
  650.5 137.6 %experts.1 = (bf16[8,1792,2048]{2,1,0:T(8,128)(2,1)}, bf16[8,1792,2176]{2,1,0:T(8,128)(2,1)}, f32[8,2048,256]{2,1,0:T(8,128)}, f32[8,2048,256]{2,1,0:T(8,128)}, f32[8,2048,256]{2,1,0:T(8,128)}) custom-call(s32[8]{0:T(128)} %copy-done.2, s32[1]{0:T(128)} %bitcast.33.first, ...), custom_call_target="tpu_custom_call", output_to_operand_aliasing={{0}: (2, {})} | custom-call | flops 135291469824 | bytes 234881024 | tf_op jit(solution)/shard_map/experts/pallas_call | solution.py:355
  788.1 42.7 %combine_grads.1 = bf16[8192,2176]{1,0:T(8,128)(2,1)} custom-call(s32[256]{0:T(256)S(1)} %reshape.493.starts, s32[256]{0:T(256)S(1)} %and_select_fusion.steps, s32[32,8,256]{2,1,0:T(8,128)S(1)} %get-tuple-element.558.rank_ref, bf16[8,1792,2176]{2,1,0:T(8,128)(2,1)} %get-tuple-element.290.y_ref), custom_call_target="tpu_custom_call" | custom-call | flops 18253611008 | bytes 106954752 | tf_op jit(solution)/shard_map/combine_grads/pallas_call | solution.py:438
  830.9 179.1 %scatter_grads.1 = f32[256,2176]{1,0:T(8,128)} custom-call(bf16[2,2,4,2,256,2176]{5,4,3,2,1,0:T(8,128)(2,1)} %bitcast.174), custom_call_target="tpu_custom_call" | custom-call | flops 17825792 | bytes 35651584 | tf_op jit(solution)/shard_map/scatter_grads/pallas_call | solution.py:725
  1010.0 40.8 %combine_outputs.1 = bf16[8192,2048]{1,0:T(8,128)(2,1)} custom-call(s32[256]{0:T(256)S(1)} %reshape.493.starts, s32[256]{0:T(256)S(1)} %and_select_fusion.steps, s32[32,8,256]{2,1,0:T(8,128)S(1)} %get-tuple-element.558.rank_ref, bf16[8,1792,2048]{2,1,0:T(8,128)(2,1)} %get-tuple-element.289.y_ref), custom_call_target="tpu_custom_call" | custom-call | flops 17179869184 | bytes 100663296 | tf_op jit(solution)/shard_map/combine_outputs/pallas_call | solution.py:438
  1050.8 146.4 %scatter_outputs.1 = f32[256,2048]{1,0:T(8,128)} custom-call(bf16[2,2,4,2,256,2048]{5,4,3,2,1,0:T(8,128)(2,1)} %bitcast.175), custom_call_target="tpu_custom_call" | custom-call | flops 16777216 | bytes 33554432 | tf_op jit(solution)/shard_map/scatter_outputs/pallas_call | solution.py:725
  1198.5 3.2 multiply_reduce_fusion.1
  1203.6 7.5 convolution_convert_fusion.3
  1213.4 3.8 all-to-all-start.1
  1219.9 23.5 %all-to-all-done.1 = bf16[256,8,256]{0,2,1:T(8,128)(2,1)S(1)} async-done(((bf16[256,8,256]{0,2,1:T(8,128)(2,1)}), bf16[256,8,256]{0,2,1:T(8,128)(2,1)S(1)}, u32[]{:S(2)}, u32[]{:S(2)}) %all-to-all-start.1) | async-done | bytes 1048608 | tf_op jit(solution)/shard_map/all_to_all | solution.py:1116
  1248.8 157.0 %while.31 = (s32[]{:T(128)}, f32[3072,2,128]{2,0,1:T(8,128)}, f32[3072,2,128]{0,2,1:T(8,128)}, bf16[4,512,2,128]{3,1,0,2:T(8,128)(2,1)}, s32[4]{0:T(128)S(1)}, /...) while((s32[]{:T(128)}, f32[3072,2,128]{2,0,1:T(8,128)}, ...), condition=%wide.region_21.22_spmd, body=%wide.region_19.21_spmd.sunk | while | flops 2033583104 | bytes 150008880 | solution.py:963
  1250.1 4.8 fusion.138
  1259.4 5.7 multiply_reduce_fusion.11
  1271.1 4.3 fusion.140
  1282.9 5.1 fusion.141
  1289.4 4.8 fusion.138
  1298.7 5.7 multiply_reduce_fusion.11
  1310.3 4.3 fusion.140
  1322.1 5.1 fusion.141
  1328.6 4.8 fusion.138
  1337.9 5.7 multiply_reduce_fusion.11
  1349.6 4.3 fusion.140
  1361.4 5.1 fusion.141
  1367.8 4.8 fusion.138
  1377.2 5.7 multiply_reduce_fusion.11
  1388.8 4.3 fusion.140
  1400.6 5.1 fusion.141
  1421.7 4.2 multiply_reduce_fusion.2
  1425.9 35.2 %psum.22 = f32[2,2048]{1,0:T(2,128)S(1)} all-reduce(f32[2,2048]{1,0:T(2,128)S(1)} %pad_maximum_fusion.7), channel_id=1, replica_groups=mesh['sp'=8,'fsdp'=4] {'sp'}, use_global_device_ids=true, to_apply=%region_24.25 | all-reduce | flops 4096 | bytes 32768 | tf_op jit(solution)/shard_map/psum | solution.py:1138
  1463.3 3.4 subtract_convert_fusion.1
  1468.0 10.4 convolution_convert_fusion.2
  1483.6 9.1 maximum_maximum_fusion
  1492.7 12.1 copy.179
  1504.8 46.4 %scatter_out_rows.1 = f32[64,2176]{1,0:T(8,128)} custom-call(bf16[2,2,4,2,64,2176]{5,4,3,2,1,0:T(8,128)(2,1)} %bitcast.176), custom_call_target="tpu_custom_call" | custom-call | flops 4456448 | bytes 8912896 | tf_op jit(solution)/shard_map/scatter_out_rows/pallas_call | solution.py:725
  1553.6 10.9 convolution_convert_fusion.1
  1564.5 119.9 %scatter_attn_in.1 = f32[256,2048]{1,0:T(8,128)} custom-call(bf16[1,1,4,2,256,2048]{5,4,3,2,1,0:T(8,128)(2,1)} %bitcast.181), custom_call_target="tpu_custom_call" | custom-call | flops 4194304 | bytes 8388608 | tf_op jit(solution)/shard_map/scatter_attn_in/pallas_call | solution.py:725
  1686.8 64.1 %psum.23 = f32[4,2048]{1,0:T(4,128)S(1)} all-reduce(f32[4,2048]{1,0:T(4,128)S(1)} %pad_maximum_fusion.5), channel_id=1, replica_groups=mesh['sp'=8,'fsdp'=4] {'sp','fsdp'}, use_global_device_ids=true, to_apply=%region_30.31 | all-reduce | flops 8192 | bytes 65536 | tf_op jit(solution)/shard_map/psum | solution.py:1172
  1751.6 4.3 fusion.51
  1757.6 4.1 slice_convert_fusion
  1761.7 10.3 all-gather.17.cloned.1.call-done
  1772.0 4.4 convert_bitcast_fusion
  1776.4 2.6 copy.212
  1779.1 2.6 copy.213
  1781.7 2.6 copy.214
  (453 shorter events, 175.2 us)
Async XLA Ops:
  7.2 228.3 %all-gather.9.cloned.1.call-start = ((), (), s32[]{:S(2)}) async-start(), calls=%async_computation.3 | async-start | bytes 3932160 | tf_op jit(solution)/shard_map/all_gather | solution.py:1046
  10.8 7.8 copy-start.9
  10.9 360.7 %all-gather.11.cloned.1.call-start = ((), (), s32[]{:S(2)}) async-start(), calls=%async_computation.4 | async-start | bytes 10485760 | tf_op jit(solution)/shard_map/all_gather | solution.py:1047
  11.6 597.3 %all-gather.15.cloned.1.call-start = ((), (), s32[]{:S(2)}) async-start(), calls=%async_computation.7 | async-start | bytes 34603008 | tf_op jit(solution)/shard_map/all_gather | solution.py:1049
  19.5 139.4 %copy-start.62 = (f32[256]{0:T(256)}, f32[256]{0:T(256)S(1)}, u32[]{:S(2)}) copy-start(f32[256]{0:T(256)S(1)} %fusion.77) | copy-start | bytes 3076
  19.5 139.4 %copy-start.55 = (f32[1,2048]{1,0:T(1,128)}, f32[1,2048]{1,0:T(1,128)S(1)}, u32[]{:S(2)}) copy-start(f32[1,2048]{1,0:T(1,128)S(1)} %get-tuple-element.567) | copy-start | bytes 24580
  19.5 358.3 %copy-start.57 = (f32[1,2048]{1,0:T(1,128)}, f32[1,2048]{1,0:T(1,128)S(1)}, u32[]{:S(2)}) copy-start(f32[1,2048]{1,0:T(1,128)S(1)} %get-tuple-element.566) | copy-start | bytes 24580
  20.8 138.1 %copy-start.87 = (s32[1,4]{1,0:T(1,128)S(1)}, s32[1,4]{1,0:T(1,128)}, u32[]{:S(2)}) copy-start(s32[1,4]{1,0:T(1,128)} %param.21) | copy-start | bytes 52
  20.8 138.5 %copy-start.77 = (s32[1,256,8]{1,2,0:T(8,128)S(1)}, s32[1,256,8]{1,2,0:T(8,128)}, u32[]{:S(2)}) copy-start(s32[1,256,8]{1,2,0:T(8,128)} %param.22) | copy-start | bytes 24580
  159.3 124.0 %copy-start.64 = (f32[1,256]{1,0:T(1,128)}, f32[1,256]{1,0:T(1,128)S(1)}, u32[]{:S(2)}) copy-start(f32[1,256]{1,0:T(1,128)S(1)} %get-tuple-element.570) | copy-start | bytes 3076
  159.3 124.0 %copy-start.66 = (f32[1,256]{1,0:T(1,128)}, f32[1,256]{1,0:T(1,128)S(1)}, u32[]{:S(2)}) copy-start(f32[1,256]{1,0:T(1,128)S(1)} %get-tuple-element.571) | copy-start | bytes 3076
  283.3 4.7 copy-start.49
  283.3 4.7 copy-start.51
  347.5 6.5 copy-start.59
  347.5 21.5 %all-to-all-start = ((bf16[8,256,256]{2,1,0:T(8,128)(2,1)}), bf16[8,256,256]{2,1,0:T(8,128)(2,1)S(1)}, u32[]{:S(2)}, u32[]{:S(2)}) async-start(bf16[8,256,256]{2,1,0:T(8,128)(2,1)} %all_to_all.26), calls=%async_computation | async-start | bytes 2097152 | tf_op jit(solution)/shard_map/all_to_all | solution.py:1070
  360.2 189.4 %copy-start.35 = (bf16[2048,64]{0,1:T(8,128)(2,1)}, bf16[2048,64]{0,1:T(8,128)(2,1)S(1)}, u32[]{:S(2)}) copy-start(bf16[2048,64]{0,1:T(8,128)(2,1)S(1)} %all_gather.31) | copy-start | bytes 786436
  360.4 248.5 %copy-start.2 = (s32[8]{0:T(128)}, s32[8]{0:T(128)S(1)}, u32[]{:S(2)}) copy-start(s32[8]{0:T(128)S(1)} %add_reduce_fusion.used) | copy-start | bytes 100
  371.5 6.2 copy-start.20
  377.8 170.5 %copy-start.75 = (f32[256]{0:T(256)}, f32[256]{0:T(256)S(1)}, u32[]{:S(2)}) copy-start(f32[256]{0:T(256)S(1)} %get-tuple-element.574) | copy-start | bytes 3076
  377.8 170.5 %copy-start.71 = (f32[256]{0:T(256)}, f32[256]{0:T(256)S(1)}, u32[]{:S(2)}) copy-start(f32[256]{0:T(256)S(1)} %fusion.78) | copy-start | bytes 3076
  380.3 168.0 %copy-start.24 = (bf16[256,2048]{1,0:T(8,128)(2,1)S(1)}, bf16[256,2048]{1,0:T(8,128)(2,1)}, u32[]{:S(2)}) copy-start(bf16[256,2048]{1,0:T(8,128)(2,1)} %multiply_convert_fusion.1.in_ref) | copy-start | bytes 3145732
  548.8 17.1 copy-start.68
  548.9 17.0 copy-start.37
  1050.8 146.5 %copy-start.38 = (f32[256,64]{1,0:T(8,128)S(1)}, f32[256,64]{1,0:T(8,128)}, u32[]{:S(2)}) copy-start(f32[256,64]{1,0:T(8,128)} %copy-done.37) | copy-start | bytes 196612
  1050.8 146.5 %copy-start.69 = (f32[256]{0:T(256)S(1)}, f32[256]{0:T(256)}, u32[]{:S(2)}) copy-start(f32[256]{0:T(256)} %copy-done.68) | copy-start | bytes 3076
  1050.8 146.5 %copy-start.79 = (f32[256]{0:T(256)S(1)}, f32[256]{0:T(256)}, u32[]{:S(2)}) copy-start(f32[256]{0:T(256)} %fusion.72) | copy-start | bytes 3076
  1050.8 147.6 %copy-start.15 = (f32[256,2048]{1,0:T(8,128)S(1)}, f32[256,2048]{1,0:T(8,128)}, u32[]{:S(2)}) copy-start(f32[256,2048]{1,0:T(8,128)} %copy-done.14) | copy-start | bytes 6291460
  1050.8 147.6 %copy-start.36 = (bf16[2048,64]{0,1:T(8,128)(2,1)S(1)}, bf16[2048,64]{0,1:T(8,128)(2,1)}, u32[]{:S(2)}) copy-start(bf16[2048,64]{0,1:T(8,128)(2,1)} %copy-done.35) | copy-start | bytes 786436
  1050.8 147.6 %copy-start.58 = (f32[1,2048]{1,0:T(1,128)S(1)}, f32[1,2048]{1,0:T(1,128)}, u32[]{:S(2)}) copy-start(f32[1,2048]{1,0:T(1,128)} %copy-done.57) | copy-start | bytes 24580
  1050.8 147.6 %copy-start.72 = (f32[256]{0:T(256)S(1)}, f32[256]{0:T(256)}, u32[]{:S(2)}) copy-start(f32[256]{0:T(256)} %copy-done.71) | copy-start | bytes 3076
  1050.8 150.9 %copy-start.29 = (bf16[1,256,2048]{2,1,0:T(8,128)(2,1)S(1)}, bf16[1,256,2048]{2,1,0:T(8,128)(2,1)}, u32[]{:S(2)}) copy-start(bf16[1,256,2048]{2,1,0:T(8,128)(2,1)} %param.35) | copy-start | bytes 3145732
  1203.6 7.5 copy-start.12
  1211.0 6.2 copy-start.18
  1213.4 5.3 copy-start.50
  1213.4 5.9 copy-start.52
  1213.4 29.9 %all-to-all-start.1 = ((bf16[256,8,256]{0,2,1:T(8,128)(2,1)}), bf16[256,8,256]{0,2,1:T(8,128)(2,1)S(1)}, u32[]{:S(2)}, u32[]{:S(2)}) async-start(bf16[256,8,256]{0,2,1:T(8,128)(2,1)} %bitcast.195), calls=%async_computation.1 | async-start | bytes 2097152 | tf_op jit(solution)/shard_map/all_to_all | solution.py:1116
  1217.2 335.9 %reduce-scatter.2.cloned.1.call-start = ((), (), s32[]{:S(2)}) async-start(), calls=%async_computation.5 | async-start | bytes 3932160 | tf_op jit(solution)/shard_map/reduce_scatter | solution.py:1156
  1248.8 6.1 copy-start.22
  1259.4 5.7 slice-start
  1259.4 5.7 slice-start.1
  1282.9 5.1 copy-start.23
  1288.0 6.1 copy-start.22
  1298.7 5.7 slice-start
  1298.7 5.7 slice-start.1
  1322.1 5.1 copy-start.23
  1327.3 6.1 copy-start.22
  1337.9 5.7 slice-start
  1337.9 5.7 slice-start.1
  1361.4 5.1 copy-start.23
  1366.5 6.1 copy-start.22
  1377.2 5.7 slice-start
  1377.2 5.7 slice-start.1
  1400.6 5.1 copy-start.23
  1425.9 37.1 %copy-start.60 = (f32[2048]{0:T(1024)S(1)}, f32[2048]{0:T(1024)}, u32[]{:S(2)}) copy-start(f32[2048]{0:T(1024)} %multiply_multiply_fusion.2) | copy-start | bytes 24580
  1425.9 37.1 %copy-start.61 = (f32[2048]{0:T(1024)S(1)}, f32[2048]{0:T(1024)}, u32[]{:S(2)}) copy-start(f32[2048]{0:T(1024)} %multiply_multiply_fusion.3) | copy-start | bytes 24580
  1478.5 277.4 %all-gather.13.cloned.1.call-start = ((), (), s32[]{:S(2)}) async-start(), calls=%async_computation.6 | async-start | bytes 2506752 | tf_op jit(solution)/shard_map/all_gather | solution.py:1160
  1504.8 48.8 %copy-start.41 = (bf16[2048,256]{0,1:T(8,128)(2,1)S(1)}, bf16[2048,256]{0,1:T(8,128)(2,1)}, u32[]{:S(2)}) copy-start(bf16[2048,256]{0,1:T(8,128)(2,1)} %copy-done.40) | copy-start | bytes 3145732
  1504.8 48.8 %copy-start.43 = (bf16[2048,256]{0,1:T(8,128)(2,1)S(1)}, bf16[2048,256]{0,1:T(8,128)(2,1)}, u32[]{:S(2)}) copy-start(bf16[2048,256]{0,1:T(8,128)(2,1)} %copy-done.42) | copy-start | bytes 3145732
  1504.8 48.8 %copy-start.46 = (bf16[2048,2,128]{0,2,1:T(8,128)(2,1)S(1)}, bf16[2048,2,128]{0,2,1:T(8,128)(2,1)}, u32[]{:S(2)}) copy-start(bf16[2048,2,128]{0,2,1:T(8,128)(2,1)} %copy-done.45) | copy-start | bytes 3145732
  1553.0 219.0 %all-gather.17.cloned.1.call-start = ((), (), s32[]{:S(2)}) async-start(), calls=%async_computation.8 | async-start | bytes 7077888 | tf_op jit(solution)/shard_map/all_gather | solution.py:1159
  1564.5 120.0 %copy-start.10 = (bf16[1,256,2048]{2,1,0:T(8,128)(2,1)S(1)}, bf16[1,256,2048]{2,1,0:T(8,128)(2,1)}, u32[]{:S(2)}) copy-start(bf16[1,256,2048]{2,1,0:T(8,128)(2,1)} %param.20) | copy-start | bytes 3145732
  1564.5 120.0 %copy-start.56 = (f32[1,2048]{1,0:T(1,128)S(1)}, f32[1,2048]{1,0:T(1,128)}, u32[]{:S(2)}) copy-start(f32[1,2048]{1,0:T(1,128)} %copy-done.55) | copy-start | bytes 24580
  1564.5 120.0 %copy-start.63 = (f32[256]{0:T(256)S(1)}, f32[256]{0:T(256)}, u32[]{:S(2)}) copy-start(f32[256]{0:T(256)} %copy-done.62) | copy-start | bytes 3076
  1684.4 67.2 %copy-start.74 = (f32[256]{0:T(256)S(1)}, f32[256]{0:T(256)}, u32[]{:S(2)}) copy-start(f32[256]{0:T(256)} %copy-done.73) | copy-start | bytes 3076
  (58 other events, 137.3 us)
Sparse Core Ops, SparseCore 0:
  11.0 31.2 all-gather.8
  43.8 58.2 all-gather.10
  105.1 201.2 all-gather.14
  1478.6 37.4 reduce-scatter.1
  1553.1 90.0 all-gather.12
  1645.6 126.4 all-gather.16

commit v3 on v2

--- a/solution.py
+++ b/solution.py
@@ -36,38 +36,6 @@
     return (jnp.cos(phase_all)[:, None, :], jnp.sin(phase_all)[:, None, :])
 
 
-def segment_ids(lengths_row, seq_rows):
-    doc_ends = jnp.cumsum(lengths_row)
-    positions = jnp.arange(seq_rows, dtype=jnp.int32)
-    return jnp.sum((positions[:, None] >= doc_ends[None, :]).astype(jnp.int32), axis=1)
-
-
-def window_geometry(seq_rows):
-    block_rows = min(512, seq_rows)
-    key_blocks = 1 + (WINDOW - 1 + block_rows - 1) // block_rows
-    return (
-        block_rows,
-        seq_rows // block_rows,
-        key_blocks * block_rows,
-        (key_blocks - 1) * block_rows,
-    )
-
-
-def window_allowed(segments, seg_padded, first_row, block_rows, key_rows, pad_rows):
-    query_pos = first_row + jnp.arange(block_rows, dtype=jnp.int32)
-    key_pos = first_row - pad_rows + jnp.arange(key_rows, dtype=jnp.int32)
-    query_seg = lax.dynamic_slice_in_dim(segments, first_row, block_rows)
-    key_seg = lax.dynamic_slice_in_dim(seg_padded, first_row, key_rows)
-    distance = query_pos[:, None] - key_pos[None, :]
-    return (query_seg[:, None] == key_seg[None, :]) & (distance >= 0) & (distance < WINDOW)
-
-
-def pad_front(values, pad_rows, filler):
-    return jnp.concatenate(
-        [jnp.full((pad_rows,) + values.shape[1:], filler, values.dtype), values], axis=0
-    )
-
-
 BLOCK = 256
 SLOTS = 64
 STEP = 16
@@ -83,7 +51,11 @@
 
 def route_plan(own_ids, sp_count, fs_count):
     local_experts = EXPERTS // sp_count
-    ids = lax.all_gather(own_ids, ("fsdp", "sp"), axis=0, tiled=True)
+    per_device = own_ids.size
+    packed = jnp.zeros((32, 128), jnp.bfloat16)
+    packed = packed.at[: per_device // 128].set(own_ids.astype(jnp.bfloat16).reshape(-1, 128))
+    packed = gather_over_all(packed, sp_count, fs_count, 10, "gather_ids")
+    ids = packed.reshape(-1, 32 * 128)[:, :per_device].reshape(-1, TOPK).astype(jnp.int32)
     tokens = ids.shape[0]
     blocks = tokens // BLOCK
     capacity = 5 * tokens * TOPK // (4 * EXPERTS)
@@ -882,93 +854,180 @@
     return out.reshape(total, width)
 
 
-def attend(query_heads, key_heads, value_heads, lengths):
-    seq_rows, head_local, _ = query_heads.shape
-    block_rows, block_count, key_rows, pad_rows = window_geometry(seq_rows)
-    segments = segment_ids(lengths, seq_rows)
-    seg_padded = pad_front(segments, pad_rows, -1)
-    key_padded = pad_front(key_heads, pad_rows, 0.0)
-    value_padded = pad_front(value_heads, pad_rows, 0.0)
-    score_scale = HEAD_DIM ** (-0.5)
-    block_numbers = jnp.arange(block_count, dtype=jnp.int32)
-
-    def block_scores(first_row):
-        query_block = lax.dynamic_slice_in_dim(query_heads, first_row, block_rows)
-        key_block = lax.dynamic_slice_in_dim(key_padded, first_row, key_rows)
-        scores = (
-            jnp.einsum("qhd,khd->hqk", query_block, key_block, preferred_element_type=jnp.float32)
-            * score_scale
+def small_sum_kernel(counts, part_ref, out_ref, first, second, s0, r0, s1, r1):
+    sp_count, fs_count = counts
+    at = {"sp": lax.axis_index("sp"), "fsdp": lax.axis_index("fsdp")}
+
+    def peer(dim, ahead, size):
+        return {dim: (at[dim] + ahead) % size}
+
+    barrier = pltpu.get_barrier_semaphore()
+    for dim, size in (("sp", sp_count), ("fsdp", fs_count)):
+        for ahead in range(1, size):
+            pl.semaphore_signal(
+                barrier, inc=1, device_id=peer(dim, ahead, size), device_id_type=MESH
+            )
+    pl.semaphore_wait(barrier, sp_count + fs_count - 2)
+
+    def exchange(src, held, send, recv, dim, size):
+        copies = [
+            pltpu.make_async_remote_copy(
+                src_ref=src, dst_ref=held.at[size - ahead - 1],
+                send_sem=send.at[ahead - 1], recv_sem=recv.at[size - ahead - 1],
+                device_id=peer(dim, ahead, size), device_id_type=MESH,
+            )
+            for ahead in range(1, size)
+        ]
+        for copy in copies:
+            copy.start()
+        total = src[...]
+        for ahead, copy in enumerate(copies, 1):
+            pltpu.make_async_remote_copy(
+                src_ref=src, dst_ref=held.at[ahead - 1],
+                send_sem=send.at[size - ahead - 1], recv_sem=recv.at[ahead - 1],
+                device_id=peer(dim, size - ahead, size), device_id_type=MESH,
+            ).wait_recv()
+            total = total + held[ahead - 1]
+        for copy in copies:
+            copy.wait_send()
+        return total
+
+    total = exchange(part_ref, first, s0, r0, "sp", sp_count)
+    out_ref[...] = total
+    if fs_count > 1:
+        total = exchange(out_ref, second, s1, r1, "fsdp", fs_count)
+        out_ref[...] = total
+
+
+def small_sum(part, sp_count, fs_count, ident, name):
+    sems = [pltpu.SemaphoreType.DMA((max(n - 1, 1),)) for n in (sp_count, sp_count, fs_count, fs_count)]
+    return pl.pallas_call(
+        functools.partial(small_sum_kernel, (sp_count, fs_count)),
+        in_specs=[pl.BlockSpec(memory_space=pltpu.VMEM)],
+        out_specs=pl.BlockSpec(memory_space=pltpu.VMEM),
+        out_shape=jax.ShapeDtypeStruct(part.shape, jnp.float32),
+        scratch_shapes=[
+            pltpu.VMEM((max(sp_count - 1, 1),) + part.shape, jnp.float32),
+            pltpu.VMEM((max(fs_count - 1, 1),) + part.shape, jnp.float32),
+        ]
+        + sems,
+        compiler_params=pltpu.CompilerParams(collective_id=ident, has_side_effects=True),
+        name=name,
+    )(part)
+
+
+ROWS = 256
+
+
+def window_scores(ends, count, q, k, first, top):
+    scores = contract(q, k, 1, 1) * HEAD_DIM ** (-0.5)
+    place = top + lax.broadcasted_iota(jnp.int32, (ROWS, 1), 0)
+    oldest = jnp.maximum(place - (WINDOW - 1), 0)
+    for n in range(count):
+        oldest = jnp.maximum(oldest, jnp.where(place >= ends[n], ends[n], 0))
+    other = first + lax.broadcasted_iota(jnp.int32, scores.shape, 1)
+    return jnp.where((other >= oldest) & (other <= place), scores, masked_score)
+
+
+def window_first(i, reach, total):
+    return pl.multiple_of(jnp.clip(i * ROWS + ROWS - reach, 0, total - reach), ROWS)
+
+
+def softmax_rows(scores):
+    weights = jnp.exp(scores - jnp.max(scores, axis=-1, keepdims=True))
+    return weights / jnp.sum(weights, axis=-1, keepdims=True)
+
+
+def attend_kernel(count, reach, ends, q_ref, k_ref, v_ref, o_ref):
+    i = pl.program_id(1)
+    first = window_first(i, reach, k_ref.shape[0])
+    keys = pl.ds(first, reach)
+    scores = window_scores(ends, count, q_ref[...], k_ref[keys, :], first, i * ROWS)
+    probs = softmax_rows(scores).astype(jnp.bfloat16)
+    o_ref[...] = jnp.dot(probs, v_ref[keys, :], preferred_element_type=jnp.float32).astype(
+        jnp.bfloat16
+    )
+
+
+def attend_back_kernel(
+    count, reach, ends, q_ref, k_ref, v_ref, g_ref, dq_ref, dk_ref, dv_ref, dk_acc, dv_acc
+):
+    i = pl.program_id(1)
+    first = window_first(i, reach, k_ref.shape[0])
+    keys = pl.ds(first, reach)
+    scale = HEAD_DIM ** (-0.5)
+
+    @pl.when(i == 0)
+    def _():
+        dk_acc[...] = jnp.zeros_like(dk_acc)
+        dv_acc[...] = jnp.zeros_like(dv_acc)
+
+    q = q_ref[...]
+    k = k_ref[keys, :]
+    grad = g_ref[...]
+    probs = softmax_rows(window_scores(ends, count, q, k, first, i * ROWS))
+    prob_grad = contract(grad, v_ref[keys, :], 1, 1)
+    delta = jnp.sum(probs * prob_grad, axis=-1, keepdims=True)
+    score_grad = (probs * (prob_grad - delta)).astype(jnp.bfloat16)
+    dq_ref[...] = (
+        jnp.dot(score_grad, k, preferred_element_type=jnp.float32) * scale
+    ).astype(jnp.bfloat16)
+    dk_acc[keys, :] += contract(score_grad, q, 0, 0) * scale
+    dv_acc[keys, :] += contract(probs.astype(jnp.bfloat16), grad, 0, 0)
+
+    @pl.when(i == pl.num_programs(1) - 1)
+    def _():
+        dk_ref[...] = dk_acc[...].astype(jnp.bfloat16)
+        dv_ref[...] = dv_acc[...].astype(jnp.bfloat16)
+
+
+def attend(query, key, value, lengths):
+    seq_rows, span = query.shape
+    heads = span // HEAD_DIM
+    reach = min(WINDOW + ROWS, seq_rows)
+    count = lengths.shape[0]
+    ends = jnp.cumsum(lengths)
+    tile = pl.BlockSpec((ROWS, HEAD_DIM), lambda h, i, ends: (i, h))
+    whole = pl.BlockSpec((seq_rows, HEAD_DIM), lambda h, i, ends: (0, h))
+    shape = jax.ShapeDtypeStruct((seq_rows, span), jnp.bfloat16)
+    pairs = seq_rows * heads * reach
+
+    def call(kernel, ins, outs, scratch, name):
+        return pl.pallas_call(
+            kernel,
+            grid_spec=pltpu.PrefetchScalarGridSpec(
+                num_scalar_prefetch=1,
+                grid=(heads, seq_rows // ROWS),
+                in_specs=ins,
+                out_specs=outs,
+                scratch_shapes=scratch,
+            ),
+            out_shape=[shape] * len(outs),
+            compiler_params=pltpu.CompilerParams(
+                dimension_semantics=("arbitrary", "arbitrary"), vmem_limit_bytes=48 * 2**20
+            ),
+            cost_estimate=pl.CostEstimate(
+                flops=4 * len(outs) * pairs * HEAD_DIM,
+                bytes_accessed=8 * seq_rows * span,
+                transcendentals=pairs,
+            ),
+            name=name,
         )
-        allowed = window_allowed(segments, seg_padded, first_row, block_rows, key_rows, pad_rows)
-        return (jnp.where(allowed[None], scores, masked_score), query_block, key_block)
-
-    def forward_block(carry_in, block_index):
-        first_row = block_index * block_rows
-        scores, query_block, key_block = block_scores(first_row)
-        value_block = lax.dynamic_slice_in_dim(value_padded, first_row, key_rows)
-        row_max = jnp.max(scores, axis=-1, keepdims=True)
-        weights = jnp.exp(scores - row_max)
-        row_total = jnp.sum(weights, axis=-1, keepdims=True)
-        probs = (weights / row_total).astype(jnp.bfloat16)
-        attended = jnp.einsum(
-            "hqk,khd->qhd", probs, value_block, preferred_element_type=jnp.float32
-        )
-        return (carry_in, (attended.astype(jnp.bfloat16), (row_max + jnp.log(row_total))[..., 0]))
-
-    _, (attended_blocks, lse_blocks) = lax.scan(forward_block, 0, block_numbers)
-    attended_heads = attended_blocks.reshape(seq_rows, head_local, HEAD_DIM)
-
-    def back(attended_grad_heads):
-        def backward_block(carry_in, block_index):
-            key_total, value_total = carry_in
-            first_row = block_index * block_rows
-            scores, query_block, key_block = block_scores(first_row)
-            value_block = lax.dynamic_slice_in_dim(value_padded, first_row, key_rows)
-            grad_block = lax.dynamic_slice_in_dim(attended_grad_heads, first_row, block_rows)
-            probs = jnp.exp(scores - lse_blocks[block_index][..., None])
-            prob_grad = jnp.einsum(
-                "qhd,khd->hqk", grad_block, value_block, preferred_element_type=jnp.float32
-            )
-            row_delta = jnp.sum(probs * prob_grad, axis=-1, keepdims=True)
-            score_grad = (probs * (prob_grad - row_delta)).astype(jnp.bfloat16)
-            query_part = (
-                jnp.einsum("hqk,khd->qhd", score_grad, key_block, preferred_element_type=jnp.float32)
-                * score_scale
-            )
-            key_part = (
-                jnp.einsum("hqk,qhd->khd", score_grad, query_block, preferred_element_type=jnp.float32)
-                * score_scale
-            )
-            value_part = jnp.einsum(
-                "hqk,qhd->khd",
-                probs.astype(jnp.bfloat16),
-                grad_block,
-                preferred_element_type=jnp.float32,
-            )
-            key_total = lax.dynamic_update_slice_in_dim(
-                key_total,
-                lax.dynamic_slice_in_dim(key_total, first_row, key_rows) + key_part,
-                first_row,
-                0,
-            )
-            value_total = lax.dynamic_update_slice_in_dim(
-                value_total,
-                lax.dynamic_slice_in_dim(value_total, first_row, key_rows) + value_part,
-                first_row,
-                0,
-            )
-            return ((key_total, value_total), query_part.astype(jnp.bfloat16))
-
-        zero_keys = jnp.zeros((pad_rows + seq_rows, head_local, HEAD_DIM), jnp.float32)
-        (key_total, value_total), query_blocks = lax.scan(
-            backward_block, (zero_keys, zero_keys), block_numbers
-        )
-        query_grad_heads = query_blocks.reshape(seq_rows, head_local, HEAD_DIM)
-        key_grad_heads = key_total[pad_rows:].astype(jnp.bfloat16)
-        value_grad_heads = value_total[pad_rows:].astype(jnp.bfloat16)
-        return query_grad_heads, key_grad_heads, value_grad_heads
-
-    return attended_heads, back
+
+    attended = call(
+        functools.partial(attend_kernel, count, reach), [tile, whole, whole], [tile], [], "attend"
+    )(ends, query, key, value)[0]
+
+    def back(grad):
+        return call(
+            functools.partial(attend_back_kernel, count, reach),
+            [tile, whole, whole, tile],
+            [tile, whole, whole],
+            [pltpu.VMEM((seq_rows, HEAD_DIM), jnp.float32)] * 2,
+            "attend_back",
+        )(ends, query, key, value, grad)
+
+    return attended, back
 
 
 def scatter_over_all(partial, rows, sp_count, fs_count, ident, name):
@@ -999,6 +1058,11 @@
     n_hi, n_lo, _, _ = mesh_counts(sp_count, 1)
     parts = 4 if own.shape[0] % 64 == 0 else 2
     return gather_rows(own, (n_hi, n_lo, 1, 1), False, parts, ident, name)
+
+
+def sum_over_sp(rows, sp_count, ident, name):
+    part = jnp.stack(rows)
+    return small_sum(part.reshape(-1, 128), sp_count, 1, ident, name).reshape(part.shape)
 
 
 def local(
@@ -1054,21 +1118,21 @@
     attn_in = gather_over_sp(attn_normed.astype(jnp.bfloat16), sp_count, 1, "gather_attn_in")
     qkv_raw = jnp.dot(attn_in, qkv_mat, preferred_element_type=jnp.float32)
     raw = (qkv_raw[:, :span], qkv_raw[:, span : 2 * span])
-    value_heads = qkv_raw[:, 2 * span :].astype(jnp.bfloat16).reshape(
-        seq_rows, head_local, HEAD_DIM
-    )
-    squares = lax.psum(jnp.stack([jnp.sum(r * r, axis=-1) for r in raw]), "sp")
+    value_heads = qkv_raw[:, 2 * span :].astype(jnp.bfloat16)
+    squares = sum_over_sp([jnp.sum(r * r, axis=-1) for r in raw], sp_count, 7, "sum_squares")
     scales = lax.rsqrt(squares / width + eps)[:, :, None]
     cosine, sine = rope_tables(jnp.arange(seq_rows, dtype=jnp.int32), HEAD_DIM)
 
     def turned(normed):
-        return rotate_pairs(normed.reshape(seq_rows, head_local, HEAD_DIM), cosine, sine)
+        return rotate_pairs(
+            normed.reshape(seq_rows, head_local, HEAD_DIM), cosine, sine
+        ).reshape(seq_rows, span)
 
     query_heads = turned(raw[0] * scales[0] * gain_query).astype(jnp.bfloat16)
     key_heads = turned(raw[1] * scales[1] * gain_key).astype(jnp.bfloat16)
     attended_heads, attend_back = attend(query_heads, key_heads, value_heads, doc_lengths[0])
     attended_tok = lax.all_to_all(
-        attended_heads.reshape(seq_rows, span), "sp", split_axis=0, concat_axis=1, tiled=True
+        attended_heads, "sp", split_axis=0, concat_axis=1, tiled=True
     )
     after_attn = hidden_in + jnp.dot(attended_tok, out_mat, preferred_element_type=jnp.float32)
     ffn_normed, ffn_pull = jax.vjp(rms_scale, after_attn, gain_ffn)
@@ -1115,7 +1179,7 @@
     )
     attended_grad_heads = lax.all_to_all(
         attended_grad, "sp", split_axis=1, concat_axis=0, tiled=True
-    ).reshape(seq_rows, head_local, HEAD_DIM)
+    )
     out_term = jnp.dot(attended_tok.T, attn_out_grad, preferred_element_type=jnp.float32)
     row_terms = jnp.concatenate(
         [
@@ -1131,12 +1195,13 @@
     query_grad_heads, key_grad_heads, value_low = attend_back(attended_grad_heads)
 
     def unturned(grad):
-        return rotate_pairs(grad.astype(jnp.float32), cosine, -sine).reshape(seq_rows, span)
+        shaped = grad.astype(jnp.float32).reshape(seq_rows, head_local, HEAD_DIM)
+        return rotate_pairs(shaped, cosine, -sine).reshape(seq_rows, span)
 
     normed_grads = (unturned(query_grad_heads), unturned(key_grad_heads))
     scaled_grads = (normed_grads[0] * gain_query, normed_grads[1] * gain_key)
-    products = lax.psum(
-        jnp.stack([jnp.sum(g * r, axis=-1) for g, r in zip(scaled_grads, raw)]), "sp"
+    products = sum_over_sp(
+        [jnp.sum(g * r, axis=-1) for g, r in zip(scaled_grads, raw)], sp_count, 8, "sum_products"
     )[:, :, None]
     gain_terms = [
         jnp.sum(g * r * s, axis=0) for g, r, s in zip(normed_grads, raw, scales)
@@ -1145,7 +1210,7 @@
         (g * s - r * (s * s * s) * (p / width)).astype(jnp.bfloat16)
         for g, r, s, p in zip(scaled_grads, raw, scales, products)
     ]
-    qkv_low = jnp.concatenate(raw_grads + [value_low.reshape(seq_rows, span)], axis=1)
+    qkv_low = jnp.concatenate(raw_grads + [value_low], axis=1)
     attn_partial = lax.dot_general(
         qkv_low, qkv_mat, (((1,), (1,)), ((), ())), preferred_element_type=jnp.float32
     ).astype(jnp.bfloat16)
@@ -1169,9 +1234,10 @@
         lax.dynamic_update_slice_in_dim(jnp.zeros((width,), jnp.float32), g, my_sp * span, 0)
         for g in gain_terms
     ]
-    gain_sums = lax.psum(
-        jnp.stack([attn_gain_term, placed[0], placed[1], ffn_gain_term]), ("sp", "fsdp")
-    )
+    gain_sums = small_sum(
+        jnp.stack([attn_gain_term, placed[0], placed[1], ffn_gain_term]).reshape(-1, 128),
+        sp_count, fs_count, 9, "sum_gains",
+    ).reshape(4, width)
     gain_sums = lax.dynamic_slice_in_dim(
         gain_sums, my_fs * (width // fs_count), width // fs_count, axis=1
     )

time: 1800 us -> 1610 us (0.89)
  blocking collectives: 217 us -> 12 us
  Pallas kernels: 1100 us -> 1230 us
  matrix products: 179 us -> 70.2 us
  waiting for transfers between devices: 44.5 us -> 107 us
  local copies, waits for them, and re-layouts: 118 us -> 60 us
    psum x3 -> x0, blocking collectives: 134 us -> none  [the longest x1 64.1 us: local(): lax.psum(jnp.stack([attn_gain_term, placed[0], placed[1], ffn_gain_term])...]
    dot_general x28 -> x0, matrix products: 109 us -> none  [the longest x8 33.9 us: block_scores(): jnp.einsum('qhd,khd->hqk', query_block, key_block, preferred_element_type...]
    pallas_call x0 -> x5, Pallas kernels: none -> 104 us  [the longest x3 56 us: small_sum(): pl.pallas_call(functools.partial(small_sum_kernel, (sp_count, fs_count)),...]
    all_gather x1 -> x0, blocking collectives: 70.6 us -> none  [route_plan(): ids = lax.all_gather(own_ids, ('fsdp', 'sp'), axis=0, tiled=True)]
    all_to_all x1, waiting for transfers between devices: 8.68 us -> 43.5 us  [local(): lax.all_to_all(attended_heads, 'sp', split_axis=0, concat_axis=1, tiled=T...]
    all_gather x1, waiting for transfers between devices: 10.3 us -> 35.7 us  [local(): qkv_every = lax.all_gather(qkv_sums, 'sp', axis=0)]
    pallas_call x2 -> x3, Pallas kernels: 306 us -> 330 us  [gather_rows(): pl.pallas_call(functools.partial(gather_kernel, counts, parts, fsdp_too),...]
    pallas_call x4, Pallas kernels: 492 us -> 470 us  [scatter_sum(): pl.pallas_call(functools.partial(scatter_kernel, counts, parts, fsdp_too)...]
  transfers between devices with their start and end apart: 8 -> 8, of which waited for: 3 -> 3; matrix products, arithmetic and copies ran while one was open for 9% -> 9% of each run, Pallas kernels for 29% -> 38%
where the time goes in v3:
time: 1610 us; the launch traced here: 1590 us
  Pallas kernels  1230 us (76%)
  waiting for transfers between devices  107 us (7%)
  other arithmetic  85.3 us (5%)
  matrix products  70.2 us (4%)
  local copies, waits for them, and re-layouts  60 us (4%)
    pallas_call x4, Pallas kernels, scatter_sum(): pl.pallas_call(functools.partial(scatter_kernel, counts, parts, fsdp_too)...  470 us
    pallas_call x3, Pallas kernels, gather_rows(): pl.pallas_call(functools.partial(gather_kernel, counts, parts, fsdp_too),...  330 us
    pallas_call x1, Pallas kernels, run_experts(): pl.pallas_call(expert_kernel, grid_spec=pltpu.PrefetchScalarGridSpec(num_...  154 us
    pallas_call x2, Pallas kernels, combine_rows(): pl.pallas_call(combine_kernel, grid_spec=pltpu.PrefetchScalarGridSpec(num...  84.9 us
    pallas_call x3, Pallas kernels, small_sum(): pl.pallas_call(functools.partial(small_sum_kernel, (sp_count, fs_count)),...  56 us
    pallas_call x1, Pallas kernels, dispatch_rows(): pl.pallas_call(dispatch_kernel, grid_spec=pltpu.PrefetchScalarGridSpec(nu...  43.9 us
    all_to_all x1, waiting for transfers between devices, local(): lax.all_to_all(attended_heads, 'sp', split_axis=0, concat_axis=1, tiled=T...  43.5 us
    pallas_call x1, Pallas kernels, dispatch_rows(): pl.pallas_call(plain, grid_spec=pltpu.PrefetchScalarGridSpec(num_scalar_p...  43 us
  transfers between devices with their start and end apart: 8, of which 3 were waited for; matrix products, arithmetic and copies ran while one was open for 9% of the time, Pallas kernels for 38%

profile of v3, /device:TPU:0, one launch (start us, length us, event | category | flops | bytes accessed | tf_op | source)
XLA Modules:
  0.0 1590.2 jit_solution(10084950395015873350)
XLA Ops:
  7.2 1.5 copy-done
  12.5 6.2 all_gather.24
  19.5 1.3 fusion.2.in_ref
  20.8 138.1 %gather_attn_in.1 = bf16[1,1,4,2,256,2048]{5,4,3,2,1,0:T(8,128)(2,1)} custom-call(bf16[256,2048]{1,0:T(8,128)(2,1)} %fusion.2.in_ref), custom_call_target="tpu_custom_call" | custom-call | bytes 16777216 | tf_op jit(solution)/shard_map/gather_attn_in/pallas_call | solution.py:842
  160.0 18.1 %gather_ids.1 = bf16[2,2,4,2,32,128]{5,4,3,2,1,0:T(8,128)(2,1)} custom-call(bf16[32,128]{1,0:T(8,128)(2,1)} %scatter.4.in_ref), custom_call_target="tpu_custom_call" | custom-call | bytes 524288 | tf_op jit(solution)/shard_map/gather_ids/pallas_call | solution.py:842
  179.2 3.6 reshape.401
  182.8 3.0 copy.99
  186.3 4.9 fusion.30
  191.2 10.0 fusion.37
  201.9 1.9 copy-done.12
  204.5 11.1 sum_squares.1
  216.4 4.0 multiply_multiply_fusion
  220.4 3.3 reshape.384
  223.6 3.2 reshape.383
  226.9 4.5 slice_negate_fusion.2
  231.4 2.3 slice_negate_fusion.3
  233.8 5.8 maximum_multiply_fusion.1
  242.2 19.1 %attend.1 = bf16[2048,256]{1,0:T(8,128)(2,1)S(1)} custom-call(s32[4]{0:T(128)S(1)} %bitcast.147, bf16[2048,256]{1,0:T(8,128)(2,1)S(1)} %get-tuple-element.146.q_ref, bf16[2048,256]{1,0:T(8,128)(2,1)S(1)} %get-tuple-element.145.k_ref, bf16[2048,256]{1,0:T(8,128)(2,1)S(1)} %slice.208.v_ref), custom_call_target="tpu_custom_call" | custom-call | flops 2684354560 | bytes 4194304 | tf_op jit(solution)/shard_map/attend/pallas_call | solution.py:1017
  261.3 1.3 copy.97
  262.6 5.0 all-to-all-start
  270.4 5.8 all_gather.27
  276.4 43.5 %all-to-all-done = bf16[8,256,256]{1,2,0:T(8,128)(2,1)S(1)} async-done(((bf16[8,256,256]{1,2,0:T(8,128)(2,1)}), bf16[8,256,256]{1,2,0:T(8,128)(2,1)S(1)}, u32[]{:S(2)}, u32[]{:S(2)}) %all-to-all-start) | async-done | bytes 1048608 | tf_op jit(solution)/shard_map/all_to_all | solution.py:1134
  319.9 6.8 multiply_reduce_fusion.6
  329.2 174.0 %gather_ffn_in.1 = bf16[2,2,4,2,256,2048]{5,4,3,2,1,0:T(8,128)(2,1)} custom-call(bf16[256,2048]{1,0:T(8,128)(2,1)} %multiply_convert_fusion.in_ref), custom_call_target="tpu_custom_call" | custom-call | bytes 67108864 | tf_op jit(solution)/shard_map/gather_ffn_in/pallas_call | solution.py:842
  504.6 16.2 %fusion.35 = (f32[8192]{0:T(1024)S(1)}, f32[8192,64]{0,1:T(8,128)S(1)}) fusion(bf16[8192,2048]{1,0:T(8,128)(2,1)} %bitcast.149, bf16[2048,64]{0,1:T(8,128)(2,1)S(1)} %all_gather.27), kind=kOutput, calls=%fused_computation.142 | convolution fusion | flops 2147999744 | bytes 35946496 | tf_op jit(solution)/shard_map/dot_general | solution.py:1144
  521.2 43.9 %dispatch_tokens.1 = (bf16[8,1792,2048]{2,1,0:T(8,128)(2,1)}, f32[8,1792,128]{2,1,0:T(8,128)}) custom-call(s32[256]{0:T(256)S(1)} %reshape.386.starts, s32[256]{0:T(256)S(1)} %and_select_fusion.steps, s32[8]{0:T(128)S(1)} %add_reduce_fusion.used, s32[32,8,256]{2,1,0:T(8,128)S(1)} %get-tuple-element.158.rank_ref, f32[32,8,256]{2,1,0:T(8,128)S(1)} %bitcast.146, ...), custom_call_target="tpu_custom_call" | custom-call | flops 17179869184 | bytes 100663296 | tf_op jit(solution)/shard_map/dispatch_tokens/pallas_call | solution.py:237
  565.1 43.0 %dispatch_cotangent.1.c_ref = bf16[8,1792,2048]{2,1,0:T(8,128)(2,1)} custom-call(s32[256]{0:T(256)S(1)} %reshape.386.starts, s32[256]{0:T(256)S(1)} %and_select_fusion.steps, s32[8]{0:T(128)S(1)} %add_reduce_fusion.used, s32[32,8,256]{2,1,0:T(8,128)S(1)} %get-tuple-element.158.rank_ref, bf16[8192,2048]{1,0:T(8,128)(2,1)} %bitcast.156), custom_call_target="tpu_custom_call" | custom-call | flops 17179869184 | bytes 100663296 | tf_op jit(solution)/shard_map/dispatch_cotangent/pallas_call | solution.py:223
  608.1 154.3 %experts.1 = (bf16[8,1792,2048]{2,1,0:T(8,128)(2,1)}, bf16[8,1792,2176]{2,1,0:T(8,128)(2,1)}, f32[8,2048,256]{2,1,0:T(8,128)}, f32[8,2048,256]{2,1,0:T(8,128)}, f32[8,2048,256]{2,1,0:T(8,128)}) custom-call(s32[8]{0:T(128)} %copy-done.7, s32[1]{0:T(128)} %bitcast.20.first, ...), custom_call_target="tpu_custom_call", output_to_operand_aliasing={{0}: (2, {})} | custom-call | flops 135291469824 | bytes 234881024 | tf_op jit(solution)/shard_map/experts/pallas_call | solution.py:327
  762.4 43.5 %combine_grads.1 = bf16[8192,2176]{1,0:T(8,128)(2,1)} custom-call(s32[256]{0:T(256)S(1)} %reshape.386.starts, s32[256]{0:T(256)S(1)} %and_select_fusion.steps, s32[32,8,256]{2,1,0:T(8,128)S(1)} %get-tuple-element.158.rank_ref, bf16[8,1792,2176]{2,1,0:T(8,128)(2,1)} %get-tuple-element.39.y_ref), custom_call_target="tpu_custom_call" | custom-call | flops 18253611008 | bytes 106954752 | tf_op jit(solution)/shard_map/combine_grads/pallas_call | solution.py:410
  805.9 154.8 %scatter_grads.1 = f32[256,2176]{1,0:T(8,128)} custom-call(bf16[2,2,4,2,256,2176]{5,4,3,2,1,0:T(8,128)(2,1)} %bitcast.151), custom_call_target="tpu_custom_call" | custom-call | flops 17825792 | bytes 35651584 | tf_op jit(solution)/shard_map/scatter_grads/pallas_call | solution.py:697
  960.7 41.5 %combine_outputs.1 = bf16[8192,2048]{1,0:T(8,128)(2,1)} custom-call(s32[256]{0:T(256)S(1)} %reshape.386.starts, s32[256]{0:T(256)S(1)} %and_select_fusion.steps, s32[32,8,256]{2,1,0:T(8,128)S(1)} %get-tuple-element.158.rank_ref, bf16[8,1792,2048]{2,1,0:T(8,128)(2,1)} %get-tuple-element.38.y_ref), custom_call_target="tpu_custom_call" | custom-call | flops 17179869184 | bytes 100663296 | tf_op jit(solution)/shard_map/combine_outputs/pallas_call | solution.py:410
  1002.3 146.3 %scatter_outputs.1 = f32[256,2048]{1,0:T(8,128)} custom-call(bf16[2,2,4,2,256,2048]{5,4,3,2,1,0:T(8,128)(2,1)} %bitcast.152), custom_call_target="tpu_custom_call" | custom-call | flops 16777216 | bytes 33554432 | tf_op jit(solution)/shard_map/scatter_outputs/pallas_call | solution.py:697
  1149.8 2.7 multiply_reduce_fusion
  1152.7 1.8 fusion.4
  1154.5 6.5 convolution_convert_fusion.3
  1162.1 3.9 all-to-all-start.1
  1166.1 26.0 %all-to-all-done.1 = bf16[256,8,256]{2,0,1:T(8,128)(2,1)S(1)} async-done(((bf16[256,8,256]{2,0,1:T(8,128)(2,1)}), bf16[256,8,256]{2,0,1:T(8,128)(2,1)S(1)}, u32[]{:S(2)}, u32[]{:S(2)}) %all-to-all-start.1) | async-done | bytes 1048608 | tf_op jit(solution)/shard_map/all_to_all | solution.py:1180
  1194.3 29.1 %attend_back.1 = (bf16[2048,256]{1,0:T(8,128)(2,1)S(1)}, bf16[2048,256]{1,0:T(8,128)(2,1)S(1)}, bf16[2048,256]{1,0:T(8,128)(2,1)S(1)}) custom-call(s32[4]{0:T(128)S(1)} %bitcast.148, bf16[2048,256]{1,0:T(8,128)(2,1)S(1)} %copy-done.5, bf16[2048,256]{1,0:T(8,128)(2,1)S(1)} %copy-done.3, bf16[2048,256]{1,0:T(8,128)(2,1)} %copy-done.6, bf16[2048,256]{1,0:T(8,128)(2,1)} %bitcast.172), custom_call_target="tpu_custom_call" | custom-call | flops 8053063680 | bytes 4194304 | tf_op jit(solution)/shard_map/attend_back/pallas_call | solution.py:1022
  1224.4 2.0 reshape.392
  1226.4 5.8 slice_negate_fusion
  1232.1 2.0 reshape.391
  1234.1 4.5 slice_negate_fusion.1
  1238.8 5.6 maximum_multiply_fusion.3
  1244.4 3.2 multiply_reduce_fusion.2
  1248.3 7.9 sum_products.1
  1256.9 5.0 subtract_convert_fusion.1
  1262.9 10.6 convolution_convert_fusion.2
  1274.7 1.4 convolution_convert_fusion.4
  1276.1 4.0 convolution_convert_fusion
  1280.1 8.9 maximum_maximum_fusion
  1289.0 11.8 copy.110
  1300.9 48.7 %scatter_out_rows.1 = f32[64,2176]{1,0:T(8,128)} custom-call(bf16[2,2,4,2,64,2176]{5,4,3,2,1,0:T(8,128)(2,1)} %bitcast.155), custom_call_target="tpu_custom_call" | custom-call | flops 4456448 | bytes 8912896 | tf_op jit(solution)/shard_map/scatter_out_rows/pallas_call | solution.py:697
  1349.6 1.8 convert_element_type.193
  1352.0 11.1 convolution_convert_fusion.1
  1363.1 120.3 %scatter_attn_in.1 = f32[256,2048]{1,0:T(8,128)} custom-call(bf16[1,1,4,2,256,2048]{5,4,3,2,1,0:T(8,128)(2,1)} %bitcast.161), custom_call_target="tpu_custom_call" | custom-call | flops 4194304 | bytes 8388608 | tf_op jit(solution)/shard_map/scatter_attn_in/pallas_call | solution.py:697
  1483.5 2.3 fusion.3
  1486.5 37.0 %sum_gains.1 = f32[64,128]{1,0:T(8,128)} custom-call(f32[64,128]{1,0:T(8,128)} %reshape.397.part_ref), custom_call_target="tpu_custom_call" | custom-call | tf_op jit(solution)/shard_map/sum_gains/pallas_call | solution.py:904
  1524.9 4.1 fusion.6
  1530.8 4.1 slice_convert_fusion
  1534.9 35.7 %all-gather.16.cloned.1.call-done = bf16[4096,768]{1,0:T(8,128)(2,1)} async-done(((bf16[512,768]{1,0:T(8,128)(2,1)}), bf16[4096,768]{1,0:T(8,128)(2,1)}) %all-gather.16.cloned.1.call-update) | async-done | bytes 6291472 | tf_op jit(solution)/shard_map/all_gather | solution.py:1224
  1570.6 4.4 convert_bitcast_fusion
  1575.0 2.6 copy.114
  1577.7 2.6 copy.115
  1580.3 2.6 copy.116
  (246 shorter events, 32.6 us)
Async XLA Ops:
  7.2 184.0 %all-gather.8.cloned.1.call-start = ((), (), s32[]{:S(2)}) async-start(), calls=%async_computation.3 | async-start | bytes 3932160 | tf_op jit(solution)/shard_map/all_gather | solution.py:1110
  10.8 7.8 copy-start.13
  10.9 309.0 %all-gather.10.cloned.1.call-start = ((), (), s32[]{:S(2)}) async-start(), calls=%async_computation.4 | async-start | bytes 10485760 | tf_op jit(solution)/shard_map/all_gather | solution.py:1111
  11.6 553.5 %all-gather.14.cloned.1.call-start = ((), (), s32[]{:S(2)}) async-start(), calls=%async_computation.7 | async-start | bytes 34603008 | tf_op jit(solution)/shard_map/all_gather | solution.py:1113
  19.5 139.4 %copy-start.55 = (f32[256]{0:T(256)}, f32[256]{0:T(256)S(1)}, u32[]{:S(2)}) copy-start(f32[256]{0:T(256)S(1)} %fusion.26) | copy-start | bytes 3076
  19.5 139.4 %copy-start.46 = (f32[1,2048]{1,0:T(1,128)}, f32[1,2048]{1,0:T(1,128)S(1)}, u32[]{:S(2)}) copy-start(f32[1,2048]{1,0:T(1,128)S(1)} %get-tuple-element.169) | copy-start | bytes 24580
  19.5 307.2 %copy-start.52 = (f32[1,2048]{1,0:T(1,128)}, f32[1,2048]{1,0:T(1,128)S(1)}, u32[]{:S(2)}) copy-start(f32[1,2048]{1,0:T(1,128)S(1)} %get-tuple-element.168) | copy-start | bytes 24580
  20.8 138.1 %copy-start.75 = (s32[1,4]{1,0:T(1,128)S(1)}, s32[1,4]{1,0:T(1,128)}, u32[]{:S(2)}) copy-start(s32[1,4]{1,0:T(1,128)} %param.19) | copy-start | bytes 52
  20.8 138.3 %copy-start.69 = (s32[1,256,8]{1,2,0:T(8,128)S(1)}, s32[1,256,8]{1,2,0:T(8,128)}, u32[]{:S(2)}) copy-start(s32[1,256,8]{1,2,0:T(8,128)} %param.20) | copy-start | bytes 24580
  159.1 83.0 %copy-start.8 = (s32[4,1]{0,1:T(1,128)}, s32[4,1]{0,1:T(1,128)S(1)}, u32[]{:S(2)}) copy-start(s32[4,1]{0,1:T(1,128)S(1)} %reduce-window.9) | copy-start | bytes 52
  186.0 30.4 %copy-start.57 = (f32[1,256]{1,0:T(1,128)}, f32[1,256]{1,0:T(1,128)S(1)}, u32[]{:S(2)}) copy-start(f32[1,256]{1,0:T(1,128)S(1)} %get-tuple-element.172) | copy-start | bytes 3076
  186.0 30.4 %copy-start.59 = (f32[1,256]{1,0:T(1,128)}, f32[1,256]{1,0:T(1,128)S(1)}, u32[]{:S(2)}) copy-start(f32[1,256]{1,0:T(1,128)S(1)} %get-tuple-element.173) | copy-start | bytes 3076
  201.3 40.8 %copy-start.6 = (bf16[2048,256]{1,0:T(8,128)(2,1)}, bf16[2048,256]{1,0:T(8,128)(2,1)S(1)}, u32[]{:S(2)}) copy-start(bf16[2048,256]{1,0:T(8,128)(2,1)S(1)} %slice.208.v_ref) | copy-start | bytes 3145732
  216.3 4.0 copy-start.44
  216.3 4.0 copy-start.48
  226.9 4.5 copy-start.24
  233.8 6.6 copy-start.23
  242.1 19.2 %copy-start.2 = (bf16[2048,256]{1,0:T(8,128)(2,1)}, bf16[2048,256]{1,0:T(8,128)(2,1)S(1)}, u32[]{:S(2)}) copy-start(bf16[2048,256]{1,0:T(8,128)(2,1)S(1)} %get-tuple-element.145.k_ref) | copy-start | bytes 3145732
  242.1 19.2 %copy-start.4 = (bf16[2048,256]{1,0:T(8,128)(2,1)}, bf16[2048,256]{1,0:T(8,128)(2,1)S(1)}, u32[]{:S(2)}) copy-start(bf16[2048,256]{1,0:T(8,128)(2,1)S(1)} %get-tuple-element.146.q_ref) | copy-start | bytes 3145732
  262.6 7.7 copy-start.54
  262.6 57.2 %copy-start.14 = (bf16[1,256,2048]{2,1,0:T(8,128)(2,1)S(1)}, bf16[1,256,2048]{2,1,0:T(8,128)(2,1)}, u32[]{:S(2)}) copy-start(bf16[1,256,2048]{2,1,0:T(8,128)(2,1)} %param.18) | copy-start | bytes 3145732
  262.6 57.2 %all-to-all-start = ((bf16[8,256,256]{1,2,0:T(8,128)(2,1)}), bf16[8,256,256]{1,2,0:T(8,128)(2,1)S(1)}, u32[]{:S(2)}, u32[]{:S(2)}) async-start(bf16[8,256,256]{1,2,0:T(8,128)(2,1)} %copy.97), calls=%async_computation | async-start | bytes 2097152 | tf_op jit(solution)/shard_map/all_to_all | solution.py:1134
  276.2 228.4 %copy-start.35 = (bf16[2048,64]{0,1:T(8,128)(2,1)}, bf16[2048,64]{0,1:T(8,128)(2,1)S(1)}, u32[]{:S(2)}) copy-start(bf16[2048,64]{0,1:T(8,128)(2,1)S(1)} %all_gather.27) | copy-start | bytes 786436
  276.4 288.7 %copy-start.7 = (s32[8]{0:T(128)}, s32[8]{0:T(128)S(1)}, u32[]{:S(2)}) copy-start(s32[8]{0:T(128)S(1)} %add_reduce_fusion.used) | copy-start | bytes 100
  319.9 6.8 copy-start.25
  326.7 176.5 %copy-start.67 = (f32[256]{0:T(256)}, f32[256]{0:T(256)S(1)}, u32[]{:S(2)}) copy-start(f32[256]{0:T(256)S(1)} %get-tuple-element.176) | copy-start | bytes 3076
  326.7 176.5 %copy-start.63 = (f32[256]{0:T(256)}, f32[256]{0:T(256)S(1)}, u32[]{:S(2)}) copy-start(f32[256]{0:T(256)S(1)} %fusion.27) | copy-start | bytes 3076
  329.2 174.0 %copy-start.27 = (bf16[256,2048]{1,0:T(8,128)(2,1)S(1)}, bf16[256,2048]{1,0:T(8,128)(2,1)}, u32[]{:S(2)}) copy-start(bf16[256,2048]{1,0:T(8,128)(2,1)} %multiply_convert_fusion.in_ref) | copy-start | bytes 3145732
  503.7 17.1 %copy-start.61 = (f32[256]{0:T(256)}, f32[256]{0:T(256)S(1)}, u32[]{:S(2)}) copy-start(f32[256]{0:T(256)S(1)} %get-tuple-element.180) | copy-start | bytes 3076
  503.8 17.0 %copy-start.37 = (f32[256,64]{1,0:T(8,128)}, f32[256,64]{1,0:T(8,128)S(1)}, u32[]{:S(2)}) copy-start(f32[256,64]{1,0:T(8,128)S(1)} %copy.105) | copy-start | bytes 196612
  1002.2 146.4 %copy-start.38 = (f32[256,64]{1,0:T(8,128)S(1)}, f32[256,64]{1,0:T(8,128)}, u32[]{:S(2)}) copy-start(f32[256,64]{1,0:T(8,128)} %copy-done.37) | copy-start | bytes 196612
  1002.2 146.4 %copy-start.62 = (f32[256]{0:T(256)S(1)}, f32[256]{0:T(256)}, u32[]{:S(2)}) copy-start(f32[256]{0:T(256)} %copy-done.61) | copy-start | bytes 3076
  1002.2 146.4 %copy-start.70 = (f32[256]{0:T(256)S(1)}, f32[256]{0:T(256)}, u32[]{:S(2)}) copy-start(f32[256]{0:T(256)} %fusion.21) | copy-start | bytes 3076
  1002.2 147.5 %copy-start.18 = (f32[256,2048]{1,0:T(8,128)S(1)}, f32[256,2048]{1,0:T(8,128)}, u32[]{:S(2)}) copy-start(f32[256,2048]{1,0:T(8,128)} %copy-done.17) | copy-start | bytes 6291460
  1002.2 147.5 %copy-start.36 = (bf16[2048,64]{0,1:T(8,128)(2,1)S(1)}, bf16[2048,64]{0,1:T(8,128)(2,1)}, u32[]{:S(2)}) copy-start(bf16[2048,64]{0,1:T(8,128)(2,1)} %copy-done.35) | copy-start | bytes 786436
  1002.2 147.5 %copy-start.53 = (f32[1,2048]{1,0:T(1,128)S(1)}, f32[1,2048]{1,0:T(1,128)}, u32[]{:S(2)}) copy-start(f32[1,2048]{1,0:T(1,128)} %copy-done.52) | copy-start | bytes 24580
  1002.2 147.5 %copy-start.64 = (f32[256]{0:T(256)S(1)}, f32[256]{0:T(256)}, u32[]{:S(2)}) copy-start(f32[256]{0:T(256)} %copy-done.63) | copy-start | bytes 3076
  1002.3 150.2 %copy-start.32 = (bf16[1,256,2048]{2,1,0:T(8,128)(2,1)S(1)}, bf16[1,256,2048]{2,1,0:T(8,128)(2,1)}, u32[]{:S(2)}) copy-start(bf16[1,256,2048]{2,1,0:T(8,128)(2,1)} %param.33) | copy-start | bytes 3145732
  1154.5 6.5 copy-start.16
  1161.0 5.1 copy-start.45
  1161.0 32.0 %copy-start.3 = (bf16[2048,256]{1,0:T(8,128)(2,1)S(1)}, bf16[2048,256]{1,0:T(8,128)(2,1)}, u32[]{:S(2)}) copy-start(bf16[2048,256]{1,0:T(8,128)(2,1)} %copy-done.2) | copy-start | bytes 3145732
  1161.0 32.0 %copy-start.9 = (s32[4,1]{0,1:T(1,128)S(1)}, s32[4,1]{0,1:T(1,128)}, u32[]{:S(2)}) copy-start(s32[4,1]{0,1:T(1,128)} %copy-done.8) | copy-start | bytes 52
  1162.1 30.0 %all-to-all-start.1 = ((bf16[256,8,256]{2,0,1:T(8,128)(2,1)}), bf16[256,8,256]{2,0,1:T(8,128)(2,1)S(1)}, u32[]{:S(2)}, u32[]{:S(2)}) async-start(bf16[256,8,256]{2,0,1:T(8,128)(2,1)} %bitcast.143), calls=%async_computation.1 | async-start | bytes 2097152 | tf_op jit(solution)/shard_map/all_to_all | solution.py:1180
  1166.0 185.5 %reduce-scatter.2.cloned.1.call-start = ((), (), s32[]{:S(2)}) async-start(), calls=%async_computation.5 | async-start | bytes 3932160 | tf_op jit(solution)/shard_map/reduce_scatter | solution.py:1221
  1234.1 4.5 copy-start.30
  1234.1 4.5 copy-start.31
  1234.1 4.5 copy-start.33
  1238.6 5.7 slice-start
  1238.7 5.7 slice-start.1
  1238.7 5.7 copy-start.21
  1238.7 5.7 copy-start.49
  1238.7 5.7 copy-start.51
  1238.7 5.7 copy-start.58
  1238.7 5.7 copy-start.60
  1256.9 6.0 copy-start.11
  1261.9 11.6 copy-start.39
  1273.5 255.5 %all-gather.12.cloned.1.call-start = ((), (), s32[]{:S(2)}) async-start(), calls=%async_computation.6 | async-start | bytes 2506752 | tf_op jit(solution)/shard_map/all_gather | solution.py:1225
  1300.9 51.1 %copy-start.40 = (bf16[2048,256]{1,0:T(8,128)(2,1)S(1)}, bf16[2048,256]{1,0:T(8,128)(2,1)}, u32[]{:S(2)}) copy-start(bf16[2048,256]{1,0:T(8,128)(2,1)} %copy-done.39) | copy-start | bytes 3145732
  1300.9 51.2 %copy-start.42 = (bf16[2048,256]{1,0:T(8,128)(2,1)S(1)}, bf16[2048,256]{1,0:T(8,128)(2,1)}, u32[]{:S(2)}) copy-start(bf16[2048,256]{1,0:T(8,128)(2,1)} %copy-done.41) | copy-start | bytes 3145732
  1351.4 219.2 %all-gather.16.cloned.1.call-start = ((), (), s32[]{:S(2)}) async-start(), calls=%async_computation.8 | async-start | bytes 7077888 | tf_op jit(solution)/shard_map/all_gather | solution.py:1224
  1363.1 120.4 %copy-start.15 = (bf16[1,256,2048]{2,1,0:T(8,128)(2,1)S(1)}, bf16[1,256,2048]{2,1,0:T(8,128)(2,1)}, u32[]{:S(2)}) copy-start(bf16[1,256,2048]{2,1,0:T(8,128)(2,1)} %param.18) | copy-start | bytes 3145732
  1363.1 120.4 %copy-start.47 = (f32[1,2048]{1,0:T(1,128)S(1)}, f32[1,2048]{1,0:T(1,128)}, u32[]{:S(2)}) copy-start(f32[1,2048]{1,0:T(1,128)} %copy-done.46) | copy-start | bytes 24580
  1363.1 120.4 %copy-start.56 = (f32[256]{0:T(256)S(1)}, f32[256]{0:T(256)}, u32[]{:S(2)}) copy-start(f32[256]{0:T(256)} %copy-done.55) | copy-start | bytes 3076
  1483.4 41.5 %copy-start.66 = (f32[256]{0:T(256)S(1)}, f32[256]{0:T(256)}, u32[]{:S(2)}) copy-start(f32[256]{0:T(256)} %copy-done.65) | copy-start | bytes 3076
  (22 other events, 41.1 us)
Sparse Core Ops, SparseCore 0:
  11.0 31.2 all-gather.7
  43.8 58.2 all-gather.9
  105.1 222.3 all-gather.13
  1273.7 40.8 reduce-scatter.1
  1351.5 90.2 all-gather.11
  1444.1 126.4 all-gather.15

commit v4 on v3

--- a/solution.py
+++ b/solution.py
@@ -36,220 +36,50 @@
     return (jnp.cos(phase_all)[:, None, :], jnp.sin(phase_all)[:, None, :])
 
 
-BLOCK = 256
-SLOTS = 64
-STEP = 16
 TILE = 256
-
-
-def exclusive_sum(values):
-    count = values.shape[0]
-    lower = (jnp.arange(count)[:, None] > jnp.arange(count)[None, :]).astype(jnp.float32)
-    total = jnp.dot(lower, values.astype(jnp.float32), precision=lax.Precision.HIGHEST)
-    return total.astype(jnp.int32)
+LANES = 128
 
 
 def route_plan(own_ids, sp_count, fs_count):
     local_experts = EXPERTS // sp_count
+    block = own_ids.shape[0]
     per_device = own_ids.size
-    packed = jnp.zeros((32, 128), jnp.bfloat16)
-    packed = packed.at[: per_device // 128].set(own_ids.astype(jnp.bfloat16).reshape(-1, 128))
+    packed = jnp.zeros((32, LANES), jnp.bfloat16)
+    packed = packed.at[: per_device // LANES].set(own_ids.astype(jnp.bfloat16).reshape(-1, LANES))
     packed = gather_over_all(packed, sp_count, fs_count, 10, "gather_ids")
-    ids = packed.reshape(-1, 32 * 128)[:, :per_device].reshape(-1, TOPK).astype(jnp.int32)
-    tokens = ids.shape[0]
-    blocks = tokens // BLOCK
-    capacity = 5 * tokens * TOPK // (4 * EXPERTS)
+    ids = packed.reshape(-1, 32 * LANES)[:, :per_device].reshape(-1, TOPK).astype(jnp.int32)
+    blocks = ids.shape[0] // block
+    capacity = 5 * ids.shape[0] * TOPK // (4 * EXPERTS)
     first = lax.axis_index("sp") * local_experts
     mine = first + jnp.arange(local_experts, dtype=jnp.int32)
     named = jnp.any(ids[:, None, :] == mine[None, :, None], axis=-1)
-    named = named.reshape(blocks, BLOCK, local_experts)
-    upto = (jnp.arange(BLOCK)[:, None] >= jnp.arange(BLOCK)[None, :]).astype(jnp.bfloat16)
+    named = named.reshape(blocks, block, local_experts)
+    upto = (jnp.arange(block)[:, None] >= jnp.arange(block)[None, :]).astype(jnp.bfloat16)
     running = jnp.einsum(
         "ts,bse->bte", upto, named.astype(jnp.bfloat16), preferred_element_type=jnp.float32
     ).astype(jnp.int32)
-    earlier = exclusive_sum(running[:, -1])
+    before = (jnp.arange(blocks)[:, None] > jnp.arange(blocks)[None, :]).astype(jnp.float32)
+    earlier = jnp.dot(
+        before, running[:, -1].astype(jnp.float32), precision=lax.Precision.HIGHEST
+    ).astype(jnp.int32)
     keep = named & (earlier[:, None, :] + running - 1 < capacity)
     rank = jnp.where(keep, running - 1, -1).transpose(0, 2, 1)
-    steps = (jnp.sum(keep.astype(jnp.int32), axis=1) + STEP - 1) // STEP
-    starts = exclusive_sum(steps)
-    used = starts[-1] + steps[-1]
-    slots_all = min(blocks * SLOTS, capacity + blocks * (STEP - 1))
-    slots_all = (slots_all + TILE - 1) // TILE * TILE
-    return rank, starts.reshape(-1), steps.reshape(-1), used, slots_all
-
-
-def steps_copy(count, make, act):
-    for size in range(1, SLOTS // STEP + 1):
-
-        @pl.when(count == size)
-        def _(size=size):
-            act(make(size * STEP))
-
-
-def start_copy(copy):
-    copy.start()
-
-
-def wait_copy(copy):
-    copy.wait()
-
-
-def pick_matrix(rank):
-    experts = rank.shape[0]
-    slot = lax.broadcasted_iota(jnp.int32, (SLOTS, BLOCK), 0)
-    parts = [slot == rank[e : e + 1, :] for e in range(experts)]
-    return parts
-
-
-def dispatch_kernel(
-    starts, steps, used, rank_ref, weight_ref, x_ref, out_ref, wout_ref, buf, wbuf, zeros,
-    sems, wsems, zsems,
-):
-    experts = rank_ref.shape[1]
-    width = x_ref.shape[1]
-    b = pl.program_id(0)
-    blocks = pl.num_programs(0)
-    slot = lax.rem(b, 2)
-
-    def make(which, e, place):
-        first = starts[which * experts + e] * STEP
-
-        def rows(size):
-            return pltpu.make_async_copy(
-                buf.at[place, pl.ds(e * SLOTS, size)],
-                out_ref.at[e, pl.ds(pl.multiple_of(first, STEP), size)],
-                sems.at[place, e],
-            )
-
-        def weights(size):
-            return pltpu.make_async_copy(
-                wbuf.at[place, pl.ds(e * SLOTS, size)],
-                wout_ref.at[e, pl.ds(pl.multiple_of(first, STEP), size)],
-                wsems.at[place, e],
-            )
-
-        return rows, weights
-
-    def each(which, place, act):
-        for e in range(experts):
-            rows, weights = make(which, e, place)
-            steps_copy(steps[which * experts + e], rows, act)
-            if weight_ref is not None:
-                steps_copy(steps[which * experts + e], weights, act)
-
-    def fill(act):
-        for e in range(experts):
-            rest = lax.rem(TILE // STEP - lax.rem(used[e], TILE // STEP), TILE // STEP)
-            done = used[e]
-            for k, size in enumerate((8, 4, 2, 1)):
-                take = lax.rem(rest // size, 2)
-
-                @pl.when(take == 1)
-                def _(e=e, k=k, size=size, done=done):
-                    act(
-                        pltpu.make_async_copy(
-                            zeros.at[pl.ds(0, size * STEP)],
-                            out_ref.at[e, pl.ds(pl.multiple_of(done * STEP, STEP), size * STEP)],
-                            zsems.at[e, k],
-                        )
-                    )
-
-                done = done + take * size
-
-    @pl.when(b == 0)
-    def _():
-        zeros[...] = jnp.zeros_like(zeros)
-        fill(start_copy)
-
-    @pl.when(b >= 2)
-    def _():
-        each(b - 2, slot, wait_copy)
-
-    parts = pick_matrix(rank_ref[0])
-    if weight_ref is not None:
-        for e in range(experts):
-            column = jnp.sum(
-                jnp.where(parts[e], weight_ref[0, e : e + 1, :], 0.0), axis=1, keepdims=True
-            )
-            wbuf[slot, pl.ds(e * SLOTS, SLOTS), :] = jnp.broadcast_to(column, (SLOTS, 128))
-    pick = jnp.concatenate([p.astype(jnp.bfloat16) for p in parts], axis=0)
-    span = 512
-    for n in range(width // span):
-        cols = pl.ds(n * span, span)
-        buf[slot, :, cols] = jnp.dot(
-            pick, x_ref[:, cols], preferred_element_type=jnp.float32
-        ).astype(jnp.bfloat16)
-    each(b, slot, start_copy)
-
-    @pl.when(b == blocks - 1)
-    def _():
-        each(b - 1, 1 - slot, wait_copy)
-        each(b, slot, wait_copy)
-        fill(wait_copy)
-
-
-def dispatch_rows(table, routing, weights):
-    rank, starts, steps, used, slots_all = routing
-    blocks, experts, _ = rank.shape
-    width = table.shape[1]
-    wide = pl.BlockSpec((1, experts, BLOCK), lambda b, *_: (b, 0, 0))
-    anywhere = pl.BlockSpec(memory_space=pl.ANY)
-    rows_shape = jax.ShapeDtypeStruct((experts, slots_all, width), jnp.bfloat16)
-    scratch = [
-        pltpu.VMEM((2, experts * SLOTS, width), jnp.bfloat16),
-        pltpu.VMEM((2, experts * SLOTS, 128), jnp.float32),
-        pltpu.VMEM((8 * STEP, width), jnp.bfloat16),
-        pltpu.SemaphoreType.DMA((2, experts)),
-        pltpu.SemaphoreType.DMA((2, experts)),
-        pltpu.SemaphoreType.DMA((experts, 4)),
-    ]
-    flops = 2 * blocks * experts * SLOTS * BLOCK * width
-    params = dict(
-        compiler_params=pltpu.CompilerParams(
-            dimension_semantics=("arbitrary",), vmem_limit_bytes=48 * 2**20
-        ),
-        cost_estimate=pl.CostEstimate(
-            flops=flops, bytes_accessed=6 * blocks * BLOCK * width, transcendentals=0
-        ),
-    )
-    x_spec = pl.BlockSpec((BLOCK, width), lambda b, *_: (b, 0))
-    if weights is None:
-
-        def plain(starts, steps, used, rank_ref, x_ref, out_ref, *rest):
-            dispatch_kernel(
-                starts, steps, used, rank_ref, None, x_ref, out_ref, None, *rest
-            )
-
-        rows = pl.pallas_call(
-            plain,
-            grid_spec=pltpu.PrefetchScalarGridSpec(
-                num_scalar_prefetch=3,
-                grid=(blocks,),
-                in_specs=[wide, x_spec],
-                out_specs=anywhere,
-                scratch_shapes=scratch,
-            ),
-            out_shape=rows_shape,
-            name="dispatch_cotangent",
-            **params,
-        )(starts, steps, used, rank, table)
-        return rows, None
-    return pl.pallas_call(
-        dispatch_kernel,
-        grid_spec=pltpu.PrefetchScalarGridSpec(
-            num_scalar_prefetch=3,
-            grid=(blocks,),
-            in_specs=[wide, wide, x_spec],
-            out_specs=[anywhere, anywhere],
-            scratch_shapes=scratch,
-        ),
-        out_shape=[
-            rows_shape,
-            jax.ShapeDtypeStruct((experts, slots_all, 128), jnp.float32),
-        ],
-        name="dispatch_tokens",
-        **params,
-    )(starts, steps, used, rank, weights, table)
+    slots = 2 * block * TOPK // EXPERTS
+    some = jnp.any(keep, axis=1).reshape(-1, TILE // slots, local_experts)
+    live = jnp.any(some, axis=1).astype(jnp.int32).T.reshape(-1)
+    return rank, live
+
+
+def pick_matrix(rank, slots):
+    experts, block = rank.shape
+    slot = lax.broadcasted_iota(jnp.int32, (slots, block), 0)
+    return jnp.concatenate(
+        [(slot == rank[e : e + 1, :]).astype(jnp.bfloat16) for e in range(experts)], axis=0
+    )
+
+
+def column_spans(width):
+    return [(done, min(512, width - done)) for done in range(0, width, 512)]
 
 
 def contract(left, right, left_dim, right_dim):
@@ -259,13 +89,12 @@
 
 
 def expert_kernel(
-    used, first, x_ref, c_ref, w_ref, gate_ref, up_ref, down_ref, y_ref, dx_ref, gg_ref, gu_ref,
+    live, first, x_ref, c_ref, gate_ref, up_ref, down_ref, dx_ref, y_ref, gg_ref, gu_ref,
     gd_ref, acc_g, acc_u, acc_d,
 ):
     e = pl.program_id(0)
     t = pl.program_id(1)
-    rows_used = used[e] * STEP
-    width = x_ref.shape[2]
+    width = c_ref.shape[2]
 
     @pl.when(t == 0)
     def _():
@@ -273,15 +102,22 @@
         acc_u[...] = jnp.zeros_like(acc_u)
         acc_d[...] = jnp.zeros_like(acc_d)
 
-    @pl.when(t * TILE < rows_used)
+    @pl.when(live[e * pl.num_programs(1) + t] == 0)
     def _():
-        x = x_ref[0]
+        dx_ref[...] = jnp.zeros_like(dx_ref)
+        y_ref[...] = jnp.zeros_like(y_ref)
+
+    @pl.when(live[e * pl.num_programs(1) + t] > 0)
+    def _():
+        x = x_ref[0, :, 0:width]
         c = c_ref[0]
         gate_mat = gate_ref[0]
         up_mat = up_ref[0]
         down_mat = down_ref[0]
-        row = t * TILE + lax.broadcasted_iota(jnp.int32, (TILE, 1), 0)
-        weight = jnp.where(row < rows_used, w_ref[0][:, 0:1], 0.0)
+        column = lax.broadcasted_iota(jnp.int32, (TILE, LANES), 1)
+        mine = lax.rem(column, EXPERTS) == first[0] + e
+        gates = jnp.where(mine, x_ref[0, :, width : width + LANES].astype(jnp.float32), 0.0)
+        weight = jnp.sum(gates, axis=1, keepdims=True)
         gate_pre = jnp.dot(x, gate_mat, preferred_element_type=jnp.float32)
         up_pre = jnp.dot(x, up_mat, preferred_element_type=jnp.float32)
         up_act = jnp.dot(c, down_mat, preferred_element_type=jnp.float32)
@@ -297,8 +133,7 @@
         dx_ref[0, :, 0:width] = (
             contract(dgate, gate_mat, 1, 1) + contract(dup, up_mat, 1, 1)
         ).astype(jnp.bfloat16)
-        column = lax.broadcasted_iota(jnp.int32, (TILE, 128), 1)
-        dx_ref[0, :, width : width + 128] = jnp.where(
+        dx_ref[0, :, width : width + LANES] = jnp.where(
             column == first[0] + e, gate_grad, 0.0
         ).astype(jnp.bfloat16)
         acc_g[...] += contract(dgate, x, 0, 0)
@@ -312,127 +147,41 @@
         gd_ref[0] = acc_d[...].T
 
 
-def run_experts(x_rows, c_rows, w_rows, w_gate, w_up, w_down, used, first):
-    experts, slots_all, width = x_rows.shape
+def run_experts(x_rows, c_rows, w_gate, w_up, w_down, live, first):
+    experts, rows, width = c_rows.shape
     hidden = w_gate.shape[2]
 
-    def tile_map(e, t, used, first):
-        last = jnp.maximum((used[e] * STEP + TILE - 1) // TILE - 1, 0)
-        return (e, jnp.minimum(t, last), 0)
-
-    def mat_map(e, t, used, first):
-        return (e, 0, 0)
-
-    mat = pl.BlockSpec((1, width, hidden), mat_map)
+    def tile_map(e, t, live, first):
+        return (e, t, 0)
+
+    mat = pl.BlockSpec((1, width, hidden), lambda e, t, live, first: (e, 0, 0))
+    wide = pl.BlockSpec((1, TILE, width + LANES), tile_map)
+    plain = pl.BlockSpec((1, TILE, width), tile_map)
     return pl.pallas_call(
         expert_kernel,
         grid_spec=pltpu.PrefetchScalarGridSpec(
             num_scalar_prefetch=2,
-            grid=(experts, slots_all // TILE),
-            in_specs=[
-                pl.BlockSpec((1, TILE, width), tile_map),
-                pl.BlockSpec((1, TILE, width), tile_map),
-                pl.BlockSpec((1, TILE, 128), tile_map),
-                mat,
-                mat,
-                mat,
-            ],
-            out_specs=[
-                pl.BlockSpec((1, TILE, width), tile_map),
-                pl.BlockSpec((1, TILE, width + 128), tile_map),
-                mat,
-                mat,
-                mat,
-            ],
+            grid=(experts, rows // TILE),
+            in_specs=[wide, plain, mat, mat, mat],
+            out_specs=[wide, plain, mat, mat, mat],
             scratch_shapes=[pltpu.VMEM((hidden, width), jnp.float32)] * 3,
         ),
         out_shape=[
-            jax.ShapeDtypeStruct((experts, slots_all, width), jnp.bfloat16),
-            jax.ShapeDtypeStruct((experts, slots_all, width + 128), jnp.bfloat16),
+            jax.ShapeDtypeStruct(x_rows.shape, jnp.bfloat16),
+            jax.ShapeDtypeStruct(c_rows.shape, jnp.bfloat16),
         ]
         + [jax.ShapeDtypeStruct((experts, width, hidden), jnp.float32)] * 3,
-        input_output_aliases={2: 0},
+        input_output_aliases={2: 0, 3: 1},
         compiler_params=pltpu.CompilerParams(
             dimension_semantics=("arbitrary", "arbitrary"), vmem_limit_bytes=60 * 2**20
         ),
         cost_estimate=pl.CostEstimate(
-            flops=18 * experts * slots_all * width * hidden,
-            bytes_accessed=8 * experts * slots_all * width,
-            transcendentals=experts * slots_all * hidden,
+            flops=18 * experts * rows * width * hidden,
+            bytes_accessed=8 * experts * rows * width,
+            transcendentals=experts * rows * hidden,
         ),
         name="experts",
-    )(used, first, x_rows, c_rows, w_rows, w_gate, w_up, w_down)
-
-
-def combine_kernel(starts, steps, rank_ref, y_ref, out_ref, buf, sems):
-    experts = rank_ref.shape[1]
-    width = out_ref.shape[1]
-    b = pl.program_id(0)
-    blocks = pl.num_programs(0)
-    slot = lax.rem(b, 2)
-
-    def each(which, place, act):
-        for e in range(experts):
-            first = starts[which * experts + e] * STEP
-
-            def rows(size, e=e, first=first):
-                return pltpu.make_async_copy(
-                    y_ref.at[e, pl.ds(pl.multiple_of(first, STEP), size)],
-                    buf.at[place, pl.ds(e * SLOTS, size)],
-                    sems.at[place, e],
-                )
-
-            steps_copy(steps[which * experts + e], rows, act)
-
-    @pl.when(b == 0)
-    def _():
-        buf[...] = jnp.zeros_like(buf)
-        each(0, 0, start_copy)
-
-    @pl.when(b + 1 < blocks)
-    def _():
-        each(b + 1, 1 - slot, start_copy)
-
-    pick = jnp.concatenate([p.astype(jnp.bfloat16) for p in pick_matrix(rank_ref[0])], axis=0)
-    each(b, slot, wait_copy)
-    done = 0
-    while done < width:
-        span = min(512, width - done)
-        cols = pl.ds(done, span)
-        out_ref[:, cols] = contract(pick, buf[slot, :, cols], 0, 0).astype(jnp.bfloat16)
-        done += span
-
-
-def combine_rows(rows, routing, name):
-    rank, starts, steps, used, slots_all = routing
-    blocks, experts, _ = rank.shape
-    width = rows.shape[2]
-    return pl.pallas_call(
-        combine_kernel,
-        grid_spec=pltpu.PrefetchScalarGridSpec(
-            num_scalar_prefetch=2,
-            grid=(blocks,),
-            in_specs=[
-                pl.BlockSpec((1, experts, BLOCK), lambda b, *_: (b, 0, 0)),
-                pl.BlockSpec(memory_space=pl.ANY),
-            ],
-            out_specs=pl.BlockSpec((BLOCK, width), lambda b, *_: (b, 0)),
-            scratch_shapes=[
-                pltpu.VMEM((2, experts * SLOTS, width), jnp.bfloat16),
-                pltpu.SemaphoreType.DMA((2, experts)),
-            ],
-        ),
-        out_shape=jax.ShapeDtypeStruct((blocks * BLOCK, width), jnp.bfloat16),
-        compiler_params=pltpu.CompilerParams(
-            dimension_semantics=("arbitrary",), vmem_limit_bytes=48 * 2**20
-        ),
-        cost_estimate=pl.CostEstimate(
-            flops=2 * blocks * experts * SLOTS * BLOCK * width,
-            bytes_accessed=6 * blocks * BLOCK * width,
-            transcendentals=0,
-        ),
-        name=name,
-    )(starts, steps, rank, rows)
+    )(live, first, x_rows, c_rows, w_gate, w_up, w_down)
 
 
 MESH = pl.DeviceIdType.MESH
@@ -484,7 +233,7 @@
 
 def scatter_kernel(
     counts, parts, fsdp_too, part_ref, out_ref, own, buf, first, second, third, own_sem, s0, r0,
-    s1, r1, s2, r2, s3, r3,
+    s1, r1, s2, r2, s3, r3, host=None,
 ):
     at = Place(counts, fsdp_too)
     n_hi, n_lo, n_x, n_core = counts
@@ -505,7 +254,10 @@
 
     def mine(t, v, core):
         hi, q = where(t, v)
-        return part_ref.at[:, core, hi, :, pl.ds(pl.multiple_of(q * rows, 16), rows), :]
+        cut = pl.ds(pl.multiple_of(q * rows, 16), rows)
+        if host is not None:
+            return host.part.at[t // pairs % 2, :, core, :, cut, :]
+        return part_ref.at[:, core, hi, :, cut, :]
 
     def load_own(t, v):
         place = own.at[t % 2, v] if n_core > 1 else buf.at[2 * t + v]
@@ -570,7 +322,11 @@
 
     def stage_core(t, v):
         u = 2 * t + v
-        load_own(t, v).wait()
+        if host is None:
+            load_own(t, v).wait()
+            own_part = own.at[t % 2, v]
+        else:
+            own_part = mine(t, v, at.core)
         if n_core > 1:
             core_copy(t, v).wait_recv()
 
@@ -578,7 +334,7 @@
             def _(j):
                 x, lo = j // n_lo, j % n_lo
                 place = buf.at[u, x, lo]
-                place[...] = (wide(place) + wide(own.at[t % 2, v, x, lo])).astype(jnp.bfloat16)
+                place[...] = (wide(place) + wide(own_part.at[x, lo])).astype(jnp.bfloat16)
 
         if orders[v]:
             start_out(t, v, 0)
@@ -612,25 +368,39 @@
         else:
             send_last(t, v)
 
+    def each_core_copy(group, act):
+        @pl.loop(0, pairs)
+        def _(g):
+            for v in range(2):
+                act(core_copy(group * pairs + g, v))
+
+    def make_group(group, piece, pieces):
+        host.run(at, (at.hi + 1 + group) % n_hi, group % 2, piece, pieces)
+
     at.meet()
-    if n_core > 1:
-
-        @pl.loop(0, steps)
-        def _(t):
-            for v in range(2):
-                core_copy(t, v).start()
-
-    for v in range(2):
-        load_own(0, v).start()
+    if host is not None:
+        make_group(0, 0, 1)
+        each_core_copy(0, lambda c: c.start())
+    else:
+        if n_core > 1:
+
+            @pl.loop(0, n_hi)
+            def _(group):
+                each_core_copy(group, lambda c: c.start())
+
+        for v in range(2):
+            load_own(0, v).start()
 
     depth = len(orders[0])
 
     @pl.loop(0, steps + depth * lag)
     def _(t):
-        @pl.when(t + 1 < steps)
-        def _():
-            for v in range(2):
-                load_own(t + 1, v).start()
+        if host is None:
+
+            @pl.when(t + 1 < steps)
+            def _():
+                for v in range(2):
+                    load_own(t + 1, v).start()
 
         @pl.when(t < steps)
         def _():
@@ -644,6 +414,22 @@
             def _(stage=stage, back=back):
                 for v in range(2):
                     stage_mid(t - back, v, stage)
+
+        if host is not None:
+
+            @pl.when(t + pairs < steps)
+            def _():
+                group = t // pairs + 1
+
+                @pl.when((t % pairs == 0) & (group >= 2))
+                def _():
+                    each_core_copy(group - 2, lambda c: c.wait_send())
+
+                make_group(group, t % pairs, pairs)
+
+                @pl.when(t % pairs == pairs - 1)
+                def _():
+                    each_core_copy(group, lambda c: c.start())
 
     for g in range(pairs):
         t = (n_hi - 1) * pairs + g
@@ -658,7 +444,7 @@
     @pl.loop(0, steps)
     def _(t):
         for v in range(2):
-            if n_core > 1:
+            if host is None and n_core > 1:
                 core_copy(t, v).wait_send()
             for stage in range(depth):
                 for ahead in range(1, at.sizes()[orders[v][stage]]):
@@ -668,18 +454,71 @@
             def _(v=v):
                 last_copy(t, v, 1).wait_send()
 
-
-def scatter_sum(partial, counts, fsdp_too, parts, out_dtype, ident, name):
-    n_hi, n_lo, n_x, n_core = counts
-    rows, width = partial.shape[4:]
-    r = rows // parts
+    if host is not None:
+        for group in range(max(n_hi - 2, 0), n_hi):
+            each_core_copy(group, lambda c: c.wait_send())
+
+
+class Combine:
+    def __init__(self, rows_ref, rank_ref, part, held, sems, counts):
+        self.rows_ref, self.rank_ref, self.part, self.held, self.sems = (
+            rows_ref, rank_ref, part, held, sems,
+        )
+        self.n_hi, self.n_lo, self.n_x, self.n_core = counts
+
+    def run(self, at, hi, slot, piece, pieces):
+        total = self.n_x * self.n_core * self.n_lo
+        count = total // pieces
+        _, experts, slots, width = self.held.shape
+
+        def spot(j):
+            j = piece * count + j
+            return j // (self.n_core * self.n_lo), j // self.n_lo % self.n_core, j % self.n_lo
+
+        def block(j):
+            x, core, lo = spot(j)
+            return ((x * self.n_core + core) * self.n_hi + hi) * self.n_lo + lo
+
+        def load(j, place):
+            return pltpu.make_async_copy(
+                self.rows_ref.at[:, block(j)], self.held.at[place], self.sems.at[place]
+            )
+
+        load(0, 0).start()
+
+        @pl.loop(0, count)
+        def _(j):
+            place = j % 2
+
+            @pl.when(j + 1 < count)
+            def _():
+                load(j + 1, 1 - place).start()
+
+            load(j, place).wait()
+            pick = pick_matrix(self.rank_ref[block(j)], slots)
+            x, core, lo = spot(j)
+            for start, size in column_spans(width):
+                cols = pl.ds(start, size)
+                found = self.held[place, :, :, cols].reshape(experts * slots, size)
+                self.part[slot, x, core, lo, :, cols] = contract(pick, found, 0, 0).astype(
+                    jnp.bfloat16
+                )
+
+
+def combine_scatter_kernel(
+    counts, parts, rows_ref, rank_ref, out_ref, part, held, held_sem, *scratch
+):
+    host = Combine(rows_ref, rank_ref, part, held, held_sem, counts)
+    scatter_kernel(counts, parts, True, None, out_ref, None, *scratch, host=host)
+
+
+def scatter_scratch(counts, parts, r, width):
+    n_hi, n_lo, n_x, _ = counts
     units = n_hi * parts
     keep = max(n_x, n_lo)
     peers = max(n_x, n_lo, 2) - 1
     b16 = jnp.bfloat16
-    own_shape = (2, 2, n_x, n_lo, r, width) if n_core > 1 else (1, 1, 1, 1, 16, 128)
-    scratch = [
-        pltpu.VMEM(own_shape, b16),
+    return [
         pltpu.VMEM((units, n_x, n_lo, r, width), b16),
         pltpu.VMEM((units, peers, keep, r, width), b16),
         pltpu.VMEM((units, peers, r, width), b16),
@@ -694,6 +533,53 @@
         pltpu.SemaphoreType.DMA((units,)),
         pltpu.SemaphoreType.DMA((max(n_hi - 1, 1), parts)),
     ]
+
+
+def scatter_bytes(counts, parts, rows, width):
+    n_hi, n_lo, n_x, _ = counts
+    keep = max(n_x, n_lo)
+    peers = max(n_x, n_lo, 2) - 1
+    held = n_hi * (n_x * n_lo + peers * keep + peers) + max(n_hi - 1, 1)
+    return (2 * held + 4) * rows * width
+
+
+VMEM_ROOM = 58 * 2**20
+
+
+def combine_sum(rows, rank, counts, parts, slots, ident, name):
+    blocks, experts, block = rank.shape
+    width = rows.shape[-1]
+    _, n_lo, n_x, n_core = counts
+    b16 = jnp.bfloat16
+    return pl.pallas_call(
+        functools.partial(combine_scatter_kernel, counts, parts),
+        in_specs=[pl.BlockSpec(memory_space=pl.ANY), pl.BlockSpec(memory_space=pltpu.VMEM)],
+        out_specs=pl.BlockSpec(memory_space=pltpu.VMEM),
+        out_shape=jax.ShapeDtypeStruct((block, width), jnp.float32),
+        scratch_shapes=[
+            pltpu.VMEM((2, n_x, n_core, n_lo, block, width), b16),
+            pltpu.VMEM((2, experts, slots, width), b16),
+            pltpu.SemaphoreType.DMA((2,)),
+        ]
+        + scatter_scratch(counts, parts, block // parts, width),
+        compiler_params=pltpu.CompilerParams(
+            collective_id=ident, has_side_effects=True, vmem_limit_bytes=62 * 2**20
+        ),
+        cost_estimate=pl.CostEstimate(
+            flops=2 * blocks * experts * slots * block * width,
+            bytes_accessed=4 * blocks * block * width,
+            transcendentals=0,
+        ),
+        name=name,
+    )(rows.reshape(experts, blocks, slots, width), rank)
+
+
+def scatter_sum(partial, counts, fsdp_too, parts, out_dtype, ident, name):
+    _, n_lo, n_x, n_core = counts
+    rows, width = partial.shape[4:]
+    r = rows // parts
+    own_shape = (2, 2, n_x, n_lo, r, width) if n_core > 1 else (1, 1, 1, 1, 16, 128)
+    scratch = [pltpu.VMEM(own_shape, jnp.bfloat16)] + scatter_scratch(counts, parts, r, width)
     return pl.pallas_call(
         functools.partial(scatter_kernel, counts, parts, fsdp_too),
         in_specs=[pl.BlockSpec(memory_space=pl.ANY)],
@@ -711,7 +597,7 @@
 
 
 def gather_kernel(
-    counts, parts, fsdp_too, in_ref, out_ref, own_sem, s0, r0, s1, r1, s2, r2, s3, r3
+    counts, parts, fsdp_too, in_ref, out_ref, own_sem, s0, r0, s1, r1, s2, r2, s3, r3, host=None
 ):
     at = Place(counts, fsdp_too)
     n_hi, n_lo, n_x, n_core = counts
@@ -778,7 +664,7 @@
             hi_copy(q, ahead).start()
     keep.wait()
 
-    @pl.loop(0, steps + depth)
+    @pl.loop(0, steps + depth + (1 if host is not None and n_core > 1 else 0))
     def _(t):
         @pl.when(t < steps)
         def _():
@@ -807,11 +693,32 @@
                     elif n_core > 1:
                         core_copy(t - back, v).start()
 
+        if host is not None:
+            for origin_step in range(n_hi):
+                done = (origin_step + 1) * pairs - 1 + depth
+                hi = (at.hi + n_hi - origin_step) % n_hi
+
+                @pl.when(t == done)
+                def _(hi=hi):
+                    host.blocks(at, at.core, hi)
+
+                if n_core > 1:
+
+                    @pl.when(t == done + 1)
+                    def _(hi=hi, origin_step=origin_step):
+                        for g in range(pairs):
+                            for v in range(2):
+                                core_copy(origin_step * pairs + g, v).wait_recv()
+                        host.blocks(at, 1 - at.core, hi)
+
+            host.others(t, steps + depth)
+
     @pl.loop(0, steps)
     def _(t):
         for v in range(2):
             if n_core > 1:
-                core_copy(t, v).wait_recv()
+                if host is None:
+                    core_copy(t, v).wait_recv()
                 core_copy(t, v).wait_send()
             for stage in range(depth):
                 each_mid(t, v, stage, lambda c: c.wait_send())
@@ -821,30 +728,145 @@
             hi_copy(q, ahead).wait_send()
 
 
+class Dispatch:
+    def __init__(self, tables, rows, bufs, ins, outs, rank_ref, geometry):
+        self.tables, self.rows, self.bufs, self.ins, self.outs = tables, rows, bufs, ins, outs
+        self.rank_ref = rank_ref
+        self.n_hi, self.n_lo, self.n_x, self.n_core = geometry
+
+    def load(self, which, place, index, slot):
+        held, _ = self.bufs[which]
+        return pltpu.make_async_copy(
+            self.tables[which].at[index], held.at[slot], self.ins[which].at[slot]
+        )
+
+    def store(self, which, block, slot):
+        _, found = self.bufs[which]
+        return pltpu.make_async_copy(
+            found.at[slot], self.rows[which].at[:, block], self.outs[which].at[slot]
+        )
+
+    def run(self, which, block_of, index_of, count):
+        held, found = self.bufs[which]
+        experts, slots, width = found.shape[1:]
+        self.load(which, None, index_of(0), 0).start()
+
+        @pl.loop(0, count)
+        def _(j):
+            slot = j % 2
+
+            @pl.when(j + 1 < count)
+            def _():
+                self.load(which, None, index_of(j + 1), 1 - slot).start()
+
+            @pl.when(j >= 2)
+            def _():
+                self.store(which, block_of(j - 2), slot).wait()
+
+            self.load(which, None, index_of(j), slot).wait()
+            pick = pick_matrix(self.rank_ref[block_of(j)], slots)
+            for start, size in column_spans(width):
+                cols = pl.ds(start, size)
+                picked = jnp.dot(
+                    pick, held[slot, :, cols], preferred_element_type=jnp.float32
+                ).astype(jnp.bfloat16)
+                found[slot, :, :, cols] = picked.reshape(experts, slots, size)
+            self.store(which, block_of(j), slot).start()
+
+        for j in range(max(count - 2, 0), count):
+            self.store(which, block_of(j), j % 2).wait()
+
+    def blocks(self, at, core, hi):
+        def spot(j):
+            return j // self.n_lo, core, hi, j % self.n_lo
+
+        def block_of(j):
+            x, c, h, lo = spot(j)
+            return ((x * self.n_core + c) * self.n_hi + h) * self.n_lo + lo
+
+        self.run(0, block_of, spot, self.n_x * self.n_lo)
+
+    def others(self, t, steps):
+        total = self.n_x * self.n_core * self.n_hi * self.n_lo
+        each = -(-total // steps)
+        for step in range(steps):
+            first = min(step * each, total)
+            count = min(each, total - first)
+            if count > 0:
+
+                @pl.when(t == step)
+                def _(first=first, count=count):
+                    self.run(1, lambda j: first + j, lambda j: first + j, count)
+
+
+def dispatch_kernel(
+    counts, parts, in_ref, other_ref, rank_ref, out_ref, rows_ref, other_rows_ref, held, found,
+    other_held, other_found, in_sem, put_sem, other_in_sem, other_put_sem, *sems,
+):
+    host = Dispatch(
+        (out_ref, other_ref), (rows_ref, other_rows_ref),
+        ((held, found), (other_held, other_found)), (in_sem, other_in_sem),
+        (put_sem, other_put_sem), rank_ref, counts,
+    )
+    gather_kernel(counts, parts, True, in_ref, out_ref, *sems, host=host)
+
+
+def gather_sems(counts, parts):
+    n_hi, n_lo, n_x, n_core = counts
+    units = n_hi * parts
+    peers = max(n_x, n_lo, 2) - 1
+    ahead = max(n_hi - 1, 1)
+    sizes = [(ahead, parts)] * 2 + [(units, peers)] * 4 + [(units,)] * 2
+    return [pltpu.SemaphoreType.DMA] + [pltpu.SemaphoreType.DMA(size) for size in sizes]
+
+
+def gather_and_dispatch(own, other_all, rank, slots, sp_count, fs_count, ident, name):
+    counts = mesh_counts(sp_count, fs_count)
+    n_hi, n_lo, n_x, n_core = counts
+    rows, width = own.shape
+    other_width = other_all.shape[1]
+    blocks, experts, _ = rank.shape
+    parts = 4 if rows % 64 == 0 else 2
+    b16 = jnp.bfloat16
+    anywhere = pl.BlockSpec(memory_space=pl.ANY)
+    scratch = [
+        pltpu.VMEM((2, rows, width), b16),
+        pltpu.VMEM((2, experts, slots, width), b16),
+        pltpu.VMEM((2, rows, other_width), b16),
+        pltpu.VMEM((2, experts, slots, other_width), b16),
+    ] + [pltpu.SemaphoreType.DMA((2,))] * 4
+    flops = 2 * blocks * experts * slots * rows * (width + other_width)
+    _, picked, other_picked = pl.pallas_call(
+        functools.partial(dispatch_kernel, counts, parts),
+        in_specs=[anywhere, anywhere, pl.BlockSpec(memory_space=pltpu.VMEM)],
+        out_specs=[anywhere] * 3,
+        out_shape=[
+            jax.ShapeDtypeStruct((n_x, n_core, n_hi, n_lo, rows, width), b16),
+            jax.ShapeDtypeStruct((experts, blocks, slots, width), b16),
+            jax.ShapeDtypeStruct((experts, blocks, slots, other_width), b16),
+        ],
+        scratch_shapes=scratch + gather_sems(counts, parts),
+        compiler_params=pltpu.CompilerParams(
+            collective_id=ident, has_side_effects=True, vmem_limit_bytes=48 * 2**20
+        ),
+        cost_estimate=pl.CostEstimate(
+            flops=flops, bytes_accessed=8 * blocks * rows * width, transcendentals=0
+        ),
+        name=name,
+    )(own, other_all.reshape(blocks, rows, other_width), rank)
+    return picked.reshape(experts, -1, width), other_picked.reshape(experts, -1, other_width)
+
+
 def gather_rows(own, counts, fsdp_too, parts, ident, name):
     n_hi, n_lo, n_x, n_core = counts
     rows, width = own.shape
-    units = n_hi * parts
-    peers = max(n_x, n_lo, 2) - 1
-    ahead = max(n_hi - 1, 1)
-    scratch = [
-        pltpu.SemaphoreType.DMA,
-        pltpu.SemaphoreType.DMA((ahead, parts)),
-        pltpu.SemaphoreType.DMA((ahead, parts)),
-        pltpu.SemaphoreType.DMA((units, peers)),
-        pltpu.SemaphoreType.DMA((units, peers)),
-        pltpu.SemaphoreType.DMA((units, peers)),
-        pltpu.SemaphoreType.DMA((units, peers)),
-        pltpu.SemaphoreType.DMA((units,)),
-        pltpu.SemaphoreType.DMA((units,)),
-    ]
     total = rows * n_hi * n_lo * n_x * n_core
     out = pl.pallas_call(
         functools.partial(gather_kernel, counts, parts, fsdp_too),
         in_specs=[pl.BlockSpec(memory_space=pl.ANY)],
         out_specs=pl.BlockSpec(memory_space=pl.ANY),
         out_shape=jax.ShapeDtypeStruct((n_x, n_core, n_hi, n_lo, rows, width), own.dtype),
-        scratch_shapes=scratch,
+        scratch_shapes=gather_sems(counts, parts),
         compiler_params=pltpu.CompilerParams(collective_id=ident, has_side_effects=True),
         cost_estimate=pl.CostEstimate(
             flops=0, bytes_accessed=4 * total * width, transcendentals=0
@@ -1034,12 +1056,31 @@
     counts = mesh_counts(sp_count, fs_count)
     width = partial.shape[1]
     parts = 4 if rows % 64 == 0 else 2
-    if 1.4 * partial.size * 2 > 52 * 2**20 or rows % (parts * 16):
+    room = scatter_bytes(counts, parts, rows, width)
+    room += 8 * counts[1] * counts[2] * rows // parts * width
+    if room > VMEM_ROOM or rows % (parts * 16):
         part = lax.psum_scatter(partial, "fsdp", scatter_dimension=0, tiled=True)
         return lax.psum_scatter(part, "sp", scatter_dimension=0, tiled=True).astype(jnp.float32)
     n_hi, n_lo, n_x, n_core = counts
     shaped = partial.reshape(n_x, n_core, n_hi, n_lo, rows, width)
     return scatter_sum(shaped, counts, True, parts, jnp.float32, ident, name)
+
+
+def combine_and_scatter(rows, rank, slots, sp_count, fs_count, ident, name):
+    blocks, experts, block = rank.shape
+    counts = mesh_counts(sp_count, fs_count)
+    n_hi, n_lo, n_x, n_core = counts
+    width = rows.shape[-1]
+    parts = 4 if block % 64 == 0 else 2
+    room = scatter_bytes(counts, parts, block, width)
+    room += 4 * (n_x * n_core * n_lo * block + experts * slots) * width
+    if n_core == 2 and room <= VMEM_ROOM and block % (parts * 16) == 0:
+        return combine_sum(rows, rank, counts, parts, slots, ident, name)
+    shaped = rows.reshape(experts, blocks, slots, -1)
+    pick = (rank[:, :, None, :] == jnp.arange(slots)[None, None, :, None]).astype(jnp.bfloat16)
+    partial = jnp.einsum("best,ebsw->btw", pick, shaped, preferred_element_type=jnp.float32)
+    partial = partial.astype(jnp.bfloat16).reshape(blocks * block, -1)
+    return scatter_over_all(partial, block, sp_count, fs_count, ident, name)
 
 
 def scatter_over_sp(partial, rows, sp_count, ident, name):
@@ -1111,8 +1152,8 @@
     out_mat = lax.all_gather(w_out, "fsdp", axis=0, tiled=True)
     router_mat = lax.all_gather(w_router, "fsdp", axis=0, tiled=True)
     cot_all = lax.all_gather(cotangent[0], ("fsdp", "sp"), axis=0, tiled=True)
-    routing = route_plan(expert_ids[0], sp_count, fs_count)
-    cot_rows, _ = dispatch_rows(cot_all, routing, None)
+    rank, live = route_plan(expert_ids[0], sp_count, fs_count)
+    slots = 2 * tok_rows * TOPK // EXPERTS
 
     attn_normed, attn_pull = jax.vjp(rms_scale, hidden_in, gain_attn)
     attn_in = gather_over_sp(attn_normed.astype(jnp.bfloat16), sp_count, 1, "gather_attn_in")
@@ -1139,27 +1180,19 @@
     ffn_in = ffn_normed.astype(jnp.bfloat16)
     logits = jnp.dot(ffn_in, router_mat, preferred_element_type=jnp.float32)
     router = jax.nn.softmax(logits, axis=-1)
-    ffn_all = gather_over_all(ffn_in, sp_count, fs_count, 2, "gather_ffn_in")
-    router_all = jax.nn.softmax(
-        jnp.dot(ffn_all, router_mat, preferred_element_type=jnp.float32), axis=-1
-    )
-    gate_rows = (
-        lax.dynamic_slice_in_dim(router_all, first_expert, expert_local, axis=1)
-        .reshape(-1, BLOCK, expert_local)
-        .transpose(0, 2, 1)
-    )
-    ffn_rows, gate_slots = dispatch_rows(ffn_all, routing, gate_rows)
-    out_rows, in_grad_rows, grad_gate, grad_up, grad_down = run_experts(
-        ffn_rows, cot_rows, gate_slots, w_gate, w_up, w_down, routing[3], first_expert[None]
-    )
-    in_grad_sum = scatter_over_all(
-        combine_rows(in_grad_rows, routing, "combine_grads"),
-        tok_rows, sp_count, fs_count, 3, "scatter_grads",
-    )
-    moe_sum = scatter_over_all(
-        combine_rows(out_rows, routing, "combine_outputs"),
-        tok_rows, sp_count, fs_count, 4, "scatter_outputs",
-    )
+    router_high = router.astype(jnp.bfloat16)
+    router_low = (router - router_high.astype(jnp.float32)).astype(jnp.bfloat16)
+    ffn_rows, cot_rows = gather_and_dispatch(
+        jnp.concatenate([ffn_in, router_high, router_low], axis=1),
+        cot_all, rank, slots, sp_count, fs_count, 2, "gather_ffn_in",
+    )
+    in_grad_rows, out_rows, grad_gate, grad_up, grad_down = run_experts(
+        ffn_rows, cot_rows, w_gate, w_up, w_down, live, first_expert[None]
+    )
+    in_grad_sum = combine_and_scatter(
+        in_grad_rows, rank, slots, sp_count, fs_count, 3, "scatter_grads"
+    )
+    moe_sum = combine_and_scatter(out_rows, rank, slots, sp_count, fs_count, 4, "scatter_outputs")
     mixed = (after_attn + moe_sum).astype(jnp.bfloat16)
     upstream = cotangent[0].astype(jnp.float32)
     ffn_in_grad = in_grad_sum[:, :width]

time: 1610 us -> 1490 us (0.925)
  Pallas kernels: 1230 us -> 1140 us
  matrix products: 70.2 us -> 49 us
    pallas_call x4 -> x3, Pallas kernels: 172 us -> 515 us  [the longest x2 349 us: combine_sum(): pl.pallas_call(functools.partial(combine_scatter_kernel, counts, parts),...]
    pallas_call x4 -> x2, Pallas kernels: 470 us -> 172 us  [scatter_sum(): pl.pallas_call(functools.partial(scatter_kernel, counts, parts, fsdp_too)...]
    pallas_call x3 -> x2, Pallas kernels: 330 us -> 156 us  [gather_rows(): pl.pallas_call(functools.partial(gather_kernel, counts, parts, fsdp_too),...]
    pallas_call x1, Pallas kernels: 154 us -> 200 us  [run_experts(): pl.pallas_call(expert_kernel, grid_spec=pltpu.PrefetchScalarGridSpec(num_...]
    dot_general x3 -> x1, matrix products: 16.4 us -> 0.13 us  [route_plan(): jnp.dot(before, running[:, -1].astype(jnp.float32), precision=lax.Precisi...]
  transfers between devices with their start and end apart: 8 -> 8, of which waited for: 3 -> 4; matrix products, arithmetic and copies ran while one was open for 9% -> 8% of each run, Pallas kernels for 38% -> 27%
where the time goes in v4:
time: 1490 us; the launch traced here: 1480 us
  Pallas kernels  1140 us (77%)
  waiting for transfers between devices  103 us (7%)
  other arithmetic  83.7 us (6%)
  local copies, waits for them, and re-layouts  63.2 us (4%)
  matrix products  49 us (3%)
  between operations  15.8 us (1%)
    pallas_call x2, Pallas kernels, combine_sum(): pl.pallas_call(functools.partial(combine_scatter_kernel, counts, parts),...  349 us
    pallas_call x1, Pallas kernels, run_experts(): pl.pallas_call(expert_kernel, grid_spec=pltpu.PrefetchScalarGridSpec(num_...  200 us
    pallas_call x2, Pallas kernels, scatter_sum(): pl.pallas_call(functools.partial(scatter_kernel, counts, parts, fsdp_too)...  172 us
    pallas_call x1, Pallas kernels, gather_and_dispatch(): pl.pallas_call(functools.partial(dispatch_kernel, counts, parts), in_spec...  165 us
    pallas_call x2, Pallas kernels, gather_rows(): pl.pallas_call(functools.partial(gather_kernel, counts, parts, fsdp_too),...  156 us
    pallas_call x3, Pallas kernels, small_sum(): pl.pallas_call(functools.partial(small_sum_kernel, (sp_count, fs_count)),...  53.6 us
    all_gather x1, waiting for transfers between devices, local(): qkv_every = lax.all_gather(qkv_sums, 'sp', axis=0)  36.1 us
    all_to_all x1, waiting for transfers between devices, local(): lax.all_to_all(attended_heads, 'sp', split_axis=0, concat_axis=1, tiled=T...  32.4 us
  transfers between devices with their start and end apart: 8, of which 4 were waited for; matrix products, arithmetic and copies ran while one was open for 8% of the time, Pallas kernels for 27%

profile of v4, /device:TPU:0, one launch (start us, length us, event | category | flops | bytes accessed | tf_op | source)
XLA Modules:
  0.0 1480.8 jit_solution(11499023674464355560)
XLA Ops:
  8.2 1.1 constant_dynamic-slice_fusion.1
  11.9 6.2 all_gather.24
  19.0 1.3 fusion.2.in_ref
  20.3 138.1 %gather_attn_in.1 = bf16[1,1,4,2,256,2048]{5,4,3,2,1,0:T(8,128)(2,1)} custom-call(bf16[256,2048]{1,0:T(8,128)(2,1)} %fusion.2.in_ref), custom_call_target="tpu_custom_call" | custom-call | bytes 16777216 | tf_op jit(solution)/shard_map/gather_attn_in/pallas_call | solution.py:864
  159.5 18.1 %gather_ids.1 = bf16[2,2,4,2,32,128]{5,4,3,2,1,0:T(8,128)(2,1)} custom-call(bf16[32,128]{1,0:T(8,128)(2,1)} %scatter.4.in_ref), custom_call_target="tpu_custom_call" | custom-call | bytes 524288 | tf_op jit(solution)/shard_map/gather_ids/pallas_call | solution.py:864
  179.1 4.9 fusion.28
  184.0 10.0 fusion.34
  194.7 2.0 copy-done.10
  197.4 8.3 sum_squares.1
  207.1 5.0 multiply_multiply_fusion
  212.1 3.3 reshape.385
  215.3 3.2 reshape.384
  218.6 4.5 slice_negate_fusion.2
  223.1 2.3 slice_negate_fusion.3
  225.5 5.6 maximum_multiply_fusion.1
  233.6 19.1 %attend.1 = bf16[2048,256]{1,0:T(8,128)(2,1)S(1)} custom-call(s32[4]{0:T(128)S(1)} %bitcast.145, bf16[2048,256]{1,0:T(8,128)(2,1)S(1)} %get-tuple-element.144.q_ref, bf16[2048,256]{1,0:T(8,128)(2,1)S(1)} %get-tuple-element.143.k_ref, bf16[2048,256]{1,0:T(8,128)(2,1)S(1)} %slice.198.v_ref), custom_call_target="tpu_custom_call" | custom-call | flops 2684354560 | bytes 4194304 | tf_op jit(solution)/shard_map/attend/pallas_call | solution.py:1039
  252.7 1.3 copy.94
  254.0 5.9 all-to-all-start
  259.9 3.6 reshape.405
  263.6 2.8 copy.96
  269.4 5.8 all_gather.27
  275.3 32.4 %all-to-all-done = bf16[8,256,256]{1,2,0:T(8,128)(2,1)S(1)} async-done(((bf16[8,256,256]{1,2,0:T(8,128)(2,1)}), bf16[8,256,256]{1,2,0:T(8,128)(2,1)S(1)}, u32[]{:S(2)}, u32[]{:S(2)}) %all-to-all-start) | async-done | bytes 1048608 | tf_op jit(solution)/shard_map/all_to_all | solution.py:1175
  307.7 6.2 multiply_reduce_fusion.6
  316.1 1.1 concatenate.44.in_ref
  317.2 6.9 all-gather.14.cloned.1.call-done
  324.1 165.3 %gather_ffn_in.1 = (bf16[2,2,4,2,256,2176]{5,4,3,2,1,0:T(8,128)(2,1)}, bf16[8,32,64,2176]{3,2,1,0:T(8,128)(2,1)}, bf16[8,32,64,2048]{3,2,1,0:T(8,128)(2,1)}) custom-call(bf16[256,2176]{1,0:T(8,128)(2,1)S(1)} %concatenate.44.in_ref, bf16[32,256,2048]{2,1,0:T(8,128)(2,1)} %bitcast.197, s32[32,8,256]{2,1,0:T(8,128)S(1)} %select_bitcast_fusion.rank_ref), custom_call_target="tpu_custom_call" | custom-call | flops 35433480192 | bytes 142606336 | tf_op jit(solution)/shard_map/gather_ffn_in/pallas_call | solution.py:839
  489.4 199.9 %experts.1 = (bf16[8,2048,2176]{2,1,0:T(8,128)(2,1)}, bf16[8,2048,2048]{2,1,0:T(8,128)(2,1)}, f32[8,2048,256]{2,1,0:T(8,128)}, f32[8,2048,256]{2,1,0:T(8,128)}, f32[8,2048,256]{2,1,0:T(8,128)}) custom-call(s32[64]{0:T(128)} %reshape.407.live, s32[1]{0:T(128)} %bitcast.21.first, ...), custom_call_target="tpu_custom_call", output_to_operand_aliasing={{0}: (2, {}), {1}: (3, {})} | custom-call | flops 154618822656 | bytes 268435456 | tf_op jit(solution)/shard_map/experts/pallas_call | solution.py:160
  689.3 189.8 %scatter_grads.1 = f32[256,2176]{1,0:T(8,128)} custom-call(bf16[8,32,64,2176]{3,2,1,0:T(8,128)(2,1)} %bitcast.30.rows_ref, s32[32,8,256]{2,1,0:T(8,128)} %copy-done), custom_call_target="tpu_custom_call" | custom-call | flops 18253611008 | bytes 71303168 | tf_op jit(solution)/shard_map/scatter_grads/pallas_call | solution.py:554
  879.1 1.1 multiply_reduce_fusion.9
  880.3 159.5 %scatter_outputs.1 = f32[256,2048]{1,0:T(8,128)} custom-call(bf16[8,32,64,2048]{3,2,1,0:T(8,128)(2,1)} %bitcast.27.rows_ref, s32[32,8,256]{2,1,0:T(8,128)} %copy-done), custom_call_target="tpu_custom_call" | custom-call | flops 17179869184 | bytes 67108864 | tf_op jit(solution)/shard_map/scatter_outputs/pallas_call | solution.py:554
  1039.9 3.3 multiply_reduce_fusion
  1043.4 1.8 fusion.4
  1045.2 2.7 copy-done.22
  1047.9 2.4 convolution_convert_fusion.3
  1051.3 3.7 all-to-all-start.1
  1055.2 26.0 %all-to-all-done.1 = bf16[256,8,256]{2,0,1:T(8,128)(2,1)S(1)} async-done(((bf16[256,8,256]{2,0,1:T(8,128)(2,1)}), bf16[256,8,256]{2,0,1:T(8,128)(2,1)S(1)}, u32[]{:S(2)}, u32[]{:S(2)}) %all-to-all-start.1) | async-done | bytes 1048608 | tf_op jit(solution)/shard_map/all_to_all | solution.py:1213
  1082.1 1.2 copy-done.4
  1083.3 29.1 %attend_back.1 = (bf16[2048,256]{1,0:T(8,128)(2,1)S(1)}, bf16[2048,256]{1,0:T(8,128)(2,1)S(1)}, bf16[2048,256]{1,0:T(8,128)(2,1)S(1)}) custom-call(s32[4]{0:T(128)S(1)} %bitcast.146, bf16[2048,256]{1,0:T(8,128)(2,1)S(1)} %copy-done.4, bf16[2048,256]{1,0:T(8,128)(2,1)S(1)} %copy-done.2, bf16[2048,256]{1,0:T(8,128)(2,1)} %copy-done.5, bf16[2048,256]{1,0:T(8,128)(2,1)} %bitcast.168), custom_call_target="tpu_custom_call" | custom-call | flops 8053063680 | bytes 4194304 | tf_op jit(solution)/shard_map/attend_back/pallas_call | solution.py:1044
  1113.4 2.0 reshape.396
  1115.4 5.8 slice_negate_fusion
  1121.3 2.0 reshape.395
  1123.3 4.5 slice_negate_fusion.1
  1127.9 5.6 maximum_multiply_fusion.3
  1133.6 3.2 multiply_reduce_fusion.2
  1137.4 7.9 sum_products.1
  1146.1 5.0 subtract_convert_fusion.1
  1152.4 10.7 convolution_convert_fusion.2
  1163.2 1.8 convolution_convert_fusion.4
  1165.3 2.4 convolution_convert_fusion
  1167.7 8.9 maximum_maximum_fusion
  1176.6 11.9 copy.106
  1188.5 50.6 %scatter_out_rows.1 = f32[64,2176]{1,0:T(8,128)} custom-call(bf16[2,2,4,2,64,2176]{5,4,3,2,1,0:T(8,128)(2,1)} %bitcast.149), custom_call_target="tpu_custom_call" | custom-call | flops 4456448 | bytes 8912896 | tf_op jit(solution)/shard_map/scatter_out_rows/pallas_call | solution.py:583
  1239.2 1.8 convert_element_type.198
  1241.6 11.4 convolution_convert_fusion.1
  1253.0 120.9 %scatter_attn_in.1 = f32[256,2048]{1,0:T(8,128)} custom-call(bf16[1,1,4,2,256,2048]{5,4,3,2,1,0:T(8,128)(2,1)} %bitcast.154), custom_call_target="tpu_custom_call" | custom-call | flops 4194304 | bytes 8388608 | tf_op jit(solution)/shard_map/scatter_attn_in/pallas_call | solution.py:583
  1374.0 2.3 fusion.3
  1377.0 37.4 %sum_gains.1 = f32[64,128]{1,0:T(8,128)} custom-call(f32[64,128]{1,0:T(8,128)} %reshape.401.part_ref), custom_call_target="tpu_custom_call" | custom-call | tf_op jit(solution)/shard_map/sum_gains/pallas_call | solution.py:926
  1415.8 3.5 fusion.6
  1421.0 4.1 slice_convert_fusion
  1425.1 36.1 %all-gather.16.cloned.1.call-done = bf16[4096,768]{1,0:T(8,128)(2,1)} async-done(((bf16[512,768]{1,0:T(8,128)(2,1)}), bf16[4096,768]{1,0:T(8,128)(2,1)}) %all-gather.16.cloned.1.call-update) | async-done | bytes 6291472 | tf_op jit(solution)/shard_map/all_gather | solution.py:1257
  1461.2 4.4 convert_bitcast_fusion
  1465.6 2.6 copy.111
  1468.2 2.6 copy.112
  1470.9 2.6 copy.113
  (229 shorter events, 28.0 us)
Async XLA Ops:
  7.2 176.8 %all-gather.8.cloned.1.call-start = ((), (), s32[]{:S(2)}) async-start(), calls=%async_computation.3 | async-start | bytes 3932160 | tf_op jit(solution)/shard_map/all_gather | solution.py:1151
  10.2 7.8 copy-start.11
  10.3 297.4 %all-gather.10.cloned.1.call-start = ((), (), s32[]{:S(2)}) async-start(), calls=%async_computation.4 | async-start | bytes 10485760 | tf_op jit(solution)/shard_map/all_gather | solution.py:1152
  11.0 313.0 %all-gather.14.cloned.1.call-start = ((), (), s32[]{:S(2)}) async-start(), calls=%async_computation.7 | async-start | bytes 34603008 | tf_op jit(solution)/shard_map/all_gather | solution.py:1154
  18.3 140.0 %copy-start.62 = (f32[256]{0:T(256)}, f32[256]{0:T(256)S(1)}, u32[]{:S(2)}) copy-start(f32[256]{0:T(256)S(1)} %fusion.7) | copy-start | bytes 3076
  18.4 140.0 %copy-start.52 = (f32[256]{0:T(256)}, f32[256]{0:T(256)S(1)}, u32[]{:S(2)}) copy-start(f32[256]{0:T(256)S(1)} %fusion.23) | copy-start | bytes 3076
  18.4 295.5 %copy-start.47 = (f32[1,2048]{1,0:T(1,128)}, f32[1,2048]{1,0:T(1,128)S(1)}, u32[]{:S(2)}) copy-start(f32[1,2048]{1,0:T(1,128)S(1)} %get-tuple-element.166) | copy-start | bytes 24580
  20.3 138.1 %copy-start.71 = (s32[1,4]{1,0:T(1,128)S(1)}, s32[1,4]{1,0:T(1,128)}, u32[]{:S(2)}) copy-start(s32[1,4]{1,0:T(1,128)} %param.19) | copy-start | bytes 52
  20.3 138.3 %copy-start.66 = (s32[1,256,8]{1,2,0:T(8,128)S(1)}, s32[1,256,8]{1,2,0:T(8,128)}, u32[]{:S(2)}) copy-start(s32[1,256,8]{1,2,0:T(8,128)} %param.20) | copy-start | bytes 24580
  158.6 75.0 %copy-start.6 = (s32[4,1]{0,1:T(1,128)}, s32[4,1]{0,1:T(1,128)S(1)}, u32[]{:S(2)}) copy-start(s32[4,1]{0,1:T(1,128)S(1)} %reduce-window.9) | copy-start | bytes 52
  178.8 28.3 %copy-start.54 = (f32[1,256]{1,0:T(1,128)}, f32[1,256]{1,0:T(1,128)S(1)}, u32[]{:S(2)}) copy-start(f32[1,256]{1,0:T(1,128)S(1)} %get-tuple-element.170) | copy-start | bytes 3076
  178.8 28.3 %copy-start.56 = (f32[1,256]{1,0:T(1,128)}, f32[1,256]{1,0:T(1,128)S(1)}, u32[]{:S(2)}) copy-start(f32[1,256]{1,0:T(1,128)S(1)} %get-tuple-element.171) | copy-start | bytes 3076
  194.0 2.8 copy-start.10
  194.1 39.5 %copy-start.5 = (bf16[2048,256]{1,0:T(8,128)(2,1)}, bf16[2048,256]{1,0:T(8,128)(2,1)S(1)}, u32[]{:S(2)}) copy-start(bf16[2048,256]{1,0:T(8,128)(2,1)S(1)} %slice.198.v_ref) | copy-start | bytes 3145732
  207.0 5.0 copy-start.43
  207.0 5.0 copy-start.45
  218.6 4.5 copy-start.21
  223.1 2.4 copy-start.31
  225.5 6.6 copy-start.20
  233.5 19.2 %copy-start.1 = (bf16[2048,256]{1,0:T(8,128)(2,1)}, bf16[2048,256]{1,0:T(8,128)(2,1)S(1)}, u32[]{:S(2)}) copy-start(bf16[2048,256]{1,0:T(8,128)(2,1)S(1)} %get-tuple-element.143.k_ref) | copy-start | bytes 3145732
  233.5 19.2 %copy-start.3 = (bf16[2048,256]{1,0:T(8,128)(2,1)}, bf16[2048,256]{1,0:T(8,128)(2,1)S(1)}, u32[]{:S(2)}) copy-start(bf16[2048,256]{1,0:T(8,128)(2,1)S(1)} %get-tuple-element.144.q_ref) | copy-start | bytes 3145732
  254.0 53.6 %all-to-all-start = ((bf16[8,256,256]{1,2,0:T(8,128)(2,1)}), bf16[8,256,256]{1,2,0:T(8,128)(2,1)S(1)}, u32[]{:S(2)}, u32[]{:S(2)}) async-start(bf16[8,256,256]{1,2,0:T(8,128)(2,1)} %copy.94), calls=%async_computation | async-start | bytes 2097152 | tf_op jit(solution)/shard_map/all_to_all | solution.py:1175
  263.6 5.8 copy-start.49
  275.1 39.0 %copy-start.37 = (bf16[2048,64]{0,1:T(8,128)(2,1)}, bf16[2048,64]{0,1:T(8,128)(2,1)S(1)}, u32[]{:S(2)}) copy-start(bf16[2048,64]{0,1:T(8,128)(2,1)S(1)} %all_gather.27) | copy-start | bytes 786436
  275.3 48.8 %copy-start = (s32[32,8,256]{2,1,0:T(8,128)}, s32[32,8,256]{2,1,0:T(8,128)S(1)}, u32[]{:S(2)}) copy-start(s32[32,8,256]{2,1,0:T(8,128)S(1)} %select_bitcast_fusion.rank_ref) | copy-start | bytes 786436
  307.6 6.2 copy-start.23
  314.2 3.0 copy-start.25
  315.2 174.2 %copy-start.50 = (f32[256]{0:T(256)}, f32[256]{0:T(256)S(1)}, u32[]{:S(2)}) copy-start(f32[256]{0:T(256)S(1)} %get-tuple-element.174) | copy-start | bytes 3076
  689.3 189.8 %copy-start.33 = (f32[256,64]{1,0:T(8,128)S(1)}, f32[256,64]{1,0:T(8,128)}, u32[]{:S(2)}) copy-start(f32[256,64]{1,0:T(8,128)} %copy-done.32) | copy-start | bytes 196612
  689.3 189.8 %copy-start.51 = (f32[256]{0:T(256)S(1)}, f32[256]{0:T(256)}, u32[]{:S(2)}) copy-start(f32[256]{0:T(256)} %copy-done.50) | copy-start | bytes 3076
  689.3 189.8 %copy-start.59 = (f32[256]{0:T(256)S(1)}, f32[256]{0:T(256)}, u32[]{:S(2)}) copy-start(f32[256]{0:T(256)} %copy-done.58) | copy-start | bytes 3076
  880.2 159.6 %copy-start.38 = (bf16[2048,64]{0,1:T(8,128)(2,1)S(1)}, bf16[2048,64]{0,1:T(8,128)(2,1)}, u32[]{:S(2)}) copy-start(bf16[2048,64]{0,1:T(8,128)(2,1)} %copy-done.37) | copy-start | bytes 786436
  880.2 159.6 %copy-start.48 = (f32[1,2048]{1,0:T(1,128)S(1)}, f32[1,2048]{1,0:T(1,128)}, u32[]{:S(2)}) copy-start(f32[1,2048]{1,0:T(1,128)} %copy-done.47) | copy-start | bytes 24580
  880.3 159.6 %copy-start.61 = (f32[256]{0:T(256)S(1)}, f32[256]{0:T(256)}, u32[]{:S(2)}) copy-start(f32[256]{0:T(256)} %copy-done.60) | copy-start | bytes 3076
  880.3 162.9 %copy-start.29 = (bf16[1,256,2048]{2,1,0:T(8,128)(2,1)S(1)}, bf16[1,256,2048]{2,1,0:T(8,128)(2,1)}, u32[]{:S(2)}) copy-start(bf16[1,256,2048]{2,1,0:T(8,128)(2,1)} %param.33) | copy-start | bytes 3145732
  1039.8 3.3 copy-start.65
  1039.8 3.3 copy-start.16
  1039.9 3.5 copy-start.26
  1043.4 4.5 copy-start.22
  1045.2 5.1 copy-start.13
  1050.3 4.9 copy-start.40
  1050.3 31.8 %copy-start.2 = (bf16[2048,256]{1,0:T(8,128)(2,1)S(1)}, bf16[2048,256]{1,0:T(8,128)(2,1)}, u32[]{:S(2)}) copy-start(bf16[2048,256]{1,0:T(8,128)(2,1)} %copy-done.1) | copy-start | bytes 3145732
  1050.3 31.8 %copy-start.7 = (s32[4,1]{0,1:T(1,128)S(1)}, s32[4,1]{0,1:T(1,128)}, u32[]{:S(2)}) copy-start(s32[4,1]{0,1:T(1,128)} %copy-done.6) | copy-start | bytes 52
  1051.3 29.8 %all-to-all-start.1 = ((bf16[256,8,256]{2,0,1:T(8,128)(2,1)}), bf16[256,8,256]{2,0,1:T(8,128)(2,1)S(1)}, u32[]{:S(2)}, u32[]{:S(2)}) async-start(bf16[256,8,256]{2,0,1:T(8,128)(2,1)} %bitcast.142), calls=%async_computation.1 | async-start | bytes 2097152 | tf_op jit(solution)/shard_map/all_to_all | solution.py:1213
  1055.1 186.0 %reduce-scatter.2.cloned.1.call-start = ((), (), s32[]{:S(2)}) async-start(), calls=%async_computation.5 | async-start | bytes 3932160 | tf_op jit(solution)/shard_map/reduce_scatter | solution.py:1254
  1123.2 4.6 copy-start.27
  1123.2 4.6 copy-start.28
  1123.3 4.6 copy-start.30
  1127.8 5.7 slice-start
  1127.8 5.7 slice-start.1
  1127.8 5.7 copy-start.18
  1127.9 5.7 copy-start.44
  1127.9 5.7 copy-start.46
  1127.9 5.7 copy-start.55
  1127.9 5.7 copy-start.57
  1146.1 6.3 copy-start.9
  1163.1 2.0 copy-start.14
  1163.1 256.2 %all-gather.12.cloned.1.call-start = ((), (), s32[]{:S(2)}) async-start(), calls=%async_computation.6 | async-start | bytes 2506752 | tf_op jit(solution)/shard_map/all_gather | solution.py:1258
  1163.1 2.1 copy-start.24
  1241.0 220.2 %all-gather.16.cloned.1.call-start = ((), (), s32[]{:S(2)}) async-start(), calls=%async_computation.8 | async-start | bytes 7077888 | tf_op jit(solution)/shard_map/all_gather | solution.py:1257
  1253.0 121.0 %copy-start.12 = (bf16[1,256,2048]{2,1,0:T(8,128)(2,1)S(1)}, bf16[1,256,2048]{2,1,0:T(8,128)(2,1)}, u32[]{:S(2)}) copy-start(bf16[1,256,2048]{2,1,0:T(8,128)(2,1)} %param.18) | copy-start | bytes 3145732
  1253.0 121.0 %copy-start.42 = (f32[1,2048]{1,0:T(1,128)S(1)}, f32[1,2048]{1,0:T(1,128)}, u32[]{:S(2)}) copy-start(f32[1,2048]{1,0:T(1,128)} %copy-done.41) | copy-start | bytes 24580
  1253.0 121.0 %copy-start.53 = (f32[256]{0:T(256)S(1)}, f32[256]{0:T(256)}, u32[]{:S(2)}) copy-start(f32[256]{0:T(256)} %copy-done.52) | copy-start | bytes 3076
  1373.9 41.9 %copy-start.63 = (f32[256]{0:T(256)S(1)}, f32[256]{0:T(256)}, u32[]{:S(2)}) copy-start(f32[256]{0:T(256)} %copy-done.62) | copy-start | bytes 3076
  (18 other events, 21.1 us)
Sparse Core Ops, SparseCore 0:
  10.4 31.2 all-gather.7
  43.2 58.2 all-gather.9
  104.5 219.4 all-gather.13
  1163.2 43.1 reduce-scatter.1
  1241.1 90.5 all-gather.11
  1334.0 127.1 all-gather.15

commit v5 on v4

--- a/solution.py
+++ b/solution.py
@@ -36,18 +36,12 @@
     return (jnp.cos(phase_all)[:, None, :], jnp.sin(phase_all)[:, None, :])
 
 
-TILE = 256
+TILE = 1024
 LANES = 128
 
 
-def route_plan(own_ids, sp_count, fs_count):
+def route_plan(ids, block, sp_count):
     local_experts = EXPERTS // sp_count
-    block = own_ids.shape[0]
-    per_device = own_ids.size
-    packed = jnp.zeros((32, LANES), jnp.bfloat16)
-    packed = packed.at[: per_device // LANES].set(own_ids.astype(jnp.bfloat16).reshape(-1, LANES))
-    packed = gather_over_all(packed, sp_count, fs_count, 10, "gather_ids")
-    ids = packed.reshape(-1, 32 * LANES)[:, :per_device].reshape(-1, TOPK).astype(jnp.int32)
     blocks = ids.shape[0] // block
     capacity = 5 * ids.shape[0] * TOPK // (4 * EXPERTS)
     first = lax.axis_index("sp") * local_experts
@@ -89,28 +83,21 @@
 
 
 def expert_kernel(
-    live, first, x_ref, c_ref, gate_ref, up_ref, down_ref, dx_ref, y_ref, gg_ref, gu_ref,
-    gd_ref, acc_g, acc_u, acc_d,
+    live, first, x_ref, c_ref, gate_ref, up_ref, down_ref, dx_ref, y_ref, dgate_ref, dup_ref,
+    act_ref,
 ):
     e = pl.program_id(0)
     t = pl.program_id(1)
     width = c_ref.shape[2]
 
-    @pl.when(t == 0)
-    def _():
-        acc_g[...] = jnp.zeros_like(acc_g)
-        acc_u[...] = jnp.zeros_like(acc_u)
-        acc_d[...] = jnp.zeros_like(acc_d)
-
     @pl.when(live[e * pl.num_programs(1) + t] == 0)
     def _():
-        dx_ref[...] = jnp.zeros_like(dx_ref)
-        y_ref[...] = jnp.zeros_like(y_ref)
+        for ref in (dx_ref, y_ref, dgate_ref, dup_ref, act_ref):
+            ref[...] = jnp.zeros_like(ref)
 
     @pl.when(live[e * pl.num_programs(1) + t] > 0)
     def _():
         x = x_ref[0, :, 0:width]
-        c = c_ref[0]
         gate_mat = gate_ref[0]
         up_mat = up_ref[0]
         down_mat = down_ref[0]
@@ -120,7 +107,7 @@
         weight = jnp.sum(gates, axis=1, keepdims=True)
         gate_pre = jnp.dot(x, gate_mat, preferred_element_type=jnp.float32)
         up_pre = jnp.dot(x, up_mat, preferred_element_type=jnp.float32)
-        up_act = jnp.dot(c, down_mat, preferred_element_type=jnp.float32)
+        up_act = jnp.dot(c_ref[0], down_mat, preferred_element_type=jnp.float32)
         sig = 1.0 / (1.0 + jnp.exp(-gate_pre))
         silu = gate_pre * sig
         act = silu * up_pre
@@ -129,6 +116,9 @@
         act_grad = up_act * weight
         dgate = (act_grad * up_pre * sig * (1.0 + gate_pre * (1.0 - sig))).astype(jnp.bfloat16)
         dup = (act_grad * silu).astype(jnp.bfloat16)
+        act_ref[0] = act_low
+        dgate_ref[0] = dgate
+        dup_ref[0] = dup
         y_ref[0] = contract(act_low, down_mat, 1, 1).astype(jnp.bfloat16)
         dx_ref[0, :, 0:width] = (
             contract(dgate, gate_mat, 1, 1) + contract(dup, up_mat, 1, 1)
@@ -136,15 +126,6 @@
         dx_ref[0, :, width : width + LANES] = jnp.where(
             column == first[0] + e, gate_grad, 0.0
         ).astype(jnp.bfloat16)
-        acc_g[...] += contract(dgate, x, 0, 0)
-        acc_u[...] += contract(dup, x, 0, 0)
-        acc_d[...] += contract(act_low, c, 0, 0)
-
-    @pl.when(t == pl.num_programs(1) - 1)
-    def _():
-        gg_ref[0] = acc_g[...].T
-        gu_ref[0] = acc_u[...].T
-        gd_ref[0] = acc_d[...].T
 
 
 def run_experts(x_rows, c_rows, w_gate, w_up, w_down, live, first):
@@ -157,26 +138,26 @@
     mat = pl.BlockSpec((1, width, hidden), lambda e, t, live, first: (e, 0, 0))
     wide = pl.BlockSpec((1, TILE, width + LANES), tile_map)
     plain = pl.BlockSpec((1, TILE, width), tile_map)
+    inner = pl.BlockSpec((1, TILE, hidden), tile_map)
+    b16 = jnp.bfloat16
     return pl.pallas_call(
         expert_kernel,
         grid_spec=pltpu.PrefetchScalarGridSpec(
             num_scalar_prefetch=2,
             grid=(experts, rows // TILE),
             in_specs=[wide, plain, mat, mat, mat],
-            out_specs=[wide, plain, mat, mat, mat],
-            scratch_shapes=[pltpu.VMEM((hidden, width), jnp.float32)] * 3,
+            out_specs=[wide, plain, inner, inner, inner],
         ),
         out_shape=[
-            jax.ShapeDtypeStruct(x_rows.shape, jnp.bfloat16),
-            jax.ShapeDtypeStruct(c_rows.shape, jnp.bfloat16),
+            jax.ShapeDtypeStruct(x_rows.shape, b16),
+            jax.ShapeDtypeStruct(c_rows.shape, b16),
         ]
-        + [jax.ShapeDtypeStruct((experts, width, hidden), jnp.float32)] * 3,
-        input_output_aliases={2: 0, 3: 1},
+        + [jax.ShapeDtypeStruct((experts, rows, hidden), b16)] * 3,
         compiler_params=pltpu.CompilerParams(
             dimension_semantics=("arbitrary", "arbitrary"), vmem_limit_bytes=60 * 2**20
         ),
         cost_estimate=pl.CostEstimate(
-            flops=18 * experts * rows * width * hidden,
+            flops=12 * experts * rows * width * hidden,
             bytes_accessed=8 * experts * rows * width,
             transcendentals=experts * rows * hidden,
         ),
@@ -210,7 +191,7 @@
     def sizes(self):
         return {"core": self.n_core, "x": self.n_x, "lo": self.n_lo, "hi": self.n_hi}
 
-    def meet(self):
+    def meet(self, other=None):
         barrier = pltpu.get_barrier_semaphore()
         met = 0
         for dim, size in self.sizes().items():
@@ -219,6 +200,12 @@
                     barrier, inc=1, device_id=self.peer(dim, ahead), device_id_type=MESH
                 )
                 met += 1
+        for dim in ("x", "core") if other is not None else ():
+            for ahead in range(1, other.sizes()[dim]):
+                pl.semaphore_signal(
+                    barrier, inc=1, device_id=other.peer(dim, ahead), device_id_type=MESH
+                )
+                met += 1
         pl.semaphore_wait(barrier, met)
 
 
@@ -233,7 +220,7 @@
 
 def scatter_kernel(
     counts, parts, fsdp_too, part_ref, out_ref, own, buf, first, second, third, own_sem, s0, r0,
-    s1, r1, s2, r2, s3, r3, host=None,
+    s1, r1, s2, r2, s3, r3, host=None, side=None,
 ):
     at = Place(counts, fsdp_too)
     n_hi, n_lo, n_x, n_core = counts
@@ -431,6 +418,9 @@
                 def _():
                     each_core_copy(group, lambda c: c.start())
 
+        if side is not None:
+            side.share(t, steps + depth * lag)
+
     for g in range(pairs):
         t = (n_hi - 1) * pairs + g
         for v in range(2):
@@ -457,6 +447,149 @@
     if host is not None:
         for group in range(max(n_hi - 2, 0), n_hi):
             each_core_copy(group, lambda c: c.wait_send())
+
+
+class WeightGrads:
+    def __init__(self, rows, grads, outs, row_bufs, grad_buf, acc, stage, in_sems, out_sems):
+        self.rows, self.grads, self.outs = rows, grads, outs
+        self.row_bufs, self.grad_buf, self.acc, self.stage = row_bufs, grad_buf, acc, stage
+        self.in_sems, self.out_sems = in_sems, out_sems
+        experts, total, _ = grads[0].shape
+        self.depth = grad_buf.shape[2]
+        self.each = total // self.depth
+        self.jobs = experts * self.each
+
+    def loads(self, j, slot):
+        e = j // self.each
+        rows = pl.ds(pl.multiple_of(j % self.each * self.depth, self.depth), self.depth)
+        copies = []
+        for k in range(2):
+            width = self.row_bufs[k].shape[2]
+            copies.append(
+                pltpu.make_async_copy(
+                    self.rows[k].at[e, rows, pl.ds(0, width)], self.row_bufs[k].at[slot],
+                    self.in_sems.at[slot, k],
+                )
+            )
+        for k in range(3):
+            copies.append(
+                pltpu.make_async_copy(
+                    self.grads[k].at[e, rows], self.grad_buf.at[slot, k],
+                    self.in_sems.at[slot, 2 + k],
+                )
+            )
+        return copies
+
+    def stores(self, e):
+        return [
+            pltpu.make_async_copy(self.stage.at[k], self.outs[k].at[e], self.out_sems.at[k])
+            for k in range(3)
+        ]
+
+    def begin(self):
+        for copy in self.loads(0, 0):
+            copy.start()
+
+    def share(self, t, turns):
+        count = -(-self.jobs // turns)
+
+        @pl.loop(0, count)
+        def _(i):
+            j = t * count + i
+
+            @pl.when(j < self.jobs)
+            def _():
+                self.job(j)
+
+    def job(self, j):
+        slot = j % 2
+
+        @pl.when(j + 1 < self.jobs)
+        def _():
+            for copy in self.loads(j + 1, 1 - slot):
+                copy.start()
+
+        for copy in self.loads(j, slot):
+            copy.wait()
+
+        @pl.when(j % self.each == 0)
+        def _():
+            self.acc[...] = jnp.zeros_like(self.acc)
+
+        for k in range(3):
+            rows = self.row_bufs[0 if k < 2 else 1]
+            for start, size in column_spans(rows.shape[2]):
+                cols = pl.ds(start, size)
+                self.acc[k, :, cols] += contract(
+                    self.grad_buf[slot, k], rows[slot, :, cols], 0, 0
+                )
+
+        @pl.when(j % self.each == self.each - 1)
+        def _():
+            e = j // self.each
+
+            @pl.when(e > 0)
+            def _():
+                for copy in self.stores(e - 1):
+                    copy.wait()
+
+            for k in range(3):
+                self.stage[k] = self.acc[k].T
+            for copy in self.stores(e):
+                copy.start()
+
+    def finish(self):
+        for copy in self.stores(self.jobs // self.each - 1):
+            copy.wait()
+
+
+def scatter_grads_kernel(
+    counts, parts, part_ref, x_ref, c_ref, dgate_ref, dup_ref, act_ref, out_ref, gg_ref, gu_ref,
+    gd_ref, x_buf, c_buf, grad_buf, acc, stage, in_sems, out_sems, own, *scratch,
+):
+    side = WeightGrads(
+        (x_ref, c_ref), (dgate_ref, dup_ref, act_ref), (gg_ref, gu_ref, gd_ref), (x_buf, c_buf),
+        grad_buf, acc, stage, in_sems, out_sems,
+    )
+    side.begin()
+    scatter_kernel(counts, parts, False, part_ref, out_ref, own, *scratch, side=side)
+    side.finish()
+
+
+def scatter_and_grads(partial, counts, parts, x_rows, c_rows, grads, ident, name):
+    n_hi, n_lo, n_x, n_core = counts
+    rows, width = partial.shape[4:]
+    experts, slots, hidden = grads[0].shape
+    depth = 512
+    b16 = jnp.bfloat16
+    anywhere = pl.BlockSpec(memory_space=pl.ANY)
+    weight = jax.ShapeDtypeStruct((experts, width, hidden), jnp.float32)
+    return pl.pallas_call(
+        functools.partial(scatter_grads_kernel, counts, parts),
+        in_specs=[anywhere] * 6,
+        out_specs=[pl.BlockSpec(memory_space=pltpu.VMEM)] + [anywhere] * 3,
+        out_shape=[jax.ShapeDtypeStruct((rows, width), jnp.float32)] + [weight] * 3,
+        scratch_shapes=[
+            pltpu.VMEM((2, depth, width), b16),
+            pltpu.VMEM((2, depth, width), b16),
+            pltpu.VMEM((2, 3, depth, hidden), b16),
+            pltpu.VMEM((3, hidden, width), jnp.float32),
+            pltpu.VMEM((3, width, hidden), jnp.float32),
+            pltpu.SemaphoreType.DMA((2, 5)),
+            pltpu.SemaphoreType.DMA((3,)),
+            pltpu.VMEM((1, 1, 1, 1, 16, 128), b16),
+        ]
+        + scatter_scratch(counts, parts, rows // parts, width),
+        compiler_params=pltpu.CompilerParams(
+            collective_id=ident, has_side_effects=True, vmem_limit_bytes=60 * 2**20
+        ),
+        cost_estimate=pl.CostEstimate(
+            flops=6 * experts * slots * width * hidden,
+            bytes_accessed=4 * experts * slots * width,
+            transcendentals=0,
+        ),
+        name=name,
+    )(partial, x_rows, c_rows, *grads)
 
 
 class Combine:
@@ -597,7 +730,8 @@
 
 
 def gather_kernel(
-    counts, parts, fsdp_too, in_ref, out_ref, own_sem, s0, r0, s1, r1, s2, r2, s3, r3, host=None
+    counts, parts, fsdp_too, in_ref, out_ref, own_sem, s0, r0, s1, r1, s2, r2, s3, r3, host=None,
+    side=None,
 ):
     at = Place(counts, fsdp_too)
     n_hi, n_lo, n_x, n_core = counts
@@ -658,7 +792,9 @@
         in_ref, out_ref.at[at.x, at.core, at.hi, at.lo], own_sem
     )
     keep.start()
-    at.meet()
+    at.meet(side.at if side is not None else None)
+    if side is not None:
+        side.begin()
     for ahead in range(1, n_hi):
         for q in range(parts):
             hi_copy(q, ahead).start()
@@ -692,6 +828,12 @@
                         each_mid(t - back, v, stage + 1, lambda c: c.start())
                     elif n_core > 1:
                         core_copy(t - back, v).start()
+
+        if side is not None:
+
+            @pl.when(t == steps // 2 + 1)
+            def _():
+                side.middle()
 
         if host is not None:
             for origin_step in range(n_hi):
@@ -727,6 +869,86 @@
         for ahead in range(1, n_hi):
             hi_copy(q, ahead).wait_send()
 
+    if side is not None:
+        side.end()
+
+
+class SideGather:
+    def __init__(self, counts, in_ref, out_ref, own_sem, s_x, r_x, s_core, r_core):
+        self.at = Place(counts, True)
+        self.in_ref, self.out_ref, self.own_sem = in_ref, out_ref, own_sem
+        self.s_x, self.r_x, self.s_core, self.r_core = s_x, r_x, s_core, r_core
+
+    def own(self):
+        at = self.at
+        return pltpu.make_async_copy(self.in_ref, self.out_ref.at[at.x, at.core], self.own_sem)
+
+    def x_copy(self, ahead):
+        at = self.at
+        return pltpu.make_async_remote_copy(
+            src_ref=self.in_ref, dst_ref=self.out_ref.at[at.x, at.core],
+            send_sem=self.s_x.at[ahead - 1], recv_sem=self.r_x.at[at.n_x - ahead - 1],
+            device_id=at.peer("x", ahead), device_id_type=MESH,
+        )
+
+    def core_copy(self):
+        ref = self.out_ref.at[:, self.at.core]
+        return pltpu.make_async_remote_copy(
+            src_ref=ref, dst_ref=ref, send_sem=self.s_core, recv_sem=self.r_core,
+            device_id=self.at.peer("core", 1), device_id_type=MESH,
+        )
+
+    def begin(self):
+        self.own().start()
+        for ahead in range(1, self.at.n_x):
+            self.x_copy(ahead).start()
+
+    def middle(self):
+        self.own().wait()
+        for ahead in range(1, self.at.n_x):
+            self.x_copy(ahead).wait_recv()
+        if self.at.n_core > 1:
+            self.core_copy().start()
+
+    def end(self):
+        for ahead in range(1, self.at.n_x):
+            self.x_copy(ahead).wait_send()
+        if self.at.n_core > 1:
+            self.core_copy().wait()
+
+
+def gather_two_kernel(
+    counts, parts, side_counts, in_ref, side_in, out_ref, side_out, own_sem, s_x, r_x, s_core,
+    r_core, *sems,
+):
+    side = SideGather(side_counts, side_in, side_out, own_sem, s_x, r_x, s_core, r_core)
+    gather_kernel(counts, parts, False, in_ref, out_ref, *sems, side=side)
+
+
+def gather_two(own, weight, counts, side_counts, parts, ident, name):
+    n_hi, n_lo, _, _ = counts
+    _, _, n_x, n_core = side_counts
+    rows, width = own.shape
+    anywhere = pl.BlockSpec(memory_space=pl.ANY)
+    dma = pltpu.SemaphoreType.DMA
+    out, side = pl.pallas_call(
+        functools.partial(gather_two_kernel, counts, parts, side_counts),
+        in_specs=[anywhere] * 2,
+        out_specs=[anywhere] * 2,
+        out_shape=[
+            jax.ShapeDtypeStruct((1, 1, n_hi, n_lo, rows, width), own.dtype),
+            jax.ShapeDtypeStruct((n_x, n_core) + weight.shape, weight.dtype),
+        ],
+        scratch_shapes=[dma, dma((max(n_x - 1, 1),)), dma((max(n_x - 1, 1),)), dma, dma]
+        + gather_sems(counts, parts),
+        compiler_params=pltpu.CompilerParams(collective_id=ident, has_side_effects=True),
+        cost_estimate=pl.CostEstimate(
+            flops=0, bytes_accessed=4 * n_hi * n_lo * rows * width, transcendentals=0
+        ),
+        name=name,
+    )(own, weight)
+    return out.reshape(-1, width), side.reshape(-1, weight.shape[1])
+
 
 class Dispatch:
     def __init__(self, tables, rows, bufs, ins, outs, rank_ref, geometry):
@@ -734,10 +956,11 @@
         self.rank_ref = rank_ref
         self.n_hi, self.n_lo, self.n_x, self.n_core = geometry
 
-    def load(self, which, place, index, slot):
+    def load(self, which, index, slot):
         held, _ = self.bufs[which]
         return pltpu.make_async_copy(
-            self.tables[which].at[index], held.at[slot], self.ins[which].at[slot]
+            self.tables[which].at[index + (slice(None), pl.ds(0, held.shape[2]))],
+            held.at[slot], self.ins[which].at[slot],
         )
 
     def store(self, which, block, slot):
@@ -749,26 +972,33 @@
     def run(self, which, block_of, index_of, count):
         held, found = self.bufs[which]
         experts, slots, width = found.shape[1:]
-        self.load(which, None, index_of(0), 0).start()
+        if held is not None:
+            self.load(which, index_of(0), 0).start()
 
         @pl.loop(0, count)
         def _(j):
             slot = j % 2
 
-            @pl.when(j + 1 < count)
-            def _():
-                self.load(which, None, index_of(j + 1), 1 - slot).start()
+            if held is not None:
+
+                @pl.when(j + 1 < count)
+                def _():
+                    self.load(which, index_of(j + 1), 1 - slot).start()
 
             @pl.when(j >= 2)
             def _():
                 self.store(which, block_of(j - 2), slot).wait()
 
-            self.load(which, None, index_of(j), slot).wait()
+            if held is not None:
+                self.load(which, index_of(j), slot).wait()
+                table = held.at[slot]
+            else:
+                table = self.tables[which].at[index_of(j)]
             pick = pick_matrix(self.rank_ref[block_of(j)], slots)
             for start, size in column_spans(width):
                 cols = pl.ds(start, size)
                 picked = jnp.dot(
-                    pick, held[slot, :, cols], preferred_element_type=jnp.float32
+                    pick, table[:, cols], preferred_element_type=jnp.float32
                 ).astype(jnp.bfloat16)
                 found[slot, :, :, cols] = picked.reshape(experts, slots, size)
             self.store(which, block_of(j), slot).start()
@@ -796,13 +1026,18 @@
 
                 @pl.when(t == step)
                 def _(first=first, count=count):
-                    self.run(1, lambda j: first + j, lambda j: first + j, count)
+                    self.run(1, lambda j: first + j, lambda j: (first + j,), count)
 
 
 def dispatch_kernel(
-    counts, parts, in_ref, other_ref, rank_ref, out_ref, rows_ref, other_rows_ref, held, found,
-    other_held, other_found, in_sem, put_sem, other_in_sem, other_put_sem, *sems,
+    counts, parts, in_ref, other_ref, rank_ref, rows_ref, other_rows_ref, *rest
 ):
+    out_ref, held, found, other_held, other_found, in_sem, put_sem, other_in_sem, other_put_sem = (
+        rest[:9]
+    )
+    sems = rest[9:]
+    if len(out_ref.shape) == 6 and held.shape[0] == 1:
+        held = None
     host = Dispatch(
         (out_ref, other_ref), (rows_ref, other_rows_ref),
         ((held, found), (other_held, other_found)), (in_sem, other_in_sem),
@@ -820,40 +1055,45 @@
     return [pltpu.SemaphoreType.DMA] + [pltpu.SemaphoreType.DMA(size) for size in sizes]
 
 
-def gather_and_dispatch(own, other_all, rank, slots, sp_count, fs_count, ident, name):
+def gather_and_dispatch(own, other_all, other_width, rank, slots, sp_count, fs_count, ident, name):
     counts = mesh_counts(sp_count, fs_count)
     n_hi, n_lo, n_x, n_core = counts
     rows, width = own.shape
-    other_width = other_all.shape[1]
     blocks, experts, _ = rank.shape
     parts = 4 if rows % 64 == 0 else 2
     b16 = jnp.bfloat16
     anywhere = pl.BlockSpec(memory_space=pl.ANY)
+    table = (n_x, n_core, n_hi, n_lo, rows, width)
+    inside = 2 * blocks * rows * width <= 36 * 2**20
     scratch = [
-        pltpu.VMEM((2, rows, width), b16),
+        pltpu.VMEM((1, 16, LANES) if inside else (2, rows, width), b16),
         pltpu.VMEM((2, experts, slots, width), b16),
         pltpu.VMEM((2, rows, other_width), b16),
         pltpu.VMEM((2, experts, slots, other_width), b16),
     ] + [pltpu.SemaphoreType.DMA((2,))] * 4
     flops = 2 * blocks * experts * slots * rows * (width + other_width)
-    _, picked, other_picked = pl.pallas_call(
+    results = [
+        jax.ShapeDtypeStruct((experts, blocks, slots, width), b16),
+        jax.ShapeDtypeStruct((experts, blocks, slots, other_width), b16),
+    ]
+    if inside:
+        scratch = [pltpu.VMEM(table, b16)] + scratch
+    else:
+        results.append(jax.ShapeDtypeStruct(table, b16))
+    picked, other_picked, *_ = pl.pallas_call(
         functools.partial(dispatch_kernel, counts, parts),
         in_specs=[anywhere, anywhere, pl.BlockSpec(memory_space=pltpu.VMEM)],
-        out_specs=[anywhere] * 3,
-        out_shape=[
-            jax.ShapeDtypeStruct((n_x, n_core, n_hi, n_lo, rows, width), b16),
-            jax.ShapeDtypeStruct((experts, blocks, slots, width), b16),
-            jax.ShapeDtypeStruct((experts, blocks, slots, other_width), b16),
-        ],
+        out_specs=[anywhere] * len(results),
+        out_shape=results,
         scratch_shapes=scratch + gather_sems(counts, parts),
         compiler_params=pltpu.CompilerParams(
-            collective_id=ident, has_side_effects=True, vmem_limit_bytes=48 * 2**20
+            collective_id=ident, has_side_effects=True, vmem_limit_bytes=56 * 2**20
         ),
         cost_estimate=pl.CostEstimate(
             flops=flops, bytes_accessed=8 * blocks * rows * width, transcendentals=0
         ),
         name=name,
-    )(own, other_all.reshape(blocks, rows, other_width), rank)
+    )(own, other_all.reshape(blocks, rows, -1), rank)
     return picked.reshape(experts, -1, width), other_picked.reshape(experts, -1, other_width)
 
 
@@ -1083,11 +1323,11 @@
     return scatter_over_all(partial, block, sp_count, fs_count, ident, name)
 
 
-def scatter_over_sp(partial, rows, sp_count, ident, name):
-    n_hi, n_lo, _, _ = mesh_counts(sp_count, 1)
+def scatter_over_fsdp(partial, rows, fs_count, ident, name):
+    _, _, n_x, n_core = mesh_counts(1, fs_count)
     parts = 4 if rows % 64 == 0 else 2
-    shaped = partial.reshape(1, 1, n_hi, n_lo, rows, partial.shape[1])
-    return scatter_sum(shaped, (n_hi, n_lo, 1, 1), False, parts, jnp.float32, ident, name)
+    shaped = partial.reshape(n_x, n_core, 1, 1, rows, partial.shape[1])
+    return scatter_sum(shaped, (1, 1, n_x, n_core), True, parts, jnp.float32, ident, name)
 
 
 def gather_over_all(own, sp_count, fs_count, ident, name):
@@ -1149,14 +1389,21 @@
         axis=1,
     )
     qkv_mat = lax.all_gather(qkv_own, "fsdp", axis=0, tiled=True)
-    out_mat = lax.all_gather(w_out, "fsdp", axis=0, tiled=True)
     router_mat = lax.all_gather(w_router, "fsdp", axis=0, tiled=True)
-    cot_all = lax.all_gather(cotangent[0], ("fsdp", "sp"), axis=0, tiled=True)
-    rank, live = route_plan(expert_ids[0], sp_count, fs_count)
+    ids_own = jnp.pad(expert_ids[0].astype(jnp.bfloat16), ((0, 0), (0, LANES - TOPK)))
+    cot_all = lax.all_gather(
+        jnp.concatenate([cotangent[0], ids_own], axis=1), ("fsdp", "sp"), axis=0, tiled=True
+    )
+    ids_all = cot_all[:, width : width + TOPK].astype(jnp.int32)
+    rank, live = route_plan(ids_all, tok_rows, sp_count)
     slots = 2 * tok_rows * TOPK // EXPERTS
 
     attn_normed, attn_pull = jax.vjp(rms_scale, hidden_in, gain_attn)
-    attn_in = gather_over_sp(attn_normed.astype(jnp.bfloat16), sp_count, 1, "gather_attn_in")
+    n_hi, n_lo, n_x, n_core = mesh_counts(sp_count, fs_count)
+    attn_in, out_mat = gather_two(
+        attn_normed.astype(jnp.bfloat16), w_out, (n_hi, n_lo, 1, 1), (1, 1, n_x, n_core),
+        4 if tok_rows % 64 == 0 else 2, 1, "gather_attn_in",
+    )
     qkv_raw = jnp.dot(attn_in, qkv_mat, preferred_element_type=jnp.float32)
     raw = (qkv_raw[:, :span], qkv_raw[:, span : 2 * span])
     value_heads = qkv_raw[:, 2 * span :].astype(jnp.bfloat16)
@@ -1184,9 +1431,9 @@
     router_low = (router - router_high.astype(jnp.float32)).astype(jnp.bfloat16)
     ffn_rows, cot_rows = gather_and_dispatch(
         jnp.concatenate([ffn_in, router_high, router_low], axis=1),
-        cot_all, rank, slots, sp_count, fs_count, 2, "gather_ffn_in",
-    )
-    in_grad_rows, out_rows, grad_gate, grad_up, grad_down = run_experts(
+        cot_all, width, rank, slots, sp_count, fs_count, 2, "gather_ffn_in",
+    )
+    in_grad_rows, out_rows, *inner_grads = run_experts(
         ffn_rows, cot_rows, w_gate, w_up, w_down, live, first_expert[None]
     )
     in_grad_sum = combine_and_scatter(
@@ -1203,7 +1450,6 @@
     ffn_in_grad = ffn_in_grad + jnp.dot(
         logit_grad, router_mat.T, preferred_element_type=jnp.float32
     )
-    router_term = jnp.dot(ffn_in.T, logit_grad, preferred_element_type=jnp.float32)
     ffn_hidden_grad, ffn_gain_term = ffn_pull(ffn_in_grad)
     after_grad = upstream + ffn_hidden_grad
     attn_out_grad = after_grad.astype(jnp.bfloat16)
@@ -1213,18 +1459,23 @@
     attended_grad_heads = lax.all_to_all(
         attended_grad, "sp", split_axis=1, concat_axis=0, tiled=True
     )
-    out_term = jnp.dot(attended_tok.T, attn_out_grad, preferred_element_type=jnp.float32)
-    row_terms = jnp.concatenate(
-        [
-            out_term.astype(jnp.bfloat16),
-            router_term.astype(jnp.bfloat16),
-            jnp.zeros((width, 128 - EXPERTS), jnp.bfloat16),
-        ],
-        axis=1,
-    )
+    row_terms = lax.dot_general(
+        jnp.concatenate([attended_tok, ffn_in], axis=0),
+        jnp.concatenate(
+            [
+                jnp.pad(attn_out_grad, ((0, 0), (0, LANES))),
+                jnp.pad(logit_grad, ((0, 0), (width, LANES - EXPERTS))),
+            ],
+            axis=0,
+        ),
+        (((0,), (0,)), ((), ())),
+        preferred_element_type=jnp.float32,
+    ).astype(jnp.bfloat16)
     row_sums = scatter_over_all(
         row_terms, width // (sp_count * fs_count), sp_count, fs_count, 5, "scatter_out_rows"
     )
+    attended_grad_heads, row_sums = lax.optimization_barrier((attended_grad_heads, row_sums))
+    rows_every = lax.all_gather(row_sums.astype(jnp.bfloat16), "sp", axis=0, tiled=True)
     query_grad_heads, key_grad_heads, value_low = attend_back(attended_grad_heads)
 
     def unturned(grad):
@@ -1244,18 +1495,20 @@
         for g, r, s, p in zip(scaled_grads, raw, scales, products)
     ]
     qkv_low = jnp.concatenate(raw_grads + [value_low], axis=1)
+    qkv_term = jnp.dot(attn_in.T, qkv_low, preferred_element_type=jnp.float32)
+    qkv_sums = scatter_over_fsdp(
+        qkv_term.astype(jnp.bfloat16), width // fs_count, fs_count, 11, "scatter_qkv"
+    ).astype(jnp.bfloat16)
+    qkv_every = lax.all_gather(qkv_sums, "sp", axis=0)
     attn_partial = lax.dot_general(
         qkv_low, qkv_mat, (((1,), (1,)), ((), ())), preferred_element_type=jnp.float32
     ).astype(jnp.bfloat16)
-    attn_in_grad = scatter_over_sp(attn_partial, tok_rows, sp_count, 6, "scatter_attn_in")
-    qkv_term = jnp.dot(attn_in.T, qkv_low, preferred_element_type=jnp.float32)
+    attn_in_grad, grad_gate, grad_up, grad_down = scatter_and_grads(
+        attn_partial.reshape(1, 1, n_hi, n_lo, tok_rows, width), (n_hi, n_lo, 1, 1),
+        4 if tok_rows % 64 == 0 else 2, ffn_rows, cot_rows, inner_grads, 6, "scatter_attn_in",
+    )
     attn_hidden_grad, attn_gain_term = attn_pull(attn_in_grad)
     grad_tokens = after_grad + attn_hidden_grad
-    qkv_sums = lax.psum_scatter(
-        qkv_term.astype(jnp.bfloat16), "fsdp", scatter_dimension=0, tiled=True
-    )
-    qkv_every = lax.all_gather(qkv_sums, "sp", axis=0)
-    rows_every = lax.all_gather(row_sums.astype(jnp.bfloat16), "sp", axis=0, tiled=True)
     dense = [
         qkv_every[:, :, k * span : (k + 1) * span]
         .transpose(1, 0, 2)

time: 1490 us -> 1410 us (0.946)
  waiting for transfers between devices: 103 us -> 46.3 us
  Pallas kernels: 1140 us -> 1110 us
    pallas_call x2, Pallas kernels: 156 us -> 265 us  [the longest x1 151 us: gather_two(): pl.pallas_call(functools.partial(gather_two_kernel, counts, parts, side_c...]
    pallas_call x2, Pallas kernels: 172 us -> 73.9 us  [scatter_sum(): pl.pallas_call(functools.partial(scatter_kernel, counts, parts, fsdp_too)...]
    pallas_call x1, Pallas kernels: 200 us -> 128 us  [run_experts(): pl.pallas_call(expert_kernel, grid_spec=pltpu.PrefetchScalarGridSpec(num_...]
    pallas_call x2, Pallas kernels: 349 us -> 387 us  [combine_sum(): pl.pallas_call(functools.partial(combine_scatter_kernel, counts, parts),...]
    all_gather x1, waiting for transfers between devices: 36.1 us -> 0.01 us  [local(): qkv_every = lax.all_gather(qkv_sums, 'sp', axis=0)]
    unnamed x150 -> x169, local copies, waits for them, and re-layouts: 14.4 us -> 42.7 us
    all_to_all x1, waiting for transfers between devices: 26 us -> 0.01 us  [local(): lax.all_to_all(attended_grad, 'sp', split_axis=1, concat_axis=0, tiled=True)]
  transfers between devices with their start and end apart: 8 -> 6, of which waited for: 4 -> 1; matrix products, arithmetic and copies ran while one was open for 8% -> 9% of each run, Pallas kernels for 27% -> 43%
where the time goes in v5:
time: 1410 us; the launch traced here: 1400 us
  Pallas kernels  1110 us (79%)
  other arithmetic  80 us (6%)
  local copies, waits for them, and re-layouts  74 us (5%)
  matrix products  53 us (4%)
  waiting for transfers between devices  46.3 us (3%)
  between operations  15.5 us (1%)
    pallas_call x2, Pallas kernels, combine_sum(): pl.pallas_call(functools.partial(combine_scatter_kernel, counts, parts),...  387 us
    pallas_call x1, Pallas kernels, gather_and_dispatch(): pl.pallas_call(functools.partial(dispatch_kernel, counts, parts), in_spec...  160 us
    pallas_call x1, Pallas kernels, gather_two(): pl.pallas_call(functools.partial(gather_two_kernel, counts, parts, side_c...  151 us
    pallas_call x1, Pallas kernels, run_experts(): pl.pallas_call(expert_kernel, grid_spec=pltpu.PrefetchScalarGridSpec(num_...  128 us
    pallas_call x1, Pallas kernels, scatter_and_grads(): pl.pallas_call(functools.partial(scatter_grads_kernel, counts, parts), in...  114 us
    pallas_call x2, Pallas kernels, scatter_sum(): pl.pallas_call(functools.partial(scatter_kernel, counts, parts, fsdp_too)...  73.9 us
    pallas_call x3, Pallas kernels, small_sum(): pl.pallas_call(functools.partial(small_sum_kernel, (sp_count, fs_count)),...  49.3 us
    all_to_all x1, waiting for transfers between devices, local(): lax.all_to_all(attended_heads, 'sp', split_axis=0, concat_axis=1, tiled=T...  46.2 us
  transfers between devices with their start and end apart: 6, of which 1 were waited for; matrix products, arithmetic and copies ran while one was open for 9% of the time, Pallas kernels for 43%

profile of v5, /device:TPU:0, one launch (start us, length us, event | category | flops | bytes accessed | tf_op | source)
XLA Modules:
  0.0 1402.5 jit_solution(1887470674734379313)
XLA Ops:
  8.3 1.1 constant_dynamic-slice_fusion.1
  10.6 1.1 fusion.24
  12.0 6.2 all_gather.21
  19.1 1.3 fusion.11.in_ref
  20.3 151.3 %gather_attn_in.1 = (bf16[1,1,4,2,256,2048]{5,4,3,2,1,0:T(8,128)(2,1)}, bf16[2,2,512,2048]{3,2,1,0:T(8,128)(2,1)}) custom-call(bf16[256,2048]{1,0:T(8,128)(2,1)} %fusion.11.in_ref, bf16[512,2048]{1,0:T(8,128)(2,1)} %side_in.1), custom_call_target="tpu_custom_call" | custom-call | bytes 16777216 | tf_op jit(solution)/shard_map/gather_attn_in/pallas_call | solution.py:934
  172.1 5.2 fusion.43
  177.3 10.1 fusion.50
  188.1 1.8 copy-done.9
  190.6 26.9 %sum_squares.1 = f32[32,128]{1,0:T(8,128)} custom-call(f32[32,128]{1,0:T(8,128)} %reshape.354.part_ref), custom_call_target="tpu_custom_call" | custom-call | tf_op jit(solution)/shard_map/sum_squares/pallas_call | solution.py:1166
  218.9 3.5 multiply_multiply_fusion
  222.4 2.1 reshape.356
  224.5 3.2 reshape.355
  227.8 4.5 slice_negate_fusion.3
  232.3 2.3 slice_negate_fusion.2
  234.7 5.6 maximum_multiply_fusion.1
  240.3 1.2 mul.421
  242.9 19.6 %attend.1 = bf16[2048,256]{1,0:T(8,128)(2,1)} custom-call(s32[4]{0:T(128)S(1)} %bitcast.147, bf16[2048,256]{1,0:T(8,128)(2,1)S(1)} %get-tuple-element.176.q_ref, bf16[2048,256]{1,0:T(8,128)(2,1)S(1)} %get-tuple-element.175.k_ref, bf16[2048,256]{1,0:T(8,128)(2,1)S(1)} %slice.180.v_ref), custom_call_target="tpu_custom_call" | custom-call | flops 2684354560 | bytes 4194304 | tf_op jit(solution)/shard_map/attend/pallas_call | solution.py:1279
  262.5 4.8 all-to-all-start
  267.3 5.8 all_gather.24
  273.1 46.2 %all-to-all-done = bf16[8,256,256]{2,1,0:T(8,128)(2,1)S(1)} async-done(((bf16[8,256,256]{2,1,0:T(8,128)(2,1)}), bf16[8,256,256]{2,1,0:T(8,128)(2,1)S(1)}, u32[]{:S(2)}, u32[]{:S(2)}) %all-to-all-start) | async-done | bytes 1048608 | tf_op jit(solution)/shard_map/all_to_all | solution.py:1422
  319.4 6.9 multiply_reduce_fusion.6
  328.7 1.9 concatenate.49.in_ref
  330.5 4.0 slice_convert_fusion.1
  334.6 2.8 copy.121
  341.1 160.3 %gather_ffn_in.1 = (bf16[8,32,64,2176]{3,2,1,0:T(8,128)(2,1)}, bf16[8,32,64,2048]{3,2,1,0:T(8,128)(2,1)}) custom-call(bf16[256,2176]{1,0:T(8,128)(2,1)} %concatenate.49.in_ref, bf16[32,256,2176]{2,1,0:T(8,128)(2,1)} %bitcast.182, s32[32,8,256]{2,1,0:T(8,128)} %select_bitcast_fusion.rank_ref), custom_call_target="tpu_custom_call" | custom-call | flops 35433480192 | bytes 142606336 | tf_op jit(solution)/shard_map/gather_ffn_in/pallas_call | solution.py:1083
  501.4 128.1 %experts.1 = (bf16[8,2048,2176]{2,1,0:T(8,128)(2,1)}, bf16[8,2048,2048]{2,1,0:T(8,128)(2,1)}, bf16[8,2048,256]{2,1,0:T(8,128)(2,1)}, bf16[8,2048,256]{2,1,0:T(8,128)(2,1)}, bf16[8,2048,256]{2,1,0:T(8,128)(2,1)}) custom-call(s32[16]{0:T(128)} %reshape.379.live, s32[1]{0:T(128)} %bitcast.23.first, bf16[8,2048,2176]{2,1,0:T(8,128)(2,1)} %bitcast.27.x_ref, ...), custom_call_target="tpu_custom_call" | custom-call | flops 103079215104 | bytes 268435456 | tf_op jit(solution)/shard_map/experts/pallas_call | solution.py:143
  629.5 188.9 %scatter_grads.1 = f32[256,2176]{1,0:T(8,128)} custom-call(bf16[8,32,64,2176]{3,2,1,0:T(8,128)(2,1)} %bitcast.31.rows_ref, s32[32,8,256]{2,1,0:T(8,128)} %select_bitcast_fusion.rank_ref), custom_call_target="tpu_custom_call" | custom-call | flops 18253611008 | bytes 71303168 | tf_op jit(solution)/shard_map/scatter_grads/pallas_call | solution.py:687
  818.5 1.1 multiply_reduce_fusion.9
  820.8 3.1 multiply_reduce_fusion
  824.0 1.3 copy-done.13
  826.0 1.2 copy-done.70
  827.1 2.4 convolution_convert_fusion.3
  830.6 4.3 all-to-all-start.1
  834.9 7.5 convolution_convert_fusion
  842.4 50.5 %scatter_out_rows.1 = f32[64,2176]{1,0:T(8,128)} custom-call(bf16[2,2,4,2,64,2176]{5,4,3,2,1,0:T(8,128)(2,1)} %bitcast.158), custom_call_target="tpu_custom_call" | custom-call | flops 4456448 | bytes 8912896 | tf_op jit(solution)/shard_map/scatter_out_rows/pallas_call | solution.py:716
  892.9 1.2 copy-done.3
  894.1 29.1 %attend_back.1 = (bf16[2048,256]{1,0:T(8,128)(2,1)S(1)}, bf16[2048,256]{1,0:T(8,128)(2,1)S(1)}, bf16[2048,256]{1,0:T(8,128)(2,1)S(1)}) custom-call(s32[4]{0:T(128)S(1)} %bitcast.148, bf16[2048,256]{1,0:T(8,128)(2,1)S(1)} %copy-done.3, bf16[2048,256]{1,0:T(8,128)(2,1)S(1)} %copy-done.1, bf16[2048,256]{1,0:T(8,128)(2,1)} %copy-done.4, ...), custom_call_target="tpu_custom_call" | custom-call | flops 8053063680 | bytes 4194304 | tf_op jit(solution)/shard_map/attend_back/pallas_call | solution.py:1284
  925.0 2.2 reshape.368
  927.2 2.0 reshape.369
  929.2 4.6 slice_negate_fusion
  933.9 2.3 slice_negate_fusion.1
  936.3 5.6 maximum_multiply_fusion.3
  942.0 3.2 multiply_reduce_fusion.2
  945.9 8.4 sum_products.1
  955.0 5.0 subtract_convert_fusion.1
  960.0 11.3 convolution_convert_fusion.2
  971.2 23.4 %scatter_qkv.1 = f32[512,768]{1,0:T(8,128)} custom-call(bf16[2,2,1,1,512,768]{5,4,3,2,1,0:T(8,128)(2,1)} %bitcast.168), custom_call_target="tpu_custom_call" | custom-call | flops 1572864 | bytes 3145728 | tf_op jit(solution)/shard_map/scatter_qkv/pallas_call | solution.py:716
  994.7 2.4 convert_element_type.185
  997.1 198.0 %scatter_outputs.1 = f32[256,2048]{1,0:T(8,128)} custom-call(bf16[8,32,64,2048]{3,2,1,0:T(8,128)(2,1)} %bitcast.29.rows_ref, s32[32,8,256]{2,1,0:T(8,128)} %select_bitcast_fusion.rank_ref), custom_call_target="tpu_custom_call" | custom-call | flops 17179869184 | bytes 67108864 | tf_op jit(solution)/shard_map/scatter_outputs/pallas_call | solution.py:687
  1195.1 11.0 convolution_convert_fusion.1
  1206.1 114.1 %scatter_attn_in.1 = (f32[256,2048]{1,0:T(8,128)}, f32[8,2048,256]{2,1,0:T(8,128)}, f32[8,2048,256]{2,1,0:T(8,128)}, f32[8,2048,256]{2,1,0:T(8,128)}) custom-call(bf16[1,1,4,2,256,2048]{5,4,3,2,1,0:T(8,128)(2,1)} %bitcast.206, bf16[8,2048,2176]{2,1,0:T(8,128)(2,1)} %bitcast.27.x_ref, bf16[8,2048,2048]{2,1,0:T(8,128)(2,1)} %bitcast.28.c_ref, ...), custom_call_target="tpu_custom_call" | custom-call | flops 51539607552 | bytes 134217728 | tf_op jit(solution)/shard_map/scatter_attn_in/pallas_call | solution.py:567
  1320.3 2.4 fusion.12
  1323.4 14.0 sum_gains.1
  1338.8 5.9 fusion.15
  1346.4 4.1 slice_convert_fusion
  1350.6 4.4 convert_bitcast_fusion
  1355.0 2.6 copy.141
  1357.6 2.6 copy.140
  1360.2 2.8 copy.139
  1363.0 13.2 copy.166
  1377.0 1.5 slice-done.9
  1378.5 8.5 copy.167
  1387.9 1.4 slice-done.5
  1389.3 6.2 copy.168
  (238 shorter events, 25.7 us)
Async XLA Ops:
  7.2 170.1 %all-gather.6.cloned.1.call-start = ((), (), s32[]{:S(2)}) async-start(), calls=%async_computation.2 | async-start | bytes 3932160 | tf_op jit(solution)/shard_map/all_gather | solution.py:1391
  10.4 7.8 copy-start.19
  10.4 320.2 %all-gather.8.cloned.1.call-start = ((), (), s32[]{:S(2)}) async-start(), calls=%async_computation.3 | async-start | bytes 36765696 | tf_op jit(solution)/shard_map/all_gather | solution.py:1394
  11.9 231.0 %copy-start.5 = (s32[4,1]{0,1:T(1,128)}, s32[4,1]{0,1:T(1,128)S(1)}, u32[]{:S(2)}) copy-start(s32[4,1]{0,1:T(1,128)S(1)} %reduce-window.9) | copy-start | bytes 52
  19.0 152.6 %copy-start.55 = (f32[256]{0:T(256)}, f32[256]{0:T(256)S(1)}, u32[]{:S(2)}) copy-start(f32[256]{0:T(256)S(1)} %fusion.35) | copy-start | bytes 3076
  19.0 152.6 %copy-start.42 = (f32[1,2048]{1,0:T(1,128)}, f32[1,2048]{1,0:T(1,128)S(1)}, u32[]{:S(2)}) copy-start(f32[1,2048]{1,0:T(1,128)S(1)} %get-tuple-element.199) | copy-start | bytes 24580
  19.1 307.3 %copy-start.38 = (f32[1,2048]{1,0:T(1,128)}, f32[1,2048]{1,0:T(1,128)S(1)}, u32[]{:S(2)}) copy-start(f32[1,2048]{1,0:T(1,128)S(1)} %get-tuple-element.198) | copy-start | bytes 24580
  171.7 47.2 %copy-start.57 = (f32[1,256]{1,0:T(1,128)}, f32[1,256]{1,0:T(1,128)S(1)}, u32[]{:S(2)}) copy-start(f32[1,256]{1,0:T(1,128)S(1)} %get-tuple-element.202) | copy-start | bytes 3076
  171.7 47.2 %copy-start.59 = (f32[1,256]{1,0:T(1,128)}, f32[1,256]{1,0:T(1,128)S(1)}, u32[]{:S(2)}) copy-start(f32[1,256]{1,0:T(1,128)S(1)} %get-tuple-element.203) | copy-start | bytes 3076
  187.5 55.4 %copy-start.4 = (bf16[2048,256]{1,0:T(8,128)(2,1)}, bf16[2048,256]{1,0:T(8,128)(2,1)S(1)}, u32[]{:S(2)}) copy-start(bf16[2048,256]{1,0:T(8,128)(2,1)S(1)} %slice.180.v_ref) | copy-start | bytes 3145732
  218.3 4.1 copy-start.44
  227.8 4.5 copy-start.17
  234.7 5.6 copy-start.26
  242.9 19.6 %copy-start = (bf16[2048,256]{1,0:T(8,128)(2,1)}, bf16[2048,256]{1,0:T(8,128)(2,1)S(1)}, u32[]{:S(2)}) copy-start(bf16[2048,256]{1,0:T(8,128)(2,1)S(1)} %get-tuple-element.175.k_ref) | copy-start | bytes 3145732
  242.9 19.6 %copy-start.2 = (bf16[2048,256]{1,0:T(8,128)(2,1)}, bf16[2048,256]{1,0:T(8,128)(2,1)S(1)}, u32[]{:S(2)}) copy-start(bf16[2048,256]{1,0:T(8,128)(2,1)S(1)} %get-tuple-element.176.q_ref) | copy-start | bytes 3145732
  262.5 4.8 copy-start.48
  262.5 56.9 %copy-start.20 = (bf16[1,256,2048]{2,1,0:T(8,128)(2,1)S(1)}, bf16[1,256,2048]{2,1,0:T(8,128)(2,1)}, u32[]{:S(2)}) copy-start(bf16[1,256,2048]{2,1,0:T(8,128)(2,1)} %param.16) | copy-start | bytes 3145732
  262.5 56.8 %all-to-all-start = ((bf16[8,256,256]{2,1,0:T(8,128)(2,1)}), bf16[8,256,256]{2,1,0:T(8,128)(2,1)S(1)}, u32[]{:S(2)}, u32[]{:S(2)}) async-start(bf16[8,256,256]{2,1,0:T(8,128)(2,1)} %bitcast.12), calls=%async_computation | async-start | bytes 2097152 | tf_op jit(solution)/shard_map/all_to_all | solution.py:1422
  273.0 53.6 %copy-start.31 = (bf16[2048,64]{0,1:T(8,128)(2,1)}, bf16[2048,64]{0,1:T(8,128)(2,1)S(1)}, u32[]{:S(2)}) copy-start(bf16[2048,64]{0,1:T(8,128)(2,1)S(1)} %all_gather.24) | copy-start | bytes 786436
  319.4 6.9 copy-start.36
  327.7 6.9 copy-start.49
  327.8 6.8 copy-start.29
  629.5 189.0 %copy-start.30 = (f32[256,64]{1,0:T(8,128)S(1)}, f32[256,64]{1,0:T(8,128)}, u32[]{:S(2)}) copy-start(f32[256,64]{1,0:T(8,128)} %copy-done.29) | copy-start | bytes 196612
  629.5 189.0 %copy-start.50 = (f32[256]{0:T(256)S(1)}, f32[256]{0:T(256)}, u32[]{:S(2)}) copy-start(f32[256]{0:T(256)} %copy-done.49) | copy-start | bytes 3076
  629.5 189.0 %copy-start.54 = (f32[256]{0:T(256)S(1)}, f32[256]{0:T(256)}, u32[]{:S(2)}) copy-start(f32[256]{0:T(256)} %copy-done.53) | copy-start | bytes 3076
  629.5 191.2 %copy-start.32 = (bf16[2048,64]{0,1:T(8,128)(2,1)S(1)}, bf16[2048,64]{0,1:T(8,128)(2,1)}, u32[]{:S(2)}) copy-start(bf16[2048,64]{0,1:T(8,128)(2,1)} %copy-done.31) | copy-start | bytes 786436
  629.5 191.2 %copy-start.39 = (f32[1,2048]{1,0:T(1,128)S(1)}, f32[1,2048]{1,0:T(1,128)}, u32[]{:S(2)}) copy-start(f32[1,2048]{1,0:T(1,128)} %copy-done.38) | copy-start | bytes 24580
  629.5 191.2 %copy-start.52 = (f32[256]{0:T(256)S(1)}, f32[256]{0:T(256)}, u32[]{:S(2)}) copy-start(f32[256]{0:T(256)} %copy-done.51) | copy-start | bytes 3076
  820.8 4.5 copy-start.11
  820.8 4.5 copy-start.23
  820.8 6.3 copy-start.70
  829.5 5.4 copy-start.41
  829.5 5.4 copy-start.25
  829.5 5.4 copy-start.37
  830.6 62.3 %all-to-all-start.1 = ((bf16[256,8,256]{2,0,1:T(8,128)(2,1)}), bf16[256,8,256]{2,0,1:T(8,128)(2,1)}, u32[]{:S(2)}, u32[]{:S(2)}) async-start(bf16[256,8,256]{2,0,1:T(8,128)(2,1)} %bitcast.146), calls=%async_computation.1 | async-start | bytes 2097152 | tf_op jit(solution)/shard_map/all_to_all | solution.py:1459
  834.8 509.9 %all-gather.10.cloned.1.call-start = ((), (), s32[]{:S(2)}) async-start(), calls=%async_computation.4 | async-start | bytes 2506752 | tf_op jit(solution)/shard_map/all_gather | solution.py:1478
  842.4 50.5 %copy-start.1 = (bf16[2048,256]{1,0:T(8,128)(2,1)S(1)}, bf16[2048,256]{1,0:T(8,128)(2,1)}, u32[]{:S(2)}) copy-start(bf16[2048,256]{1,0:T(8,128)(2,1)} %copy-done) | copy-start | bytes 3145732
  842.4 50.5 %copy-start.6 = (s32[4,1]{0,1:T(1,128)S(1)}, s32[4,1]{0,1:T(1,128)}, u32[]{:S(2)}) copy-start(s32[4,1]{0,1:T(1,128)} %copy-done.5) | copy-start | bytes 52
  894.1 30.1 %copy-start.33 = (f32[64,2176]{1,0:T(8,128)S(1)}, f32[64,2176]{1,0:T(8,128)}, u32[]{:S(2)}) copy-start(f32[64,2176]{1,0:T(8,128)} %scatter_out_rows.1) | copy-start | bytes 1671172
  925.0 425.6 %all-gather.12.cloned.1.call-start = ((), (), s32[]{:S(2)}) async-start(), calls=%async_computation.5 | async-start | bytes 7077888 | tf_op jit(solution)/shard_map/all_gather | solution.py:1502
  929.2 4.7 copy-start.18
  936.2 5.7 slice-start
  936.3 5.7 slice-start.1
  936.3 5.7 copy-start.15
  936.3 5.7 copy-start.45
  936.3 5.7 copy-start.47
  936.3 5.7 copy-start.58
  936.3 5.7 copy-start.60
  955.0 5.0 copy-start.8
  960.0 11.3 copy-start.34
  960.0 11.3 copy-start.35
  1206.1 114.2 %copy-start.21 = (bf16[1,256,2048]{2,1,0:T(8,128)(2,1)S(1)}, bf16[1,256,2048]{2,1,0:T(8,128)(2,1)}, u32[]{:S(2)}) copy-start(bf16[1,256,2048]{2,1,0:T(8,128)(2,1)} %param.16) | copy-start | bytes 3145732
  1206.1 114.2 %copy-start.43 = (f32[1,2048]{1,0:T(1,128)S(1)}, f32[1,2048]{1,0:T(1,128)}, u32[]{:S(2)}) copy-start(f32[1,2048]{1,0:T(1,128)} %copy-done.42) | copy-start | bytes 24580
  1206.1 114.2 %copy-start.56 = (f32[256]{0:T(256)S(1)}, f32[256]{0:T(256)}, u32[]{:S(2)}) copy-start(f32[256]{0:T(256)} %copy-done.55) | copy-start | bytes 3076
  1320.2 18.6 %copy-start.62 = (f32[256]{0:T(256)S(1)}, f32[256]{0:T(256)}, u32[]{:S(2)}) copy-start(f32[256]{0:T(256)} %copy-done.61) | copy-start | bytes 3076
  1320.2 18.6 %copy-start.12 = (f32[256,2048]{1,0:T(8,128)S(1)}, f32[256,2048]{1,0:T(8,128)}, u32[]{:S(2)}) copy-start(f32[256,2048]{1,0:T(8,128)} %copy-done.10) | copy-start | bytes 6291460
  1360.2 15.9 %slice-start.6 = ((s8[16777216]{0:T(1024)(128)(4,1)}), s8[4194304]{0:T(1024)(128)(4,1)S(1)}, s32[]{:S(2)}) async-start(s8[16777216]{0:T(1024)(128)(4,1)} %bitcast.155), calls=%async_computation.12 | async-start | bytes 8388608
  1363.0 13.2 slice-start.7
  1363.0 14.0 slice-start.8
  1363.0 15.5 %slice-start.9 = ((s8[16777216]{0:T(1024)(128)(4,1)}), s8[4194304]{0:T(1024)(128)(4,1)S(1)}, s32[]{:S(2)}) async-start(s8[16777216]{0:T(1024)(128)(4,1)} %bitcast.155), calls=%async_computation.15 | async-start | bytes 8388608
  1363.0 24.0 %slice-start.2 = ((s8[16777216]{0:T(1024)(128)(4,1)}), s8[4194304]{0:T(1024)(128)(4,1)S(1)}, s32[]{:S(2)}) async-start(s8[16777216]{0:T(1024)(128)(4,1)} %bitcast.153), calls=%async_computation.8 | async-start | bytes 8388608
  1363.0 24.0 %slice-start.3 = ((s8[16777216]{0:T(1024)(128)(4,1)}), s8[4194304]{0:T(1024)(128)(4,1)S(1)}, s32[]{:S(2)}) async-start(s8[16777216]{0:T(1024)(128)(4,1)} %bitcast.153), calls=%async_computation.9 | async-start | bytes 8388608
  1378.5 9.4 slice-start.4
  1378.5 10.8 slice-start.5
  (24 other events, 45.0 us)
Sparse Core Ops, SparseCore 0:
  10.5 44.4 all-gather.5
  58.5 268.2 all-gather.7
  925.1 49.1 all-gather.9
  997.2 162.3 all-gather.11

commit v6 on v5

--- a/solution.py
+++ b/solution.py
@@ -366,8 +366,9 @@
 
     at.meet()
     if host is not None:
-        make_group(0, 0, 1)
+        make_group(0, 0, 2)
         each_core_copy(0, lambda c: c.start())
+        make_group(0, 1, 2)
     else:
         if n_core > 1:
 
@@ -414,7 +415,7 @@
 
                 make_group(group, t % pairs, pairs)
 
-                @pl.when(t % pairs == pairs - 1)
+                @pl.when(t % pairs == (pairs + 1) // 2 - 1)
                 def _():
                     each_core_copy(group, lambda c: c.start())
 
@@ -606,7 +607,8 @@
 
         def spot(j):
             j = piece * count + j
-            return j // (self.n_core * self.n_lo), j // self.n_lo % self.n_core, j % self.n_lo
+            core = (at.core + 1 + j // (self.n_x * self.n_lo)) % self.n_core
+            return j // self.n_lo % self.n_x, core, j % self.n_lo
 
         def block(j):
             x, core, lo = spot(j)
@@ -1200,29 +1202,52 @@
     return weights / jnp.sum(weights, axis=-1, keepdims=True)
 
 
-def attend_kernel(count, reach, ends, q_ref, k_ref, v_ref, o_ref):
-    i = pl.program_id(1)
-    first = window_first(i, reach, k_ref.shape[0])
-    keys = pl.ds(first, reach)
-    scores = window_scores(ends, count, q_ref[...], k_ref[keys, :], first, i * ROWS)
-    probs = softmax_rows(scores).astype(jnp.bfloat16)
-    o_ref[...] = jnp.dot(probs, v_ref[keys, :], preferred_element_type=jnp.float32).astype(
-        jnp.bfloat16
-    )
-
-
-def attend_back_kernel(
-    count, reach, ends, q_ref, k_ref, v_ref, g_ref, dq_ref, dk_ref, dv_ref, dk_acc, dv_acc
+def turn_pairs(values, cosine, sine):
+    return values * cosine + pltpu.roll(values, HEAD_DIM // 2, 1) * sine
+
+
+def attend_kernel(
+    count, reach, ends, q_ref, k_ref, v_ref, scale_ref, gain_ref, cos_ref, sin_ref, o_ref, qo_ref,
+    ko_ref, vo_ref,
 ):
     i = pl.program_id(1)
     first = window_first(i, reach, k_ref.shape[0])
     keys = pl.ds(first, reach)
+    here = pl.ds(pl.multiple_of(i * ROWS, ROWS), ROWS)
+
+    @pl.when(i == 0)
+    def _():
+        normed = k_ref[...] * scale_ref[:, 1:2] * gain_ref[1:2, :]
+        ko_ref[...] = turn_pairs(normed, cos_ref[...], sin_ref[...]).astype(jnp.bfloat16)
+        vo_ref[...] = v_ref[...].astype(jnp.bfloat16)
+
+    normed = q_ref[...] * scale_ref[here, 0:1] * gain_ref[0:1, :]
+    q = turn_pairs(normed, cos_ref[here, :], sin_ref[here, :]).astype(jnp.bfloat16)
+    qo_ref[...] = q
+    scores = window_scores(ends, count, q, ko_ref[keys, :], first, i * ROWS)
+    probs = softmax_rows(scores).astype(jnp.bfloat16)
+    o_ref[...] = jnp.dot(probs, vo_ref[keys, :], preferred_element_type=jnp.float32).astype(
+        jnp.bfloat16
+    )
+
+
+def attend_back_kernel(
+    count, reach, ends, q_ref, k_ref, v_ref, g_ref, cos_ref, sin_ref, dq_ref, dk_ref, dv_ref,
+    dk_acc, dv_acc,
+):
+    i = pl.program_id(1)
+    first = window_first(i, reach, k_ref.shape[0])
+    keys = pl.ds(first, reach)
+    here = pl.ds(pl.multiple_of(i * ROWS, ROWS), ROWS)
     scale = HEAD_DIM ** (-0.5)
 
     @pl.when(i == 0)
     def _():
         dk_acc[...] = jnp.zeros_like(dk_acc)
         dv_acc[...] = jnp.zeros_like(dv_acc)
+
+    def turned_back(grad, cosine, sine):
+        return turn_pairs(grad.astype(jnp.bfloat16).astype(jnp.float32), cosine, -sine)
 
     q = q_ref[...]
     k = k_ref[keys, :]
@@ -1231,30 +1256,40 @@
     prob_grad = contract(grad, v_ref[keys, :], 1, 1)
     delta = jnp.sum(probs * prob_grad, axis=-1, keepdims=True)
     score_grad = (probs * (prob_grad - delta)).astype(jnp.bfloat16)
-    dq_ref[...] = (
-        jnp.dot(score_grad, k, preferred_element_type=jnp.float32) * scale
-    ).astype(jnp.bfloat16)
+    dq = jnp.dot(score_grad, k, preferred_element_type=jnp.float32) * scale
+    dq_ref[...] = turned_back(dq, cos_ref[here, :], sin_ref[here, :])
     dk_acc[keys, :] += contract(score_grad, q, 0, 0) * scale
     dv_acc[keys, :] += contract(probs.astype(jnp.bfloat16), grad, 0, 0)
 
     @pl.when(i == pl.num_programs(1) - 1)
     def _():
-        dk_ref[...] = dk_acc[...].astype(jnp.bfloat16)
+        dk_ref[...] = turned_back(dk_acc[...], cos_ref[...], sin_ref[...])
         dv_ref[...] = dv_acc[...].astype(jnp.bfloat16)
 
 
-def attend(query, key, value, lengths):
-    seq_rows, span = query.shape
+def attend(raw, scales, gains, lengths):
+    seq_rows = raw.shape[0]
+    span = raw.shape[1] // 3
     heads = span // HEAD_DIM
     reach = min(WINDOW + ROWS, seq_rows)
     count = lengths.shape[0]
     ends = jnp.cumsum(lengths)
-    tile = pl.BlockSpec((ROWS, HEAD_DIM), lambda h, i, ends: (i, h))
-    whole = pl.BlockSpec((seq_rows, HEAD_DIM), lambda h, i, ends: (0, h))
-    shape = jax.ShapeDtypeStruct((seq_rows, span), jnp.bfloat16)
+    cosine, sine = rope_tables(jnp.arange(seq_rows, dtype=jnp.int32), HEAD_DIM)
+    sign = jnp.where(jnp.arange(HEAD_DIM) < HEAD_DIM // 2, -1.0, 1.0)
+    cosine, sine = cosine[:, 0], sine[:, 0] * sign
+
+    def tile(group=0):
+        return pl.BlockSpec((ROWS, HEAD_DIM), lambda h, i, ends: (i, group * heads + h))
+
+    def whole(group=0):
+        return pl.BlockSpec((seq_rows, HEAD_DIM), lambda h, i, ends: (0, group * heads + h))
+
+    def fixed(array):
+        return pl.BlockSpec(array.shape, lambda h, i, ends: (0, 0))
+
     pairs = seq_rows * heads * reach
 
-    def call(kernel, ins, outs, scratch, name):
+    def call(kernel, ins, outs, types, scratch, name):
         return pl.pallas_call(
             kernel,
             grid_spec=pltpu.PrefetchScalarGridSpec(
@@ -1264,30 +1299,41 @@
                 out_specs=outs,
                 scratch_shapes=scratch,
             ),
-            out_shape=[shape] * len(outs),
+            out_shape=[jax.ShapeDtypeStruct((seq_rows, span), t) for t in types],
             compiler_params=pltpu.CompilerParams(
-                dimension_semantics=("arbitrary", "arbitrary"), vmem_limit_bytes=48 * 2**20
+                dimension_semantics=("arbitrary", "arbitrary"), vmem_limit_bytes=56 * 2**20
             ),
             cost_estimate=pl.CostEstimate(
                 flops=4 * len(outs) * pairs * HEAD_DIM,
-                bytes_accessed=8 * seq_rows * span,
+                bytes_accessed=16 * seq_rows * span,
                 transcendentals=pairs,
             ),
             name=name,
         )
 
-    attended = call(
-        functools.partial(attend_kernel, count, reach), [tile, whole, whole], [tile], [], "attend"
-    )(ends, query, key, value)[0]
+    b16, f32 = jnp.bfloat16, jnp.float32
+    tables = [fixed(cosine), fixed(sine)]
+    row_scales = scales.T
+    attended, query, key, value = call(
+        functools.partial(attend_kernel, count, reach),
+        [tile(0), whole(1), whole(2), fixed(row_scales)]
+        + [pl.BlockSpec((2, HEAD_DIM), lambda h, i, ends: (0, h))]
+        + tables,
+        [tile(), tile(), whole(), whole()],
+        [b16] * 4,
+        [],
+        "attend",
+    )(ends, raw, raw, raw, row_scales, gains, cosine, sine)
 
     def back(grad):
         return call(
             functools.partial(attend_back_kernel, count, reach),
-            [tile, whole, whole, tile],
-            [tile, whole, whole],
-            [pltpu.VMEM((seq_rows, HEAD_DIM), jnp.float32)] * 2,
+            [tile(), whole(), whole(), tile()] + tables,
+            [tile(), whole(), whole()],
+            [f32, f32, b16],
+            [pltpu.VMEM((seq_rows, HEAD_DIM), f32)] * 2,
             "attend_back",
-        )(ends, query, key, value, grad)
+        )(ends, query, key, value, grad, cosine, sine)
 
     return attended, back
 
@@ -1406,19 +1452,10 @@
     )
     qkv_raw = jnp.dot(attn_in, qkv_mat, preferred_element_type=jnp.float32)
     raw = (qkv_raw[:, :span], qkv_raw[:, span : 2 * span])
-    value_heads = qkv_raw[:, 2 * span :].astype(jnp.bfloat16)
     squares = sum_over_sp([jnp.sum(r * r, axis=-1) for r in raw], sp_count, 7, "sum_squares")
-    scales = lax.rsqrt(squares / width + eps)[:, :, None]
-    cosine, sine = rope_tables(jnp.arange(seq_rows, dtype=jnp.int32), HEAD_DIM)
-
-    def turned(normed):
-        return rotate_pairs(
-            normed.reshape(seq_rows, head_local, HEAD_DIM), cosine, sine
-        ).reshape(seq_rows, span)
-
-    query_heads = turned(raw[0] * scales[0] * gain_query).astype(jnp.bfloat16)
-    key_heads = turned(raw[1] * scales[1] * gain_key).astype(jnp.bfloat16)
-    attended_heads, attend_back = attend(query_heads, key_heads, value_heads, doc_lengths[0])
+    scales = lax.rsqrt(squares / width + eps)
+    attended_heads, attend_back = attend(qkv_raw, scales, own_cols[1:3], doc_lengths[0])
+    scales = scales[:, :, None]
     attended_tok = lax.all_to_all(
         attended_heads, "sp", split_axis=0, concat_axis=1, tiled=True
     )
@@ -1476,13 +1513,7 @@
     )
     attended_grad_heads, row_sums = lax.optimization_barrier((attended_grad_heads, row_sums))
     rows_every = lax.all_gather(row_sums.astype(jnp.bfloat16), "sp", axis=0, tiled=True)
-    query_grad_heads, key_grad_heads, value_low = attend_back(attended_grad_heads)
-
-    def unturned(grad):
-        shaped = grad.astype(jnp.float32).reshape(seq_rows, head_local, HEAD_DIM)
-        return rotate_pairs(shaped, cosine, -sine).reshape(seq_rows, span)
-
-    normed_grads = (unturned(query_grad_heads), unturned(key_grad_heads))
+    *normed_grads, value_low = attend_back(attended_grad_heads)
     scaled_grads = (normed_grads[0] * gain_query, normed_grads[1] * gain_key)
     products = sum_over_sp(
         [jnp.sum(g * r, axis=-1) for g, r in zip(scaled_grads, raw)], sp_count, 8, "sum_products"

time: 1410 us -> 1390 us (0.986)
  other arithmetic: 80 us -> 52.1 us
    neg x5 -> x0, other arithmetic: 19.1 us -> none  [the longest x4 13.8 us: rotate_pairs(): -values[..., half_dim:]]
    unnamed x169 -> x121, local copies, waits for them, and re-layouts: 42.7 us -> 40.4 us
  transfers between devices with their start and end apart: 6 -> 6, of which waited for: 1 -> 2; matrix products, arithmetic and copies ran while one was open for 9% -> 7% of each run, Pallas kernels for 43% -> 47%
where the time goes in v6:
time: 1390 us
  Pallas kernels  1120 us (81%)
  local copies, waits for them, and re-layouts  63.5 us (5%)
  waiting for transfers between devices  55.4 us (4%)
  matrix products  54.1 us (4%)
  other arithmetic  52.1 us (4%)
  between operations  15 us (1%)
  blocking collectives  14 us (1%)
    pallas_call x2, Pallas kernels, combine_sum(): pl.pallas_call(functools.partial(combine_scatter_kernel, counts, parts),...  387 us
    pallas_call x1, Pallas kernels, gather_and_dispatch(): pl.pallas_call(functools.partial(dispatch_kernel, counts, parts), in_spec...  162 us
    pallas_call x1, Pallas kernels, gather_two(): pl.pallas_call(functools.partial(gather_two_kernel, counts, parts, side_c...  151 us
    pallas_call x1, Pallas kernels, run_experts(): pl.pallas_call(expert_kernel, grid_spec=pltpu.PrefetchScalarGridSpec(num_...  128 us
    pallas_call x1, Pallas kernels, scatter_and_grads(): pl.pallas_call(functools.partial(scatter_grads_kernel, counts, parts), in...  115 us
    pallas_call x2, Pallas kernels, scatter_sum(): pl.pallas_call(functools.partial(scatter_kernel, counts, parts, fsdp_too)...  71.2 us
    pallas_call x3, Pallas kernels, small_sum(): pl.pallas_call(functools.partial(small_sum_kernel, (sp_count, fs_count)),...  49.4 us
    all_to_all x1, waiting for transfers between devices, local(): lax.all_to_all(attended_heads, 'sp', split_axis=0, concat_axis=1, tiled=T...  46.6 us
  transfers between devices with their start and end apart: 6, of which 2 were waited for; matrix products, arithmetic and copies ran while one was open for 7% of the time, Pallas kernels for 47%

profile of v6, /device:TPU:0, one launch (start us, length us, event | category | flops | bytes accessed | tf_op | source)
XLA Modules:
  0.0 1385.7 jit_solution(12047995661340564576)
XLA Ops:
  7.3 1.1 constant_dynamic-slice_fusion.3
  8.3 1.1 constant_dynamic-slice_fusion.1
  9.4 0.9 pad_maximum_fusion.4
  10.6 1.1 fusion.22
  12.5 6.2 all_gather.21
  20.3 1.3 fusion.11.in_ref
  21.6 151.3 %gather_attn_in.1 = (bf16[1,1,4,2,256,2048]{5,4,3,2,1,0:T(8,128)(2,1)}, bf16[2,2,512,2048]{3,2,1,0:T(8,128)(2,1)}) custom-call(bf16[256,2048]{1,0:T(8,128)(2,1)} %fusion.11.in_ref, bf16[512,2048]{1,0:T(8,128)(2,1)} %side_in.1), custom_call_target="tpu_custom_call" | custom-call | bytes 16777216 | tf_op jit(solution)/shard_map/gather_attn_in/pallas_call | solution.py:936
  173.2 4.9 sine_multiply_fusion
  178.1 10.1 fusion.46.q_ref.k_ref.v_ref
  188.2 2.6 copy-done.3
  192.1 26.7 %sum_squares.1 = f32[32,128]{1,0:T(8,128)} custom-call(f32[32,128]{1,0:T(8,128)} %reshape.267.part_ref), custom_call_target="tpu_custom_call" | custom-call | tf_op jit(solution)/shard_map/sum_squares/pallas_call | solution.py:1168
  219.5 1.3 copy.135
  220.9 26.8 %attend.1 = (bf16[2048,256]{1,0:T(8,128)(2,1)}, bf16[2048,256]{1,0:T(8,128)(2,1)}, bf16[2048,256]{1,0:T(8,128)(2,1)}, bf16[2048,256]{1,0:T(8,128)(2,1)}) custom-call(s32[4]{0:T(128)} %bitcast.167, f32[2048,768]{1,0:T(8,128)} %copy-done.3, f32[2048,768]{1,0:T(8,128)} %copy-done.3, f32[2048,768]{1,0:T(8,128)} %copy-done.3, f32[2048,2]{1,0:T(8,128)} %bitcast.135, ...), custom_call_target="tpu_custom_call" | custom-call | flops 10737418240 | bytes 8388608 | tf_op jit(solution)/shard_map/attend/pallas_call | solution.py:1317
  247.7 5.1 all-to-all-start
  252.8 7.8 all_gather.24
  260.6 46.6 %all-to-all-done = bf16[8,256,256]{2,1,0:T(8,128)(2,1)S(1)} async-done(((bf16[8,256,256]{2,1,0:T(8,128)(2,1)}), bf16[8,256,256]{2,1,0:T(8,128)(2,1)S(1)}, u32[]{:S(2)}, u32[]{:S(2)}) %all-to-all-start) | async-done | bytes 1048608 | tf_op jit(solution)/shard_map/all_to_all | solution.py:1459
  307.4 6.9 multiply_reduce_fusion.6
  316.6 1.9 concatenate.24.in_ref
  318.5 8.7 all-gather.8.cloned.1.call-done
  327.2 4.0 slice_convert_fusion.1
  331.2 2.8 copy.141
  334.0 0.8 compare_reduce_fusion
  336.2 0.8 select_bitcast_fusion.rank_ref
  337.7 161.6 %gather_ffn_in.1 = (bf16[8,32,64,2176]{3,2,1,0:T(8,128)(2,1)}, bf16[8,32,64,2048]{3,2,1,0:T(8,128)(2,1)}) custom-call(bf16[256,2176]{1,0:T(8,128)(2,1)} %concatenate.24.in_ref, bf16[32,256,2176]{2,1,0:T(8,128)(2,1)} %bitcast.144, s32[32,8,256]{2,1,0:T(8,128)} %select_bitcast_fusion.rank_ref), custom_call_target="tpu_custom_call" | custom-call | flops 35433480192 | bytes 142606336 | tf_op jit(solution)/shard_map/gather_ffn_in/pallas_call | solution.py:1085
  499.4 128.1 %experts.1 = (bf16[8,2048,2176]{2,1,0:T(8,128)(2,1)}, bf16[8,2048,2048]{2,1,0:T(8,128)(2,1)}, bf16[8,2048,256]{2,1,0:T(8,128)(2,1)}, bf16[8,2048,256]{2,1,0:T(8,128)(2,1)}, bf16[8,2048,256]{2,1,0:T(8,128)(2,1)}) custom-call(s32[16]{0:T(128)} %reshape.288.live, s32[1]{0:T(128)} %bitcast.20.first, bf16[8,2048,2176]{2,1,0:T(8,128)(2,1)} %bitcast.24.x_ref, ...), custom_call_target="tpu_custom_call" | custom-call | flops 103079215104 | bytes 268435456 | tf_op jit(solution)/shard_map/experts/pallas_call | solution.py:143
  627.5 187.4 %scatter_grads.1 = f32[256,2176]{1,0:T(8,128)} custom-call(bf16[8,32,64,2176]{3,2,1,0:T(8,128)(2,1)} %bitcast.28.rows_ref, s32[32,8,256]{2,1,0:T(8,128)} %select_bitcast_fusion.rank_ref), custom_call_target="tpu_custom_call" | custom-call | flops 18253611008 | bytes 71303168 | tf_op jit(solution)/shard_map/scatter_grads/pallas_call | solution.py:689
  814.9 1.1 multiply_reduce_fusion.9
  816.1 1.1 multiply_convert_fusion.1
  817.2 3.1 multiply_reduce_fusion
  820.4 1.3 copy-done.4
  822.4 1.2 copy-done.45
  823.6 2.4 convolution_convert_fusion.3
  826.0 1.0 copy.163
  827.0 3.6 all-to-all-start.1
  830.6 0.8 fusion.43
  831.4 8.7 convolution_convert_fusion
  840.1 47.8 %scatter_out_rows.1 = f32[64,2176]{1,0:T(8,128)} custom-call(bf16[2,2,4,2,64,2176]{5,4,3,2,1,0:T(8,128)(2,1)} %bitcast.121), custom_call_target="tpu_custom_call" | custom-call | flops 4456448 | bytes 8912896 | tf_op jit(solution)/shard_map/scatter_out_rows/pallas_call | solution.py:718
  887.9 2.2 convert_element_type.178
  890.2 32.0 %attend_back.1 = (f32[2048,256]{1,0:T(8,128)}, f32[2048,256]{1,0:T(8,128)}, bf16[2048,256]{1,0:T(8,128)(2,1)}) custom-call(s32[4]{0:T(128)} %bitcast.168, bf16[2048,256]{1,0:T(8,128)(2,1)} %get-tuple-element.43.q_ref, bf16[2048,256]{1,0:T(8,128)(2,1)} %get-tuple-element.44.k_ref, bf16[2048,256]{1,0:T(8,128)(2,1)} %get-tuple-element.45.v_ref, ...), custom_call_target="tpu_custom_call" | custom-call | flops 8053063680 | bytes 8388608 | tf_op jit(solution)/shard_map/attend_back/pallas_call | solution.py:1329
  922.2 3.2 multiply_reduce_fusion.2
  926.0 9.0 sum_products.1
  935.7 5.0 subtract_convert_fusion.1
  940.7 10.9 convolution_convert_fusion.2
  951.6 23.4 %scatter_qkv.1 = f32[512,768]{1,0:T(8,128)} custom-call(bf16[2,2,1,1,512,768]{5,4,3,2,1,0:T(8,128)(2,1)} %bitcast.127), custom_call_target="tpu_custom_call" | custom-call | flops 1572864 | bytes 3145728 | tf_op jit(solution)/shard_map/scatter_qkv/pallas_call | solution.py:718
  975.0 2.4 convert_element_type.168
  977.4 199.7 %scatter_outputs.1 = f32[256,2048]{1,0:T(8,128)} custom-call(bf16[8,32,64,2048]{3,2,1,0:T(8,128)(2,1)} %bitcast.26.rows_ref, s32[32,8,256]{2,1,0:T(8,128)} %select_bitcast_fusion.rank_ref), custom_call_target="tpu_custom_call" | custom-call | flops 17179869184 | bytes 67108864 | tf_op jit(solution)/shard_map/scatter_outputs/pallas_call | solution.py:689
  1177.1 11.2 convolution_convert_fusion.1
  1188.3 115.5 %scatter_attn_in.1 = (f32[256,2048]{1,0:T(8,128)}, f32[8,2048,256]{2,1,0:T(8,128)}, f32[8,2048,256]{2,1,0:T(8,128)}, f32[8,2048,256]{2,1,0:T(8,128)}) custom-call(bf16[1,1,4,2,256,2048]{5,4,3,2,1,0:T(8,128)(2,1)} %bitcast.166, bf16[8,2048,2176]{2,1,0:T(8,128)(2,1)} %bitcast.24.x_ref, bf16[8,2048,2048]{2,1,0:T(8,128)(2,1)} %bitcast.25.c_ref, ...), custom_call_target="tpu_custom_call" | custom-call | flops 51539607552 | bytes 134217728 | tf_op jit(solution)/shard_map/scatter_attn_in/pallas_call | solution.py:568
  1303.9 2.4 fusion.12
  1307.0 13.8 sum_gains.1
  1322.2 5.9 fusion.15
  1328.1 0.9 slice_convert_fusion.2
  1329.8 4.1 slice_convert_fusion
  1333.9 4.4 convert_bitcast_fusion
  1338.3 2.6 copy.161
  1341.0 2.6 copy.160
  1343.6 2.8 copy.159
  1346.4 13.2 copy.169
  1359.6 0.8 slice-done.8
  1360.4 1.5 slice-done.9
  1361.9 8.5 copy.170
  1370.4 0.9 slice-done.4
  1371.3 1.4 slice-done.5
  1372.7 6.2 copy.171
  (180 shorter events, 14.7 us)
Async XLA Ops:
  7.2 3.3 copy-start.38
  7.2 170.9 %all-gather.6.cloned.1.call-start = ((), (), s32[]{:S(2)}) async-start(), calls=%async_computation.2 | async-start | bytes 3932160 | tf_op jit(solution)/shard_map/all_gather | solution.py:1437
  7.2 3.4 copy-start.7
  10.3 1.4 copy-start.46
  10.3 2.1 copy-start.41
  10.3 2.1 copy-start.42
  10.3 2.1 copy-start.43
  10.3 2.1 copy-start.44
  10.4 9.0 copy-start.5
  10.4 316.8 %all-gather.8.cloned.1.call-start = ((), (), s32[]{:S(2)}) async-start(), calls=%async_computation.3 | async-start | bytes 36765696 | tf_op jit(solution)/shard_map/all_gather | solution.py:1440
  18.7 154.1 %copy-start.26 = (bf16[4,2048]{1,0:T(4,128)(2,1)}, bf16[4,2048]{1,0:T(4,128)(2,1)S(1)}, u32[]{:S(2)}) copy-start(bf16[4,2048]{1,0:T(4,128)(2,1)S(1)} %all_gather.21) | copy-start | bytes 49156
  19.6 0.6 copy-start.36
  20.2 152.6 %copy-start.34 = (f32[256]{0:T(256)}, f32[256]{0:T(256)S(1)}, u32[]{:S(2)}) copy-start(f32[256]{0:T(256)S(1)} %fusion.32) | copy-start | bytes 3076
  20.3 152.6 %copy-start.24 = (f32[1,2048]{1,0:T(1,128)}, f32[1,2048]{1,0:T(1,128)S(1)}, u32[]{:S(2)}) copy-start(f32[1,2048]{1,0:T(1,128)S(1)} %get-tuple-element.192) | copy-start | bytes 24580
  20.3 294.1 %copy-start.22 = (f32[1,2048]{1,0:T(1,128)}, f32[1,2048]{1,0:T(1,128)S(1)}, u32[]{:S(2)}) copy-start(f32[1,2048]{1,0:T(1,128)S(1)} %get-tuple-element.191) | copy-start | bytes 24580
  188.2 2.6 copy-start.3
  219.5 28.2 %copy-start.20 = (f32[32,128]{1,0:T(8,128)}, f32[32,128]{1,0:T(8,128)S(1)}, u32[]{:S(2)}) copy-start(f32[32,128]{1,0:T(8,128)S(1)} %add_rsqrt_fusion) | copy-start | bytes 49156
  247.7 5.1 copy-start.27
  247.7 59.5 %all-to-all-start = ((bf16[8,256,256]{2,1,0:T(8,128)(2,1)}), bf16[8,256,256]{2,1,0:T(8,128)(2,1)S(1)}, u32[]{:S(2)}, u32[]{:S(2)}) async-start(bf16[8,256,256]{2,1,0:T(8,128)(2,1)} %bitcast.134), calls=%async_computation | async-start | bytes 2097152 | tf_op jit(solution)/shard_map/all_to_all | solution.py:1459
  260.6 54.0 %copy-start.13 = (bf16[2048,64]{0,1:T(8,128)(2,1)}, bf16[2048,64]{0,1:T(8,128)(2,1)S(1)}, u32[]{:S(2)}) copy-start(bf16[2048,64]{0,1:T(8,128)(2,1)S(1)} %all_gather.24) | copy-start | bytes 786436
  307.4 6.9 copy-start.16
  314.3 1.3 copy-start
  314.3 1.3 copy-start.39
  314.3 1.3 copy-start.30
  314.6 3.9 copy-start.9
  315.6 15.6 %copy-start.28 = (f32[256]{0:T(256)}, f32[256]{0:T(256)S(1)}, u32[]{:S(2)}) copy-start(f32[256]{0:T(256)S(1)} %get-tuple-element.195) | copy-start | bytes 3076
  315.7 15.5 %copy-start.11 = (f32[256,64]{1,0:T(8,128)}, f32[256,64]{1,0:T(8,128)S(1)}, u32[]{:S(2)}) copy-start(f32[256,64]{1,0:T(8,128)S(1)} %copy.147) | copy-start | bytes 196612
  315.9 0.6 copy-start.32
  627.5 187.4 %copy-start.12 = (f32[256,64]{1,0:T(8,128)S(1)}, f32[256,64]{1,0:T(8,128)}, u32[]{:S(2)}) copy-start(f32[256,64]{1,0:T(8,128)} %copy-done.11) | copy-start | bytes 196612
  627.5 187.4 %copy-start.29 = (f32[256]{0:T(256)S(1)}, f32[256]{0:T(256)}, u32[]{:S(2)}) copy-start(f32[256]{0:T(256)} %copy-done.28) | copy-start | bytes 3076
  627.5 187.4 %copy-start.33 = (f32[256]{0:T(256)S(1)}, f32[256]{0:T(256)}, u32[]{:S(2)}) copy-start(f32[256]{0:T(256)} %copy-done.32) | copy-start | bytes 3076
  627.5 189.7 %copy-start.14 = (bf16[2048,64]{0,1:T(8,128)(2,1)S(1)}, bf16[2048,64]{0,1:T(8,128)(2,1)}, u32[]{:S(2)}) copy-start(bf16[2048,64]{0,1:T(8,128)(2,1)} %copy-done.13) | copy-start | bytes 786436
  627.5 189.7 %copy-start.23 = (f32[1,2048]{1,0:T(1,128)S(1)}, f32[1,2048]{1,0:T(1,128)}, u32[]{:S(2)}) copy-start(f32[1,2048]{1,0:T(1,128)} %copy-done.22) | copy-start | bytes 24580
  627.5 189.6 %copy-start.31 = (f32[256]{0:T(256)S(1)}, f32[256]{0:T(256)}, u32[]{:S(2)}) copy-start(f32[256]{0:T(256)} %copy-done.30) | copy-start | bytes 3076
  817.2 3.2 copy-start.40
  817.2 4.5 copy-start.1
  817.2 4.5 copy-start.8
  817.2 6.3 copy-start.45
  820.4 1.3 copy-start.4
  823.6 2.4 copy-start.19
  825.9 5.5 copy-start.21
  825.9 5.5 copy-start.10
  826.0 5.5 copy-start.17
  827.0 60.9 %all-to-all-start.1 = ((bf16[256,8,256]{2,0,1:T(8,128)(2,1)}), bf16[256,8,256]{2,0,1:T(8,128)(2,1)S(1)}, u32[]{:S(2)}, u32[]{:S(2)}) async-start(bf16[256,8,256]{2,0,1:T(8,128)(2,1)} %bitcast.113), calls=%async_computation.1 | async-start | bytes 2097152 | tf_op jit(solution)/shard_map/all_to_all | solution.py:1496
  830.6 497.5 %all-gather.10.cloned.1.call-start = ((), (), s32[]{:S(2)}) async-start(), calls=%async_computation.4 | async-start | bytes 2506752 | tf_op jit(solution)/shard_map/all_gather | solution.py:1515
  887.9 2.3 copy-start.18
  890.1 443.8 %all-gather.12.cloned.1.call-start = ((), (), s32[]{:S(2)}) async-start(), calls=%async_computation.5 | async-start | bytes 7077888 | tf_op jit(solution)/shard_map/all_gather | solution.py:1533
  890.2 32.0 %slice-start = ((s8[6291456]{0:T(1024)(128)(4,1)}), s8[4194304]{0:T(1024)(128)(4,1)S(1)}, s32[]{:S(2)}) async-start(s8[6291456]{0:T(1024)(128)(4,1)} %bitcast.114), calls=%async_computation.6 | async-start | bytes 8388608
  890.2 32.0 %slice-start.1 = ((s8[6291456]{0:T(1024)(128)(4,1)}), s8[2097152]{0:T(1024)(128)(4,1)S(1)}, s32[]{:S(2)}) async-start(s8[6291456]{0:T(1024)(128)(4,1)} %bitcast.114), calls=%async_computation.7 | async-start | bytes 4194304
  935.7 5.0 copy-start.47
  940.7 10.9 copy-start.15
  1188.3 115.6 %copy-start.6 = (bf16[1,256,2048]{2,1,0:T(8,128)(2,1)S(1)}, bf16[1,256,2048]{2,1,0:T(8,128)(2,1)}, u32[]{:S(2)}) copy-start(bf16[1,256,2048]{2,1,0:T(8,128)(2,1)} %param.16) | copy-start | bytes 3145732
  1188.3 115.6 %copy-start.25 = (f32[1,2048]{1,0:T(1,128)S(1)}, f32[1,2048]{1,0:T(1,128)}, u32[]{:S(2)}) copy-start(f32[1,2048]{1,0:T(1,128)} %copy-done.24) | copy-start | bytes 24580
  1188.3 115.6 %copy-start.35 = (f32[256]{0:T(256)S(1)}, f32[256]{0:T(256)}, u32[]{:S(2)}) copy-start(f32[256]{0:T(256)} %copy-done.34) | copy-start | bytes 3076
  1303.8 18.4 %copy-start.37 = (f32[256]{0:T(256)S(1)}, f32[256]{0:T(256)}, u32[]{:S(2)}) copy-start(f32[256]{0:T(256)} %copy-done.36) | copy-start | bytes 3076
  1303.8 18.4 %copy-start.2 = (f32[256,2048]{1,0:T(8,128)S(1)}, f32[256,2048]{1,0:T(8,128)}, u32[]{:S(2)}) copy-start(f32[256,2048]{1,0:T(8,128)} %copy-done) | copy-start | bytes 6291460
  1343.6 15.9 %slice-start.6 = ((s8[16777216]{0:T(1024)(128)(4,1)}), s8[4194304]{0:T(1024)(128)(4,1)S(1)}, s32[]{:S(2)}) async-start(s8[16777216]{0:T(1024)(128)(4,1)} %bitcast.118), calls=%async_computation.12 | async-start | bytes 8388608
  1346.4 13.2 slice-start.7
  1346.4 14.0 %slice-start.8 = ((s8[16777216]{0:T(1024)(128)(4,1)}), s8[4194304]{0:T(1024)(128)(4,1)S(1)}, s32[]{:S(2)}) async-start(s8[16777216]{0:T(1024)(128)(4,1)} %bitcast.118), calls=%async_computation.14 | async-start | bytes 8388608
  1346.4 15.5 %slice-start.9 = ((s8[16777216]{0:T(1024)(128)(4,1)}), s8[4194304]{0:T(1024)(128)(4,1)S(1)}, s32[]{:S(2)}) async-start(s8[16777216]{0:T(1024)(128)(4,1)} %bitcast.118), calls=%async_computation.15 | async-start | bytes 8388608
  1346.4 24.0 %slice-start.2 = ((s8[16777216]{0:T(1024)(128)(4,1)}), s8[4194304]{0:T(1024)(128)(4,1)S(1)}, s32[]{:S(2)}) async-start(s8[16777216]{0:T(1024)(128)(4,1)} %bitcast.116), calls=%async_computation.8 | async-start | bytes 8388608
  1346.4 24.0 %slice-start.3 = ((s8[16777216]{0:T(1024)(128)(4,1)}), s8[4194304]{0:T(1024)(128)(4,1)S(1)}, s32[]{:S(2)}) async-start(s8[16777216]{0:T(1024)(128)(4,1)} %bitcast.116), calls=%async_computation.9 | async-start | bytes 8388608
  1361.9 9.4 slice-start.4
  1361.9 10.8 slice-start.5
Sparse Core Ops, SparseCore 0:
  10.5 43.2 all-gather.5
  57.3 269.8 all-gather.7
  890.2 51.0 all-gather.9
  977.5 165.3 all-gather.11

commit v7 on v6

--- a/solution.py
+++ b/solution.py
@@ -535,7 +535,7 @@
                     copy.wait()
 
             for k in range(3):
-                self.stage[k] = self.acc[k].T
+                self.stage[k] = self.acc[k].T.astype(self.stage.dtype)
             for copy in self.stores(e):
                 copy.start()
 
@@ -564,7 +564,7 @@
     depth = 512
     b16 = jnp.bfloat16
     anywhere = pl.BlockSpec(memory_space=pl.ANY)
-    weight = jax.ShapeDtypeStruct((experts, width, hidden), jnp.float32)
+    weight = jax.ShapeDtypeStruct((experts, width, hidden), b16)
     return pl.pallas_call(
         functools.partial(scatter_grads_kernel, counts, parts),
         in_specs=[anywhere] * 6,
@@ -575,7 +575,7 @@
             pltpu.VMEM((2, depth, width), b16),
             pltpu.VMEM((2, 3, depth, hidden), b16),
             pltpu.VMEM((3, hidden, width), jnp.float32),
-            pltpu.VMEM((3, width, hidden), jnp.float32),
+            pltpu.VMEM((3, width, hidden), b16),
             pltpu.SemaphoreType.DMA((2, 5)),
             pltpu.SemaphoreType.DMA((3,)),
             pltpu.VMEM((1, 1, 1, 1, 16, 128), b16),
@@ -1570,9 +1570,9 @@
         dense[2],
         rows_every[:, :width].astype(jnp.float32),
         rows_every[:, width : width + EXPERTS].astype(jnp.float32),
-        grad_gate,
-        grad_up,
-        grad_down,
+        grad_gate.astype(jnp.float32),
+        grad_up.astype(jnp.float32),
+        grad_down.astype(jnp.float32),
     )
 
 

time: 1390 us -> 1390 us (level)
  other arithmetic: 52.1 us -> 84.4 us
  local copies, waits for them, and re-layouts: 63.5 us -> 31.4 us
    convert_element_type x0 -> x3, other arithmetic: none -> 33.3 us  [the longest x1 11.2 us: local(): grad_down.astype(jnp.float32)]
    unnamed x121 -> x114, local copies, waits for them, and re-layouts: 40.4 us -> 8.37 us
  transfers between devices with their start and end apart: 6 -> 6, of which waited for: 2 -> 2; matrix products, arithmetic and copies ran while one was open for 7% -> 9% of each run, Pallas kernels for 47% -> 46%
where the time goes in v7:
time: 1390 us; the launch traced here: 1380 us
  Pallas kernels  1120 us (81%)
  other arithmetic  84.4 us (6%)
  waiting for transfers between devices  55.4 us (4%)
  matrix products  54.1 us (4%)
  local copies, waits for them, and re-layouts  31.4 us (2%)
  between operations  15 us (1%)
  blocking collectives  14 us (1%)
    pallas_call x2, Pallas kernels, combine_sum(): pl.pallas_call(functools.partial(combine_scatter_kernel, counts, parts),...  386 us
    pallas_call x1, Pallas kernels, gather_and_dispatch(): pl.pallas_call(functools.partial(dispatch_kernel, counts, parts), in_spec...  162 us
    pallas_call x1, Pallas kernels, gather_two(): pl.pallas_call(functools.partial(gather_two_kernel, counts, parts, side_c...  151 us
    pallas_call x1, Pallas kernels, run_experts(): pl.pallas_call(expert_kernel, grid_spec=pltpu.PrefetchScalarGridSpec(num_...  128 us
    pallas_call x1, Pallas kernels, scatter_and_grads(): pl.pallas_call(functools.partial(scatter_grads_kernel, counts, parts), in...  112 us
    pallas_call x2, Pallas kernels, scatter_sum(): pl.pallas_call(functools.partial(scatter_kernel, counts, parts, fsdp_too)...  71.1 us
    pallas_call x3, Pallas kernels, small_sum(): pl.pallas_call(functools.partial(small_sum_kernel, (sp_count, fs_count)),...  50.3 us
    all_to_all x1, waiting for transfers between devices, local(): lax.all_to_all(attended_heads, 'sp', split_axis=0, concat_axis=1, tiled=T...  46.6 us
  transfers between devices with their start and end apart: 6, of which 2 were waited for; matrix products, arithmetic and copies ran while one was open for 9% of the time, Pallas kernels for 46%

profile of v7, /device:TPU:0, one launch (start us, length us, event | category | flops | bytes accessed | tf_op | source)
XLA Modules:
  0.0 1383.3 jit_solution(14831676874230771256)
XLA Ops:
  7.3 1.1 constant_dynamic-slice_fusion.3
  8.3 1.1 constant_dynamic-slice_fusion.1
  9.4 0.9 pad_maximum_fusion.4
  10.6 1.1 fusion.22
  12.5 6.2 all_gather.21
  20.8 1.3 fusion.11.in_ref
  22.1 151.3 %gather_attn_in.1 = (bf16[1,1,4,2,256,2048]{5,4,3,2,1,0:T(8,128)(2,1)}, bf16[2,2,512,2048]{3,2,1,0:T(8,128)(2,1)}) custom-call(bf16[256,2048]{1,0:T(8,128)(2,1)} %fusion.11.in_ref, bf16[512,2048]{1,0:T(8,128)(2,1)} %side_in.1), custom_call_target="tpu_custom_call" | custom-call | bytes 16777216 | tf_op jit(solution)/shard_map/gather_attn_in/pallas_call | solution.py:936
  173.7 4.9 sine_multiply_fusion
  178.6 10.1 fusion.46.q_ref.k_ref.v_ref
  188.7 2.6 copy-done.3
  192.5 26.7 %sum_squares.1 = f32[32,128]{1,0:T(8,128)} custom-call(f32[32,128]{1,0:T(8,128)} %reshape.267.part_ref), custom_call_target="tpu_custom_call" | custom-call | tf_op jit(solution)/shard_map/sum_squares/pallas_call | solution.py:1168
  219.3 0.7 add_rsqrt_fusion
  220.0 1.3 copy.135
  221.4 26.8 %attend.1 = (bf16[2048,256]{1,0:T(8,128)(2,1)}, bf16[2048,256]{1,0:T(8,128)(2,1)}, bf16[2048,256]{1,0:T(8,128)(2,1)}, bf16[2048,256]{1,0:T(8,128)(2,1)}) custom-call(s32[4]{0:T(128)} %bitcast.163, f32[2048,768]{1,0:T(8,128)} %copy-done.3, f32[2048,768]{1,0:T(8,128)} %copy-done.3, f32[2048,768]{1,0:T(8,128)} %copy-done.3, f32[2048,2]{1,0:T(8,128)} %bitcast.131, ...), custom_call_target="tpu_custom_call" | custom-call | flops 10737418240 | bytes 8388608 | tf_op jit(solution)/shard_map/attend/pallas_call | solution.py:1317
  248.2 5.1 all-to-all-start
  253.3 7.8 all_gather.24
  261.1 46.6 %all-to-all-done = bf16[8,256,256]{2,1,0:T(8,128)(2,1)S(1)} async-done(((bf16[8,256,256]{2,1,0:T(8,128)(2,1)}), bf16[8,256,256]{2,1,0:T(8,128)(2,1)S(1)}, u32[]{:S(2)}, u32[]{:S(2)}) %all-to-all-start) | async-done | bytes 1048608 | tf_op jit(solution)/shard_map/all_to_all | solution.py:1459
  307.9 6.9 multiply_reduce_fusion.6
  317.1 1.9 concatenate.24.in_ref
  319.0 8.7 all-gather.8.cloned.1.call-done
  327.7 4.0 slice_convert_fusion.1
  331.7 2.8 copy.141
  334.5 0.8 compare_reduce_fusion
  335.9 0.7 fusion.39
  336.7 0.9 select_bitcast_fusion.rank_ref
  338.3 161.7 %gather_ffn_in.1 = (bf16[8,32,64,2176]{3,2,1,0:T(8,128)(2,1)}, bf16[8,32,64,2048]{3,2,1,0:T(8,128)(2,1)}) custom-call(bf16[256,2176]{1,0:T(8,128)(2,1)} %concatenate.24.in_ref, bf16[32,256,2176]{2,1,0:T(8,128)(2,1)} %bitcast.140, s32[32,8,256]{2,1,0:T(8,128)} %select_bitcast_fusion.rank_ref), custom_call_target="tpu_custom_call" | custom-call | flops 35433480192 | bytes 142606336 | tf_op jit(solution)/shard_map/gather_ffn_in/pallas_call | solution.py:1085
  500.0 128.1 %experts.1 = (bf16[8,2048,2176]{2,1,0:T(8,128)(2,1)}, bf16[8,2048,2048]{2,1,0:T(8,128)(2,1)}, bf16[8,2048,256]{2,1,0:T(8,128)(2,1)}, bf16[8,2048,256]{2,1,0:T(8,128)(2,1)}, bf16[8,2048,256]{2,1,0:T(8,128)(2,1)}) custom-call(s32[16]{0:T(128)} %reshape.288.live, s32[1]{0:T(128)} %bitcast.20.first, bf16[8,2048,2176]{2,1,0:T(8,128)(2,1)} %bitcast.24.x_ref, ...), custom_call_target="tpu_custom_call" | custom-call | flops 103079215104 | bytes 268435456 | tf_op jit(solution)/shard_map/experts/pallas_call | solution.py:143
  628.2 187.3 %scatter_grads.1 = f32[256,2176]{1,0:T(8,128)} custom-call(bf16[8,32,64,2176]{3,2,1,0:T(8,128)(2,1)} %bitcast.28.rows_ref, s32[32,8,256]{2,1,0:T(8,128)} %select_bitcast_fusion.rank_ref), custom_call_target="tpu_custom_call" | custom-call | flops 18253611008 | bytes 71303168 | tf_op jit(solution)/shard_map/scatter_grads/pallas_call | solution.py:689
  815.5 1.1 multiply_reduce_fusion.9
  816.6 1.1 multiply_convert_fusion.1
  817.8 3.1 multiply_reduce_fusion
  821.0 1.3 copy-done.4
  823.0 1.2 copy-done.51
  824.1 2.4 convolution_convert_fusion.3
  826.5 1.0 copy.163
  827.6 3.6 all-to-all-start.1
  831.2 0.8 fusion.43
  832.1 8.7 convolution_convert_fusion
  840.8 47.7 %scatter_out_rows.1 = f32[64,2176]{1,0:T(8,128)} custom-call(bf16[2,2,4,2,64,2176]{5,4,3,2,1,0:T(8,128)(2,1)} %bitcast.117), custom_call_target="tpu_custom_call" | custom-call | flops 4456448 | bytes 8912896 | tf_op jit(solution)/shard_map/scatter_out_rows/pallas_call | solution.py:718
  888.5 2.2 convert_element_type.187
  890.8 31.9 %attend_back.1 = (f32[2048,256]{1,0:T(8,128)}, f32[2048,256]{1,0:T(8,128)}, bf16[2048,256]{1,0:T(8,128)(2,1)}) custom-call(s32[4]{0:T(128)} %bitcast.164, bf16[2048,256]{1,0:T(8,128)(2,1)} %get-tuple-element.43.q_ref, bf16[2048,256]{1,0:T(8,128)(2,1)} %get-tuple-element.44.k_ref, bf16[2048,256]{1,0:T(8,128)(2,1)} %get-tuple-element.45.v_ref, ...), custom_call_target="tpu_custom_call" | custom-call | flops 8053063680 | bytes 8388608 | tf_op jit(solution)/shard_map/attend_back/pallas_call | solution.py:1329
  922.7 3.2 multiply_reduce_fusion.2
  926.6 9.1 sum_products.1
  936.4 5.0 subtract_convert_fusion.1
  941.3 10.9 convolution_convert_fusion.2
  952.2 23.4 %scatter_qkv.1 = f32[512,768]{1,0:T(8,128)} custom-call(bf16[2,2,1,1,512,768]{5,4,3,2,1,0:T(8,128)(2,1)} %bitcast.123), custom_call_target="tpu_custom_call" | custom-call | flops 1572864 | bytes 3145728 | tf_op jit(solution)/shard_map/scatter_qkv/pallas_call | solution.py:718
  975.6 2.4 convert_element_type.177
  978.0 199.2 %scatter_outputs.1 = f32[256,2048]{1,0:T(8,128)} custom-call(bf16[8,32,64,2048]{3,2,1,0:T(8,128)(2,1)} %bitcast.26.rows_ref, s32[32,8,256]{2,1,0:T(8,128)} %select_bitcast_fusion.rank_ref), custom_call_target="tpu_custom_call" | custom-call | flops 17179869184 | bytes 67108864 | tf_op jit(solution)/shard_map/scatter_outputs/pallas_call | solution.py:689
  1177.3 11.2 convolution_convert_fusion.1
  1188.5 112.4 %scatter_attn_in.1 = (f32[256,2048]{1,0:T(8,128)}, bf16[8,2048,256]{2,1,0:T(8,128)(2,1)}, bf16[8,2048,256]{2,1,0:T(8,128)(2,1)}, bf16[8,2048,256]{2,1,0:T(8,128)(2,1)}) custom-call(bf16[1,1,4,2,256,2048]{5,4,3,2,1,0:T(8,128)(2,1)} %bitcast.162, bf16[8,2048,2176]{2,1,0:T(8,128)(2,1)} %bitcast.24.x_ref, bf16[8,2048,2048]{2,1,0:T(8,128)(2,1)} %bitcast.25.c_ref, ...), custom_call_target="tpu_custom_call" | custom-call | flops 51539607552 | bytes 134217728 | tf_op jit(solution)/shard_map/scatter_attn_in/pallas_call | solution.py:568
  1301.0 2.3 fusion.12
  1303.9 14.5 %sum_gains.1 = f32[64,128]{1,0:T(8,128)} custom-call(f32[64,128]{1,0:T(8,128)} %reshape.283.part_ref), custom_call_target="tpu_custom_call" | custom-call | tf_op jit(solution)/shard_map/sum_gains/pallas_call | solution.py:1168
  1318.4 0.8 reshape.284
  1319.2 11.1 convert_element_type.190
  1330.3 11.1 convert_element_type.191
  1341.4 11.2 convert_element_type.192
  1353.3 5.1 fusion.15
  1358.4 0.9 slice_convert_fusion.2
  1359.3 0.8 copy.152
  1360.1 4.1 slice_convert_fusion
  1364.2 4.4 convert_bitcast_fusion
  1368.6 2.6 copy.161
  1371.2 2.6 copy.160
  1373.9 2.6 copy.159
  (174 shorter events, 12.1 us)
Async XLA Ops:
  7.2 3.3 copy-start.44
  7.2 171.4 %all-gather.6.cloned.1.call-start = ((), (), s32[]{:S(2)}) async-start(), calls=%async_computation.2 | async-start | bytes 3932160 | tf_op jit(solution)/shard_map/all_gather | solution.py:1437
  7.2 3.4 copy-start.8
  10.3 1.4 copy-start.52
  10.3 2.1 copy-start.47
  10.3 2.1 copy-start.48
  10.3 2.1 copy-start.49
  10.3 2.1 copy-start.50
  10.4 9.0 copy-start.6
  10.4 317.3 %all-gather.8.cloned.1.call-start = ((), (), s32[]{:S(2)}) async-start(), calls=%async_computation.3 | async-start | bytes 36765696 | tf_op jit(solution)/shard_map/all_gather | solution.py:1440
  18.7 1.0 copy-start.29
  19.6 0.5 copy-start.42
  19.7 0.6 copy-start.38
  20.2 0.6 copy-start.27
  20.2 294.7 %copy-start.24 = (f32[1,2048]{1,0:T(1,128)}, f32[1,2048]{1,0:T(1,128)S(1)}, u32[]{:S(2)}) copy-start(f32[1,2048]{1,0:T(1,128)S(1)} %get-tuple-element.191) | copy-start | bytes 24580
  188.7 2.6 copy-start.3
  220.0 28.2 %copy-start.22 = (f32[32,128]{1,0:T(8,128)}, f32[32,128]{1,0:T(8,128)S(1)}, u32[]{:S(2)}) copy-start(f32[32,128]{1,0:T(8,128)S(1)} %add_rsqrt_fusion) | copy-start | bytes 49156
  248.2 5.1 copy-start.30
  248.2 59.5 %all-to-all-start = ((bf16[8,256,256]{2,1,0:T(8,128)(2,1)}), bf16[8,256,256]{2,1,0:T(8,128)(2,1)S(1)}, u32[]{:S(2)}, u32[]{:S(2)}) async-start(bf16[8,256,256]{2,1,0:T(8,128)(2,1)} %bitcast.130), calls=%async_computation | async-start | bytes 2097152 | tf_op jit(solution)/shard_map/all_to_all | solution.py:1459
  261.1 54.0 %copy-start.15 = (bf16[2048,64]{0,1:T(8,128)(2,1)}, bf16[2048,64]{0,1:T(8,128)(2,1)S(1)}, u32[]{:S(2)}) copy-start(bf16[2048,64]{0,1:T(8,128)(2,1)S(1)} %all_gather.24) | copy-start | bytes 786436
  307.9 6.9 copy-start.18
  314.8 1.3 copy-start
  314.8 1.3 copy-start.45
  314.8 1.3 copy-start.33
  315.1 3.9 copy-start.11
  316.1 15.6 %copy-start.31 = (f32[256]{0:T(256)}, f32[256]{0:T(256)S(1)}, u32[]{:S(2)}) copy-start(f32[256]{0:T(256)S(1)} %get-tuple-element.195) | copy-start | bytes 3076
  316.2 15.5 %copy-start.13 = (f32[256,64]{1,0:T(8,128)}, f32[256,64]{1,0:T(8,128)S(1)}, u32[]{:S(2)}) copy-start(f32[256,64]{1,0:T(8,128)S(1)} %copy.147) | copy-start | bytes 196612
  316.4 0.6 copy-start.36
  628.1 187.3 %copy-start.14 = (f32[256,64]{1,0:T(8,128)S(1)}, f32[256,64]{1,0:T(8,128)}, u32[]{:S(2)}) copy-start(f32[256,64]{1,0:T(8,128)} %copy-done.13) | copy-start | bytes 196612
  628.2 187.3 %copy-start.32 = (f32[256]{0:T(256)S(1)}, f32[256]{0:T(256)}, u32[]{:S(2)}) copy-start(f32[256]{0:T(256)} %copy-done.31) | copy-start | bytes 3076
  628.2 187.3 %copy-start.37 = (f32[256]{0:T(256)S(1)}, f32[256]{0:T(256)}, u32[]{:S(2)}) copy-start(f32[256]{0:T(256)} %copy-done.36) | copy-start | bytes 3076
  628.2 189.5 %copy-start.16 = (bf16[2048,64]{0,1:T(8,128)(2,1)S(1)}, bf16[2048,64]{0,1:T(8,128)(2,1)}, u32[]{:S(2)}) copy-start(bf16[2048,64]{0,1:T(8,128)(2,1)} %copy-done.15) | copy-start | bytes 786436
  628.2 189.5 %copy-start.25 = (f32[1,2048]{1,0:T(1,128)S(1)}, f32[1,2048]{1,0:T(1,128)}, u32[]{:S(2)}) copy-start(f32[1,2048]{1,0:T(1,128)} %copy-done.24) | copy-start | bytes 24580
  628.2 189.5 %copy-start.34 = (f32[256]{0:T(256)S(1)}, f32[256]{0:T(256)}, u32[]{:S(2)}) copy-start(f32[256]{0:T(256)} %copy-done.33) | copy-start | bytes 3076
  817.8 3.2 copy-start.46
  817.8 4.5 copy-start.1
  817.8 4.5 copy-start.9
  817.8 6.3 copy-start.51
  820.9 1.3 copy-start.4
  821.0 2.0 copy-start.40
  824.1 2.4 copy-start.21
  826.5 5.5 copy-start.23
  826.5 5.5 copy-start.12
  826.5 5.5 copy-start.19
  827.6 60.9 %all-to-all-start.1 = ((bf16[256,8,256]{2,0,1:T(8,128)(2,1)}), bf16[256,8,256]{2,0,1:T(8,128)(2,1)S(1)}, u32[]{:S(2)}, u32[]{:S(2)}) async-start(bf16[256,8,256]{2,0,1:T(8,128)(2,1)} %bitcast.113), calls=%async_computation.1 | async-start | bytes 2097152 | tf_op jit(solution)/shard_map/all_to_all | solution.py:1496
  831.2 527.2 %all-gather.10.cloned.1.call-start = ((), (), s32[]{:S(2)}) async-start(), calls=%async_computation.4 | async-start | bytes 2506752 | tf_op jit(solution)/shard_map/all_gather | solution.py:1515
  888.5 2.3 copy-start.20
  890.7 473.5 %all-gather.12.cloned.1.call-start = ((), (), s32[]{:S(2)}) async-start(), calls=%async_computation.5 | async-start | bytes 7077888 | tf_op jit(solution)/shard_map/all_gather | solution.py:1533
  890.7 31.9 %slice-start = ((s8[6291456]{0:T(1024)(128)(4,1)}), s8[4194304]{0:T(1024)(128)(4,1)S(1)}, s32[]{:S(2)}) async-start(s8[6291456]{0:T(1024)(128)(4,1)} %bitcast.114), calls=%async_computation.6 | async-start | bytes 8388608
  890.8 31.9 %slice-start.1 = ((s8[6291456]{0:T(1024)(128)(4,1)}), s8[2097152]{0:T(1024)(128)(4,1)S(1)}, s32[]{:S(2)}) async-start(s8[6291456]{0:T(1024)(128)(4,1)} %bitcast.114), calls=%async_computation.7 | async-start | bytes 4194304
  936.4 5.0 copy-start.53
  941.3 10.9 copy-start.17
  1188.5 112.5 %copy-start.7 = (bf16[1,256,2048]{2,1,0:T(8,128)(2,1)S(1)}, bf16[1,256,2048]{2,1,0:T(8,128)(2,1)}, u32[]{:S(2)}) copy-start(bf16[1,256,2048]{2,1,0:T(8,128)(2,1)} %param.16) | copy-start | bytes 3145732
  1188.5 112.5 %copy-start.28 = (f32[1,2048]{1,0:T(1,128)S(1)}, f32[1,2048]{1,0:T(1,128)}, u32[]{:S(2)}) copy-start(f32[1,2048]{1,0:T(1,128)} %copy-done.27) | copy-start | bytes 24580
  1188.5 112.5 %copy-start.39 = (f32[256]{0:T(256)S(1)}, f32[256]{0:T(256)}, u32[]{:S(2)}) copy-start(f32[256]{0:T(256)} %copy-done.38) | copy-start | bytes 3076
  1341.3 11.9 copy-start.43
  1341.3 11.9 copy-start.2
  1341.3 11.9 copy-start.5
  1341.3 11.9 copy-start.10
  1341.3 12.0 copy-start.26
  1341.3 12.0 copy-start.35
  1341.3 12.0 copy-start.41
Sparse Core Ops, SparseCore 0:
  10.5 42.7 all-gather.5
  56.8 270.8 all-gather.7
  890.8 51.0 all-gather.9
  978.2 164.8 all-gather.11
